TPU v7x, 32 devices: a whole 2x2x4 slice. The times are simulated.
32 devices in a mesh: wide: 16 (over z, x, core), req: 2 (over y).
Axes of the slice: x: 2, y: 2, z: 4, core: 2. Of those that a mesh axis runs over, the one named last changes fastest.
Arguments:
- x_in: bfloat16 [512, 8192], P('req', 'wide'), may hold values from -6 to 6
- w_xz: bfloat16 [8192, 2, 16384], P('req', None, 'wide'), may hold values from -0.0625 to 0.0625
- w_dt: bfloat16 [8192, 256], P('req', 'wide'), may hold values from -0.0625 to 0.0625
- w_bc: bfloat16 [8192, 4096], P('req', 'wide'), may hold values from -0.0625 to 0.0625
- dt_bias: float32 [256], P('wide'), may hold values from -7 to -3
- a_log: float32 [256], P('wide'), may hold values from 0 to 2.77
- d_skip: float32 [256], P('wide'), may hold values from 0.5 to 1.5
- conv_x_w: float32 [4, 16384], P(None, 'wide'), may hold values from -3 to 3
- conv_x_b: float32 [16384], P('wide'), may hold values from -3 to 3
- conv_bc_w: float32 [4, 4096], P(None, 'wide'), may hold values from -3 to 3
- conv_bc_b: float32 [4096], P('wide'), may hold values from -3 to 3
- norm_gain: float32 [16384], P('wide'), may hold values from 0.5 to 1.5
- stretch_start: int32 [2, 2], P('req'), may hold values from 0 to 255, as said below
- prefix_len: int32 [4], P('req'), may hold values from 0 to 32768, as said below
- state_slot: int32 [4], replicated, may hold values from 0 to 15, as said below
- ssm_pool: float32 [16, 256, 64, 256], P('req', 'wide'), may hold values from -6 to 6
- conv_x_pool: bfloat16 [16, 3, 16384], P('req', None, 'wide'), may hold values from -6 to 6
- conv_bc_pool: bfloat16 [16, 3, 4096], P('req', None, 'wide'), may hold values from -6 to 6
Outputs:
- y_out: bfloat16 [512, 16384], P('req', 'wide')
- new_state: float32 [4, 256, 64, 256], P('req', 'wide')
Inputs may be any that keep to these rules, and one draw needn't show every extreme that they name: `stretch_start`: each row is 0 first and rises strictly; the 2 requests of an index of req cover its 256 tokens in order. `prefix_len`: zero means no cached state; in every draw some request has zero and one has 32768. `state_slot`: distinct slots; slot s is owned by index s // 8 of req; owners hold very uneven numbers of the requested slots.
All inputs are finite; a program needn't handle non-finite values.
Results may differ from a plain program's by a relative error of at most 0.014.
Values may be sent and summed in bfloat16 or wider, within the bound.
No kernel may reach another device: no remote copies, remote signals or barrier semaphores. Data moves between devices by JAX's collectives and lax.ppermute only.
A program may use at most 192 MiB of HBM per device.

v0:
```python
import jax
import jax.numpy as jnp
from jax import lax
from jax.sharding import PartitionSpec as P

HEADS = 256
HEAD_DIM = 64
GROUPS = 8


NORM_EPS = 1e-05


def partner_2(block, axis, bit):
    count = lax.axis_size(axis)
    route = []
    for low in range(count):
        high = low | 1 << bit
        if high != low and high < count:
            route += [(low, high), (high, low)]
    return lax.ppermute(block, axis, route)


def segments(starts, count_tok):
    position = jnp.arange(count_tok, dtype=jnp.int32)
    seg_ids = jnp.sum((position[:, None] >= starts[None, :]).astype(jnp.int32), 1) - 1
    member = seg_ids[:, None] == jnp.arange(starts.shape[0], dtype=jnp.int32)[None, :]
    offset = position - jnp.sum(jnp.where(member, starts[None, :], 0), 1)
    same_req = seg_ids[:, None] == seg_ids[None, :]
    causal = position[:, None] >= position[None, :]
    return (member.astype(jnp.float32), offset, (same_req & causal).astype(jnp.float32))


def causal_conv(inputs, cache, kernel, bias, member, offset):
    kernel_len = kernel.shape[0]
    count_tok, channels = inputs.shape
    count_req = cache.shape[0]
    history = jnp.dot(
        member,
        cache.reshape(count_req, (kernel_len - 1) * channels),
        precision=lax.Precision.HIGHEST,
    )
    history = history.reshape(count_tok, kernel_len - 1, channels)
    values = inputs.astype(jnp.float32)
    total = bias[None, :] + kernel[kernel_len - 1][None, :] * values
    for lag_step in range(1, kernel_len):
        shifted = jnp.concatenate(
            [jnp.zeros((lag_step, channels), jnp.float32), values[: count_tok - lag_step]], 0
        )
        earlier = jnp.zeros((count_tok, channels), jnp.float32)
        for slot_place in range(kernel_len - 1):
            hit_place = offset - lag_step + kernel_len - 1 == slot_place
            earlier = earlier + jnp.where(hit_place[:, None], history[:, slot_place], 0.0)
        chosen = jnp.where((offset >= lag_step)[:, None], shifted, earlier)
        total = total + kernel[kernel_len - 1 - lag_step][None, :] * chosen
    return jax.nn.silu(total).astype(jnp.bfloat16)


def mixer(inputs, dt_raw, b_maps, c_maps, start_state, member, mask, dt_bias, a_log, d_skip):
    high = lax.Precision.HIGHEST
    step_size = jax.nn.softplus(dt_raw.astype(jnp.float32) + dt_bias[None, :])
    decay_rate = step_size * (-jnp.exp(a_log))[None, :]
    cumulative = jnp.dot(mask, decay_rate, precision=high)
    scores = jnp.dot(c_maps, b_maps.T, preferred_element_type=jnp.float32)
    spread_gap = jnp.minimum(cumulative.T[:, :, None] - cumulative.T[:, None, :], 0.0)
    decay = jnp.exp(spread_gap) * mask[None] * step_size.T[:, None, :]
    weights = (decay * scores[None]).astype(jnp.bfloat16)
    intra = jnp.einsum("hts,shp->thp", weights, inputs, preferred_element_type=jnp.float32)
    values = inputs.astype(jnp.float32)
    from_state = jnp.einsum(
        "tn,jhpn->jthp", c_maps.astype(jnp.float32), start_state, precision=high
    )
    from_state = jnp.einsum("tj,jthp->thp", member, from_state, precision=high)
    from_state = from_state * jnp.exp(cumulative)[:, :, None]
    result = intra + from_state + d_skip[None, :, None] * values
    ends = jnp.dot(member.T, decay_rate, precision=high)
    to_end = jnp.exp(jnp.dot(member, ends, precision=high) - cumulative)
    carried = (to_end * step_size)[:, :, None] * values
    split_req = (member.T[:, :, None, None] * carried[None]).astype(jnp.bfloat16)
    fresh = jnp.einsum("jthp,tn->jhpn", split_req, b_maps, preferred_element_type=jnp.float32)
    final_state = jnp.exp(ends)[:, :, None, None] * start_state + fresh
    return (result, final_state)


def on_device(
    x_in,
    w_xz,
    w_dt,
    w_bc,
    dt_bias,
    a_log,
    d_skip,
    conv_x_w,
    conv_x_b,
    conv_bc_w,
    conv_bc_b,
    norm_gain,
    stretch_start,
    prefix_len,
    state_slot,
    ssm_pool,
    conv_x_pool,
    conv_bc_pool,
):
    features = lax.all_gather(x_in, "wide", axis=1, tiled=True)
    count_tok = features.shape[0]
    local_width = w_xz.shape[2]
    local_heads = w_dt.shape[1]
    acc_xz = jnp.einsum(
        "td,dkc->tkc",
        features,
        lax.all_gather(w_xz, "req", axis=0, tiled=True),
        preferred_element_type=jnp.float32,
    )
    acc_dt = jnp.dot(
        features,
        lax.all_gather(w_dt, "req", axis=0, tiled=True),
        preferred_element_type=jnp.float32,
    )
    acc_bc = jnp.dot(
        features,
        lax.all_gather(w_bc, "req", axis=0, tiled=True),
        preferred_element_type=jnp.float32,
    )
    proj_xz = acc_xz.astype(jnp.bfloat16)
    dt_raw = acc_dt.astype(jnp.bfloat16)
    bc_raw = acc_bc.astype(jnp.bfloat16)
    owner = lax.axis_index("req")
    req_count = lax.axis_size("req")
    slot_count = conv_x_pool.shape[0]
    local_slot = jnp.clip(state_slot - owner * slot_count, 0, slot_count - 1)
    is_owner = state_slot // slot_count == owner
    send_ssm = jnp.where(is_owner[:, None, None, None], ssm_pool[local_slot], 0.0)
    send_cx = jnp.where(is_owner[:, None, None], conv_x_pool[local_slot].astype(jnp.float32), 0.0)
    send_cbc = jnp.where(is_owner[:, None, None], conv_bc_pool[local_slot].astype(jnp.float32), 0.0)
    got_ssm, got_cx, got_cbc = (
        lax.all_to_all(send_ssm, "req", split_axis=0, concat_axis=0, tiled=True),
        lax.all_to_all(send_cx, "req", split_axis=0, concat_axis=0, tiled=True),
        lax.all_to_all(send_cbc, "req", split_axis=0, concat_axis=0, tiled=True),
    )
    group_reqs = prefix_len.shape[0]
    has_cache = (prefix_len > 0).astype(jnp.float32)
    start_state = (
        jnp.sum(got_ssm.reshape((req_count, group_reqs) + got_ssm.shape[1:]), 0)
        * has_cache[:, None, None, None]
    )
    cache_x = (
        jnp.sum(got_cx.reshape((req_count, group_reqs) + got_cx.shape[1:]), 0)
        * has_cache[:, None, None]
    )
    cache_bc = (
        jnp.sum(got_cbc.reshape((req_count, group_reqs) + got_cbc.shape[1:]), 0)
        * has_cache[:, None, None]
    )
    member, offset, mask = segments(stretch_start[0], count_tok)
    x_conv = causal_conv(proj_xz[:, 1], cache_x, conv_x_w, conv_x_b, member, offset)
    bc_conv = causal_conv(bc_raw, cache_bc, conv_bc_w, conv_bc_b, member, offset)
    wide_index = lax.axis_index("wide")
    group_span = lax.axis_size("wide") // GROUPS
    bit_total = group_span.bit_length() - 1
    joined = bc_conv
    for bit_index in range(bit_total):
        partner = partner_2(joined, "wide", bit_index)
        upper_half = wide_index // (1 << bit_index) % 2 == 1
        joined = jnp.where(
            upper_half, jnp.concatenate([partner, joined], 1), jnp.concatenate([joined, partner], 1)
        )
    state_width = joined.shape[1] // 2
    b_maps = joined[:, :state_width]
    c_maps = joined[:, state_width:]
    head_width = local_width // local_heads
    result, final_state = mixer(
        x_conv.reshape(count_tok, local_heads, head_width),
        dt_raw,
        b_maps,
        c_maps,
        start_state,
        member,
        mask,
        dt_bias,
        a_log,
        d_skip,
    )
    gated = result.reshape(count_tok, local_width) * jax.nn.silu(proj_xz[:, 0].astype(jnp.float32))
    square_sum = jnp.sum(gated * gated, 1)
    for bit_index in range(bit_total):
        square_sum = square_sum + partner_2(square_sum, "wide", bit_index)
    mean_sq = square_sum / (HEADS * HEAD_DIM // GROUPS)
    normed = gated * lax.rsqrt(mean_sq + NORM_EPS)[:, None] * norm_gain[None, :]
    return (normed.astype(jnp.bfloat16), final_state)


def solution(mesh):
    in_specs = (
        P("req", "wide"),
        P("req", None, "wide"),
        P("req", "wide"),
        P("req", "wide"),
        P("wide"),
        P("wide"),
        P("wide"),
        P(None, "wide"),
        P("wide"),
        P(None, "wide"),
        P("wide"),
        P("wide"),
        P("req", None),
        P("req"),
        P(),
        P("req", "wide", None, None),
        P("req", None, "wide"),
        P("req", None, "wide"),
    )
    out_specs = (P("req", "wide"), P("req", "wide", None, None))
    return jax.shard_map(
        on_device, mesh=mesh, in_specs=in_specs, out_specs=out_specs, check_vma=False
    )
```

profile of v0, /device:TPU:0, one launch (start us, length us, event | category | flops | bytes accessed | tf_op | source)
XLA Modules:
  0.0 567.9 jit_solution(18292588567760595455)
XLA Ops:
  8.7 16.7 %copy.42 = bf16[4096,2,1024]{2,0,1:T(8,128)(2,1)} copy(bf16[4096,2,1024]{2,1,0:T(2,128)(2,1)} %param.19) | data formatting | bytes 33554432 | tf_op args[1]
  27.4 4.2 all-to-all-start.1
  32.3 6.2 %gather_fusion.2 = f32[4,16,64,256]{3,2,1,0:T(8,128)} fusion(f32[8,16,64,256]{3,2,1,0:T(8,128)} %param.33, s32[1024]{0:T(1024)S(1)} %pad_clamp_fusion), kind=kCustom, calls=%fused_computation.2 | custom fusion | bytes 8388624 | tf_op jit(solution)/shard_map/gather | solution.py:133
  38.8 4.9 broadcast_select_fusion
  44.4 3.3 all-to-all-start
  47.8 10.4 %all_gather.14 = bf16[8192,16]{0,1:T(8,128)(2,1)S(1)} all-gather(bf16[4096,16]{0,1:T(8,128)(2,1)S(1)} %copy-done.5), channel_id=1, replica_groups=mesh['wide'=16,'req'=2] {'req'}, dimensions={0}, use_global_device_ids=true | all-gather | bytes 393216 | tf_op jit(solution)/shard_map/all_gather | solution.py:117
  58.2 5.8 %all-to-all-start.2 = ((f32[4,16,64,256]{3,2,1,0:T(8,128)}), f32[4,16,64,256]{3,2,1,0:T(8,128)}, u32[]{:S(2)}, u32[]{:S(2)}) async-start(f32[4,16,64,256]{3,2,1,0:T(8,128)} %broadcast_select_fusion), calls=%async_computation.2 | async-start | bytes 8388608 | tf_op jit(solution)/shard_map/all_to_all | solution.py:137
  65.6 3.1 fusion.61
  68.8 48.8 %all-to-all-done.2 = f32[4,16,64,256]{3,2,1,0:T(8,128)} async-done(((f32[4,16,64,256]{3,2,1,0:T(8,128)}), f32[4,16,64,256]{3,2,1,0:T(8,128)}, u32[]{:S(2)}, u32[]{:S(2)}) %all-to-all-start.2) | async-done | bytes 4194336 | tf_op jit(solution)/shard_map/all_to_all | solution.py:137
  117.5 2.8 reduce_sum.64
  120.4 13.3 %all-gather.4.cloned.1.call-done = bf16[256,8192]{1,0:T(8,128)(2,1)} async-done(((bf16[256,512]{1,0:T(8,128)(2,1)}), bf16[256,8192]{1,0:T(8,128)(2,1)}) %all-gather.4.cloned.1.call-update) | async-done | bytes 4194320 | tf_op jit(solution)/shard_map/all_gather | solution.py:105
  133.7 5.3 fusion.18
  139.9 1.2 compare_select_fusion
  142.6 1.2 fusion.10
  143.8 1.3 fusion.3
  146.0 376.0 %all-gather.6.cloned.1.call-done = bf16[8192,2,1024]{2,0,1:T(8,128)(2,1)} async-done(((bf16[4096,2,1024]{2,0,1:T(8,128)(2,1)}), bf16[8192,2,1024]{2,0,1:T(8,128)(2,1)}) %all-gather.6.cloned.1.call-update) | async-done | bytes 33554448 | tf_op jit(solution)/shard_map/all_gather | solution.py:112
  522.0 16.2 %fusion.12 = bf16[256,2,1024]{2,0,1:T(8,128)(2,1)S(1)} fusion(bf16[8192,2,1024]{2,0,1:T(8,128)(2,1)} %all-gather.6.cloned.1.call-done, bf16[256,8192]{1,0:T(8,128)(2,1)} %all-gather.4.cloned.1.call-done), kind=kOutput, calls=%fused_computation.20 | convolution fusion | flops 8590458880 | bytes 38797312 | tf_op jit(solution)/shard_map/td,dkc->tkc/dot_general | solution.py:109
  538.3 1.2 slice_convert_fusion
  542.7 2.5 copy.52
  545.3 4.9 multiply_convert_fusion.10
  550.1 2.0 copy.46
  552.2 4.4 multiply_reduce_fusion
  556.7 1.9 multiply_add_fusion
  558.6 1.6 copy.51
  (86 shorter events, 14.5 us)
Async XLA Ops:
  7.2 24.5 %copy-start = (bf16[8,3,1024]{2,0,1:T(8,128)(2,1)S(1)}, bf16[8,3,1024]{2,0,1:T(8,128)(2,1)}, u32[]{:S(2)}) copy-start(bf16[8,3,1024]{2,0,1:T(8,128)(2,1)} %param.34) | copy-start | bytes 147460
  7.2 113.2 %all-gather.8.cloned.1.call-start = ((), (), s32[]{:S(2)}) async-start(), calls=%async_computation.5 | async-start | bytes 6291456 | tf_op jit(solution)/shard_map/all_gather | solution.py:122
  7.9 125.8 %all-gather.4.cloned.1.call-start = ((), (), s32[]{:S(2)}) async-start(), calls=%async_computation.3 | async-start | bytes 4456448 | tf_op jit(solution)/shard_map/all_gather | solution.py:105
  8.7 513.4 %all-gather.6.cloned.1.call-start = ((), (), s32[]{:S(2)}) async-start(), calls=%async_computation.4 | async-start | bytes 50331648 | tf_op jit(solution)/shard_map/all_gather | solution.py:112
  25.4 0.7 copy-start.4
  27.4 17.0 %all-to-all-start.1 = ((f32[4,3,256]{2,1,0:T(4,128)}), f32[4,3,256]{2,1,0:T(4,128)S(1)}, u32[]{:S(2)}, u32[]{:S(2)}) async-start(f32[4,3,256]{2,1,0:T(4,128)} %copy.47), calls=%async_computation.1 | async-start | bytes 32768 | tf_op jit(solution)/shard_map/all_to_all | solution.py:139
  32.3 6.2 %copy-start.12 = (s32[1,2]{1,0:T(1,128)S(1)}, s32[1,2]{1,0:T(1,128)}, u32[]{:S(2)}) copy-start(s32[1,2]{1,0:T(1,128)} %param.30) | copy-start | bytes 28
  32.3 6.4 %copy-start.9 = (f32[4,256]{1,0:T(4,128)S(1)}, f32[4,256]{1,0:T(4,128)}, u32[]{:S(2)}) copy-start(f32[4,256]{1,0:T(4,128)} %param.27) | copy-start | bytes 12292
  38.8 4.9 copy-start.14
  38.8 8.9 %copy-start.5 = (bf16[4096,16]{0,1:T(8,128)(2,1)S(1)}, bf16[4096,16]{0,1:T(8,128)(2,1)}, u32[]{:S(2)}) copy-start(bf16[4096,16]{0,1:T(8,128)(2,1)} %param.20) | copy-start | bytes 393220
  44.4 13.8 %all-to-all-start = ((f32[4,3,1024]{2,1,0:T(4,128)}), f32[4,3,1024]{2,1,0:T(4,128)S(1)}, u32[]{:S(2)}, u32[]{:S(2)}) async-start(f32[4,3,1024]{2,1,0:T(4,128)} %copy.43), calls=%async_computation | async-start | bytes 131072 | tf_op jit(solution)/shard_map/all_to_all | solution.py:138
  58.2 5.8 %copy-start.15 = (f32[16]{0:T(128)S(1)}, f32[16]{0:T(128)}, u32[]{:S(2)}) copy-start(f32[16]{0:T(128)} %param.23) | copy-start | bytes 196
  58.2 5.8 %copy-start.6 = (f32[4,1024]{1,0:T(4,128)S(1)}, f32[4,1024]{1,0:T(4,128)}, u32[]{:S(2)}) copy-start(f32[4,1024]{1,0:T(4,128)} %param.25) | copy-start | bytes 49156
  58.2 59.3 %all-to-all-start.2 = ((f32[4,16,64,256]{3,2,1,0:T(8,128)}), f32[4,16,64,256]{3,2,1,0:T(8,128)}, u32[]{:S(2)}, u32[]{:S(2)}) async-start(f32[4,16,64,256]{3,2,1,0:T(8,128)} %broadcast_select_fusion), calls=%async_computation.2 | async-start | bytes 8388608 | tf_op jit(solution)/shard_map/all_to_all | solution.py:137
  120.4 18.7 %copy-start.11 = (f32[256]{0:T(256)S(1)}, f32[256]{0:T(256)}, u32[]{:S(2)}) copy-start(f32[256]{0:T(256)} %param.28) | copy-start | bytes 3076
  120.4 19.5 %copy-start.10 = (f32[16]{0:T(128)S(1)}, f32[16]{0:T(128)}, u32[]{:S(2)}) copy-start(f32[16]{0:T(128)} %param.22) | copy-start | bytes 196
  133.7 6.2 %copy-start.2 = (bf16[256,8192]{1,0:T(8,128)(2,1)S(1)}, bf16[256,8192]{1,0:T(8,128)(2,1)}, u32[]{:S(2)}) copy-start(bf16[256,8192]{1,0:T(8,128)(2,1)} %all-gather.4.cloned.1.call-done) | copy-start | bytes 12582916
  139.6 2.9 collective-permute-start
  539.5 5.8 %copy-start.7 = (f32[1024]{0:T(1024)S(1)}, f32[1024]{0:T(1024)}, u32[]{:S(2)}) copy-start(f32[1024]{0:T(1024)} %param.26) | copy-start | bytes 12292
  545.3 6.9 %copy-start.16 = (f32[16]{0:T(128)S(1)}, f32[16]{0:T(128)}, u32[]{:S(2)}) copy-start(f32[16]{0:T(128)} %param.24) | copy-start | bytes 196
  552.2 4.4 copy-start.3
  556.6 3.6 copy-start.8
  556.6 3.6 collective-permute-start.1
  556.7 4.6 copy-start.1
  (1 other events, 0.7 us)
Sparse Core Ops, SparseCore 0:
  9.6 69.2 all-gather.7
  81.0 52.7 all-gather.3
  135.3 386.7 all-gather.5
where the time goes:
time: 569 us; the launch traced here: 568 us
  waiting for transfers between devices  439 us (77%)
  matrix products  36.2 us (6%)
  local copies, waits for them, and re-layouts  35.6 us (6%)
  other arithmetic  18.4 us (3%)
  between operations  14.1 us (2%)
  starting transfers between devices  13.7 us (2%)
  blocking collectives  10.4 us (2%)
    all_gather x1, waiting for transfers between devices, on_device(): lax.all_gather(w_xz, 'req', axis=0, tiled=True)  376 us
    all_to_all x1, waiting for transfers between devices, on_device(): lax.all_to_all(send_ssm, 'req', split_axis=0, concat_axis=0, tiled=True)  48.8 us
    unnamed x37, local copies, waits for them, and re-layouts  17.5 us
    dot_general x1, matrix products, on_device(): jnp.einsum('td,dkc->tkc', features, lax.all_gather(w_xz, 'req', axis=0, t...  16.2 us
    all_gather x1, waiting for transfers between devices, on_device(): features = lax.all_gather(x_in, 'wide', axis=1, tiled=True)  13.3 us
  transfers between devices with their start and end apart: 8, of which 3 were waited for; matrix products, arithmetic and copies ran while one was open for 9% of the time, Pallas kernels for 0%

commit v1 on v0

v1 whole, which is shorter than its diff:
```python
import jax
import jax.numpy as jnp
from jax import lax
from jax.sharding import PartitionSpec as P

GROUPS = 8
NORM_EPS = 1e-05
F32 = jnp.float32
BF16 = jnp.bfloat16


def partner_2(block, axis, bit):
    count = lax.axis_size(axis)
    route = []
    for low in range(count):
        high = low | 1 << bit
        if high != low and high < count:
            route += [(low, high), (high, low)]
    return lax.ppermute(block, axis, route)


def shift_req(block, step):
    count = lax.axis_size("req")
    return lax.ppermute(block, "req", [(i, (i + step) % count) for i in range(count)])


def segments(starts, count_tok):
    position = jnp.arange(count_tok, dtype=jnp.int32)
    seg_ids = jnp.sum((position[:, None] >= starts[None, :]).astype(jnp.int32), 1) - 1
    member = seg_ids[:, None] == jnp.arange(starts.shape[0], dtype=jnp.int32)[None, :]
    offset = position - jnp.sum(jnp.where(member, starts[None, :], 0), 1)
    same_req = seg_ids[:, None] == seg_ids[None, :]
    causal = position[:, None] >= position[None, :]
    return (member.astype(F32), offset, (same_req & causal).astype(F32))


def causal_conv(inputs, cache, kernel, bias, member, offset):
    kernel_len = kernel.shape[0]
    count_tok, channels = inputs.shape
    count_req = cache.shape[0]
    history = jnp.dot(
        member.astype(BF16),
        cache.astype(BF16).reshape(count_req, (kernel_len - 1) * channels),
        preferred_element_type=F32,
    )
    history = history.reshape(count_tok, kernel_len - 1, channels)
    values = inputs.astype(F32)
    total = bias[None, :] + kernel[kernel_len - 1][None, :] * values
    for lag_step in range(1, kernel_len):
        shifted = jnp.concatenate(
            [jnp.zeros((lag_step, channels), F32), values[: count_tok - lag_step]], 0
        )
        earlier = jnp.zeros((count_tok, channels), F32)
        for slot_place in range(kernel_len - 1):
            hit_place = offset - lag_step + kernel_len - 1 == slot_place
            earlier = earlier + jnp.where(hit_place[:, None], history[:, slot_place], 0.0)
        chosen = jnp.where((offset >= lag_step)[:, None], shifted, earlier)
        total = total + kernel[kernel_len - 1 - lag_step][None, :] * chosen
    return jax.nn.silu(total).astype(BF16)


def mixer(inputs, dt_raw, b_maps, c_maps, start_state, member, mask, dt_bias, a_log, d_skip):
    high = lax.Precision.HIGHEST
    step_size = jax.nn.softplus(dt_raw.astype(F32) + dt_bias[None, :])
    decay_rate = step_size * (-jnp.exp(a_log))[None, :]
    cumulative = jnp.dot(mask, decay_rate, precision=high)
    scores = jnp.dot(c_maps, b_maps.T, preferred_element_type=F32)
    spread_gap = jnp.minimum(cumulative.T[:, :, None] - cumulative.T[:, None, :], 0.0)
    decay = jnp.exp(spread_gap) * mask[None] * step_size.T[:, None, :]
    weights = (decay * scores[None]).astype(BF16)
    intra = jnp.einsum("hts,shp->thp", weights, inputs, preferred_element_type=F32)
    values = inputs.astype(F32)
    from_state = jnp.einsum(
        "tn,jhpn->jthp", c_maps, start_state.astype(BF16), preferred_element_type=F32
    )
    from_state = jnp.sum(member.T[:, :, None, None] * from_state, 0)
    from_state = from_state * jnp.exp(cumulative)[:, :, None]
    result = intra + from_state + d_skip[None, :, None] * values
    ends = jnp.dot(member.T, decay_rate, precision=high)
    to_end = jnp.exp(jnp.dot(member, ends, precision=high) - cumulative)
    carried = (to_end * step_size)[:, :, None] * values
    split_req = (member.T[:, :, None, None] * carried[None]).astype(BF16)
    fresh = jnp.einsum("jthp,tn->jhpn", split_req, b_maps, preferred_element_type=F32)
    final_state = jnp.exp(ends)[:, :, None, None] * start_state + fresh
    return (result, final_state)


def spread_plan():
    far, across = [], []
    for z in range(4):
        for rest in range(4):
            for r in range(2):
                place = (z * 4 + rest) * 2 + r
                if z // 2 == r:
                    other = (z + 2) % 4
                    far.append((place, (other * 4 + rest) * 2 + r))
                if z // 2 != r:
                    across.append((place, place ^ 1))
    return far, across


def spread(block, far):
    wide_index = lax.axis_index("wide")
    axes = ("wide", "req")
    moved = lax.ppermute(block, axes, far)
    block = jnp.where(wide_index // 8 == lax.axis_index("req"), block, moved)
    tokens, width = block.shape
    for bit in (2, 1, 0):
        other = partner_2(block, "wide", bit)
        upper = (wide_index >> bit) % 2 == 1
        if bit:
            block = jnp.where(
                upper, jnp.concatenate([other, block], 1), jnp.concatenate([block, other], 1)
            )
    mine, other = (half.reshape(tokens, 2, 2, width) for half in (block, other))
    pair = jnp.stack([jnp.where(upper, other, mine), jnp.where(upper, mine, other)], 1)
    return pair.transpose(0, 3, 2, 1, 4).reshape(tokens, 8 * width)


def features_of(x_in):
    req_count = lax.axis_size("req")
    wide_count = lax.axis_size("wide")
    me = lax.axis_index("req")
    if req_count == 2 and wide_count == 16:
        far, across = spread_plan()
        crossed = lax.ppermute(x_in, ("wide", "req"), across)
        return [spread(x_in, far), spread(crossed, far)]
    own = lax.all_gather(x_in, "wide", axis=1, tiled=True)
    parts = own.reshape(own.shape[0], req_count, own.shape[1] // req_count).transpose(1, 0, 2)
    got = lax.all_to_all(parts, "req", split_axis=0, concat_axis=0, tiled=True)
    return [
        lax.dynamic_index_in_dim(got, (me + step) % req_count, 0, False)
        for step in range(req_count)
    ]


def on_device(
    x_in,
    w_xz,
    w_dt,
    w_bc,
    dt_bias,
    a_log,
    d_skip,
    conv_x_w,
    conv_x_b,
    conv_bc_w,
    conv_bc_b,
    norm_gain,
    stretch_start,
    prefix_len,
    state_slot,
    ssm_pool,
    conv_x_pool,
    conv_bc_pool,
):
    count_tok = x_in.shape[0]
    local_width = w_xz.shape[2]
    local_heads = w_dt.shape[1]
    state_part = w_bc.shape[1]
    me = lax.axis_index("req")
    req_count = lax.axis_size("req")
    slot_count = ssm_pool.shape[0]
    group_reqs = prefix_len.shape[0]

    conv_pool = jnp.concatenate([conv_x_pool, conv_bc_pool], 2)

    def of_request(pool, request):
        slot = jnp.clip(state_slot[request] - me * slot_count, 0, slot_count - 1)
        return lax.dynamic_index_in_dim(pool, slot, 0, False)

    got_state = [[] for _ in range(group_reqs)]
    got_conv = [[] for _ in range(group_reqs)]
    for step in range(1, req_count):
        to = (me + step) % req_count
        for j in range(group_reqs):
            got_conv[j].append(shift_req(of_request(conv_pool, to * group_reqs + j), step))
    for step in range(1, req_count):
        to = (me + step) % req_count
        for j in range(group_reqs):
            block = of_request(ssm_pool, to * group_reqs + j).astype(BF16)
            got_state[j].append(shift_req(block, step))
    start_state, cache = [], []
    for j in range(group_reqs):
        request = me * group_reqs + j
        came_from = (me - state_slot[request] // slot_count) % req_count
        state = of_request(ssm_pool, request)
        conv = of_request(conv_pool, request)
        for step in range(1, req_count):
            state = jnp.where(came_from == step, got_state[j][step - 1].astype(F32), state)
            conv = jnp.where(came_from == step, got_conv[j][step - 1], conv)
        live = prefix_len[j] > 0
        start_state.append(jnp.where(live, state, 0.0))
        cache.append(jnp.where(live, conv, 0))
    start_state = jnp.stack(start_state)
    cache = jnp.stack(cache)

    w_pair = lax.optimization_barrier(jnp.transpose(w_xz, (1, 0, 2)))
    w_map = jnp.concatenate([w_bc, w_dt], 1)
    features = features_of(x_in)
    sums = {}
    for name, weight in (("map", w_map), ("xr", w_pair[1]), ("z", w_pair[0])):
        total = None
        for step in range(1, req_count):
            part = jnp.dot(features[step], weight, preferred_element_type=F32).astype(BF16)
            came = shift_req(part, step).astype(F32)
            total = came if total is None else total + came
        sums[name] = total
    for name, weight in (("map", w_map), ("xr", w_pair[1]), ("z", w_pair[0])):
        own = jnp.dot(features[0], weight, preferred_element_type=F32)
        sums[name] = (own if sums[name] is None else own + sums[name]).astype(BF16)

    bc_raw = sums["map"][:, :state_part]
    dt_raw = sums["map"][:, state_part:]
    member, offset, mask = segments(stretch_start[0], count_tok)
    bc_conv = causal_conv(bc_raw, cache[:, :, local_width:], conv_bc_w, conv_bc_b, member, offset)
    x_conv = causal_conv(sums["xr"], cache[:, :, :local_width], conv_x_w, conv_x_b, member, offset)
    wide_index = lax.axis_index("wide")
    group_span = lax.axis_size("wide") // GROUPS
    bit_total = group_span.bit_length() - 1
    joined = bc_conv
    for bit_index in range(bit_total):
        partner = partner_2(joined, "wide", bit_index)
        upper_half = wide_index // (1 << bit_index) % 2 == 1
        joined = jnp.where(
            upper_half, jnp.concatenate([partner, joined], 1), jnp.concatenate([joined, partner], 1)
        )
    state_width = joined.shape[1] // 2
    b_maps = joined[:, :state_width]
    c_maps = joined[:, state_width:]
    head_width = local_width // local_heads
    result, final_state = mixer(
        x_conv.reshape(count_tok, local_heads, head_width),
        dt_raw,
        b_maps,
        c_maps,
        start_state,
        member,
        mask,
        dt_bias,
        a_log,
        d_skip,
    )
    gated = result.reshape(count_tok, local_width) * jax.nn.silu(sums["z"].astype(F32))
    square_sum = jnp.sum(gated * gated, 1)
    for bit_index in range(bit_total):
        square_sum = square_sum + partner_2(square_sum, "wide", bit_index)
    mean_sq = square_sum / (local_width * group_span)
    normed = gated * lax.rsqrt(mean_sq + NORM_EPS)[:, None] * norm_gain[None, :]
    return (normed.astype(BF16), final_state)


def solution(mesh):
    in_specs = (
        P("req", "wide"),
        P("req", None, "wide"),
        P("req", "wide"),
        P("req", "wide"),
        P("wide"),
        P("wide"),
        P("wide"),
        P(None, "wide"),
        P("wide"),
        P(None, "wide"),
        P("wide"),
        P("wide"),
        P("req", None),
        P("req"),
        P(),
        P("req", "wide", None, None),
        P("req", None, "wide"),
        P("req", None, "wide"),
    )
    out_specs = (P("req", "wide"), P("req", "wide", None, None))
    return jax.shard_map(
        on_device, mesh=mesh, in_specs=in_specs, out_specs=out_specs, check_vma=False
    )
```

time: 569 us -> 140 us (0.25)
  waiting for transfers between devices: 439 us -> 33.6 us
  starting transfers between devices: 13.7 us -> 29 us
  blocking collectives: 10.4 us -> 0 us
  matrix products: 36.2 us -> 26.9 us
  other arithmetic: 18.4 us -> 9.41 us
    all_gather x3 -> x0, waiting for transfers between devices: 389 us -> none  [the longest x1 376 us: on_device(): lax.all_gather(w_xz, 'req', axis=0, tiled=True)]
    all_to_all x3 -> x0, waiting for transfers between devices: 48.8 us -> none  [the longest x1 48.8 us: on_device(): lax.all_to_all(send_ssm, 'req', split_axis=0, concat_axis=0, tiled=True)]
    ppermute x0 -> x10, starting transfers between devices: none -> 23.9 us  [the longest x7 13.1 us: shift_req(): lax.ppermute(block, 'req', [(i, (i + step) % count) for i in range(count)])]
    ppermute x2 -> x8, waiting for transfers between devices: 0.01 us -> 16.8 us  [partner_2(): return lax.ppermute(block, axis, route)]
    ppermute x0 -> x10, waiting for transfers between devices: none -> 16.7 us  [the longest x2 10.2 us: spread(): moved = lax.ppermute(block, axes, far)]
    all_to_all x3 -> x0, starting transfers between devices: 13.3 us -> none  [the longest x1 5.77 us: on_device(): lax.all_to_all(send_ssm, 'req', split_axis=0, concat_axis=0, tiled=True)]
    all_gather x1 -> x0, blocking collectives: 10.4 us -> none  [on_device(): lax.all_gather(w_dt, 'req', axis=0, tiled=True)]
    dot_general x9 -> x12, matrix products: 34.9 us -> 26.2 us  [the longest x3 10.8 us: on_device(): own = jnp.dot(features[0], weight, preferred_element_type=F32)]
  transfers between devices with their start and end apart: 8 -> 18, of which waited for: 3 -> 6; matrix products, arithmetic and copies ran while one was open for 9% -> 35% of each run, Pallas kernels for 0% -> 0%
where the time goes in v1:
time: 140 us
  waiting for transfers between devices  33.6 us (24%)
  local copies, waits for them, and re-layouts  30.6 us (22%)
  starting transfers between devices  29 us (21%)
  matrix products  26.9 us (19%)
  between operations  10.3 us (7%)
  other arithmetic  9.41 us (7%)
    unnamed x40, local copies, waits for them, and re-layouts  23.1 us
    ppermute x8, waiting for transfers between devices, partner_2(): return lax.ppermute(block, axis, route)  16.8 us
    ppermute x7, starting transfers between devices, shift_req(): lax.ppermute(block, 'req', [(i, (i + step) % count) for i in range(count)])  13.1 us
    dot_general x3, matrix products, on_device(): own = jnp.dot(features[0], weight, preferred_element_type=F32)  10.8 us
    ppermute x2, waiting for transfers between devices, spread(): moved = lax.ppermute(block, axes, far)  10.2 us
    ppermute x2, starting transfers between devices, spread(): moved = lax.ppermute(block, axes, far)  9.58 us
    dot_general x3, matrix products, on_device(): jnp.dot(features[step], weight, preferred_element_type=F32).astype(BF16)  6.72 us
    ppermute x7, waiting for transfers between devices, shift_req(): lax.ppermute(block, 'req', [(i, (i + step) % count) for i in range(count)])  6.51 us
  transfers between devices with their start and end apart: 18, of which 6 were waited for; matrix products, arithmetic and copies ran while one was open for 35% of the time, Pallas kernels for 0%

profile of v1, /device:TPU:0, one launch (start us, length us, event | category | flops | bytes accessed | tf_op | source)
XLA Modules:
  0.0 139.8 jit_solution(6714196757801223497)
XLA Ops:
  3.1 8.1 %collective-permute-start = (bf16[256,512]{0,1:T(8,128)(2,1)S(1)}, bf16[256,512]{0,1:T(8,128)(2,1)S(1)}, u32[]{:S(2)}, u32[]{:S(2)}) collective-permute-start(bf16[256,512]{0,1:T(8,128)(2,1)S(1)} %copy.41), channel_id=1, source_target_pairs={{0,16},{2,18},{4,20},{6,22},{8,24},{10,26},{12,28},{14,30},{17,1},... | collective-permute-start | bytes 786440 | tf_op jit(solution)/shard_map/ppermute | solution.py:105
  16.9 2.0 %collective-permute-start.11 = (bf16[3,1280]{1,0:T(4,128)(2,1)S(1)}, bf16[3,1280]{1,0:T(4,128)(2,1)S(1)}, u32[]{:S(2)}, u32[]{:S(2)}) collective-permute-start(bf16[3,1280]{1,0:T(4,128)(2,1)S(1)} %bitcast.200), channel_id=1, source_target_pairs={{0,1},{1,0},{2,3},{3,2},{4,5},{5,4},{6,7},{7,6},{8,9},{9,8},{10,11... | collective-permute-start | bytes 23048 | tf_op jit(solution)/shard_map/ppermute | solution.py:24
  18.9 1.7 %fusion.34 = (bf16[16,64,256]{2,1,0:T(8,128)(2,1)S(1)}, bf16[16,64,256]{2,1,0:T(8,128)(2,1)S(1)}) fusion(f32[8,16,64,256]{3,2,1,0:T(8,128)} %param.33, s32[]{:T(128)S(6)} %min.23, s32[]{:T(128)S(6)} %min.25), kind=kLoop, calls=%fused_computation.70 | loop fusion | bytes 2097160 | tf_op jit(solution)/shard_map/convert_element_type | solution.py:181
  27.6 16.5 %copy.74 = bf16[4096,2,1024]{2,0,1:T(8,128)(2,1)} copy(bf16[4096,2,1024]{2,1,0:T(2,128)(2,1)} %param.19) | data formatting | bytes 33554432 | tf_op args[1]
  45.9 2.0 %collective-permute-start.15 = (bf16[16,64,256]{2,1,0:T(8,128)(2,1)S(1)}, bf16[16,64,256]{2,1,0:T(8,128)(2,1)S(1)}, u32[]{:S(2)}, u32[]{:S(2)}) collective-permute-start(bf16[16,64,256]{2,1,0:T(8,128)(2,1)S(1)} %get-tuple-element.7), channel_id=1, source_target_pairs={{0,1},{1,0},{2,3},{3,2},{4,5},{5,4},{6,7},{7,6},{8,9},{9,8},{10,11... | collective-permute-start | bytes 1572872 | tf_op jit(solution)/shard_map/ppermute | solution.py:24
  48.0 1.6 %collective-permute-start.1 = (bf16[256,512]{0,1:T(8,128)(2,1)S(1)}, bf16[256,512]{0,1:T(8,128)(2,1)S(1)}, u32[]{:S(2)}, u32[]{:S(2)}) collective-permute-start(bf16[256,512]{0,1:T(8,128)(2,1)S(1)} %broadcast_select_fusion.5), channel_id=1, source_target_pairs={{0,8},{8,0},{2,10},{10,2},{4,12},{12,4},{6,14},{14,6},{16,24},{24,... | collective-permute-start | bytes 786440 | tf_op jit(solution)/shard_map/ppermute | solution.py:19
  51.1 10.2 %collective-permute-done.5 = bf16[256,512]{0,1:T(8,128)(2,1)S(1)} collective-permute-done((bf16[256,512]{0,1:T(8,128)(2,1)S(1)}, bf16[256,512]{0,1:T(8,128)(2,1)S(1)}, u32[]{:S(2)}, u32[]{:S(2)}) %collective-permute-start.5) | collective-permute-done | bytes 262176 | tf_op jit(solution)/shard_map/ppermute | solution.py:105
  63.3 4.5 %collective-permute-done.6 = bf16[256,512]{0,1:T(8,128)(2,1)S(1)} collective-permute-done((bf16[256,512]{0,1:T(8,128)(2,1)S(1)}, bf16[256,512]{0,1:T(8,128)(2,1)S(1)}, u32[]{:S(2)}, u32[]{:S(2)}) %collective-permute-start.6) | collective-permute-done | bytes 262176 | tf_op jit(solution)/shard_map/ppermute | solution.py:19
  68.0 1.6 %collective-permute-start.7 = (bf16[256,1024]{0,1:T(8,128)(2,1)S(1)}, bf16[256,1024]{0,1:T(8,128)(2,1)S(1)}, u32[]{:S(2)}, u32[]{:S(2)}) collective-permute-start(bf16[256,1024]{0,1:T(8,128)(2,1)S(1)} %maximum_select_fusion.5), channel_id=1, source_target_pairs={{0,4},{4,0},{2,6},{6,2},{8,12},{12,8},{10,14},{14,10},{16,20},{20,... | collective-permute-start | bytes 1572872 | tf_op jit(solution)/shard_map/ppermute | solution.py:19
  69.6 6.6 %collective-permute-done.2 = bf16[256,1024]{0,1:T(8,128)(2,1)S(1)} collective-permute-done((bf16[256,1024]{0,1:T(8,128)(2,1)S(1)}, bf16[256,1024]{0,1:T(8,128)(2,1)S(1)}, u32[]{:S(2)}, u32[]{:S(2)}) %collective-permute-start.2) | collective-permute-done | bytes 524320 | tf_op jit(solution)/shard_map/ppermute | solution.py:19
  77.2 4.7 %collective-permute-done.7 = bf16[256,1024]{0,1:T(8,128)(2,1)S(1)} collective-permute-done((bf16[256,1024]{0,1:T(8,128)(2,1)S(1)}, bf16[256,1024]{0,1:T(8,128)(2,1)S(1)}, u32[]{:S(2)}, u32[]{:S(2)}) %collective-permute-start.7) | collective-permute-done | bytes 524320 | tf_op jit(solution)/shard_map/ppermute | solution.py:19
  82.5 2.1 %fusion.30 = (f32[1,16,64,256]{3,2,1,0:T(8,128)S(1)}, f32[1,16,64,256]{3,2,1,0:T(8,128)S(1)}) fusion(f32[8,16,64,256]{3,2,1,0:T(8,128)} %param.33, s32[]{:T(128)S(6)} %min.24, bf16[16,64,256]{2,1,0:T(8,128)(2,1)} %collective-permute-done.14, pred[]{:T(512)S(6)} %eq.160, pred[]{:T(512)} %bitcast.16, s32[]{:T(128)S(6)} %min.26, ...), kind=kLoop, calls=%fused_computation.55 | loop fusion | flops 1572864 | bytes 5242892 | tf_op jit(solution)/shard_map/stack | solution.py:195
  85.9 1.9 %slice-done.1 = s8[4194304]{0:T(1024)(128)(4,1)S(1)} async-done(((s8[16777216]{0:T(1024)(128)(4,1)}), s8[4194304]{0:T(1024)(128)(4,1)S(1)}, s32[]{:S(2)}) %slice-start.1) | async-done | bytes 4194328
  90.0 2.3 %fusion.18 = bf16[256,1024]{1,0:T(8,128)(2,1)S(1)} fusion(bf16[256,4096]{0,1:T(8,128)(2,1)S(1)} %bitcast.190, bf16[2,4096,1024]{2,1,0:T(8,128)(2,1)S(1)} %bitcast.175), kind=kOutput, calls=%fused_computation.33 | convolution fusion | flops 2147745792 | bytes 11010048 | tf_op jit(solution)/shard_map/dot_general | solution.py:205
  93.7 6.8 %collective-permute-start.12 = (bf16[256,272]{0,1:T(8,128)(2,1)S(1)}, bf16[256,272]{0,1:T(8,128)(2,1)S(1)}, u32[]{:S(2)}, u32[]{:S(2)}) collective-permute-start(bf16[256,272]{0,1:T(8,128)(2,1)S(1)} %fusion.19), channel_id=1, source_target_pairs={{0,1},{1,0},{2,3},{3,2},{4,5},{5,4},{6,7},{7,6},{8,9},{9,8},{10,11... | collective-permute-start | bytes 417800 | tf_op jit(solution)/shard_map/ppermute | solution.py:24
  100.5 3.1 %fusion.17 = bf16[256,1024]{1,0:T(8,128)(2,1)} fusion(bf16[256,4096]{0,1:T(8,128)(2,1)S(1)} %bitcast.192, bf16[2,4096,1024]{2,1,0:T(8,128)(2,1)S(1)} %bitcast.176), kind=kOutput, calls=%fused_computation.32 | convolution fusion | flops 2147745792 | bytes 11010048 | tf_op jit(solution)/shard_map/dot_general | solution.py:205
  103.6 2.0 %collective-permute-start.16 = (bf16[256,1024]{1,0:T(8,128)(2,1)}, bf16[256,1024]{1,0:T(8,128)(2,1)}, u32[]{:S(2)}, u32[]{:S(2)}) collective-permute-start(bf16[256,1024]{1,0:T(8,128)(2,1)} %fusion.17), channel_id=1, source_target_pairs={{0,1},{1,0},{2,3},{3,2},{4,5},{5,4},{6,7},{7,6},{8,9},{9,8},{10,11... | collective-permute-start | bytes 1572872 | tf_op jit(solution)/shard_map/ppermute | solution.py:24
  111.9 6.5 %collective-permute-done.9 = bf16[256,1024]{1,0:T(8,128)(2,1)S(1)} collective-permute-done((bf16[256,1024]{1,0:T(8,128)(2,1)S(1)}, bf16[256,1024]{1,0:T(8,128)(2,1)S(1)}, u32[]{:S(2)}, u32[]{:S(2)}) %collective-permute-start.9) | collective-permute-done | bytes 524320 | tf_op jit(solution)/shard_map/ppermute | solution.py:24
  118.4 2.6 %fusion.33 = f32[256,1024]{1,0:T(8,128)S(1)} fusion(bf16[256,1024]{1,0:T(8,128)(2,1)S(1)} %collective-permute-done.9, bf16[256,4096]{0,1:T(8,128)(2,1)S(1)} %bitcast.188, bf16[2,4096,1024]{2,1,0:T(8,128)(2,1)S(1)} %bitcast.177), kind=kOutput, calls=%fused_computation.69 | convolution fusion | flops 2148532224 | bytes 12058624 | tf_op jit(solution)/shard_map/dot_general | solution.py:210
  121.0 2.5 %multiply_convert_fusion.11 = bf16[256,1024]{1,0:T(8,128)(2,1)S(1)} fusion(f32[253,1024]{1,0:T(8,128)S(1)} %bitcast.169, f32[254,1024]{1,0:T(8,128)S(1)} %bitcast.170, f32[256,3,1024]{2,0,1:T(8,128)S(1)} %fusion.67, f32[255,1024]{1,0:T(8,128)S(1)} %bitcast.171, f32[256,1024]{1,0:T(8,128)S(1)} %fusion.33, f32[1024]{0:T(1024)S(1)} %bitcast.198, ...), kind=kLoop, calls=%fused_computation.63 | loop fusion | flops 8126464 | bytes 7863296 | tf_op jit(solution)/shard_map/convert_element_type | solution.py:59
  123.7 3.6 %fusion.16 = f32[256,16,64]{0,2,1:T(8,128)} fusion(bf16[256,16,64]{0,2,1:T(8,128)(2,1)S(1)} %bitcast.185, f32[256,256]{1,0:T(8,128)} %fusion.45, f32[16,256]{1,0:T(8,128)S(1)} %fusion.73, f32[256,256]{1,0:T(8,128)} %fusion.37, f32[16,256]{1,0:T(8,128)S(1)} %bitcast.208, f32[16,64,256]{2,1,0:T(8,128)} %multiply_reduce_fusion, f32[16]{0:T(128)S(1)} %copy-done.12, ...), kind=kOutput, calls=%fused_computation.27 | convolution fusion | flops 141819904 | bytes 3194944 | tf_op jit(solution)/shard_map/hts,shp->thp/dot_general | solution.py:71
  127.3 2.5 %copy.49 = f32[256,1024]{1,0:T(8,128)} copy(f32[256,1024]{0,1:T(8,128)} %bitcast.195) | data formatting | bytes 2097152 | tf_op jit(solution)/shard_map/reshape | solution.py:244
  129.8 7.0 %multiply_reduce_fusion.1 = (f32[256]{0:T(256)S(1)}, f32[256,1024]{1,0:T(8,128)S(1)}) fusion(f32[256,1024]{1,0:T(8,128)} %copy.49, bf16[256,1024]{1,0:T(8,128)(2,1)} %collective-permute-done.16, bf16[256,4096]{0,1:T(8,128)(2,1)} %bitcast.189, bf16[2,4096,1024]{2,1,0:T(8,128)(2,1)} %bitcast.172), kind=kOutput, calls=%fused_computation.59 | convolution fusion | flops 2150366976 | bytes 13108224 | tf_op jit(solution)/shard_map/dot_general | solution.py:210
  137.0 1.8 %multiply_add_fusion = f32[2,16,64,256]{3,2,1,0:T(8,128)} fusion(f32[1,16,64,256]{3,2,1,0:T(8,128)S(1)} %get-tuple-element.5, f32[1,16,64,256]{3,2,1,0:T(8,128)S(1)} %get-tuple-element.4, f32[256,16,64]{0,2,1:T(8,128)S(1)} %convert_multiply_fusion.1, f32[2,256]{1,0:T(2,128)S(1)} %compare_convert_fusion, f32[2,16]{1,0:T(2,128)S(1)} %get-tuple-element.44, ...), kind=kOutput, calls=%fused_computation.14 | convolution fusion | flops 271056896 | bytes 5377024 | tf_op jit(solution)/shard_map/jthp,tn->jhpn/dot_general | solution.py:83
  (109 shorter events, 25.2 us)
Async XLA Ops:
  0.6 20.2 %copy-start.8 = (s32[1,2]{1,0:T(1,128)S(1)}, s32[1,2]{1,0:T(1,128)}, u32[]{:S(2)}) copy-start(s32[1,2]{1,0:T(1,128)} %param.30) | copy-start | bytes 28
  0.6 21.1 %copy-start.2 = (f32[4,1024]{1,0:T(4,128)S(1)}, f32[4,1024]{1,0:T(4,128)}, u32[]{:S(2)}) copy-start(f32[4,1024]{1,0:T(4,128)} %param.25) | copy-start | bytes 49156
  0.7 21.2 %copy-start.5 = (f32[4,256]{1,0:T(4,128)S(1)}, f32[4,256]{1,0:T(4,128)}, u32[]{:S(2)}) copy-start(f32[4,256]{1,0:T(4,128)} %param.27) | copy-start | bytes 12292
  0.7 21.2 %copy-start.11 = (f32[16]{0:T(128)S(1)}, f32[16]{0:T(128)}, u32[]{:S(2)}) copy-start(f32[16]{0:T(128)} %param.23) | copy-start | bytes 196
  0.7 21.2 %copy-start.6 = (s32[2]{0:T(128)S(1)}, s32[2]{0:T(128)}, u32[]{:S(2)}) copy-start(s32[2]{0:T(128)} %param.31) | copy-start | bytes 28
  1.8 47.8 %collective-permute-start.4 = (bf16[256,512]{0,1:T(8,128)(2,1)S(1)}, bf16[256,512]{0,1:T(8,128)(2,1)S(1)}, u32[]{:S(2)}, u32[]{:S(2)}) collective-permute-start(bf16[256,512]{0,1:T(8,128)(2,1)S(1)} %copy.41), channel_id=1, source_target_pairs={{1,0},{3,2},{5,4},{7,6},{9,8},{11,10},{13,12},{15,14},{16,17},{18,... | collective-permute-start | bytes 786440 | tf_op jit(solution)/shard_map/ppermute | solution.py:126
  3.1 42.8 %collective-permute-start = (bf16[256,512]{0,1:T(8,128)(2,1)S(1)}, bf16[256,512]{0,1:T(8,128)(2,1)S(1)}, u32[]{:S(2)}, u32[]{:S(2)}) collective-permute-start(bf16[256,512]{0,1:T(8,128)(2,1)S(1)} %copy.41), channel_id=1, source_target_pairs={{0,16},{2,18},{4,20},{6,22},{8,24},{10,26},{12,28},{14,30},{17,1},... | collective-permute-start | bytes 786440 | tf_op jit(solution)/shard_map/ppermute | solution.py:105
  16.8 31.1 %collective-permute-start.10 = (bf16[3,1280]{1,0:T(4,128)(2,1)S(1)}, bf16[3,1280]{1,0:T(4,128)(2,1)S(1)}, u32[]{:S(2)}, u32[]{:S(2)}) collective-permute-start(bf16[3,1280]{1,0:T(4,128)(2,1)S(1)} %bitcast.201), channel_id=1, source_target_pairs={{0,1},{1,0},{2,3},{3,2},{4,5},{5,4},{6,7},{7,6},{8,9},{9,8},{10,11... | collective-permute-start | bytes 23048 | tf_op jit(solution)/shard_map/ppermute | solution.py:24
  16.9 46.3 %collective-permute-start.11 = (bf16[3,1280]{1,0:T(4,128)(2,1)S(1)}, bf16[3,1280]{1,0:T(4,128)(2,1)S(1)}, u32[]{:S(2)}, u32[]{:S(2)}) collective-permute-start(bf16[3,1280]{1,0:T(4,128)(2,1)S(1)} %bitcast.200), channel_id=1, source_target_pairs={{0,1},{1,0},{2,3},{3,2},{4,5},{5,4},{6,7},{7,6},{8,9},{9,8},{10,11... | collective-permute-start | bytes 23048 | tf_op jit(solution)/shard_map/ppermute | solution.py:24
  20.6 61.9 %collective-permute-start.14 = (bf16[16,64,256]{2,1,0:T(8,128)(2,1)S(1)}, bf16[16,64,256]{2,1,0:T(8,128)(2,1)}, u32[]{:S(2)}, u32[]{:S(2)}) collective-permute-start(bf16[16,64,256]{2,1,0:T(8,128)(2,1)S(1)} %get-tuple-element.6), channel_id=1, source_target_pairs={{0,1},{1,0},{2,3},{3,2},{4,5},{5,4},{6,7},{7,6},{8,9},{9,8},{10,11... | collective-permute-start | bytes 1572872 | tf_op jit(solution)/shard_map/ppermute | solution.py:24
  45.9 36.6 %collective-permute-start.15 = (bf16[16,64,256]{2,1,0:T(8,128)(2,1)S(1)}, bf16[16,64,256]{2,1,0:T(8,128)(2,1)S(1)}, u32[]{:S(2)}, u32[]{:S(2)}) collective-permute-start(bf16[16,64,256]{2,1,0:T(8,128)(2,1)S(1)} %get-tuple-element.7), channel_id=1, source_target_pairs={{0,1},{1,0},{2,3},{3,2},{4,5},{5,4},{6,7},{7,6},{8,9},{9,8},{10,11... | collective-permute-start | bytes 1572872 | tf_op jit(solution)/shard_map/ppermute | solution.py:24
  48.0 13.5 %collective-permute-start.1 = (bf16[256,512]{0,1:T(8,128)(2,1)S(1)}, bf16[256,512]{0,1:T(8,128)(2,1)S(1)}, u32[]{:S(2)}, u32[]{:S(2)}) collective-permute-start(bf16[256,512]{0,1:T(8,128)(2,1)S(1)} %broadcast_select_fusion.5), channel_id=1, source_target_pairs={{0,8},{8,0},{2,10},{10,2},{4,12},{12,4},{6,14},{14,6},{16,24},{24,... | collective-permute-start | bytes 786440 | tf_op jit(solution)/shard_map/ppermute | solution.py:19
  49.6 11.7 %collective-permute-start.5 = (bf16[256,512]{0,1:T(8,128)(2,1)S(1)}, bf16[256,512]{0,1:T(8,128)(2,1)S(1)}, u32[]{:S(2)}, u32[]{:S(2)}) collective-permute-start(bf16[256,512]{0,1:T(8,128)(2,1)S(1)} %collective-permute-done.4), channel_id=1, source_target_pairs={{0,16},{2,18},{4,20},{6,22},{8,24},{10,26},{12,28},{14,30},{17,1},... | collective-permute-start | bytes 786440 | tf_op jit(solution)/shard_map/ppermute | solution.py:105
  61.4 6.4 %collective-permute-start.6 = (bf16[256,512]{0,1:T(8,128)(2,1)S(1)}, bf16[256,512]{0,1:T(8,128)(2,1)S(1)}, u32[]{:S(2)}, u32[]{:S(2)}) collective-permute-start(bf16[256,512]{0,1:T(8,128)(2,1)S(1)} %broadcast_select_fusion.4), channel_id=1, source_target_pairs={{0,8},{8,0},{2,10},{10,2},{4,12},{12,4},{6,14},{14,6},{16,24},{24,... | collective-permute-start | bytes 786440 | tf_op jit(solution)/shard_map/ppermute | solution.py:19
  61.7 14.5 %collective-permute-start.2 = (bf16[256,1024]{0,1:T(8,128)(2,1)S(1)}, bf16[256,1024]{0,1:T(8,128)(2,1)S(1)}, u32[]{:S(2)}, u32[]{:S(2)}) collective-permute-start(bf16[256,1024]{0,1:T(8,128)(2,1)S(1)} %maximum_select_fusion.4), channel_id=1, source_target_pairs={{0,4},{4,0},{2,6},{6,2},{8,12},{12,8},{10,14},{14,10},{16,20},{20,... | collective-permute-start | bytes 1572872 | tf_op jit(solution)/shard_map/ppermute | solution.py:19
  68.0 13.8 %collective-permute-start.7 = (bf16[256,1024]{0,1:T(8,128)(2,1)S(1)}, bf16[256,1024]{0,1:T(8,128)(2,1)S(1)}, u32[]{:S(2)}, u32[]{:S(2)}) collective-permute-start(bf16[256,1024]{0,1:T(8,128)(2,1)S(1)} %maximum_select_fusion.5), channel_id=1, source_target_pairs={{0,4},{4,0},{2,6},{6,2},{8,12},{12,8},{10,14},{14,10},{16,20},{20,... | collective-permute-start | bytes 1572872 | tf_op jit(solution)/shard_map/ppermute | solution.py:19
  76.5 8.2 %collective-permute-start.3 = (bf16[256,2048]{0,1:T(8,128)(2,1)S(1)}, bf16[256,2048]{0,1:T(8,128)(2,1)S(1)}, u32[]{:S(2)}, u32[]{:S(2)}) collective-permute-start(bf16[256,2048]{0,1:T(8,128)(2,1)S(1)} %maximum_select_fusion), channel_id=1, source_target_pairs={{0,2},{2,0},{4,6},{6,4},{8,10},{10,8},{12,14},{14,12},{16,18},{18,... | collective-permute-start | bytes 3145736 | tf_op jit(solution)/shard_map/ppermute | solution.py:19
  82.1 3.2 %collective-permute-start.8 = (bf16[256,2048]{0,1:T(8,128)(2,1)S(1)}, bf16[256,2048]{0,1:T(8,128)(2,1)S(1)}, u32[]{:S(2)}, u32[]{:S(2)}) collective-permute-start(bf16[256,2048]{0,1:T(8,128)(2,1)S(1)} %maximum_select_fusion.2), channel_id=1, source_target_pairs={{0,2},{2,0},{4,6},{6,4},{8,10},{10,8},{12,14},{14,12},{16,18},{18,... | collective-permute-start | bytes 3145736 | tf_op jit(solution)/shard_map/ppermute | solution.py:19
  85.3 33.0 %copy-start = (bf16[256,2,2,2,512]{0,4,3,2,1:T(8,128)(2,1)}, bf16[256,2,2,2,512]{0,4,3,2,1:T(8,128)(2,1)S(1)}, u32[]{:S(2)}) copy-start(bf16[256,2,2,2,512]{0,4,3,2,1:T(8,128)(2,1)S(1)} %copy.42) | copy-start | bytes 6291460
  93.7 12.0 %collective-permute-start.12 = (bf16[256,272]{0,1:T(8,128)(2,1)S(1)}, bf16[256,272]{0,1:T(8,128)(2,1)S(1)}, u32[]{:S(2)}, u32[]{:S(2)}) collective-permute-start(bf16[256,272]{0,1:T(8,128)(2,1)S(1)} %fusion.19), channel_id=1, source_target_pairs={{0,1},{1,0},{2,3},{3,2},{4,5},{5,4},{6,7},{7,6},{8,9},{9,8},{10,11... | collective-permute-start | bytes 417800 | tf_op jit(solution)/shard_map/ppermute | solution.py:24
  103.6 14.8 %collective-permute-start.9 = (bf16[256,1024]{1,0:T(8,128)(2,1)S(1)}, bf16[256,1024]{1,0:T(8,128)(2,1)S(1)}, u32[]{:S(2)}, u32[]{:S(2)}) collective-permute-start(bf16[256,1024]{1,0:T(8,128)(2,1)S(1)} %fusion.18), channel_id=1, source_target_pairs={{0,1},{1,0},{2,3},{3,2},{4,5},{5,4},{6,7},{7,6},{8,9},{9,8},{10,11... | collective-permute-start | bytes 1572872 | tf_op jit(solution)/shard_map/ppermute | solution.py:24
  103.6 26.2 %collective-permute-start.16 = (bf16[256,1024]{1,0:T(8,128)(2,1)}, bf16[256,1024]{1,0:T(8,128)(2,1)}, u32[]{:S(2)}, u32[]{:S(2)}) collective-permute-start(bf16[256,1024]{1,0:T(8,128)(2,1)} %fusion.17), channel_id=1, source_target_pairs={{0,1},{1,0},{2,3},{3,2},{4,5},{5,4},{6,7},{7,6},{8,9},{9,8},{10,11... | collective-permute-start | bytes 1572872 | tf_op jit(solution)/shard_map/ppermute | solution.py:24
  108.0 1.4 %collective-permute-start.13 = (bf16[256,256]{0,1:T(8,128)(2,1)S(1)}, bf16[256,256]{0,1:T(8,128)(2,1)S(1)}, u32[]{:S(2)}, u32[]{:S(2)}) collective-permute-start(bf16[256,256]{0,1:T(8,128)(2,1)S(1)} %multiply_convert_fusion.12), channel_id=1, source_target_pairs={{0,2},{2,0},{4,6},{6,4},{8,10},{10,8},{12,14},{14,12},{16,18},{18,... | collective-permute-start | bytes 393224 | tf_op jit(solution)/shard_map/ppermute | solution.py:19
  136.8 2.0 %collective-permute-start.17 = (f32[256]{0:T(256)S(1)}, f32[256]{0:T(256)S(1)}, u32[]{:S(2)}, u32[]{:S(2)}) collective-permute-start(f32[256]{0:T(256)S(1)} %get-tuple-element.2), channel_id=1, source_target_pairs={{0,2},{2,0},{4,6},{6,4},{8,10},{10,8},{12,14},{14,12},{16,18},{18,... | collective-permute-start | bytes 3080 | tf_op jit(solution)/shard_map/ppermute | solution.py:19
  (11 other events, 51.8 us)

commit v2 on v1

v2 whole, which is shorter than its diff:
```python
import functools

import jax
import jax.numpy as jnp
from jax import lax
from jax.experimental import pallas as pl
from jax.experimental.pallas import tpu as pltpu
from jax.sharding import PartitionSpec as P

GROUPS = 8
NORM_EPS = 1e-05
F32 = jnp.float32
BF16 = jnp.bfloat16
HIGH = lax.Precision.HIGHEST
VMEM_BYTES = 48 * 1024 * 1024
HEADS_STEP = 4
COLUMNS = 256


def cost(flops, bytes_accessed):
    return pl.CostEstimate(flops=int(flops), bytes_accessed=int(bytes_accessed), transcendentals=0)


def params():
    return pltpu.CompilerParams(vmem_limit_bytes=VMEM_BYTES)


def partner_2(block, axis, bit):
    count = lax.axis_size(axis)
    route = []
    for low in range(count):
        high = low | 1 << bit
        if high != low and high < count:
            route += [(low, high), (high, low)]
    return lax.ppermute(block, axis, route)


def shift_req(block, step):
    count = lax.axis_size("req")
    return lax.ppermute(block, "req", [(i, (i + step) % count) for i in range(count)])


def spread_routes():
    far, across, diagonal = [], [], []
    for z in range(4):
        for rest in range(4):
            for r in range(2):
                place = (z * 4 + rest) * 2 + r
                other = (((z + 2) % 4) * 4 + rest) * 2 + r
                if z // 2 == r:
                    far.append((place, other))
                else:
                    across.append((place, place ^ 1))
                    diagonal.append((place, other ^ 1))
    return far, across, diagonal


def quad(block):
    along_z = partner_2(block, "wide", 2)
    along_x = partner_2(block, "wide", 1)
    both = partner_2(along_z, "wide", 1)
    four = jnp.stack([block, along_x, along_z, both])
    return [four, partner_2(four, "wide", 0)]


def features_of(x_in):
    req_count = lax.axis_size("req")
    wide_count = lax.axis_size("wide")
    me = lax.axis_index("req")
    if req_count == 2 and wide_count == 16:
        wide_index = lax.axis_index("wide")
        axes = ("wide", "req")
        far, across, diagonal = spread_routes()
        across = lax.ppermute(x_in, axes, across)
        diagonal = lax.ppermute(x_in, axes, diagonal)
        far = lax.ppermute(x_in, axes, far)
        near = wide_index // 8 == me
        theirs = quad(jnp.where(near, across, diagonal))
        own = quad(jnp.where(near, x_in, far))
        rows = (wide_index % 8) ^ jnp.array([0, 2, 4, 6, 1, 3, 5, 7], jnp.int32)
        return [own, theirs], rows
    own = lax.all_gather(x_in, "wide", axis=1, tiled=True)
    parts = own.reshape(own.shape[0], req_count, own.shape[1] // req_count).transpose(1, 0, 2)
    got = lax.all_to_all(parts, "req", split_axis=0, concat_axis=0, tiled=True)
    blocks = [
        [lax.dynamic_index_in_dim(got, (me + step) % req_count, 0, True)]
        for step in range(req_count)
    ]
    return blocks, jnp.zeros((1,), jnp.int32)


def project_kernel(block_total, weight_total, rows_ref, *refs):
    blocks = refs[:block_total]
    weights = refs[block_total : block_total + weight_total]
    out_ref = refs[block_total + weight_total]
    held = refs[block_total + weight_total + 1 : block_total + 2 * weight_total + 1]
    sems = refs[-1]
    copies = []
    for place in range(weight_total):
        copy = pltpu.make_async_copy(weights[place], held[place], sems.at[place])
        copy.start()
        copies.append(copy)
    column = 0
    for place in range(weight_total):
        copies[place].wait()
        total = None
        index = 0
        for block in blocks:
            for part in range(block.shape[0]):
                depth = block.shape[2]
                start = pl.multiple_of(rows_ref[index] * depth, depth)
                term = jnp.dot(
                    block[part],
                    held[place][pl.ds(start, depth), :],
                    preferred_element_type=F32,
                )
                total = term if total is None else total + term
                index += 1
        width = held[place].shape[1]
        out_ref[:, column : column + width] = total.astype(out_ref.dtype)
        column += width


def project(blocks, rows, weights, kind):
    tokens = blocks[0].shape[1]
    width = sum(weight.shape[1] for weight in weights)
    depth = weights[0].shape[0]
    any_space = pl.BlockSpec(memory_space=pl.ANY)
    return pl.pallas_call(
        functools.partial(project_kernel, len(blocks), len(weights)),
        out_shape=jax.ShapeDtypeStruct((tokens, width), kind),
        in_specs=[pl.BlockSpec(memory_space=pltpu.SMEM)]
        + [pl.BlockSpec(memory_space=pltpu.VMEM)] * len(blocks)
        + [any_space] * len(weights),
        out_specs=pl.BlockSpec(memory_space=pltpu.VMEM),
        scratch_shapes=[pltpu.VMEM(weight.shape, BF16) for weight in weights]
        + [pltpu.SemaphoreType.DMA((len(weights),))],
        compiler_params=params(),
        cost_estimate=cost(2 * tokens * width * depth, 2 * depth * (width + tokens)),
    )(rows, *blocks, *weights)


def token_places(starts, count_tok, shape, axis):
    position = lax.broadcasted_iota(jnp.int32, shape, axis)
    seg = jnp.full(shape, -1, jnp.int32)
    first = jnp.zeros(shape, jnp.int32)
    for start in starts:
        seg = seg + (position >= start).astype(jnp.int32)
        first = jnp.where(position >= start, start, first)
    return position, seg, first


def conv_silu(values, cache_ref, kernel_ref, bias_ref, seg, offset):
    kernel_len = kernel_ref.shape[0]
    taps = [kernel_ref[k : k + 1, :] for k in range(kernel_len)]
    total = bias_ref[...] + taps[kernel_len - 1] * values
    for lag in range(1, kernel_len):
        earlier = pltpu.roll(values, lag, 0)
        total = total + taps[kernel_len - 1 - lag] * jnp.where(offset >= lag, earlier, 0.0)
    cached = jnp.zeros_like(values)
    for request in range(cache_ref.shape[0]):
        for place in range(kernel_len - 1):
            history = jnp.zeros_like(bias_ref[...])
            for lag in range(place + 1, kernel_len):
                at = kernel_len - 1 + place - lag
                history = history + taps[kernel_len - 1 - lag] * cache_ref[request, at : at + 1, :]
            cached = jnp.where((seg == request) & (offset == place), history, cached)
    total = total + cached
    return total * jax.nn.sigmoid(total)


def prep_kernel(
    count_req, got_total, starts_ref, own_ref, *refs
):
    got = refs[:got_total]
    cache_ref, kernel_ref, bias_ref, dt_bias_ref, a_log_ref = refs[got_total : got_total + 5]
    bc_ref, cum_ref, step_ref, coef_ref, decay_ref = refs[got_total + 5 :]
    tokens = own_ref.shape[0]
    channels = bias_ref.shape[1]
    heads = dt_bias_ref.shape[1]
    starts = [starts_ref[0, j] for j in range(count_req)]
    total = own_ref[...]
    for ref in got:
        total = total + ref[...].astype(F32)
    total = total.astype(BF16).astype(F32)
    position, seg, first = token_places(starts, tokens, (tokens, channels), 0)
    bc = conv_silu(total[:, :channels], cache_ref, kernel_ref, bias_ref, seg, position - first)
    bc_ref[...] = bc.astype(BF16)
    raw = total[:, channels : channels + heads] + dt_bias_ref[...]
    step = jnp.maximum(raw, 0.0) + jnp.log1p(jnp.exp(-jnp.abs(raw)))
    rate = step * (-jnp.exp(a_log_ref[...]))
    position, seg, first = token_places(starts, tokens, (tokens, tokens), 0)
    other, seg_other, first_other = token_places(starts, tokens, (tokens, tokens), 1)
    same = seg == seg_other
    mask = jnp.where(same & (position >= other), 1.0, 0.0)
    after = jnp.where(same & (position < other), 1.0, 0.0)
    cum = jnp.dot(mask, rate, precision=HIGH, preferred_element_type=F32)
    left = jnp.dot(after, rate, precision=HIGH, preferred_element_type=F32)
    cum_ref[...] = cum
    step_ref[...] = step
    coef_ref[...] = jnp.exp(left) * step
    at, seg_at, _ = token_places(starts, tokens, (8, tokens), 1)
    row = lax.broadcasted_iota(jnp.int32, (8, tokens), 0)
    ends = jnp.dot(
        jnp.where(seg_at == row, 1.0, 0.0), rate, precision=HIGH, preferred_element_type=F32
    )
    decay_ref[...] = jnp.exp(ends)


def prep(starts, own, got, cache, kernel, bias, dt_bias, a_log):
    tokens = own.shape[0]
    channels = bias.shape[0]
    heads = dt_bias.shape[0]
    count_req = cache.shape[0]
    vmem = pl.BlockSpec(memory_space=pltpu.VMEM)
    small = jax.ShapeDtypeStruct((tokens, heads), F32)
    return pl.pallas_call(
        functools.partial(prep_kernel, count_req, len(got)),
        out_shape=[
            jax.ShapeDtypeStruct((tokens, channels), BF16),
            small,
            small,
            small,
            jax.ShapeDtypeStruct((8, heads), F32),
        ],
        in_specs=[pl.BlockSpec(memory_space=pltpu.SMEM)] + [vmem] * (6 + len(got)),
        out_specs=[vmem] * 5,
        compiler_params=params(),
        cost_estimate=cost(4e8, 1e6),
    )(starts, own, *got, cache, kernel, bias[None], dt_bias[None], a_log[None])


def pack_kernel(slots_ref, pool_ref, conv_ref, out_ref):
    heads, width, state = pool_ref.shape[1:]
    out_ref[0, : heads * width, :] = pool_ref[0].reshape(heads * width, state).astype(BF16)
    out_ref[0, heads * width :, :] = conv_ref[0]


def pack(pool, conv_rows, slots):
    _, heads, width, state = pool.shape
    count_req, rows, _ = conv_rows.shape
    return pl.pallas_call(
        pack_kernel,
        out_shape=jax.ShapeDtypeStruct((count_req, heads * width + rows, state), BF16),
        grid_spec=pltpu.PrefetchScalarGridSpec(
            num_scalar_prefetch=1,
            grid=(count_req,),
            in_specs=[
                pl.BlockSpec((1, heads, width, state), lambda j, slots: (slots[j], 0, 0, 0)),
                pl.BlockSpec((1, rows, state), lambda j, slots: (j, 0, 0)),
            ],
            out_specs=pl.BlockSpec((1, heads * width + rows, state), lambda j, slots: (j, 0, 0)),
        ),
        compiler_params=params(),
        cost_estimate=cost(0, 6 * count_req * heads * width * state),
    )(slots, pool, conv_rows)


def mixer_kernel(count_req, got_total, slots_ref, flags_ref, starts_ref, *refs):
    own_ref = refs[0]
    got = refs[1 : 1 + got_total]
    rest = refs[1 + got_total :]
    cache_ref, kernel_ref, bias_ref, b_ref, c_ref = rest[:5]
    cum_ref, cum_t_ref, step_t_ref, coef_ref, decay_ref, skip_ref = rest[5:11]
    pools = rest[11 : 11 + count_req]
    states = rest[11 + count_req : 11 + count_req + got_total]
    out_ref, state_ref, scores_ref, c_part_ref, b_part_ref = rest[11 + count_req + got_total :]
    tokens, channels = own_ref.shape
    heads, width, state = pools[0].shape[1:]
    starts = [starts_ref[j] for j in range(count_req)]

    @pl.when(pl.program_id(0) == 0)
    def _():
        position, seg, _ = token_places(starts, tokens, (tokens, tokens), 0)
        other, seg_other, _ = token_places(starts, tokens, (tokens, tokens), 1)
        scores = lax.dot_general(
            c_ref[...], b_ref[...], (((1,), (1,)), ((), ())), preferred_element_type=F32
        )
        scores_ref[...] = jnp.where((seg == seg_other) & (position >= other), scores, 0.0)
        _, seg, _ = token_places(starts, tokens, (tokens, state), 0)
        b_maps = b_ref[...].astype(F32)
        c_maps = c_ref[...].astype(F32)
        for j in range(count_req):
            place = slice(j * state, (j + 1) * state)
            b_part_ref[:, place] = jnp.where(seg == j, b_maps, 0.0).astype(BF16)
            c_part_ref[:, place] = jnp.where(seg == j, c_maps, 0.0).astype(BF16)

    total = own_ref[...]
    for ref in got:
        total = total + ref[...].astype(F32)
    total = total.astype(BF16).astype(F32)
    position, seg, first = token_places(starts, tokens, (tokens, channels), 0)
    values = conv_silu(total, cache_ref, kernel_ref, bias_ref, seg, position - first)
    inputs = values.astype(BF16)
    values = inputs.astype(F32)

    lane_head = lax.broadcasted_iota(jnp.int32, (tokens, channels), 1) // width
    scores = scores_ref[...]
    cum = cum_ref[0]
    cum_t = cum_t_ref[0]
    step_t = step_t_ref[0]
    coef = coef_ref[0]
    grown = jnp.exp(cum)
    grown_wide = jnp.zeros((tokens, channels), F32)
    coef_wide = jnp.zeros((tokens, channels), F32)
    result = jnp.zeros((tokens, channels), F32)
    for h in range(heads):
        gap = jnp.minimum(cum[:, h : h + 1] - cum_t[h : h + 1, :], 0.0)
        weights = (jnp.exp(gap) * scores * step_t[h : h + 1, :]).astype(BF16)
        mine = lane_head == h
        result = result + jnp.dot(
            weights, jnp.where(mine, values, 0.0).astype(BF16), preferred_element_type=F32
        )
        grown_wide = jnp.where(mine, grown[:, h : h + 1], grown_wide)
        coef_wide = jnp.where(mine, coef[:, h : h + 1], coef_wide)

    from_state = jnp.zeros((tokens, channels), F32)
    carried = (coef_wide * values).astype(BF16)
    fresh = lax.dot_general(
        carried, b_part_ref[...], (((0,), (0,)), ((), ())), preferred_element_type=F32
    )
    for j in range(count_req):
        place = slice(j * state, (j + 1) * state)
        start = pools[j][0].reshape(channels, state) * flags_ref[j, 0].astype(F32)
        for step in range(got_total):
            start = start + states[step][j].astype(F32) * flags_ref[j, step + 1].astype(F32)
        from_state = from_state + lax.dot_general(
            c_part_ref[:, place],
            start.astype(BF16),
            (((1,), (1,)), ((), ())),
            preferred_element_type=F32,
        )
        first_head = pl.program_id(0) * heads
        for h in range(heads):
            rows = slice(h * width, (h + 1) * width)
            state_ref[j, h] = decay_ref[j, first_head + h] * start[rows] + fresh[rows, place]
    out_ref[...] = result + grown_wide * from_state + skip_ref[...] * values


def mixer(
    slots, flags, starts, own, got, cache, kernel, bias, b_maps, c_maps, cum, step, coef, decay,
    skip, pool, states
):
    tokens, channels = own.shape
    _, heads, width, state = pool.shape
    count_req = cache.shape[0]
    kernel_len = kernel.shape[0]
    part = min(HEADS_STEP, heads)
    steps = heads // part
    wide = part * width
    columns = lambda i, *_: (0, i)
    whole = lambda i, *_: (0, 0)

    def by_step(array):
        return array.reshape(tokens, steps, part).transpose(1, 0, 2)

    def by_step_t(array):
        return array.T.reshape(steps, part, tokens)

    in_specs = (
        [pl.BlockSpec((tokens, wide), columns)] * (1 + len(got))
        + [
            pl.BlockSpec((count_req, kernel_len - 1, wide), lambda i, *_: (0, 0, i)),
            pl.BlockSpec((kernel_len, wide), columns),
            pl.BlockSpec((1, wide), columns),
            pl.BlockSpec((tokens, state), whole),
            pl.BlockSpec((tokens, state), whole),
            pl.BlockSpec((1, tokens, part), lambda i, *_: (i, 0, 0)),
            pl.BlockSpec((1, part, tokens), lambda i, *_: (i, 0, 0)),
            pl.BlockSpec((1, part, tokens), lambda i, *_: (i, 0, 0)),
            pl.BlockSpec((1, tokens, part), lambda i, *_: (i, 0, 0)),
            pl.BlockSpec(memory_space=pltpu.SMEM),
            pl.BlockSpec((1, wide), columns),
        ]
        + [
            pl.BlockSpec(
                (1, part, width, state),
                functools.partial(lambda j, i, slots, *_: (slots[j], i, 0, 0), j),
            )
            for j in range(count_req)
        ]
        + [pl.BlockSpec((count_req, wide, state), lambda i, *_: (0, i, 0))] * len(states)
    )
    return pl.pallas_call(
        functools.partial(mixer_kernel, count_req, len(got)),
        out_shape=[
            jax.ShapeDtypeStruct((tokens, channels), F32),
            jax.ShapeDtypeStruct((count_req, heads, width, state), F32),
        ],
        grid_spec=pltpu.PrefetchScalarGridSpec(
            num_scalar_prefetch=3,
            grid=(steps,),
            in_specs=in_specs,
            out_specs=[
                pl.BlockSpec((tokens, wide), columns),
                pl.BlockSpec((count_req, part, width, state), lambda i, *_: (0, i, 0, 0)),
            ],
            scratch_shapes=[
                pltpu.VMEM((tokens, tokens), F32),
                pltpu.VMEM((tokens, count_req * state), BF16),
                pltpu.VMEM((tokens, count_req * state), BF16),
            ],
        ),
        compiler_params=params(),
        cost_estimate=cost(5e9, 8e6),
    )(
        slots, flags, starts, own, *got, cache, kernel, bias[None], b_maps, c_maps,
        by_step(cum), by_step_t(cum), by_step_t(step), by_step(coef), decay,
        jnp.repeat(skip, width)[None], *([pool] * count_req), *states
    )


def on_device(
    x_in,
    w_xz,
    w_dt,
    w_bc,
    dt_bias,
    a_log,
    d_skip,
    conv_x_w,
    conv_x_b,
    conv_bc_w,
    conv_bc_b,
    norm_gain,
    stretch_start,
    prefix_len,
    state_slot,
    ssm_pool,
    conv_x_pool,
    conv_bc_pool,
):
    local_width = w_xz.shape[2]
    state_part = w_bc.shape[1]
    me = lax.axis_index("req")
    req_count = lax.axis_size("req")
    slot_count, heads, head_width, state = ssm_pool.shape
    group_reqs = prefix_len.shape[0]
    lags = conv_x_pool.shape[1]
    conv_width = local_width + state_part

    features, rows = features_of(x_in)

    def slots_of(index):
        asked = lax.dynamic_slice_in_dim(state_slot, index * group_reqs, group_reqs)
        return jnp.clip(asked - me * slot_count, 0, slot_count - 1)

    def conv_of(slots):
        hit = slots[:, None] == jnp.arange(slot_count)[None, :]
        parts = [
            jnp.sum(jnp.where(hit[:, :, None, None], pool[None], 0), 1)
            for pool in (conv_x_pool, conv_bc_pool)
        ]
        return jnp.concatenate(parts, 2)

    conv_size = lags * conv_width
    conv_rows = -(-conv_size // (16 * state)) * 16
    got_states = []
    for step in range(1, req_count):
        slots = slots_of((me + step) % req_count)
        flat = conv_of(slots).reshape(group_reqs, conv_size)
        flat = jnp.pad(flat, ((0, 0), (0, conv_rows * state - conv_size)))
        packed = pack(ssm_pool, flat.reshape(group_reqs, conv_rows, state), slots)
        got_states.append(shift_req(packed, step))

    own_slots = slots_of(me)
    asked = lax.dynamic_slice_in_dim(state_slot, me * group_reqs, group_reqs)
    came_from = (me - asked // slot_count) % req_count
    live = prefix_len > 0
    flags = (live[:, None] & (came_from[:, None] == jnp.arange(req_count)[None, :])).astype(
        jnp.int32
    )
    cache = conv_of(own_slots)
    for step in range(1, req_count):
        got = got_states[step - 1][:, heads * head_width :].reshape(group_reqs, -1)
        got = got[:, :conv_size].reshape(cache.shape)
        cache = jnp.where((came_from == step)[:, None, None], got, cache)
    cache = jnp.where(live[:, None, None], cache, 0).astype(F32)

    pieces = []
    for first in range(0, local_width, COLUMNS):
        piece = jnp.transpose(w_xz[:, :, first : first + COLUMNS], (1, 0, 2))
        pieces.append(lax.optimization_barrier(piece))
    weights = {
        "map": [w_bc, w_dt],
        "xr": [piece[1] for piece in pieces],
        "z": [piece[0] for piece in pieces],
    }
    came = {name: [] for name in weights}
    for step in range(1, req_count):
        for name in weights:
            part = project(features[step], rows, weights[name], BF16)
            came[name].append(shift_req(part, step))
    own = {name: project(features[0], rows, weights[name], F32) for name in weights}

    bc_conv, cum, step, coef, decay = prep(
        stretch_start, own["map"], came["map"], cache[:, :, local_width:], conv_bc_w, conv_bc_b,
        dt_bias, a_log
    )
    wide_index = lax.axis_index("wide")
    group_span = lax.axis_size("wide") // GROUPS
    bit_total = group_span.bit_length() - 1
    joined = bc_conv
    for bit_index in range(bit_total):
        partner = partner_2(joined, "wide", bit_index)
        upper_half = wide_index // (1 << bit_index) % 2 == 1
        joined = jnp.where(
            upper_half, jnp.concatenate([partner, joined], 1), jnp.concatenate([joined, partner], 1)
        )
    state_width = joined.shape[1] // 2
    result, final_state = mixer(
        own_slots, flags, stretch_start[0], own["xr"], came["xr"], cache[:, :, :local_width],
        conv_x_w, conv_x_b, joined[:, :state_width], joined[:, state_width:], cum, step, coef,
        decay, d_skip, ssm_pool, got_states
    )
    gate = own["z"]
    for got in came["z"]:
        gate = gate + got.astype(F32)
    gated = result * jax.nn.silu(gate.astype(BF16).astype(F32))
    square_sum = jnp.sum(gated * gated, 1)
    for bit_index in range(bit_total):
        square_sum = square_sum + partner_2(square_sum, "wide", bit_index)
    mean_sq = square_sum / (local_width * group_span)
    normed = gated * lax.rsqrt(mean_sq + NORM_EPS)[:, None] * norm_gain[None, :]
    return (normed.astype(BF16), final_state)


def solution(mesh):
    in_specs = (
        P("req", "wide"),
        P("req", None, "wide"),
        P("req", "wide"),
        P("req", "wide"),
        P("wide"),
        P("wide"),
        P("wide"),
        P(None, "wide"),
        P("wide"),
        P(None, "wide"),
        P("wide"),
        P("wide"),
        P("req", None),
        P("req"),
        P(),
        P("req", "wide", None, None),
        P("req", None, "wide"),
        P("req", None, "wide"),
    )
    out_specs = (P("req", "wide"), P("req", "wide", None, None))
    return jax.shard_map(
        on_device, mesh=mesh, in_specs=in_specs, out_specs=out_specs, check_vma=False
    )
```

time: 140 us -> 144 us (1.029)
  Pallas kernels: 0 us -> 50.1 us
  matrix products: 26.9 us -> 0 us
  waiting for transfers between devices: 33.6 us -> 17.6 us
  local copies, waits for them, and re-layouts: 30.6 us -> 41.2 us
  between operations: 10.3 us -> 1.12 us
  starting transfers between devices: 29 us -> 22.6 us
    pallas_call x0 -> x9, Pallas kernels: none -> 50.1 us  [the longest x6 37.6 us: project(): pl.pallas_call(functools.partial(project_kernel, len(blocks), len(weights...]
    dot_general x15 -> x0, matrix products: 26.9 us -> none  [the longest x3 10.8 us: on_device(): own = jnp.dot(features[0], weight, preferred_element_type=F32)]
    unnamed x40 -> x55, local copies, waits for them, and re-layouts: 23.1 us -> 9.16 us
    slice x3 -> x5, local copies, waits for them, and re-layouts: 0.6 us -> 13.4 us  [the longest x1 13.3 us: on_device(): piece = jnp.transpose(w_xz[:, :, first:first + COLUMNS], (1, 0, 2))]
    squeeze x0 -> x4, local copies, waits for them, and re-layouts: none -> 10.7 us  [on_device(): piece[0]]
    ppermute x3, waiting for transfers between devices: 10.2 us -> 0.01 us  [the longest x1 0.01 us: features_of(): far = lax.ppermute(x_in, axes, far)]
    ppermute x7 -> x4, starting transfers between devices: 13.1 us -> 4.24 us  [shift_req(): lax.ppermute(block, 'req', [(i, (i + step) % count) for i in range(count)])]
    transpose x2 -> x4, local copies, waits for them, and re-layouts: 0.27 us -> 6.2 us  [the longest x2 5.17 us: on_device(): piece = jnp.transpose(w_xz[:, :, first:first + COLUMNS], (1, 0, 2))]
  transfers between devices with their start and end apart: 18 -> 17, of which waited for: 6 -> 7; matrix products, arithmetic and copies ran while one was open for 35% -> 30% of each run, Pallas kernels for 0% -> 35%
where the time goes in v2:
time: 144 us; the launch traced here: 143 us
  Pallas kernels  50.1 us (35%)
  local copies, waits for them, and re-layouts  41.2 us (29%)
  starting transfers between devices  22.6 us (16%)
  waiting for transfers between devices  17.6 us (12%)
  other arithmetic  9.87 us (7%)
    pallas_call x6, Pallas kernels, project(): pl.pallas_call(functools.partial(project_kernel, len(blocks), len(weights...  37.6 us
    ppermute x10, waiting for transfers between devices, partner_2(): return lax.ppermute(block, axis, route)  15.1 us
    slice x1, local copies, waits for them, and re-layouts, on_device(): piece = jnp.transpose(w_xz[:, :, first:first + COLUMNS], (1, 0, 2))  13.3 us
    squeeze x4, local copies, waits for them, and re-layouts, on_device(): piece[0]  10.7 us
    ppermute x1, starting transfers between devices, features_of(): far = lax.ppermute(x_in, axes, far)  9.35 us
    unnamed x55, local copies, waits for them, and re-layouts  9.16 us
    pallas_call x1, Pallas kernels, mixer(): pl.pallas_call(functools.partial(mixer_kernel, count_req, len(got)), out_...  7.91 us
    ppermute x10, starting transfers between devices, partner_2(): return lax.ppermute(block, axis, route)  7.05 us
  transfers between devices with their start and end apart: 17, of which 7 were waited for; matrix products, arithmetic and copies ran while one was open for 30% of the time, Pallas kernels for 35%

profile of v2, /device:TPU:0, one launch (start us, length us, event | category | flops | bytes accessed | tf_op | source)
XLA Modules:
  0.0 142.6 jit_solution(16071790277532884463)
XLA Ops:
  2.6 9.4 %collective-permute-start = (bf16[256,512]{1,0:T(8,128)(2,1)}, bf16[256,512]{1,0:T(8,128)(2,1)S(1)}, u32[]{:S(2)}, u32[]{:S(2)}) collective-permute-start(bf16[256,512]{1,0:T(8,128)(2,1)} %param.19), channel_id=1, source_target_pairs={{0,16},{2,18},{4,20},{6,22},{8,24},{10,26},{12,28},{14,30},{17,1},... | collective-permute-start | bytes 786440 | tf_op jit(solution)/shard_map/ppermute | solution.py:76
  14.7 3.0 %shard_map.196 = bf16[2,1040,256]{2,1,0:T(8,128)(2,1)} custom-call(s32[2]{0:T(128)S(1)} %get-tuple-element.38.slots_ref, f32[8,16,64,256]{3,2,1,0:T(8,128)} %refs_14_.1, bf16[2,16,256]{2,1,0:T(8,128)(2,1)S(1)} %bitcast.59), custom_call_target="tpu_custom_call" | custom-call | bytes 3145728 | tf_op jit(solution)/shard_map/pallas_call | solution.py:242
  18.5 13.3 %fusion.8 = (bf16[4096,2,256]{2,1,0:T(2,128)(2,1)S(1)}, bf16[4096,2,256]{2,1,0:T(2,128)(2,1)S(1)}, bf16[4096,2,256]{2,1,0:T(2,128)(2,1)S(1)}, bf16[4096,2,256]{2,1,0:T(2,128)(2,1)S(1)}) fusion(bf16[4096,2,1024]{2,1,0:T(2,128)(2,1)} %param.20), kind=kLoop, calls=%fused_computation.53 | loop fusion | bytes 33554432 | tf_op jit(solution)/shard_map/slice | solution.py:482
  31.9 1.9 %copy_bitcast_fusion = (bf16[2,4096,256]{2,1,0:T(8,128)(2,1)S(1)}, bf16[2,4096,256]{2,1,0:T(8,128)(2,1)S(1)}) fusion(bf16[4096,2,256]{2,1,0:T(2,128)(2,1)S(1)} %get-tuple-element.24, bf16[4096,2,256]{2,1,0:T(2,128)(2,1)S(1)} %get-tuple-element.25), kind=kLoop, calls=%fused_computation | loop fusion | bytes 16777216 | tf_op jit(solution)/shard_map/transpose | solution.py:482
  33.8 2.3 %slice_bitcast_fusion = (bf16[4096,256]{1,0:T(8,128)(2,1)}, bf16[4096,256]{1,0:T(8,128)(2,1)}) fusion(bf16[2,4096,256]{2,1,0:T(8,128)(2,1)S(1)} %get-tuple-element.42), kind=kLoop, calls=%fused_computation.4 | loop fusion | bytes 8388608 | tf_op jit(solution)/shard_map/squeeze | solution.py:487
  36.2 2.3 %slice_bitcast_fusion.1 = (bf16[4096,256]{1,0:T(8,128)(2,1)}, bf16[4096,256]{1,0:T(8,128)(2,1)}) fusion(bf16[2,4096,256]{2,1,0:T(8,128)(2,1)S(1)} %get-tuple-element.43), kind=kLoop, calls=%fused_computation.5 | loop fusion | bytes 8388608 | tf_op jit(solution)/shard_map/squeeze | solution.py:487
  38.5 3.2 %copy_bitcast_fusion.2 = (bf16[2,4096,256]{2,1,0:T(8,128)(2,1)S(1)}, bf16[2,4096,256]{2,1,0:T(8,128)(2,1)}) fusion(bf16[4096,2,256]{2,1,0:T(2,128)(2,1)S(1)} %get-tuple-element.26, bf16[4096,2,256]{2,1,0:T(2,128)(2,1)S(1)} %get-tuple-element.27), kind=kLoop, calls=%fused_computation.2 | loop fusion | bytes 16777216 | tf_op jit(solution)/shard_map/transpose | solution.py:482
  41.7 2.3 %slice_bitcast_fusion.2 = (bf16[4096,256]{1,0:T(8,128)(2,1)}, bf16[4096,256]{1,0:T(8,128)(2,1)}) fusion(bf16[2,4096,256]{2,1,0:T(8,128)(2,1)S(1)} %get-tuple-element.44), kind=kLoop, calls=%fused_computation.6 | loop fusion | bytes 8388608 | tf_op jit(solution)/shard_map/squeeze | solution.py:487
  44.1 1.6 %collective-permute-start.8 = (bf16[256,512]{1,0:T(8,128)(2,1)S(1)}, bf16[256,512]{1,0:T(8,128)(2,1)S(1)}, u32[]{:S(2)}, u32[]{:S(2)}) collective-permute-start(bf16[256,512]{1,0:T(8,128)(2,1)S(1)} %broadcast_select_fusion), channel_id=1, source_target_pairs={{0,8},{8,0},{2,10},{10,2},{4,12},{12,4},{6,14},{14,6},{16,24},{24,... | collective-permute-start | bytes 786440 | tf_op jit(solution)/shard_map/ppermute | solution.py:35
  45.7 3.8 %slice_bitcast_fusion.3 = (bf16[4096,256]{1,0:T(8,128)(2,1)}, bf16[4096,256]{1,0:T(8,128)(2,1)S(1)}) fusion(bf16[2,4096,256]{2,1,0:T(8,128)(2,1)} %get-tuple-element.45), kind=kLoop, calls=%fused_computation.7 | loop fusion | bytes 8388608 | tf_op jit(solution)/shard_map/squeeze | solution.py:487
  53.7 4.1 %collective-permute-done.2 = bf16[256,512]{1,0:T(8,128)(2,1)S(1)} collective-permute-done((bf16[256,512]{1,0:T(8,128)(2,1)S(1)}, bf16[256,512]{1,0:T(8,128)(2,1)S(1)}, u32[]{:S(2)}, u32[]{:S(2)}) %collective-permute-start.2) | collective-permute-done | bytes 262176 | tf_op jit(solution)/shard_map/ppermute | solution.py:35
  58.9 5.6 %collective-permute-done.9 = bf16[256,512]{1,0:T(8,128)(2,1)} collective-permute-done((bf16[256,512]{1,0:T(8,128)(2,1)S(1)}, bf16[256,512]{1,0:T(8,128)(2,1)}, u32[]{:S(2)}, u32[]{:S(2)}) %collective-permute-start.9) | collective-permute-done | bytes 262176 | tf_op jit(solution)/shard_map/ppermute | solution.py:35
  64.5 2.1 %pad_maximum_fusion.1.refs_0_ = bf16[4,256,512]{2,1,0:T(8,128)(2,1)} fusion(bf16[1,256,512]{2,1,0:T(8,128)(2,1)} %bitcast.16, bf16[1,256,512]{2,1,0:T(8,128)(2,1)S(1)} %bitcast.69, bf16[1,256,512]{2,1,0:T(8,128)(2,1)} %bitcast.14, bf16[1,256,512]{2,1,0:T(8,128)(2,1)S(1)} %bitcast.66), kind=kLoop, calls=%fused_computation.19 | loop fusion | flops 1572864 | bytes 2097152 | tf_op jit(solution)/shard_map/stack | solution.py:62
  66.8 2.2 %copy.49.refs_3_ = bf16[4096,16]{1,0:T(8,128)(2,1)} copy(bf16[4096,16]{0,1:T(8,128)(2,1)} %param.21) | data formatting | bytes 262144 | tf_op args[2]
  70.0 3.4 %collective-permute-done.3 = bf16[256,512]{1,0:T(8,128)(2,1)} collective-permute-done((bf16[256,512]{1,0:T(8,128)(2,1)S(1)}, bf16[256,512]{1,0:T(8,128)(2,1)}, u32[]{:S(2)}, u32[]{:S(2)}) %collective-permute-start.3) | collective-permute-done | bytes 262176 | tf_op jit(solution)/shard_map/ppermute | solution.py:35
  77.3 7.8 %shard_map.202 = bf16[256,1024]{1,0:T(8,128)(2,1)} custom-call(s32[8]{0:T(128)S(1)} %broadcast_xor_fusion.rows_ref, bf16[4,256,512]{2,1,0:T(8,128)(2,1)} %pad_maximum_fusion.1.refs_0_, bf16[4,256,512]{2,1,0:T(8,128)(2,1)} %collective-permute-done.10.refs_1_, bf16[4096,256]{1,0:T(8,128)(2,1)S(1)} %copy-done, bf16[4096,256]{1,0:T(8,128)(2,1)} %get-tuple-element.32.refs_3_, ...), custom_call_target="tpu_custom_call" | custom-call | flops 2147483648 | bytes 10485760 | tf_op jit(solution)/shard_map/pallas_call | solution.py:129
  86.4 8.0 %shard_map.195 = bf16[256,1024]{1,0:T(8,128)(2,1)} custom-call(s32[8]{0:T(128)S(1)} %broadcast_xor_fusion.rows_ref, bf16[4,256,512]{2,1,0:T(8,128)(2,1)} %pad_maximum_fusion.1.refs_0_, bf16[4,256,512]{2,1,0:T(8,128)(2,1)} %collective-permute-done.10.refs_1_, bf16[4096,256]{1,0:T(8,128)(2,1)S(1)} %get-tuple-element.35.refs_2_, ...), custom_call_target="tpu_custom_call" | custom-call | flops 2147483648 | bytes 10485760 | tf_op jit(solution)/shard_map/pallas_call | solution.py:129
  95.2 4.4 %shard_map.198 = bf16[256,272]{1,0:T(8,128)(2,1)S(1)} custom-call(s32[8]{0:T(128)S(1)} %broadcast_xor_fusion.rows_ref, bf16[4,256,512]{2,1,0:T(8,128)(2,1)} %pad_maximum_fusion.1.refs_0_, bf16[4,256,512]{2,1,0:T(8,128)(2,1)} %collective-permute-done.10.refs_1_, bf16[4096,256]{1,0:T(8,128)(2,1)S(1)} %copy-done.3, bf16[4096,16]{1,0:T(8,128)(2,1)S(1)} %copy-done.2), custom_call_target="tpu_custom_call" | custom-call | flops 570425344 | bytes 4325376 | tf_op jit(solution)/shard_map/pallas_call | solution.py:129
  101.0 3.9 %shard_map.197.own_ref = f32[256,272]{1,0:T(8,128)S(1)} custom-call(s32[8]{0:T(128)S(1)} %broadcast_xor_fusion.rows_ref, bf16[4,256,512]{2,1,0:T(8,128)(2,1)S(1)} %pad_maximum_fusion.refs_0_, bf16[4,256,512]{2,1,0:T(8,128)(2,1)} %collective-permute-done.4.refs_1_, bf16[4096,256]{1,0:T(8,128)(2,1)S(1)} %copy-done.3, bf16[4096,16]{1,0:T(8,128)(2,1)S(1)} %copy-done.2), custom_call_target="tpu_custom_call" | custom-call | flops 570425344 | bytes 4325376 | tf_op jit(solution)/shard_map/pallas_call | solution.py:129
  105.0 6.7 %shard_map.201 = f32[256,1024]{1,0:T(8,128)S(1)} custom-call(s32[8]{0:T(128)S(1)} %broadcast_xor_fusion.rows_ref, bf16[4,256,512]{2,1,0:T(8,128)(2,1)S(1)} %pad_maximum_fusion.refs_0_, bf16[4,256,512]{2,1,0:T(8,128)(2,1)} %collective-permute-done.4.refs_1_, bf16[4096,256]{1,0:T(8,128)(2,1)S(1)} %copy-done.1, bf16[4096,256]{1,0:T(8,128)(2,1)} %get-tuple-element.32.refs_3_, ...), custom_call_target="tpu_custom_call" | custom-call | flops 2147483648 | bytes 10485760 | tf_op jit(solution)/shard_map/pallas_call | solution.py:129
  112.7 2.5 %collective-permute-done.13.refs_0_ = bf16[256,272]{1,0:T(8,128)(2,1)S(1)} collective-permute-done((bf16[256,272]{1,0:T(8,128)(2,1)S(1)}, bf16[256,272]{1,0:T(8,128)(2,1)S(1)}, u32[]{:S(2)}, u32[]{:S(2)}) %collective-permute-start.13) | collective-permute-done | bytes 139296 | tf_op jit(solution)/shard_map/ppermute | solution.py:40
  115.2 1.7 %shard_map.199 = (bf16[256,256]{1,0:T(8,128)(2,1)S(1)}, f32[256,16]{1,0:T(8,128)S(1)}, f32[256,16]{1,0:T(8,128)S(1)}, f32[256,16]{1,0:T(8,128)S(1)}, f32[8,16]{1,0:T(8,128)S(1)}) custom-call(s32[1,2]{1,0:T(1,128)S(1)} %copy-done.12, f32[256,272]{1,0:T(8,128)S(1)} %shard_map.197.own_ref, bf16[256,272]{1,0:T(8,128)(2,1)S(1)} %collective-permute-done.13.refs_0_, ...), custom_call_target="tpu_custom_call" | custom-call | flops 400000000 | bytes 1000000 | tf_op jit(solution)/shard_map/pallas_call | solution.py:217
  118.2 6.7 %shard_map.194.refs_0_ = f32[256,1024]{1,0:T(8,128)S(1)} custom-call(s32[8]{0:T(128)S(1)} %broadcast_xor_fusion.rows_ref, bf16[4,256,512]{2,1,0:T(8,128)(2,1)S(1)} %pad_maximum_fusion.refs_0_, bf16[4,256,512]{2,1,0:T(8,128)(2,1)} %collective-permute-done.4.refs_1_, bf16[4096,256]{1,0:T(8,128)(2,1)S(1)} %get-tuple-element.35.refs_2_, ...), custom_call_target="tpu_custom_call" | custom-call | flops 2147483648 | bytes 10485760 | tf_op jit(solution)/shard_map/pallas_call | solution.py:129
  130.8 7.9 %shard_map.200 = (f32[256,1024]{1,0:T(8,128)S(1)}, f32[2,16,64,256]{3,2,1,0:T(8,128)}) custom-call(s32[2]{0:T(128)S(1)} %get-tuple-element.39.slots_ref, s32[2,2]{1,0:T(2,128)S(1)} %and_convert_fusion.flags_ref, s32[2]{0:T(128)S(1)} %bitcast.61, f32[256,1024]{1,0:T(8,128)S(1)} %copy-done.5, bf16[256,1024]{1,0:T(8,128)(2,1)} %collective-permute-done.11.refs_1_, ...), custom_call_target="tpu_custom_call" | custom-call | flops 5000000000 | bytes 8000000 | tf_op jit(solution)/shard_map/pallas_call | solution.py:384
  (117 shorter events, 31.2 us)
Async XLA Ops:
  0.6 43.4 %collective-permute-start.5 = (bf16[256,512]{1,0:T(8,128)(2,1)}, bf16[256,512]{1,0:T(8,128)(2,1)S(1)}, u32[]{:S(2)}, u32[]{:S(2)}) collective-permute-start(bf16[256,512]{1,0:T(8,128)(2,1)} %param.19), channel_id=1, source_target_pairs={{1,0},{3,2},{5,4},{7,6},{9,8},{11,10},{13,12},{15,14},{16,17},{18,... | collective-permute-start | bytes 786440 | tf_op jit(solution)/shard_map/ppermute | solution.py:74
  1.9 42.1 %collective-permute-start.6 = (bf16[256,512]{1,0:T(8,128)(2,1)}, bf16[256,512]{1,0:T(8,128)(2,1)S(1)}, u32[]{:S(2)}, u32[]{:S(2)}) collective-permute-start(bf16[256,512]{1,0:T(8,128)(2,1)} %param.19), channel_id=1, source_target_pairs={{1,16},{3,18},{5,20},{7,22},{9,24},{11,26},{13,28},{15,30},{16,1},... | collective-permute-start | bytes 786440 | tf_op jit(solution)/shard_map/ppermute | solution.py:75
  2.6 48.4 %collective-permute-start = (bf16[256,512]{1,0:T(8,128)(2,1)}, bf16[256,512]{1,0:T(8,128)(2,1)S(1)}, u32[]{:S(2)}, u32[]{:S(2)}) collective-permute-start(bf16[256,512]{1,0:T(8,128)(2,1)} %param.19), channel_id=1, source_target_pairs={{0,16},{2,18},{4,20},{6,22},{8,24},{10,26},{12,28},{14,30},{17,1},... | collective-permute-start | bytes 786440 | tf_op jit(solution)/shard_map/ppermute | solution.py:76
  17.7 57.1 %collective-permute-start.12 = (bf16[2,1040,256]{2,1,0:T(8,128)(2,1)}, bf16[2,1040,256]{2,1,0:T(8,128)(2,1)}, u32[]{:S(2)}, u32[]{:S(2)}) collective-permute-start(bf16[2,1040,256]{2,1,0:T(8,128)(2,1)} %shard_map.196), channel_id=1, source_target_pairs={{0,1},{1,0},{2,3},{3,2},{4,5},{5,4},{6,7},{7,6},{8,9},{9,8},{10,11... | collective-permute-start | bytes 3194888 | tf_op jit(solution)/shard_map/ppermute | solution.py:40
  44.1 22.6 %copy-start.20 = (s32[4]{0:T(128)S(1)}, s32[4]{0:T(128)}, u32[]{:S(2)}) copy-start(s32[4]{0:T(128)} %param.33) | copy-start | bytes 52
  44.1 24.9 %copy-start.22 = (f32[16]{0:T(128)S(1)}, f32[16]{0:T(128)}, u32[]{:S(2)}) copy-start(f32[16]{0:T(128)} %param.25) | copy-start | bytes 196
  44.1 7.5 %collective-permute-start.8 = (bf16[256,512]{1,0:T(8,128)(2,1)S(1)}, bf16[256,512]{1,0:T(8,128)(2,1)S(1)}, u32[]{:S(2)}, u32[]{:S(2)}) collective-permute-start(bf16[256,512]{1,0:T(8,128)(2,1)S(1)} %broadcast_select_fusion), channel_id=1, source_target_pairs={{0,8},{8,0},{2,10},{10,2},{4,12},{12,4},{6,14},{14,6},{16,24},{24,... | collective-permute-start | bytes 786440 | tf_op jit(solution)/shard_map/ppermute | solution.py:35
  49.5 9.4 %collective-permute-start.7 = (bf16[256,512]{1,0:T(8,128)(2,1)S(1)}, bf16[256,512]{1,0:T(8,128)(2,1)}, u32[]{:S(2)}, u32[]{:S(2)}) collective-permute-start(bf16[256,512]{1,0:T(8,128)(2,1)S(1)} %broadcast_select_fusion), channel_id=1, source_target_pairs={{0,4},{4,0},{2,6},{6,2},{8,12},{12,8},{10,14},{14,10},{16,20},{20,... | collective-permute-start | bytes 786440 | tf_op jit(solution)/shard_map/ppermute | solution.py:35
  51.1 6.7 %collective-permute-start.2 = (bf16[256,512]{1,0:T(8,128)(2,1)S(1)}, bf16[256,512]{1,0:T(8,128)(2,1)S(1)}, u32[]{:S(2)}, u32[]{:S(2)}) collective-permute-start(bf16[256,512]{1,0:T(8,128)(2,1)S(1)} %broadcast_select_fusion.1), channel_id=1, source_target_pairs={{0,8},{8,0},{2,10},{10,2},{4,12},{12,4},{6,14},{14,6},{16,24},{24,... | collective-permute-start | bytes 786440 | tf_op jit(solution)/shard_map/ppermute | solution.py:35
  51.6 12.9 %collective-permute-start.9 = (bf16[256,512]{1,0:T(8,128)(2,1)S(1)}, bf16[256,512]{1,0:T(8,128)(2,1)}, u32[]{:S(2)}, u32[]{:S(2)}) collective-permute-start(bf16[256,512]{1,0:T(8,128)(2,1)S(1)} %collective-permute-done.8), channel_id=1, source_target_pairs={{0,4},{4,0},{2,6},{6,2},{8,12},{12,8},{10,14},{14,10},{16,20},{20,... | collective-permute-start | bytes 786440 | tf_op jit(solution)/shard_map/ppermute | solution.py:35
  53.2 16.8 %collective-permute-start.1 = (bf16[256,512]{1,0:T(8,128)(2,1)S(1)}, bf16[256,512]{1,0:T(8,128)(2,1)S(1)}, u32[]{:S(2)}, u32[]{:S(2)}) collective-permute-start(bf16[256,512]{1,0:T(8,128)(2,1)S(1)} %broadcast_select_fusion.1), channel_id=1, source_target_pairs={{0,4},{4,0},{2,6},{6,2},{8,12},{12,8},{10,14},{14,10},{16,20},{20,... | collective-permute-start | bytes 786440 | tf_op jit(solution)/shard_map/ppermute | solution.py:35
  57.8 15.6 %copy-start.18 = (bf16[256,512]{1,0:T(8,128)(2,1)}, bf16[256,512]{1,0:T(8,128)(2,1)S(1)}, u32[]{:S(2)}) copy-start(bf16[256,512]{1,0:T(8,128)(2,1)S(1)} %collective-permute-done.2) | copy-start | bytes 786436
  57.8 15.6 %collective-permute-start.3 = (bf16[256,512]{1,0:T(8,128)(2,1)S(1)}, bf16[256,512]{1,0:T(8,128)(2,1)}, u32[]{:S(2)}, u32[]{:S(2)}) collective-permute-start(bf16[256,512]{1,0:T(8,128)(2,1)S(1)} %collective-permute-done.2), channel_id=1, source_target_pairs={{0,4},{4,0},{2,6},{6,2},{8,12},{12,8},{10,14},{14,10},{16,20},{20,... | collective-permute-start | bytes 786440 | tf_op jit(solution)/shard_map/ppermute | solution.py:35
  66.7 9.0 %collective-permute-start.10 = (bf16[4,256,512]{2,1,0:T(8,128)(2,1)}, bf16[4,256,512]{2,1,0:T(8,128)(2,1)}, u32[]{:S(2)}, u32[]{:S(2)}) collective-permute-start(bf16[4,256,512]{2,1,0:T(8,128)(2,1)} %pad_maximum_fusion.1.refs_0_), channel_id=1, source_target_pairs={{0,2},{2,0},{4,6},{6,4},{8,10},{10,8},{12,14},{14,12},{16,18},{18,... | collective-permute-start | bytes 3145736 | tf_op jit(solution)/shard_map/ppermute | solution.py:35
  74.7 26.3 %collective-permute-start.4 = (bf16[4,256,512]{2,1,0:T(8,128)(2,1)S(1)}, bf16[4,256,512]{2,1,0:T(8,128)(2,1)}, u32[]{:S(2)}, u32[]{:S(2)}) collective-permute-start(bf16[4,256,512]{2,1,0:T(8,128)(2,1)S(1)} %pad_maximum_fusion.refs_0_), channel_id=1, source_target_pairs={{0,2},{2,0},{4,6},{6,4},{8,10},{10,8},{12,14},{14,12},{16,18},{18,... | collective-permute-start | bytes 3145736 | tf_op jit(solution)/shard_map/ppermute | solution.py:35
  85.1 53.6 %collective-permute-start.15 = (bf16[256,1024]{1,0:T(8,128)(2,1)}, bf16[256,1024]{1,0:T(8,128)(2,1)}, u32[]{:S(2)}, u32[]{:S(2)}) collective-permute-start(bf16[256,1024]{1,0:T(8,128)(2,1)} %shard_map.202), channel_id=1, source_target_pairs={{0,1},{1,0},{2,3},{3,2},{4,5},{5,4},{6,7},{7,6},{8,9},{9,8},{10,11... | collective-permute-start | bytes 1572872 | tf_op jit(solution)/shard_map/ppermute | solution.py:40
  94.3 10.6 %copy-start.1 = (bf16[4096,256]{1,0:T(8,128)(2,1)S(1)}, bf16[4096,256]{1,0:T(8,128)(2,1)}, u32[]{:S(2)}) copy-start(bf16[4096,256]{1,0:T(8,128)(2,1)} %get-tuple-element.34.refs_2_) | copy-start | bytes 6291460
  94.4 35.2 %collective-permute-start.11 = (bf16[256,1024]{1,0:T(8,128)(2,1)}, bf16[256,1024]{1,0:T(8,128)(2,1)}, u32[]{:S(2)}, u32[]{:S(2)}) collective-permute-start(bf16[256,1024]{1,0:T(8,128)(2,1)} %shard_map.195), channel_id=1, source_target_pairs={{0,1},{1,0},{2,3},{3,2},{4,5},{5,4},{6,7},{7,6},{8,9},{9,8},{10,11... | collective-permute-start | bytes 1572872 | tf_op jit(solution)/shard_map/ppermute | solution.py:40
  99.7 15.5 %collective-permute-start.13 = (bf16[256,272]{1,0:T(8,128)(2,1)S(1)}, bf16[256,272]{1,0:T(8,128)(2,1)S(1)}, u32[]{:S(2)}, u32[]{:S(2)}) collective-permute-start(bf16[256,272]{1,0:T(8,128)(2,1)S(1)} %shard_map.198), channel_id=1, source_target_pairs={{0,1},{1,0},{2,3},{3,2},{4,5},{5,4},{6,7},{7,6},{8,9},{9,8},{10,11... | collective-permute-start | bytes 417800 | tf_op jit(solution)/shard_map/ppermute | solution.py:40
  118.2 11.4 %copy-start.10 = (f32[4,1024]{1,0:T(4,128)S(1)}, f32[4,1024]{1,0:T(4,128)}, u32[]{:S(2)}) copy-start(f32[4,1024]{1,0:T(4,128)} %refs_3_.3) | copy-start | bytes 49156
  118.2 11.4 %copy-start.11 = (f32[1024]{0:T(1024)S(1)}, f32[1024]{0:T(1024)}, u32[]{:S(2)}) copy-start(f32[1024]{0:T(1024)} %param.27) | copy-start | bytes 12292
  118.2 10.3 %collective-permute-start.14 = (bf16[256,256]{1,0:T(8,128)(2,1)S(1)}, bf16[256,256]{1,0:T(8,128)(2,1)}, u32[]{:S(2)}, u32[]{:S(2)}) collective-permute-start(bf16[256,256]{1,0:T(8,128)(2,1)S(1)} %get-tuple-element.9), channel_id=1, source_target_pairs={{0,2},{2,0},{4,6},{6,4},{8,10},{10,8},{12,14},{14,12},{16,18},{18,... | collective-permute-start | bytes 393224 | tf_op jit(solution)/shard_map/ppermute | solution.py:35
  130.8 10.8 %copy-start.21 = (f32[1024]{0:T(1024)S(1)}, f32[1024]{0:T(1024)}, u32[]{:S(2)}) copy-start(f32[1024]{0:T(1024)} %param.30) | copy-start | bytes 12292
  140.2 1.4 collective-permute-start.16
  (18 other events, 111.5 us)

commit v3 on v2

--- a/solution.py
+++ b/solution.py
@@ -12,9 +12,8 @@
 F32 = jnp.float32
 BF16 = jnp.bfloat16
 HIGH = lax.Precision.HIGHEST
-VMEM_BYTES = 48 * 1024 * 1024
+VMEM_BYTES = 16 * 1024 * 1024
 HEADS_STEP = 4
-COLUMNS = 256
 
 
 def cost(flops, bytes_accessed):
@@ -55,12 +54,28 @@
     return far, across, diagonal
 
 
-def quad(block):
+def quad(block, along_x_last):
+    wide_index = lax.axis_index("wide")
+    upper_z, upper_x, upper = ((wide_index >> bit) % 2 == 1 for bit in (2, 1, 0))
     along_z = partner_2(block, "wide", 2)
     along_x = partner_2(block, "wide", 1)
-    both = partner_2(along_z, "wide", 1)
-    four = jnp.stack([block, along_x, along_z, both])
-    return [four, partner_2(four, "wide", 0)]
+    if along_x_last:
+        both = partner_2(along_z, "wide", 1)
+    else:
+        both = partner_2(along_x, "wide", 2)
+
+    def ordered(flag, mine, other):
+        return [jnp.where(flag, other, mine), jnp.where(flag, mine, other)]
+
+    here = ordered(upper_x, block, along_x)
+    there = ordered(upper_x, along_z, both)
+    rows = [ordered(upper_z, here[x], there[x]) for x in range(2)]
+    mine = jnp.concatenate([rows[x][z] for z in range(2) for x in range(2)], 1)
+    other = partner_2(mine, "wide", 0)
+    tokens, width = block.shape
+    pair = ordered(upper, mine, other)
+    pair = jnp.stack([half.reshape(tokens, 4, width) for half in pair], 2)
+    return pair.reshape(tokens, 8 * width)
 
 
 def features_of(x_in):
@@ -68,76 +83,22 @@
     wide_count = lax.axis_size("wide")
     me = lax.axis_index("req")
     if req_count == 2 and wide_count == 16:
-        wide_index = lax.axis_index("wide")
         axes = ("wide", "req")
         far, across, diagonal = spread_routes()
         across = lax.ppermute(x_in, axes, across)
         diagonal = lax.ppermute(x_in, axes, diagonal)
         far = lax.ppermute(x_in, axes, far)
-        near = wide_index // 8 == me
-        theirs = quad(jnp.where(near, across, diagonal))
-        own = quad(jnp.where(near, x_in, far))
-        rows = (wide_index % 8) ^ jnp.array([0, 2, 4, 6, 1, 3, 5, 7], jnp.int32)
-        return [own, theirs], rows
+        near = lax.axis_index("wide") // 8 == me
+        theirs = jnp.where(near, across, diagonal)
+        return [quad(jnp.where(near, x_in, far), False), quad(theirs, True)], theirs
     own = lax.all_gather(x_in, "wide", axis=1, tiled=True)
     parts = own.reshape(own.shape[0], req_count, own.shape[1] // req_count).transpose(1, 0, 2)
     got = lax.all_to_all(parts, "req", split_axis=0, concat_axis=0, tiled=True)
     blocks = [
-        [lax.dynamic_index_in_dim(got, (me + step) % req_count, 0, True)]
+        lax.dynamic_index_in_dim(got, (me + step) % req_count, 0, False)
         for step in range(req_count)
     ]
-    return blocks, jnp.zeros((1,), jnp.int32)
-
-
-def project_kernel(block_total, weight_total, rows_ref, *refs):
-    blocks = refs[:block_total]
-    weights = refs[block_total : block_total + weight_total]
-    out_ref = refs[block_total + weight_total]
-    held = refs[block_total + weight_total + 1 : block_total + 2 * weight_total + 1]
-    sems = refs[-1]
-    copies = []
-    for place in range(weight_total):
-        copy = pltpu.make_async_copy(weights[place], held[place], sems.at[place])
-        copy.start()
-        copies.append(copy)
-    column = 0
-    for place in range(weight_total):
-        copies[place].wait()
-        total = None
-        index = 0
-        for block in blocks:
-            for part in range(block.shape[0]):
-                depth = block.shape[2]
-                start = pl.multiple_of(rows_ref[index] * depth, depth)
-                term = jnp.dot(
-                    block[part],
-                    held[place][pl.ds(start, depth), :],
-                    preferred_element_type=F32,
-                )
-                total = term if total is None else total + term
-                index += 1
-        width = held[place].shape[1]
-        out_ref[:, column : column + width] = total.astype(out_ref.dtype)
-        column += width
-
-
-def project(blocks, rows, weights, kind):
-    tokens = blocks[0].shape[1]
-    width = sum(weight.shape[1] for weight in weights)
-    depth = weights[0].shape[0]
-    any_space = pl.BlockSpec(memory_space=pl.ANY)
-    return pl.pallas_call(
-        functools.partial(project_kernel, len(blocks), len(weights)),
-        out_shape=jax.ShapeDtypeStruct((tokens, width), kind),
-        in_specs=[pl.BlockSpec(memory_space=pltpu.SMEM)]
-        + [pl.BlockSpec(memory_space=pltpu.VMEM)] * len(blocks)
-        + [any_space] * len(weights),
-        out_specs=pl.BlockSpec(memory_space=pltpu.VMEM),
-        scratch_shapes=[pltpu.VMEM(weight.shape, BF16) for weight in weights]
-        + [pltpu.SemaphoreType.DMA((len(weights),))],
-        compiler_params=params(),
-        cost_estimate=cost(2 * tokens * width * depth, 2 * depth * (width + tokens)),
-    )(rows, *blocks, *weights)
+    return blocks, x_in
 
 
 def token_places(starts, count_tok, shape, axis):
@@ -174,7 +135,7 @@
 ):
     got = refs[:got_total]
     cache_ref, kernel_ref, bias_ref, dt_bias_ref, a_log_ref = refs[got_total : got_total + 5]
-    bc_ref, cum_ref, step_ref, coef_ref, decay_ref = refs[got_total + 5 :]
+    bc_ref, cum_ref, cum_t_ref, step_t_ref, coef_ref, decay_ref = refs[got_total + 5 :]
     tokens = own_ref.shape[0]
     channels = bias_ref.shape[1]
     heads = dt_bias_ref.shape[1]
@@ -196,9 +157,18 @@
     after = jnp.where(same & (position < other), 1.0, 0.0)
     cum = jnp.dot(mask, rate, precision=HIGH, preferred_element_type=F32)
     left = jnp.dot(after, rate, precision=HIGH, preferred_element_type=F32)
-    cum_ref[...] = cum
-    step_ref[...] = step
-    coef_ref[...] = jnp.exp(left) * step
+    cum_t = lax.dot_general(
+        rate, mask, (((0,), (1,)), ((), ())), precision=HIGH, preferred_element_type=F32
+    )
+    step_t = step.T
+    coef = jnp.exp(left) * step
+    part = cum_ref.shape[2]
+    for i in range(cum_ref.shape[0]):
+        place = slice(i * part, (i + 1) * part)
+        cum_ref[i] = cum[:, place]
+        cum_t_ref[i] = cum_t[place, :]
+        step_t_ref[i] = step_t[place, :]
+        coef_ref[i] = coef[:, place]
     at, seg_at, _ = token_places(starts, tokens, (8, tokens), 1)
     row = lax.broadcasted_iota(jnp.int32, (8, tokens), 0)
     ends = jnp.dot(
@@ -213,18 +183,21 @@
     heads = dt_bias.shape[0]
     count_req = cache.shape[0]
     vmem = pl.BlockSpec(memory_space=pltpu.VMEM)
-    small = jax.ShapeDtypeStruct((tokens, heads), F32)
+    part = min(HEADS_STEP, heads)
+    tall = jax.ShapeDtypeStruct((heads // part, tokens, part), F32)
+    flat = jax.ShapeDtypeStruct((heads // part, part, tokens), F32)
     return pl.pallas_call(
         functools.partial(prep_kernel, count_req, len(got)),
         out_shape=[
             jax.ShapeDtypeStruct((tokens, channels), BF16),
-            small,
-            small,
-            small,
+            tall,
+            flat,
+            flat,
+            tall,
             jax.ShapeDtypeStruct((8, heads), F32),
         ],
         in_specs=[pl.BlockSpec(memory_space=pltpu.SMEM)] + [vmem] * (6 + len(got)),
-        out_specs=[vmem] * 5,
+        out_specs=[vmem] * 6,
         compiler_params=params(),
         cost_estimate=cost(4e8, 1e6),
     )(starts, own, *got, cache, kernel, bias[None], dt_bias[None], a_log[None])
@@ -338,8 +311,8 @@
 
 
 def mixer(
-    slots, flags, starts, own, got, cache, kernel, bias, b_maps, c_maps, cum, step, coef, decay,
-    skip, pool, states
+    slots, flags, starts, own, got, cache, kernel, bias, b_maps, c_maps, cum, cum_t, step_t, coef,
+    decay, skip, pool, states
 ):
     tokens, channels = own.shape
     _, heads, width, state = pool.shape
@@ -350,12 +323,6 @@
     wide = part * width
     columns = lambda i, *_: (0, i)
     whole = lambda i, *_: (0, 0)
-
-    def by_step(array):
-        return array.reshape(tokens, steps, part).transpose(1, 0, 2)
-
-    def by_step_t(array):
-        return array.T.reshape(steps, part, tokens)
 
     in_specs = (
         [pl.BlockSpec((tokens, wide), columns)] * (1 + len(got))
@@ -405,7 +372,7 @@
         cost_estimate=cost(5e9, 8e6),
     )(
         slots, flags, starts, own, *got, cache, kernel, bias[None], b_maps, c_maps,
-        by_step(cum), by_step_t(cum), by_step_t(step), by_step(coef), decay,
+        cum, cum_t, step_t, coef, decay,
         jnp.repeat(skip, width)[None], *([pool] * count_req), *states
     )
 
@@ -439,7 +406,7 @@
     lags = conv_x_pool.shape[1]
     conv_width = local_width + state_part
 
-    features, rows = features_of(x_in)
+    features, arrived = features_of(x_in)
 
     def slots_of(index):
         asked = lax.dynamic_slice_in_dim(state_slot, index * group_reqs, group_reqs)
@@ -477,23 +444,35 @@
         cache = jnp.where((came_from == step)[:, None, None], got, cache)
     cache = jnp.where(live[:, None, None], cache, 0).astype(F32)
 
-    pieces = []
-    for first in range(0, local_width, COLUMNS):
-        piece = jnp.transpose(w_xz[:, :, first : first + COLUMNS], (1, 0, 2))
-        pieces.append(lax.optimization_barrier(piece))
+    half = w_xz.shape[0] // 2
+    first = lax.optimization_barrier(jnp.transpose(w_xz[:half], (1, 0, 2)))
+    last, _ = lax.optimization_barrier((w_xz[half:], arrived))
+    last = lax.optimization_barrier(jnp.transpose(last, (1, 0, 2)))
+    w_map = jnp.concatenate([w_bc, w_dt], 1)
     weights = {
-        "map": [w_bc, w_dt],
-        "xr": [piece[1] for piece in pieces],
-        "z": [piece[0] for piece in pieces],
+        "map": (w_map[:half], w_map[half:]),
+        "xr": (first[1], last[1]),
+        "z": (first[0], last[0]),
     }
+
+    def project(block, name):
+        return jnp.dot(
+            block[:, :half], weights[name][0], preferred_element_type=F32
+        ) + jnp.dot(block[:, half:], weights[name][1], preferred_element_type=F32)
+
     came = {name: [] for name in weights}
+    order = features[0]
     for step in range(1, req_count):
+        block = features[step]
         for name in weights:
-            part = project(features[step], rows, weights[name], BF16)
+            part, block = lax.optimization_barrier((project(block, name).astype(BF16), block))
             came[name].append(shift_req(part, step))
-    own = {name: project(features[0], rows, weights[name], F32) for name in weights}
-
-    bc_conv, cum, step, coef, decay = prep(
+            order, _ = lax.optimization_barrier((order, part))
+    own = {}
+    for name in weights:
+        own[name], order = lax.optimization_barrier((project(order, name), order))
+
+    bc_conv, cum, cum_t, step_t, coef, decay = prep(
         stretch_start, own["map"], came["map"], cache[:, :, local_width:], conv_bc_w, conv_bc_b,
         dt_bias, a_log
     )
@@ -510,8 +489,8 @@
     state_width = joined.shape[1] // 2
     result, final_state = mixer(
         own_slots, flags, stretch_start[0], own["xr"], came["xr"], cache[:, :, :local_width],
-        conv_x_w, conv_x_b, joined[:, :state_width], joined[:, state_width:], cum, step, coef,
-        decay, d_skip, ssm_pool, got_states
+        conv_x_w, conv_x_b, joined[:, :state_width], joined[:, state_width:], cum, cum_t,
+        step_t, coef, decay, d_skip, ssm_pool, got_states
     )
     gate = own["z"]
     for got in came["z"]:

time: 144 us -> 144 us (level)
  Pallas kernels: 50.1 us -> 10 us
  matrix products: 0 us -> 20.5 us
  starting transfers between devices: 22.6 us -> 31.8 us
  local copies, waits for them, and re-layouts: 41.2 us -> 49.2 us
  other arithmetic: 9.87 us -> 17.3 us
  waiting for transfers between devices: 17.6 us -> 13.3 us
    pallas_call x6 -> x0, Pallas kernels: 37.6 us -> none  [project(): pl.pallas_call(functools.partial(project_kernel, len(blocks), len(weights...]
    dot_general x0 -> x12, matrix products: none -> 20.5 us  [the longest x6 10.9 us: project(): jnp.dot(block[:, :half], weights[name][0], preferred_element_type=F32)]
    squeeze x4 -> x0, local copies, waits for them, and re-layouts: 10.7 us -> none  [on_device(): piece[0]]
    optimization_barrier x0 -> x1, local copies, waits for them, and re-layouts: none -> 9.36 us  [on_device(): last, _ = lax.optimization_barrier((w_xz[half:], arrived))]
    ppermute x4, starting transfers between devices: 4.24 us -> 12.8 us  [shift_req(): lax.ppermute(block, 'req', [(i, (i + step) % count) for i in range(count)])]
    unnamed x55 -> x76, local copies, waits for them, and re-layouts: 9.16 us -> 17.4 us
    select_n x0 -> x4, local copies, waits for them, and re-layouts: none -> 8.12 us  [ordered(): return [jnp.where(flag, other, mine), jnp.where(flag, mine, other)]]
    select_n x2 -> x5, other arithmetic: 0.07 us -> 6.75 us  [the longest x3 5.96 us: ordered(): return [jnp.where(flag, other, mine), jnp.where(flag, mine, other)]]
  transfers between devices with their start and end apart: 17 -> 17, of which waited for: 7 -> 6; matrix products, arithmetic and copies ran while one was open for 30% -> 38% of each run, Pallas kernels for 35% -> 7%
where the time goes in v3:
time: 144 us
  local copies, waits for them, and re-layouts  49.2 us (34%)
  starting transfers between devices  31.8 us (22%)
  matrix products  20.5 us (14%)
  other arithmetic  17.3 us (12%)
  waiting for transfers between devices  13.3 us (9%)
  Pallas kernels  10 us (7%)
    unnamed x76, local copies, waits for them, and re-layouts  17.4 us
    slice x1, local copies, waits for them, and re-layouts, on_device(): last, _ = lax.optimization_barrier((w_xz[half:], arrived))  14.1 us
    ppermute x4, starting transfers between devices, shift_req(): lax.ppermute(block, 'req', [(i, (i + step) % count) for i in range(count)])  12.8 us
    dot_general x6, matrix products, project(): jnp.dot(block[:, :half], weights[name][0], preferred_element_type=F32)  10.9 us
    dot_general x6, matrix products, project(): jnp.dot(block[:, half:], weights[name][1], preferred_element_type=F32)  9.56 us
    optimization_barrier x1, local copies, waits for them, and re-layouts, on_device(): last, _ = lax.optimization_barrier((w_xz[half:], arrived))  9.36 us
    ppermute x1, starting transfers between devices, features_of(): far = lax.ppermute(x_in, axes, far)  9.35 us
    ppermute x10, waiting for transfers between devices, partner_2(): return lax.ppermute(block, axis, route)  8.65 us
  transfers between devices with their start and end apart: 17, of which 6 were waited for; matrix products, arithmetic and copies ran while one was open for 38% of the time, Pallas kernels for 7%

profile of v3, /device:TPU:0, one launch (start us, length us, event | category | flops | bytes accessed | tf_op | source)
XLA Modules:
  0.0 143.5 jit_solution(15332531501571374212)
XLA Ops:
  2.6 9.4 %collective-permute-start = (bf16[256,512]{1,0:T(8,128)(2,1)}, bf16[256,512]{1,0:T(8,128)(2,1)S(1)}, u32[]{:S(2)}, u32[]{:S(2)}) collective-permute-start(bf16[256,512]{1,0:T(8,128)(2,1)} %param.18), channel_id=1, source_target_pairs={{0,16},{2,18},{4,20},{6,22},{8,24},{10,26},{12,28},{14,30},{17,1},... | collective-permute-start | bytes 786440 | tf_op jit(solution)/shard_map/ppermute | solution.py:90
  14.7 1.9 %collective-permute-start.7 = (bf16[256,512]{1,0:T(8,128)(2,1)S(1)}, bf16[256,512]{1,0:T(8,128)(2,1)S(1)}, u32[]{:S(2)}, u32[]{:S(2)}) collective-permute-start(bf16[256,512]{1,0:T(8,128)(2,1)S(1)} %broadcast_select_fusion.4), channel_id=1, source_target_pairs={{0,8},{8,0},{2,10},{10,2},{4,12},{12,4},{6,14},{14,6},{16,24},{24,... | collective-permute-start | bytes 786440 | tf_op jit(solution)/shard_map/ppermute | solution.py:34
  16.7 3.4 %copy-done = f32[8,16,64,256]{3,2,1,0:T(8,128)S(1)} copy-done((f32[8,16,64,256]{3,2,1,0:T(8,128)S(1)}, f32[8,16,64,256]{3,2,1,0:T(8,128)}, u32[]{:S(2)}) %copy-start) | copy-done | bytes 8388632
  20.8 7.7 %collective-permute-start.12 = (bf16[2,1040,256]{2,1,0:T(8,128)(2,1)S(1)}, bf16[2,1040,256]{2,1,0:T(8,128)(2,1)S(1)}, u32[]{:S(2)}, u32[]{:S(2)}) collective-permute-start(bf16[2,1040,256]{2,1,0:T(8,128)(2,1)S(1)} %shard_map.185), channel_id=1, source_target_pairs={{0,1},{1,0},{2,3},{3,2},{4,5},{5,4},{6,7},{7,6},{8,9},{9,8},{10,11... | collective-permute-start | bytes 3194888 | tf_op jit(solution)/shard_map/ppermute | solution.py:39
  32.8 14.1 %fusion.42 = (bf16[2048,2,1024]{2,1,0:T(2,128)(2,1)}, bf16[2048,2,1024]{2,1,0:T(2,128)(2,1)}) fusion(bf16[4096,2,1024]{2,1,0:T(2,128)(2,1)} %param.19), kind=kLoop, calls=%fused_computation.104 | loop fusion | bytes 33554432 | tf_op jit(solution)/shard_map/slice | solution.py:449
  52.2 4.2 %collective-permute-done.3 = bf16[256,512]{1,0:T(8,128)(2,1)S(1)} collective-permute-done((bf16[256,512]{1,0:T(8,128)(2,1)}, bf16[256,512]{1,0:T(8,128)(2,1)S(1)}, u32[]{:S(2)}, u32[]{:S(2)}) %collective-permute-start.3) | collective-permute-done | bytes 262176 | tf_op jit(solution)/shard_map/ppermute | solution.py:34
  56.5 3.2 %collective-permute-done.2 = bf16[256,512]{1,0:T(8,128)(2,1)S(1)} collective-permute-done((bf16[256,512]{1,0:T(8,128)(2,1)}, bf16[256,512]{1,0:T(8,128)(2,1)S(1)}, u32[]{:S(2)}, u32[]{:S(2)}) %collective-permute-start.2) | collective-permute-done | bytes 262176 | tf_op jit(solution)/shard_map/ppermute | solution.py:34
  62.8 2.2 %copy.44 = bf16[4096,16]{1,0:T(8,128)(2,1)} copy(bf16[4096,16]{0,1:T(8,128)(2,1)} %param.20) | data formatting | bytes 262144 | tf_op args[2]
  65.0 9.4 %copy.62 = bf16[2048,2,1024]{2,0,1:T(8,128)(2,1)} copy(bf16[2048,2,1024]{2,1,0:T(2,128)(2,1)} %get-tuple-element.55) | data formatting | bytes 16777216
  74.3 9.4 %copy.56 = bf16[2048,2,1024]{2,0,1:T(8,128)(2,1)} copy(bf16[2048,2,1024]{2,1,0:T(2,128)(2,1)} %get-tuple-element.54) | data formatting | bytes 16777216 | tf_op jit(solution)/shard_map/optimization_barrier | solution.py:449
  84.2 3.6 %broadcast_select_fusion.1 = (bf16[256,2048]{1,0:T(8,128)(2,1)}, bf16[256,2048]{1,0:T(8,128)(2,1)}, bf16[256,2048]{1,0:T(8,128)(2,1)S(1)}, bf16[256,2048]{1,0:T(8,128)(2,1)}) fusion(bf16[256,2048]{1,0:T(8,128)(2,1)} %collective-permute-done.10, pred[]{:T(512)S(6)} %eq.82, bf16[256,512]{1,0:T(8,128)(2,1)} %copy-done.10, bf16[256,512]{1,0:T(8,128)(2,1)} %copy-done.9, ...), kind=kLoop, calls=%fused_computation.54 | loop fusion | flops 10485760 | bytes 8388609 | tf_op jit(solution)/shard_map/jit(_where)/select_n | solution.py:68
  87.9 2.3 %copy.42 = bf16[256,2048]{0,1:T(8,128)(2,1)} copy(bf16[256,2048]{1,0:T(8,128)(2,1)} %get-tuple-element.56) | data formatting | bytes 2097152 | tf_op jit(solution)/shard_map/jit(_where)/select_n | solution.py:68
  90.1 2.3 %copy.43 = bf16[256,2048]{0,1:T(8,128)(2,1)} copy(bf16[256,2048]{1,0:T(8,128)(2,1)} %get-tuple-element.57) | data formatting | bytes 2097152 | tf_op jit(solution)/shard_map/jit(_where)/select_n | solution.py:68
  92.4 1.9 %pad_maximum_fusion.1 = bf16[256,4,2,512]{0,3,2,1:T(8,128)(2,1)S(1)} fusion(bf16[256,4,1,512]{0,3,2,1:T(8,128)(2,1)} %bitcast.80, bf16[256,4,1,512]{0,3,2,1:T(8,128)(2,1)} %bitcast.79), kind=kLoop, calls=%fused_computation.16 | loop fusion | flops 1048576 | bytes 4194304 | tf_op jit(solution)/shard_map/stack | solution.py:77
  96.5 4.1 %fusion.1 = f32[256,1024]{1,0:T(8,128)S(1)} fusion(bf16[2,2048,1024]{2,1,0:T(8,128)(2,1)} %bitcast.69, bf16[256,4096]{0,1:T(8,128)(2,1)S(1)} %bitcast.89), kind=kOutput, calls=%fused_computation.6 | convolution fusion | flops 1073741824 | bytes 6291456 | tf_op jit(solution)/shard_map/dot_general | solution.py:459
  100.7 2.1 %fusion.13 = bf16[256,1024]{1,0:T(8,128)(2,1)} fusion(f32[256,1024]{1,0:T(8,128)S(1)} %fusion.1, bf16[2,2048,1024]{2,1,0:T(8,128)(2,1)S(1)} %bitcast.63, bf16[256,4096]{0,1:T(8,128)(2,1)S(1)} %bitcast.90), kind=kOutput, calls=%fused_computation.25 | convolution fusion | flops 1074266112 | bytes 6815744 | tf_op jit(solution)/shard_map/dot_general | solution.py:461
  104.2 2.1 %fusion.14 = bf16[256,1024]{1,0:T(8,128)(2,1)} fusion(f32[256,1024]{1,0:T(8,128)S(1)} %fusion.5, bf16[2,2048,1024]{2,1,0:T(8,128)(2,1)S(1)} %bitcast.64, bf16[256,4096]{0,1:T(8,128)(2,1)S(1)} %bitcast.92), kind=kOutput, calls=%fused_computation.26 | convolution fusion | flops 1074266112 | bytes 6815744 | tf_op jit(solution)/shard_map/dot_general | solution.py:461
  106.3 2.3 %copy.40 = bf16[256,2048]{0,1:T(8,128)(2,1)} copy(bf16[256,2048]{1,0:T(8,128)(2,1)} %get-tuple-element.75) | data formatting | bytes 2097152 | tf_op jit(solution)/shard_map/jit(_where)/select_n | solution.py:68
  109.9 3.0 %collective-permute-start.13 = (bf16[256,272]{1,0:T(8,128)(2,1)S(1)}, bf16[256,272]{1,0:T(8,128)(2,1)S(1)}, u32[]{:S(2)}, u32[]{:S(2)}) collective-permute-start(bf16[256,272]{1,0:T(8,128)(2,1)S(1)} %fusion.15), channel_id=1, source_target_pairs={{0,1},{1,0},{2,3},{3,2},{4,5},{5,4},{6,7},{7,6},{8,9},{9,8},{10,11... | collective-permute-start | bytes 417800 | tf_op jit(solution)/shard_map/ppermute | solution.py:39
  114.9 2.0 %collective-permute-start.15 = (bf16[256,1024]{1,0:T(8,128)(2,1)}, bf16[256,1024]{1,0:T(8,128)(2,1)S(1)}, u32[]{:S(2)}, u32[]{:S(2)}) collective-permute-start(bf16[256,1024]{1,0:T(8,128)(2,1)} %fusion.14), channel_id=1, source_target_pairs={{0,1},{1,0},{2,3},{3,2},{4,5},{5,4},{6,7},{7,6},{8,9},{9,8},{10,11... | collective-permute-start | bytes 1572872 | tf_op jit(solution)/shard_map/ppermute | solution.py:39
  116.9 2.3 %fusion.28 = f32[256,272]{1,0:T(8,128)S(1)} fusion(bf16[256,4096]{0,1:T(8,128)(2,1)S(1)} %bitcast.81, bf16[4096,256]{1,0:T(8,128)(2,1)} %param.21, bf16[4096,16]{1,0:T(8,128)(2,1)} %copy.44), kind=kOutput, calls=%fused_computation.47 | convolution fusion | flops 287440896 | bytes 3555328 | tf_op jit(solution)/shard_map/dot_general | solution.py:459
  119.2 2.1 %convolution_add_fusion.own_ref = f32[256,272]{1,0:T(8,128)S(1)} fusion(f32[256,272]{1,0:T(8,128)S(1)} %fusion.28, bf16[256,4096]{0,1:T(8,128)(2,1)S(1)} %bitcast.82, bf16[4096,16]{1,0:T(8,128)(2,1)S(1)} %copy-done.16, bf16[4096,256]{1,0:T(8,128)(2,1)} %param.21), kind=kOutput, calls=%fused_computation.27 | convolution fusion | flops 287510528 | bytes 4866048 | tf_op jit(solution)/shard_map/dot_general | solution.py:461
  129.9 7.6 %shard_map.187 = (f32[256,1024]{1,0:T(8,128)S(1)}, f32[2,16,64,256]{3,2,1,0:T(8,128)}) custom-call(s32[2]{0:T(128)S(1)} %get-tuple-element.71.slots_ref, s32[2,2]{1,0:T(2,128)S(1)} %and_convert_fusion.flags_ref, s32[2]{0:T(128)S(1)} %bitcast.57, f32[256,1024]{1,0:T(8,128)S(1)} %fusion.12.refs_0_, bf16[256,1024]{1,0:T(8,128)(2,1)S(1)} %collective-permute-done.11.refs_1_, ...), custom_call_target="tpu_custom_call" | custom-call | flops 5000000000 | bytes 8000000 | tf_op jit(solution)/shard_map/pallas_call | solution.py:351
  137.5 3.5 %collective-permute-done.15 = bf16[256,1024]{1,0:T(8,128)(2,1)S(1)} collective-permute-done((bf16[256,1024]{1,0:T(8,128)(2,1)}, bf16[256,1024]{1,0:T(8,128)(2,1)S(1)}, u32[]{:S(2)}, u32[]{:S(2)}) %collective-permute-start.15) | collective-permute-done | bytes 524320 | tf_op jit(solution)/shard_map/ppermute | solution.py:39
  (142 shorter events, 36.3 us)
Async XLA Ops:
  0.6 14.0 %collective-permute-start.5 = (bf16[256,512]{1,0:T(8,128)(2,1)}, bf16[256,512]{1,0:T(8,128)(2,1)S(1)}, u32[]{:S(2)}, u32[]{:S(2)}) collective-permute-start(bf16[256,512]{1,0:T(8,128)(2,1)} %param.18), channel_id=1, source_target_pairs={{1,0},{3,2},{5,4},{7,6},{9,8},{11,10},{13,12},{15,14},{16,17},{18,... | collective-permute-start | bytes 786440 | tf_op jit(solution)/shard_map/ppermute | solution.py:88
  1.9 12.7 %collective-permute-start.6 = (bf16[256,512]{1,0:T(8,128)(2,1)}, bf16[256,512]{1,0:T(8,128)(2,1)S(1)}, u32[]{:S(2)}, u32[]{:S(2)}) collective-permute-start(bf16[256,512]{1,0:T(8,128)(2,1)} %param.18), channel_id=1, source_target_pairs={{1,16},{3,18},{5,20},{7,22},{9,24},{11,26},{13,28},{15,30},{16,1},... | collective-permute-start | bytes 786440 | tf_op jit(solution)/shard_map/ppermute | solution.py:89
  2.6 27.4 %collective-permute-start = (bf16[256,512]{1,0:T(8,128)(2,1)}, bf16[256,512]{1,0:T(8,128)(2,1)S(1)}, u32[]{:S(2)}, u32[]{:S(2)}) collective-permute-start(bf16[256,512]{1,0:T(8,128)(2,1)} %param.18), channel_id=1, source_target_pairs={{0,16},{2,18},{4,20},{6,22},{8,24},{10,26},{12,28},{14,30},{17,1},... | collective-permute-start | bytes 786440 | tf_op jit(solution)/shard_map/ppermute | solution.py:90
  14.7 16.6 %collective-permute-start.7 = (bf16[256,512]{1,0:T(8,128)(2,1)S(1)}, bf16[256,512]{1,0:T(8,128)(2,1)S(1)}, u32[]{:S(2)}, u32[]{:S(2)}) collective-permute-start(bf16[256,512]{1,0:T(8,128)(2,1)S(1)} %broadcast_select_fusion.4), channel_id=1, source_target_pairs={{0,8},{8,0},{2,10},{10,2},{4,12},{12,4},{6,14},{14,6},{16,24},{24,... | collective-permute-start | bytes 786440 | tf_op jit(solution)/shard_map/ppermute | solution.py:34
  20.1 9.9 %copy-start.17 = (bf16[256,512]{1,0:T(8,128)(2,1)S(1)}, bf16[256,512]{1,0:T(8,128)(2,1)}, u32[]{:S(2)}) copy-start(bf16[256,512]{1,0:T(8,128)(2,1)} %param.18) | copy-start | bytes 786436
  20.8 63.2 %collective-permute-start.12 = (bf16[2,1040,256]{2,1,0:T(8,128)(2,1)S(1)}, bf16[2,1040,256]{2,1,0:T(8,128)(2,1)S(1)}, u32[]{:S(2)}, u32[]{:S(2)}) collective-permute-start(bf16[2,1040,256]{2,1,0:T(8,128)(2,1)S(1)} %shard_map.185), channel_id=1, source_target_pairs={{0,1},{1,0},{2,3},{3,2},{4,5},{5,4},{6,7},{7,6},{8,9},{9,8},{10,11... | collective-permute-start | bytes 3194888 | tf_op jit(solution)/shard_map/ppermute | solution.py:39
  28.5 20.5 %collective-permute-start.9 = (bf16[256,512]{1,0:T(8,128)(2,1)S(1)}, bf16[256,512]{1,0:T(8,128)(2,1)S(1)}, u32[]{:S(2)}, u32[]{:S(2)}) collective-permute-start(bf16[256,512]{1,0:T(8,128)(2,1)S(1)} %broadcast_select_fusion.4), channel_id=1, source_target_pairs={{0,4},{4,0},{2,6},{6,2},{8,12},{12,8},{10,14},{14,10},{16,20},{20,... | collective-permute-start | bytes 786440 | tf_op jit(solution)/shard_map/ppermute | solution.py:34
  30.8 17.5 %collective-permute-start.1 = (bf16[256,512]{1,0:T(8,128)(2,1)}, bf16[256,512]{1,0:T(8,128)(2,1)}, u32[]{:S(2)}, u32[]{:S(2)}) collective-permute-start(bf16[256,512]{1,0:T(8,128)(2,1)} %broadcast_select_fusion.5), channel_id=1, source_target_pairs={{0,4},{4,0},{2,6},{6,2},{8,12},{12,8},{10,14},{14,10},{16,20},{20,... | collective-permute-start | bytes 786440 | tf_op jit(solution)/shard_map/ppermute | solution.py:34
  31.4 15.6 %copy-start.18 = (bf16[256,512]{1,0:T(8,128)(2,1)}, bf16[256,512]{1,0:T(8,128)(2,1)S(1)}, u32[]{:S(2)}) copy-start(bf16[256,512]{1,0:T(8,128)(2,1)S(1)} %collective-permute-done.7) | copy-start | bytes 786436
  31.4 18.4 %collective-permute-start.8 = (bf16[256,512]{1,0:T(8,128)(2,1)S(1)}, bf16[256,512]{1,0:T(8,128)(2,1)}, u32[]{:S(2)}, u32[]{:S(2)}) collective-permute-start(bf16[256,512]{1,0:T(8,128)(2,1)S(1)} %collective-permute-done.7), channel_id=1, source_target_pairs={{0,4},{4,0},{2,6},{6,2},{8,12},{12,8},{10,14},{14,10},{16,20},{20,... | collective-permute-start | bytes 786440 | tf_op jit(solution)/shard_map/ppermute | solution.py:34
  47.0 9.5 %collective-permute-start.3 = (bf16[256,512]{1,0:T(8,128)(2,1)}, bf16[256,512]{1,0:T(8,128)(2,1)S(1)}, u32[]{:S(2)}, u32[]{:S(2)}) collective-permute-start(bf16[256,512]{1,0:T(8,128)(2,1)} %broadcast_select_fusion.5), channel_id=1, source_target_pairs={{0,8},{8,0},{2,10},{10,2},{4,12},{12,4},{6,14},{14,6},{16,24},{24,... | collective-permute-start | bytes 786440 | tf_op jit(solution)/shard_map/ppermute | solution.py:34
  48.3 11.4 %collective-permute-start.2 = (bf16[256,512]{1,0:T(8,128)(2,1)}, bf16[256,512]{1,0:T(8,128)(2,1)S(1)}, u32[]{:S(2)}, u32[]{:S(2)}) collective-permute-start(bf16[256,512]{1,0:T(8,128)(2,1)} %collective-permute-done.1), channel_id=1, source_target_pairs={{0,8},{8,0},{2,10},{10,2},{4,12},{12,4},{6,14},{14,6},{16,24},{24,... | collective-permute-start | bytes 786440 | tf_op jit(solution)/shard_map/ppermute | solution.py:34
  51.0 9.8 %copy-start.8 = (bf16[256,512]{1,0:T(8,128)(2,1)}, bf16[256,512]{1,0:T(8,128)(2,1)S(1)}, u32[]{:S(2)}) copy-start(bf16[256,512]{1,0:T(8,128)(2,1)S(1)} %get-tuple-element.61) | copy-start | bytes 786436
  51.0 9.8 %copy-start.9 = (bf16[256,512]{1,0:T(8,128)(2,1)}, bf16[256,512]{1,0:T(8,128)(2,1)S(1)}, u32[]{:S(2)}) copy-start(bf16[256,512]{1,0:T(8,128)(2,1)S(1)} %get-tuple-element.62) | copy-start | bytes 786436
  51.0 9.8 %copy-start.10 = (bf16[256,512]{1,0:T(8,128)(2,1)}, bf16[256,512]{1,0:T(8,128)(2,1)S(1)}, u32[]{:S(2)}) copy-start(bf16[256,512]{1,0:T(8,128)(2,1)S(1)} %get-tuple-element.63) | copy-start | bytes 786436
  52.2 10.5 %copy-start.24 = (s32[2]{0:T(128)S(1)}, s32[2]{0:T(128)}, u32[]{:S(2)}) copy-start(s32[2]{0:T(128)} %param.31) | copy-start | bytes 28
  52.2 32.0 %collective-permute-start.10 = (bf16[256,2048]{1,0:T(8,128)(2,1)}, bf16[256,2048]{1,0:T(8,128)(2,1)}, u32[]{:S(2)}, u32[]{:S(2)}) collective-permute-start(bf16[256,2048]{1,0:T(8,128)(2,1)} %pad_maximum_fusion.4), channel_id=1, source_target_pairs={{0,2},{2,0},{4,6},{6,4},{8,10},{10,8},{12,14},{14,12},{16,18},{18,... | collective-permute-start | bytes 3145736 | tf_op jit(solution)/shard_map/ppermute | solution.py:34
  60.9 13.5 %copy-start.11 = (bf16[256,512]{1,0:T(8,128)(2,1)}, bf16[256,512]{1,0:T(8,128)(2,1)S(1)}, u32[]{:S(2)}) copy-start(bf16[256,512]{1,0:T(8,128)(2,1)S(1)} %get-tuple-element.64) | copy-start | bytes 786436
  62.7 21.5 %collective-permute-start.4 = (bf16[256,2048]{1,0:T(8,128)(2,1)}, bf16[256,2048]{1,0:T(8,128)(2,1)}, u32[]{:S(2)}, u32[]{:S(2)}) collective-permute-start(bf16[256,2048]{1,0:T(8,128)(2,1)} %pad_maximum_fusion.3), channel_id=1, source_target_pairs={{0,2},{2,0},{4,6},{6,4},{8,10},{10,8},{12,14},{14,12},{16,18},{18,... | collective-permute-start | bytes 3145736 | tf_op jit(solution)/shard_map/ppermute | solution.py:34
  109.9 15.4 %collective-permute-start.13 = (bf16[256,272]{1,0:T(8,128)(2,1)S(1)}, bf16[256,272]{1,0:T(8,128)(2,1)S(1)}, u32[]{:S(2)}, u32[]{:S(2)}) collective-permute-start(bf16[256,272]{1,0:T(8,128)(2,1)S(1)} %fusion.15), channel_id=1, source_target_pairs={{0,1},{1,0},{2,3},{3,2},{4,5},{5,4},{6,7},{7,6},{8,9},{9,8},{10,11... | collective-permute-start | bytes 417800 | tf_op jit(solution)/shard_map/ppermute | solution.py:39
  114.8 15.1 %collective-permute-start.11 = (bf16[256,1024]{1,0:T(8,128)(2,1)}, bf16[256,1024]{1,0:T(8,128)(2,1)S(1)}, u32[]{:S(2)}, u32[]{:S(2)}) collective-permute-start(bf16[256,1024]{1,0:T(8,128)(2,1)} %fusion.13), channel_id=1, source_target_pairs={{0,1},{1,0},{2,3},{3,2},{4,5},{5,4},{6,7},{7,6},{8,9},{9,8},{10,11... | collective-permute-start | bytes 1572872 | tf_op jit(solution)/shard_map/ppermute | solution.py:39
  114.9 26.0 %collective-permute-start.15 = (bf16[256,1024]{1,0:T(8,128)(2,1)}, bf16[256,1024]{1,0:T(8,128)(2,1)S(1)}, u32[]{:S(2)}, u32[]{:S(2)}) collective-permute-start(bf16[256,1024]{1,0:T(8,128)(2,1)} %fusion.14), channel_id=1, source_target_pairs={{0,1},{1,0},{2,3},{3,2},{4,5},{5,4},{6,7},{7,6},{8,9},{9,8},{10,11... | collective-permute-start | bytes 1572872 | tf_op jit(solution)/shard_map/ppermute | solution.py:39
  127.2 1.4 collective-permute-start.14
  141.4 1.2 collective-permute-start.16
  (28 other events, 107.4 us)

commit v4 on v3

--- a/solution.py
+++ b/solution.py
@@ -20,8 +20,8 @@
     return pl.CostEstimate(flops=int(flops), bytes_accessed=int(bytes_accessed), transcendentals=0)
 
 
-def params():
-    return pltpu.CompilerParams(vmem_limit_bytes=VMEM_BYTES)
+def params(limit=VMEM_BYTES):
+    return pltpu.CompilerParams(vmem_limit_bytes=limit)
 
 
 def partner_2(block, axis, bit):
@@ -54,28 +54,42 @@
     return far, across, diagonal
 
 
+def arrange_kernel(places_ref, *refs):
+    out_ref = refs[-1]
+    index = 0
+    for ref in refs[:-1]:
+        for part in range(ref.shape[0]):
+            width = ref.shape[2]
+            place = pl.multiple_of(places_ref[index] * width, width)
+            out_ref[:, pl.ds(place, width)] = ref[part]
+            index += 1
+
+
+def arrange(stacks, places):
+    tokens, width = stacks[0].shape[1:]
+    total = sum(stack.shape[0] for stack in stacks) * width
+    return pl.pallas_call(
+        arrange_kernel,
+        out_shape=jax.ShapeDtypeStruct((tokens, total), stacks[0].dtype),
+        in_specs=[pl.BlockSpec(memory_space=pltpu.SMEM)]
+        + [pl.BlockSpec(memory_space=pltpu.VMEM)] * len(stacks),
+        out_specs=pl.BlockSpec(memory_space=pltpu.VMEM),
+        compiler_params=params(),
+        cost_estimate=cost(0, 4 * tokens * total),
+    )(places, *stacks)
+
+
 def quad(block, along_x_last):
-    wide_index = lax.axis_index("wide")
-    upper_z, upper_x, upper = ((wide_index >> bit) % 2 == 1 for bit in (2, 1, 0))
     along_z = partner_2(block, "wide", 2)
     along_x = partner_2(block, "wide", 1)
     if along_x_last:
         both = partner_2(along_z, "wide", 1)
     else:
         both = partner_2(along_x, "wide", 2)
-
-    def ordered(flag, mine, other):
-        return [jnp.where(flag, other, mine), jnp.where(flag, mine, other)]
-
-    here = ordered(upper_x, block, along_x)
-    there = ordered(upper_x, along_z, both)
-    rows = [ordered(upper_z, here[x], there[x]) for x in range(2)]
-    mine = jnp.concatenate([rows[x][z] for z in range(2) for x in range(2)], 1)
-    other = partner_2(mine, "wide", 0)
-    tokens, width = block.shape
-    pair = ordered(upper, mine, other)
-    pair = jnp.stack([half.reshape(tokens, 4, width) for half in pair], 2)
-    return pair.reshape(tokens, 8 * width)
+    four = jnp.stack([block, along_x, along_z, both])
+    other = partner_2(four, "wide", 0)
+    apart = jnp.array([0, 2, 4, 6, 1, 3, 5, 7], jnp.int32)
+    return arrange([four, other], (lax.axis_index("wide") % 8) ^ apart)
 
 
 def features_of(x_in):
@@ -90,7 +104,7 @@
         far = lax.ppermute(x_in, axes, far)
         near = lax.axis_index("wide") // 8 == me
         theirs = jnp.where(near, across, diagonal)
-        return [quad(jnp.where(near, x_in, far), False), quad(theirs, True)], theirs
+        return [quad(jnp.where(near, x_in, far), False), quad(theirs, True)]
     own = lax.all_gather(x_in, "wide", axis=1, tiled=True)
     parts = own.reshape(own.shape[0], req_count, own.shape[1] // req_count).transpose(1, 0, 2)
     got = lax.all_to_all(parts, "req", split_axis=0, concat_axis=0, tiled=True)
@@ -98,7 +112,7 @@
         lax.dynamic_index_in_dim(got, (me + step) % req_count, 0, False)
         for step in range(req_count)
     ]
-    return blocks, x_in
+    return blocks
 
 
 def token_places(starts, count_tok, shape, axis):
@@ -224,7 +238,7 @@
             ],
             out_specs=pl.BlockSpec((1, heads * width + rows, state), lambda j, slots: (j, 0, 0)),
         ),
-        compiler_params=params(),
+        compiler_params=params(3 * VMEM_BYTES),
         cost_estimate=cost(0, 6 * count_req * heads * width * state),
     )(slots, pool, conv_rows)
 
@@ -406,7 +420,7 @@
     lags = conv_x_pool.shape[1]
     conv_width = local_width + state_part
 
-    features, arrived = features_of(x_in)
+    features = features_of(x_in)
 
     def slots_of(index):
         asked = lax.dynamic_slice_in_dim(state_slot, index * group_reqs, group_reqs)
@@ -444,33 +458,22 @@
         cache = jnp.where((came_from == step)[:, None, None], got, cache)
     cache = jnp.where(live[:, None, None], cache, 0).astype(F32)
 
-    half = w_xz.shape[0] // 2
-    first = lax.optimization_barrier(jnp.transpose(w_xz[:half], (1, 0, 2)))
-    last, _ = lax.optimization_barrier((w_xz[half:], arrived))
-    last = lax.optimization_barrier(jnp.transpose(last, (1, 0, 2)))
     w_map = jnp.concatenate([w_bc, w_dt], 1)
-    weights = {
-        "map": (w_map[:half], w_map[half:]),
-        "xr": (first[1], last[1]),
-        "z": (first[0], last[0]),
-    }
-
-    def project(block, name):
-        return jnp.dot(
-            block[:, :half], weights[name][0], preferred_element_type=F32
-        ) + jnp.dot(block[:, half:], weights[name][1], preferred_element_type=F32)
-
-    came = {name: [] for name in weights}
+
+    def project(block, kind):
+        low = jnp.dot(block, w_map, preferred_element_type=F32).astype(kind)
+        low, block = lax.optimization_barrier((low, block))
+        high = jnp.einsum("td,dkc->ktc", block, w_xz, preferred_element_type=F32)
+        return {"map": low, "xr": high[1].astype(kind), "z": high[0].astype(kind)}
+
+    came = {"map": [], "xr": [], "z": []}
     order = features[0]
     for step in range(1, req_count):
-        block = features[step]
-        for name in weights:
-            part, block = lax.optimization_barrier((project(block, name).astype(BF16), block))
-            came[name].append(shift_req(part, step))
-            order, _ = lax.optimization_barrier((order, part))
-    own = {}
-    for name in weights:
-        own[name], order = lax.optimization_barrier((project(order, name), order))
+        part = project(features[step], BF16)
+        for name in came:
+            came[name].append(shift_req(part[name], step))
+        order, _ = lax.optimization_barrier((order, part))
+    own = lax.optimization_barrier(project(order, F32))
 
     bc_conv, cum, cum_t, step_t, coef, decay = prep(
         stretch_start, own["map"], came["map"], cache[:, :, local_width:], conv_bc_w, conv_bc_b,

time: 144 us -> 108 us (0.75)
  local copies, waits for them, and re-layouts: 49.2 us -> 10 us
  other arithmetic: 17.3 us -> 5.9 us
  matrix products: 20.5 us -> 27.2 us
  Pallas kernels: 10 us -> 15.1 us
  waiting for transfers between devices: 13.3 us -> 15.5 us
    slice x1 -> x0, local copies, waits for them, and re-layouts: 14.1 us -> none  [on_device(): last, _ = lax.optimization_barrier((w_xz[half:], arrived))]
    unnamed x76 -> x43, local copies, waits for them, and re-layouts: 17.4 us -> 6.38 us
    optimization_barrier x1, local copies, waits for them, and re-layouts: 9.36 us -> 1.17 us  [on_device(): own = lax.optimization_barrier(project(order, F32))]
    select_n x4 -> x0, local copies, waits for them, and re-layouts: 8.12 us -> none  [ordered(): return [jnp.where(flag, other, mine), jnp.where(flag, mine, other)]]
    select_n x4 -> x1, other arithmetic: 6.71 us -> 0.03 us  [features_of(): return [quad(jnp.where(near, x_in, far), False), quad(theirs, True)]]
    dot_general x12 -> x4, matrix products: 20.5 us -> 27.2 us  [the longest x2 23.3 us: project(): high = jnp.einsum('td,dkc->ktc', block, w_xz, preferred_element_type=F32)]
    ppermute x10, waiting for transfers between devices: 8.65 us -> 14 us  [partner_2(): return lax.ppermute(block, axis, route)]
    ppermute x4, waiting for transfers between devices: 4.62 us -> 1.48 us  [shift_req(): lax.ppermute(block, 'req', [(i, (i + step) % count) for i in range(count)])]
  transfers between devices with their start and end apart: 17 -> 17, of which waited for: 6 -> 6; matrix products, arithmetic and copies ran while one was open for 38% -> 35% of each run, Pallas kernels for 7% -> 14%
where the time goes in v4:
time: 108 us; the launch traced here: 106 us
  starting transfers between devices  31.7 us (29%)
  matrix products  27.2 us (25%)
  waiting for transfers between devices  15.5 us (14%)
  Pallas kernels  15.1 us (14%)
  local copies, waits for them, and re-layouts  10 us (9%)
  other arithmetic  5.9 us (5%)
  between operations  1.08 us (1%)
    dot_general x2, matrix products, project(): high = jnp.einsum('td,dkc->ktc', block, w_xz, preferred_element_type=F32)  23.3 us
    ppermute x10, waiting for transfers between devices, partner_2(): return lax.ppermute(block, axis, route)  14 us
    ppermute x4, starting transfers between devices, shift_req(): lax.ppermute(block, 'req', [(i, (i + step) % count) for i in range(count)])  11.6 us
    ppermute x1, starting transfers between devices, features_of(): far = lax.ppermute(x_in, axes, far)  9.35 us
    ppermute x10, starting transfers between devices, partner_2(): return lax.ppermute(block, axis, route)  8.79 us
    pallas_call x1, Pallas kernels, mixer(): pl.pallas_call(functools.partial(mixer_kernel, count_req, len(got)), out_...  7.59 us
    unnamed x43, local copies, waits for them, and re-layouts  6.38 us
    dot_general x2, matrix products, project(): low = jnp.dot(block, w_map, preferred_element_type=F32).astype(kind)  3.89 us
  transfers between devices with their start and end apart: 17, of which 6 were waited for; matrix products, arithmetic and copies ran while one was open for 35% of the time, Pallas kernels for 14%

profile of v4, /device:TPU:0, one launch (start us, length us, event | category | flops | bytes accessed | tf_op | source)
XLA Modules:
  0.0 106.4 jit_solution(15215245678045126956)
XLA Ops:
  0.6 1.3 %collective-permute-start.5 = (bf16[256,512]{1,0:T(8,128)(2,1)}, bf16[256,512]{1,0:T(8,128)(2,1)S(1)}, u32[]{:S(2)}, u32[]{:S(2)}) collective-permute-start(bf16[256,512]{1,0:T(8,128)(2,1)} %param.20), channel_id=1, source_target_pairs={{1,0},{3,2},{5,4},{7,6},{9,8},{11,10},{13,12},{15,14},{16,17},{18,... | collective-permute-start | bytes 786440 | tf_op jit(solution)/shard_map/ppermute | solution.py:102
  2.6 9.4 %collective-permute-start = (bf16[256,512]{1,0:T(8,128)(2,1)}, bf16[256,512]{1,0:T(8,128)(2,1)S(1)}, u32[]{:S(2)}, u32[]{:S(2)}) collective-permute-start(bf16[256,512]{1,0:T(8,128)(2,1)} %param.20), channel_id=1, source_target_pairs={{0,16},{2,18},{4,20},{6,22},{8,24},{10,26},{12,28},{14,30},{17,1},... | collective-permute-start | bytes 786440 | tf_op jit(solution)/shard_map/ppermute | solution.py:104
  14.7 1.9 %collective-permute-start.8 = (bf16[256,512]{1,0:T(8,128)(2,1)S(1)}, bf16[256,512]{1,0:T(8,128)(2,1)S(1)}, u32[]{:S(2)}, u32[]{:S(2)}) collective-permute-start(bf16[256,512]{1,0:T(8,128)(2,1)S(1)} %broadcast_select_fusion), channel_id=1, source_target_pairs={{0,8},{8,0},{2,10},{10,2},{4,12},{12,4},{6,14},{14,6},{16,24},{24,... | collective-permute-start | bytes 786440 | tf_op jit(solution)/shard_map/ppermute | solution.py:34
  16.7 2.8 %shard_map.205 = bf16[2,1040,256]{2,1,0:T(8,128)(2,1)} custom-call(s32[2]{0:T(128)S(1)} %get-tuple-element.48.slots_ref, f32[8,16,64,256]{3,2,1,0:T(8,128)} %refs_14_.1, bf16[2,16,256]{2,1,0:T(8,128)(2,1)S(1)} %bitcast.49), custom_call_target="tpu_custom_call" | custom-call | bytes 3145728 | tf_op jit(solution)/shard_map/pallas_call | solution.py:229
  19.5 7.7 %collective-permute-start.12 = (bf16[2,1040,256]{2,1,0:T(8,128)(2,1)}, bf16[2,1040,256]{2,1,0:T(8,128)(2,1)S(1)}, u32[]{:S(2)}, u32[]{:S(2)}) collective-permute-start(bf16[2,1040,256]{2,1,0:T(8,128)(2,1)} %shard_map.205), channel_id=1, source_target_pairs={{0,1},{1,0},{2,3},{3,2},{4,5},{5,4},{6,7},{7,6},{8,9},{9,8},{10,11... | collective-permute-start | bytes 3194888 | tf_op jit(solution)/shard_map/ppermute | solution.py:39
  27.3 1.6 %collective-permute-start.1 = (bf16[256,512]{1,0:T(8,128)(2,1)S(1)}, bf16[256,512]{1,0:T(8,128)(2,1)S(1)}, u32[]{:S(2)}, u32[]{:S(2)}) collective-permute-start(bf16[256,512]{1,0:T(8,128)(2,1)S(1)} %broadcast_select_fusion.1), channel_id=1, source_target_pairs={{0,4},{4,0},{2,6},{6,2},{8,12},{12,8},{10,14},{14,10},{16,20},{20,... | collective-permute-start | bytes 786440 | tf_op jit(solution)/shard_map/ppermute | solution.py:34
  29.4 1.5 %collective-permute-start.9 = (bf16[256,512]{1,0:T(8,128)(2,1)S(1)}, bf16[256,512]{1,0:T(8,128)(2,1)S(1)}, u32[]{:S(2)}, u32[]{:S(2)}) collective-permute-start(bf16[256,512]{1,0:T(8,128)(2,1)S(1)} %collective-permute-done.8), channel_id=1, source_target_pairs={{0,4},{4,0},{2,6},{6,2},{8,12},{12,8},{10,14},{14,10},{16,20},{20,... | collective-permute-start | bytes 786440 | tf_op jit(solution)/shard_map/ppermute | solution.py:34
  32.2 4.4 %collective-permute-done.1 = bf16[256,512]{1,0:T(8,128)(2,1)S(1)} collective-permute-done((bf16[256,512]{1,0:T(8,128)(2,1)S(1)}, bf16[256,512]{1,0:T(8,128)(2,1)S(1)}, u32[]{:S(2)}, u32[]{:S(2)}) %collective-permute-start.1) | collective-permute-done | bytes 262176 | tf_op jit(solution)/shard_map/ppermute | solution.py:34
  36.6 1.3 %collective-permute-start.3 = (bf16[256,512]{1,0:T(8,128)(2,1)S(1)}, bf16[256,512]{1,0:T(8,128)(2,1)}, u32[]{:S(2)}, u32[]{:S(2)}) collective-permute-start(bf16[256,512]{1,0:T(8,128)(2,1)S(1)} %collective-permute-done.1), channel_id=1, source_target_pairs={{0,8},{8,0},{2,10},{10,2},{4,12},{12,4},{6,14},{14,6},{16,24},{24,... | collective-permute-start | bytes 786440 | tf_op jit(solution)/shard_map/ppermute | solution.py:34
  37.9 4.3 %collective-permute-done.7 = bf16[256,512]{1,0:T(8,128)(2,1)S(1)} collective-permute-done((bf16[256,512]{1,0:T(8,128)(2,1)S(1)}, bf16[256,512]{1,0:T(8,128)(2,1)S(1)}, u32[]{:S(2)}, u32[]{:S(2)}) %collective-permute-start.7) | collective-permute-done | bytes 262176 | tf_op jit(solution)/shard_map/ppermute | solution.py:34
  42.2 4.0 %collective-permute-done.9 = bf16[256,512]{1,0:T(8,128)(2,1)S(1)} collective-permute-done((bf16[256,512]{1,0:T(8,128)(2,1)S(1)}, bf16[256,512]{1,0:T(8,128)(2,1)S(1)}, u32[]{:S(2)}, u32[]{:S(2)}) %collective-permute-start.9) | collective-permute-done | bytes 262176 | tf_op jit(solution)/shard_map/ppermute | solution.py:34
  46.6 2.2 %copy.36 = bf16[4096,16]{1,0:T(8,128)(2,1)} copy(bf16[4096,16]{0,1:T(8,128)(2,1)} %param.22) | data formatting | bytes 262144 | tf_op args[2]
  51.1 1.5 %shard_map.204 = bf16[256,4096]{1,0:T(8,128)(2,1)S(1)} custom-call(s32[8]{0:T(128)S(1)} %broadcast_xor_fusion.places_ref, bf16[4,256,512]{2,1,0:T(8,128)(2,1)S(1)} %pad_maximum_fusion.6.refs_0_, bf16[4,256,512]{2,1,0:T(8,128)(2,1)} %collective-permute-done.10.refs_1_), custom_call_target="tpu_custom_call" | custom-call | bytes 4194304 | tf_op jit(solution)/shard_map/pallas_call | solution.py:71
  53.3 1.9 %fusion.23 = bf16[256,272]{1,0:T(8,128)(2,1)} fusion(bf16[256,4096]{1,0:T(8,128)(2,1)S(1)} %shard_map.204, bf16[4096,16]{1,0:T(8,128)(2,1)S(1)} %copy-done.9, bf16[4096,256]{1,0:T(8,128)(2,1)S(1)} %copy-done.16), kind=kOutput, calls=%fused_computation.14 | convolution fusion | flops 574951424 | bytes 4464640 | tf_op jit(solution)/shard_map/dot_general | solution.py:464
  55.2 1.7 %collective-permute-start.13 = (bf16[256,272]{1,0:T(8,128)(2,1)}, bf16[256,272]{1,0:T(8,128)(2,1)S(1)}, u32[]{:S(2)}, u32[]{:S(2)}) collective-permute-start(bf16[256,272]{1,0:T(8,128)(2,1)} %fusion.23), channel_id=1, source_target_pairs={{0,1},{1,0},{2,3},{3,2},{4,5},{5,4},{6,7},{7,6},{8,9},{9,8},{10,11... | collective-permute-start | bytes 417800 | tf_op jit(solution)/shard_map/ppermute | solution.py:39
  57.0 11.2 %fusion.18 = bf16[2,256,1024]{2,1,0:T(8,128)(2,1)S(1)} fusion(bf16[4096,2,1024]{2,1,0:T(2,128)(2,1)} %param.21, bf16[256,4096]{1,0:T(8,128)(2,1)S(1)} %shard_map.204), kind=kOutput, calls=%fused_computation.11 | convolution fusion | flops 4295491584 | bytes 19922944 | tf_op jit(solution)/shard_map/td,dkc->ktc/dot_general | solution.py:466
  69.6 1.4 %shard_map.203 = bf16[256,4096]{1,0:T(8,128)(2,1)S(1)} custom-call(s32[8]{0:T(128)S(1)} %broadcast_xor_fusion.places_ref, bf16[4,256,512]{2,1,0:T(8,128)(2,1)S(1)} %pad_maximum_fusion.5.refs_0_, bf16[4,256,512]{2,1,0:T(8,128)(2,1)} %collective-permute-done.4.refs_1_), custom_call_target="tpu_custom_call" | custom-call | bytes 4194304 | tf_op jit(solution)/shard_map/pallas_call | solution.py:71
  71.0 2.0 %fusion.6 = f32[256,272]{0,1:T(8,128)} fusion(bf16[256,4096]{1,0:T(8,128)(2,1)S(1)} %shard_map.203, bf16[4096,16]{1,0:T(8,128)(2,1)S(1)} %copy-done.9, bf16[4096,256]{1,0:T(8,128)(2,1)S(1)} %copy-done.16), kind=kOutput, calls=%fused_computation.7 | convolution fusion | flops 574881792 | bytes 4603904 | tf_op jit(solution)/shard_map/dot_general | solution.py:464
  72.9 12.0 %fusion.8 = f32[2,256,1024]{2,1,0:T(8,128)S(1)} fusion(bf16[4096,2,1024]{2,1,0:T(2,128)(2,1)} %param.21, bf16[256,4096]{1,0:T(8,128)(2,1)S(1)} %shard_map.203), kind=kOutput, calls=%fused_computation.9 | convolution fusion | flops 4294967296 | bytes 20971520 | tf_op jit(solution)/shard_map/td,dkc->ktc/dot_general | solution.py:466
  87.4 1.8 %shard_map.206 = (bf16[256,256]{1,0:T(8,128)(2,1)S(1)}, f32[4,256,4]{2,1,0:T(8,128)S(1)}, f32[4,4,256]{2,1,0:T(4,128)S(1)}, f32[4,4,256]{2,1,0:T(4,128)S(1)}, f3...) custom-call(s32[1,2]{1,0:T(1,128)S(1)} %copy-done.3, f32[256,272]{1,0:T(8,128)S(1)} %copy.40.own_ref, ...), custom_call_target="tpu_custom_call" | custom-call | flops 400000000 | bytes 1000000 | tf_op jit(solution)/shard_map/pallas_call | solution.py:203
  89.4 1.8 %collective-permute-start.15 = (bf16[256,1024]{1,0:T(8,128)(2,1)S(1)}, bf16[256,1024]{1,0:T(8,128)(2,1)S(1)}, u32[]{:S(2)}, u32[]{:S(2)}) collective-permute-start(bf16[256,1024]{1,0:T(8,128)(2,1)S(1)} %copy-done.10), channel_id=1, source_target_pairs={{0,1},{1,0},{2,3},{3,2},{4,5},{5,4},{6,7},{7,6},{8,9},{9,8},{10,11... | collective-permute-start | bytes 1572872 | tf_op jit(solution)/shard_map/ppermute | solution.py:39
  91.4 3.4 %copy-done = f32[8,16,64,256]{3,2,1,0:T(8,128)S(1)} copy-done((f32[8,16,64,256]{3,2,1,0:T(8,128)S(1)}, f32[8,16,64,256]{3,2,1,0:T(8,128)}, u32[]{:S(2)}) %copy-start) | copy-done | bytes 8388632
  94.8 7.6 %shard_map.207 = (f32[256,1024]{1,0:T(8,128)S(1)}, f32[2,16,64,256]{3,2,1,0:T(8,128)}) custom-call(s32[2]{0:T(128)S(1)} %get-tuple-element.49.slots_ref, s32[2,2]{1,0:T(2,128)S(1)} %and_convert_fusion.flags_ref, s32[2]{0:T(128)S(1)} %bitcast.51, f32[256,1024]{1,0:T(8,128)S(1)} %get-tuple-element.23.refs_0_, ...), custom_call_target="tpu_custom_call" | custom-call | flops 5000000000 | bytes 8000000 | tf_op jit(solution)/shard_map/pallas_call | solution.py:365
  102.4 1.4 %collective-permute-done.15 = bf16[256,1024]{1,0:T(8,128)(2,1)S(1)} collective-permute-done((bf16[256,1024]{1,0:T(8,128)(2,1)S(1)}, bf16[256,1024]{1,0:T(8,128)(2,1)S(1)}, u32[]{:S(2)}, u32[]{:S(2)}) %collective-permute-start.15) | collective-permute-done | bytes 524320 | tf_op jit(solution)/shard_map/ppermute | solution.py:39
  (91 shorter events, 15.1 us)
Async XLA Ops:
  0.6 14.0 %collective-permute-start.5 = (bf16[256,512]{1,0:T(8,128)(2,1)}, bf16[256,512]{1,0:T(8,128)(2,1)S(1)}, u32[]{:S(2)}, u32[]{:S(2)}) collective-permute-start(bf16[256,512]{1,0:T(8,128)(2,1)} %param.20), channel_id=1, source_target_pairs={{1,0},{3,2},{5,4},{7,6},{9,8},{11,10},{13,12},{15,14},{16,17},{18,... | collective-permute-start | bytes 786440 | tf_op jit(solution)/shard_map/ppermute | solution.py:102
  1.9 12.7 %collective-permute-start.6 = (bf16[256,512]{1,0:T(8,128)(2,1)}, bf16[256,512]{1,0:T(8,128)(2,1)S(1)}, u32[]{:S(2)}, u32[]{:S(2)}) collective-permute-start(bf16[256,512]{1,0:T(8,128)(2,1)} %param.20), channel_id=1, source_target_pairs={{1,16},{3,18},{5,20},{7,22},{9,24},{11,26},{13,28},{15,30},{16,1},... | collective-permute-start | bytes 786440 | tf_op jit(solution)/shard_map/ppermute | solution.py:103
  2.6 24.7 %collective-permute-start = (bf16[256,512]{1,0:T(8,128)(2,1)}, bf16[256,512]{1,0:T(8,128)(2,1)S(1)}, u32[]{:S(2)}, u32[]{:S(2)}) collective-permute-start(bf16[256,512]{1,0:T(8,128)(2,1)} %param.20), channel_id=1, source_target_pairs={{0,16},{2,18},{4,20},{6,22},{8,24},{10,26},{12,28},{14,30},{17,1},... | collective-permute-start | bytes 786440 | tf_op jit(solution)/shard_map/ppermute | solution.py:104
  14.7 14.7 %collective-permute-start.8 = (bf16[256,512]{1,0:T(8,128)(2,1)S(1)}, bf16[256,512]{1,0:T(8,128)(2,1)S(1)}, u32[]{:S(2)}, u32[]{:S(2)}) collective-permute-start(bf16[256,512]{1,0:T(8,128)(2,1)S(1)} %broadcast_select_fusion), channel_id=1, source_target_pairs={{0,8},{8,0},{2,10},{10,2},{4,12},{12,4},{6,14},{14,6},{16,24},{24,... | collective-permute-start | bytes 786440 | tf_op jit(solution)/shard_map/ppermute | solution.py:34
  16.7 10.6 %copy-start.11 = (bf16[256,512]{1,0:T(8,128)(2,1)S(1)}, bf16[256,512]{1,0:T(8,128)(2,1)}, u32[]{:S(2)}) copy-start(bf16[256,512]{1,0:T(8,128)(2,1)} %param.20) | copy-start | bytes 786436
  16.7 14.2 %copy-start.17 = (s32[2]{0:T(128)S(1)}, s32[2]{0:T(128)}, u32[]{:S(2)}) copy-start(s32[2]{0:T(128)} %param.33) | copy-start | bytes 28
  19.5 27.0 %copy-start.13 = (s32[4]{0:T(128)S(1)}, s32[4]{0:T(128)}, u32[]{:S(2)}) copy-start(s32[4]{0:T(128)} %param.34) | copy-start | bytes 52
  19.5 29.3 %copy-start.15 = (f32[16]{0:T(128)S(1)}, f32[16]{0:T(128)}, u32[]{:S(2)}) copy-start(f32[16]{0:T(128)} %param.26) | copy-start | bytes 196
  19.5 29.5 %copy-start.18 = (s32[8]{0:T(128)S(1)}, s32[8]{0:T(128)}, u32[]{:S(2)}) copy-start(s32[8]{0:T(128)} %constant.99.clone) | copy-start | bytes 100
  19.5 31.4 %collective-permute-start.12 = (bf16[2,1040,256]{2,1,0:T(8,128)(2,1)}, bf16[2,1040,256]{2,1,0:T(8,128)(2,1)S(1)}, u32[]{:S(2)}, u32[]{:S(2)}) collective-permute-start(bf16[2,1040,256]{2,1,0:T(8,128)(2,1)} %shard_map.205), channel_id=1, source_target_pairs={{0,1},{1,0},{2,3},{3,2},{4,5},{5,4},{6,7},{7,6},{8,9},{9,8},{10,11... | collective-permute-start | bytes 3194888 | tf_op jit(solution)/shard_map/ppermute | solution.py:39
  27.3 9.3 %collective-permute-start.1 = (bf16[256,512]{1,0:T(8,128)(2,1)S(1)}, bf16[256,512]{1,0:T(8,128)(2,1)S(1)}, u32[]{:S(2)}, u32[]{:S(2)}) collective-permute-start(bf16[256,512]{1,0:T(8,128)(2,1)S(1)} %broadcast_select_fusion.1), channel_id=1, source_target_pairs={{0,4},{4,0},{2,6},{6,2},{8,12},{12,8},{10,14},{14,10},{16,20},{20,... | collective-permute-start | bytes 786440 | tf_op jit(solution)/shard_map/ppermute | solution.py:34
  28.9 13.4 %collective-permute-start.7 = (bf16[256,512]{1,0:T(8,128)(2,1)S(1)}, bf16[256,512]{1,0:T(8,128)(2,1)S(1)}, u32[]{:S(2)}, u32[]{:S(2)}) collective-permute-start(bf16[256,512]{1,0:T(8,128)(2,1)S(1)} %broadcast_select_fusion), channel_id=1, source_target_pairs={{0,4},{4,0},{2,6},{6,2},{8,12},{12,8},{10,14},{14,10},{16,20},{20,... | collective-permute-start | bytes 786440 | tf_op jit(solution)/shard_map/ppermute | solution.py:34
  29.4 16.8 %collective-permute-start.9 = (bf16[256,512]{1,0:T(8,128)(2,1)S(1)}, bf16[256,512]{1,0:T(8,128)(2,1)S(1)}, u32[]{:S(2)}, u32[]{:S(2)}) collective-permute-start(bf16[256,512]{1,0:T(8,128)(2,1)S(1)} %collective-permute-done.8), channel_id=1, source_target_pairs={{0,4},{4,0},{2,6},{6,2},{8,12},{12,8},{10,14},{14,10},{16,20},{20,... | collective-permute-start | bytes 786440 | tf_op jit(solution)/shard_map/ppermute | solution.py:34
  30.9 18.1 %collective-permute-start.2 = (bf16[256,512]{1,0:T(8,128)(2,1)S(1)}, bf16[256,512]{1,0:T(8,128)(2,1)}, u32[]{:S(2)}, u32[]{:S(2)}) collective-permute-start(bf16[256,512]{1,0:T(8,128)(2,1)S(1)} %broadcast_select_fusion.1), channel_id=1, source_target_pairs={{0,8},{8,0},{2,10},{10,2},{4,12},{12,4},{6,14},{14,6},{16,24},{24,... | collective-permute-start | bytes 786440 | tf_op jit(solution)/shard_map/ppermute | solution.py:34
  36.6 12.4 %copy-start.12 = (bf16[256,512]{1,0:T(8,128)(2,1)}, bf16[256,512]{1,0:T(8,128)(2,1)S(1)}, u32[]{:S(2)}) copy-start(bf16[256,512]{1,0:T(8,128)(2,1)S(1)} %collective-permute-done.1) | copy-start | bytes 786436
  36.6 12.4 %collective-permute-start.3 = (bf16[256,512]{1,0:T(8,128)(2,1)S(1)}, bf16[256,512]{1,0:T(8,128)(2,1)}, u32[]{:S(2)}, u32[]{:S(2)}) collective-permute-start(bf16[256,512]{1,0:T(8,128)(2,1)S(1)} %collective-permute-done.1), channel_id=1, source_target_pairs={{0,8},{8,0},{2,10},{10,2},{4,12},{12,4},{6,14},{14,6},{16,24},{24,... | collective-permute-start | bytes 786440 | tf_op jit(solution)/shard_map/ppermute | solution.py:34
  46.4 4.7 %collective-permute-start.10 = (bf16[4,256,512]{2,1,0:T(8,128)(2,1)S(1)}, bf16[4,256,512]{2,1,0:T(8,128)(2,1)}, u32[]{:S(2)}, u32[]{:S(2)}) collective-permute-start(bf16[4,256,512]{2,1,0:T(8,128)(2,1)S(1)} %pad_maximum_fusion.6.refs_0_), channel_id=1, source_target_pairs={{0,2},{2,0},{4,6},{6,4},{8,10},{10,8},{12,14},{14,12},{16,18},{18,... | collective-permute-start | bytes 3145736 | tf_op jit(solution)/shard_map/ppermute | solution.py:34
  50.3 19.3 %collective-permute-start.4 = (bf16[4,256,512]{2,1,0:T(8,128)(2,1)S(1)}, bf16[4,256,512]{2,1,0:T(8,128)(2,1)}, u32[]{:S(2)}, u32[]{:S(2)}) collective-permute-start(bf16[4,256,512]{2,1,0:T(8,128)(2,1)S(1)} %pad_maximum_fusion.5.refs_0_), channel_id=1, source_target_pairs={{0,2},{2,0},{4,6},{6,4},{8,10},{10,8},{12,14},{14,12},{16,18},{18,... | collective-permute-start | bytes 3145736 | tf_op jit(solution)/shard_map/ppermute | solution.py:34
  55.2 32.1 %collective-permute-start.13 = (bf16[256,272]{1,0:T(8,128)(2,1)}, bf16[256,272]{1,0:T(8,128)(2,1)S(1)}, u32[]{:S(2)}, u32[]{:S(2)}) collective-permute-start(bf16[256,272]{1,0:T(8,128)(2,1)} %fusion.23), channel_id=1, source_target_pairs={{0,1},{1,0},{2,3},{3,2},{4,5},{5,4},{6,7},{7,6},{8,9},{9,8},{10,11... | collective-permute-start | bytes 417800 | tf_op jit(solution)/shard_map/ppermute | solution.py:39
  69.3 22.1 %collective-permute-start.11 = (bf16[256,1024]{1,0:T(8,128)(2,1)}, bf16[256,1024]{1,0:T(8,128)(2,1)}, u32[]{:S(2)}, u32[]{:S(2)}) collective-permute-start(bf16[256,1024]{1,0:T(8,128)(2,1)} %get-tuple-element.45), channel_id=1, source_target_pairs={{0,1},{1,0},{2,3},{3,2},{4,5},{5,4},{6,7},{7,6},{8,9},{9,8},{10,11... | collective-permute-start | bytes 1572872 | tf_op jit(solution)/shard_map/ppermute | solution.py:39
  89.2 2.0 %collective-permute-start.14 = (bf16[256,256]{1,0:T(8,128)(2,1)S(1)}, bf16[256,256]{1,0:T(8,128)(2,1)S(1)}, u32[]{:S(2)}, u32[]{:S(2)}) collective-permute-start(bf16[256,256]{1,0:T(8,128)(2,1)S(1)} %get-tuple-element.25), channel_id=1, source_target_pairs={{0,2},{2,0},{4,6},{6,4},{8,10},{10,8},{12,14},{14,12},{16,18},{18,... | collective-permute-start | bytes 393224 | tf_op jit(solution)/shard_map/ppermute | solution.py:34
  89.4 14.4 %collective-permute-start.15 = (bf16[256,1024]{1,0:T(8,128)(2,1)S(1)}, bf16[256,1024]{1,0:T(8,128)(2,1)S(1)}, u32[]{:S(2)}, u32[]{:S(2)}) collective-permute-start(bf16[256,1024]{1,0:T(8,128)(2,1)S(1)} %copy-done.10), channel_id=1, source_target_pairs={{0,1},{1,0},{2,3},{3,2},{4,5},{5,4},{6,7},{7,6},{8,9},{9,8},{10,11... | collective-permute-start | bytes 1572872 | tf_op jit(solution)/shard_map/ppermute | solution.py:39
  94.8 9.0 %copy-start.8 = (f32[256,1024]{1,0:T(8,128)S(1)}, f32[256,1024]{1,0:T(8,128)}, u32[]{:S(2)}) copy-start(f32[256,1024]{1,0:T(8,128)} %get-tuple-element.32) | copy-start | bytes 3145732
  104.2 1.2 %collective-permute-start.16 = (f32[256]{0:T(256)S(1)}, f32[256]{0:T(256)S(1)}, u32[]{:S(2)}, u32[]{:S(2)}) collective-permute-start(f32[256]{0:T(256)S(1)} %get-tuple-element.38), channel_id=1, source_target_pairs={{0,2},{2,0},{4,6},{6,4},{8,10},{10,8},{12,14},{14,12},{16,18},{18,... | collective-permute-start | bytes 3080 | tf_op jit(solution)/shard_map/ppermute | solution.py:34
  (12 other events, 36.0 us)

commit v5 on v4

--- a/solution.py
+++ b/solution.py
@@ -4,6 +4,7 @@
 import jax.numpy as jnp
 from jax import lax
 from jax.experimental import pallas as pl
+from jax.experimental.layout import Layout, with_layout_constraint
 from jax.experimental.pallas import tpu as pltpu
 from jax.sharding import PartitionSpec as P
 
@@ -40,18 +41,18 @@
 
 
 def spread_routes():
-    far, across, diagonal = [], [], []
+    first, second = [], []
     for z in range(4):
         for rest in range(4):
             for r in range(2):
                 place = (z * 4 + rest) * 2 + r
                 other = (((z + 2) % 4) * 4 + rest) * 2 + r
                 if z // 2 == r:
-                    far.append((place, other))
+                    first.append((place, other))
                 else:
-                    across.append((place, place ^ 1))
-                    diagonal.append((place, other ^ 1))
-    return far, across, diagonal
+                    first.append((place, place ^ 1))
+                    second.append((place, other ^ 1))
+    return first, second
 
 
 def arrange_kernel(places_ref, *refs):
@@ -75,44 +76,60 @@
         + [pl.BlockSpec(memory_space=pltpu.VMEM)] * len(stacks),
         out_specs=pl.BlockSpec(memory_space=pltpu.VMEM),
         compiler_params=params(),
-        cost_estimate=cost(0, 4 * tokens * total),
+        cost_estimate=cost(1e6, 1e4),
     )(places, *stacks)
 
 
-def quad(block, along_x_last):
-    along_z = partner_2(block, "wide", 2)
-    along_x = partner_2(block, "wide", 1)
-    if along_x_last:
-        both = partner_2(along_z, "wide", 1)
-    else:
-        both = partner_2(along_x, "wide", 2)
-    four = jnp.stack([block, along_x, along_z, both])
-    other = partner_2(four, "wide", 0)
+def after(value, *others):
+    return lax.optimization_barrier((value, others))[0]
+
+
+def near_blocks(x_in):
+    axes = ("wide", "req")
+    first, second = spread_routes()
+    first = lax.ppermute(x_in, axes, first)
+    second = lax.ppermute(x_in, axes, second)
+    near = lax.axis_index("wide") // 8 == lax.axis_index("req")
+    return jnp.where(near, x_in, first), jnp.where(near, first, second)
+
+
+def quad_arrange(four, other):
     apart = jnp.array([0, 2, 4, 6, 1, 3, 5, 7], jnp.int32)
     return arrange([four, other], (lax.axis_index("wide") % 8) ^ apart)
 
 
-def features_of(x_in):
+def features_in_general(x_in):
     req_count = lax.axis_size("req")
-    wide_count = lax.axis_size("wide")
     me = lax.axis_index("req")
-    if req_count == 2 and wide_count == 16:
-        axes = ("wide", "req")
-        far, across, diagonal = spread_routes()
-        across = lax.ppermute(x_in, axes, across)
-        diagonal = lax.ppermute(x_in, axes, diagonal)
-        far = lax.ppermute(x_in, axes, far)
-        near = lax.axis_index("wide") // 8 == me
-        theirs = jnp.where(near, across, diagonal)
-        return [quad(jnp.where(near, x_in, far), False), quad(theirs, True)]
     own = lax.all_gather(x_in, "wide", axis=1, tiled=True)
     parts = own.reshape(own.shape[0], req_count, own.shape[1] // req_count).transpose(1, 0, 2)
     got = lax.all_to_all(parts, "req", split_axis=0, concat_axis=0, tiled=True)
-    blocks = [
+    return [
         lax.dynamic_index_in_dim(got, (me + step) % req_count, 0, False)
         for step in range(req_count)
     ]
-    return blocks
+
+
+def grab_kernel(first, w_ref, _, out_ref, sem):
+    copy = pltpu.make_async_copy(w_ref.at[pl.ds(first, out_ref.shape[0])], out_ref, sem)
+    copy.start()
+    copy.wait()
+
+
+def relayout(w_xz, chunk, chunks, behind):
+    rows = w_xz.shape[0] // chunks
+    in_hbm = pl.BlockSpec(memory_space=pltpu.HBM)
+    held = pl.pallas_call(
+        functools.partial(grab_kernel, chunk * rows),
+        out_shape=jax.ShapeDtypeStruct((rows,) + w_xz.shape[1:], w_xz.dtype),
+        in_specs=[in_hbm, pl.BlockSpec(memory_space=pl.ANY)],
+        out_specs=pl.BlockSpec(memory_space=pltpu.VMEM),
+        scratch_shapes=[pltpu.SemaphoreType.DMA],
+        compiler_params=params(),
+        cost_estimate=cost(0, 4 * rows * w_xz.shape[1] * w_xz.shape[2]),
+    )(w_xz, behind)
+    rows_last = with_layout_constraint(jnp.transpose(held, (1, 0, 2)), Layout((0, 1, 2)))
+    return lax.optimization_barrier(rows_last)
 
 
 def token_places(starts, count_tok, shape, axis):
@@ -213,47 +230,56 @@
         in_specs=[pl.BlockSpec(memory_space=pltpu.SMEM)] + [vmem] * (6 + len(got)),
         out_specs=[vmem] * 6,
         compiler_params=params(),
-        cost_estimate=cost(4e8, 1e6),
+        cost_estimate=cost(1e6, 1e4),
     )(starts, own, *got, cache, kernel, bias[None], dt_bias[None], a_log[None])
 
 
-def pack_kernel(slots_ref, pool_ref, conv_ref, out_ref):
+def pack_kernel(slots_ref, own_slots_ref, pool_ref, own_pool_ref, conv_ref, out_ref, own_ref):
     heads, width, state = pool_ref.shape[1:]
     out_ref[0, : heads * width, :] = pool_ref[0].reshape(heads * width, state).astype(BF16)
     out_ref[0, heads * width :, :] = conv_ref[0]
-
-
-def pack(pool, conv_rows, slots):
+    own_ref[...] = own_pool_ref[...]
+
+
+def pack(pool, conv_rows, slots, own_slots):
     _, heads, width, state = pool.shape
     count_req, rows, _ = conv_rows.shape
+    block = (1, heads, width, state)
     return pl.pallas_call(
         pack_kernel,
-        out_shape=jax.ShapeDtypeStruct((count_req, heads * width + rows, state), BF16),
+        out_shape=[
+            jax.ShapeDtypeStruct((count_req, heads * width + rows, state), BF16),
+            jax.ShapeDtypeStruct((count_req, heads, width, state), F32),
+        ],
         grid_spec=pltpu.PrefetchScalarGridSpec(
-            num_scalar_prefetch=1,
+            num_scalar_prefetch=2,
             grid=(count_req,),
             in_specs=[
-                pl.BlockSpec((1, heads, width, state), lambda j, slots: (slots[j], 0, 0, 0)),
-                pl.BlockSpec((1, rows, state), lambda j, slots: (j, 0, 0)),
+                pl.BlockSpec(block, lambda j, slots, own: (slots[j], 0, 0, 0)),
+                pl.BlockSpec(block, lambda j, slots, own: (own[j], 0, 0, 0)),
+                pl.BlockSpec((1, rows, state), lambda j, *_: (j, 0, 0)),
             ],
-            out_specs=pl.BlockSpec((1, heads * width + rows, state), lambda j, slots: (j, 0, 0)),
+            out_specs=[
+                pl.BlockSpec((1, heads * width + rows, state), lambda j, *_: (j, 0, 0)),
+                pl.BlockSpec(block, lambda j, *_: (j, 0, 0, 0)),
+            ],
         ),
         compiler_params=params(3 * VMEM_BYTES),
-        cost_estimate=cost(0, 6 * count_req * heads * width * state),
-    )(slots, pool, conv_rows)
-
-
-def mixer_kernel(count_req, got_total, slots_ref, flags_ref, starts_ref, *refs):
+        cost_estimate=cost(0, 14 * count_req * heads * width * state),
+    )(slots, own_slots, pool, pool, conv_rows)
+
+
+def mixer_kernel(count_req, got_total, flags_ref, starts_ref, *refs):
     own_ref = refs[0]
     got = refs[1 : 1 + got_total]
     rest = refs[1 + got_total :]
     cache_ref, kernel_ref, bias_ref, b_ref, c_ref = rest[:5]
     cum_ref, cum_t_ref, step_t_ref, coef_ref, decay_ref, skip_ref = rest[5:11]
-    pools = rest[11 : 11 + count_req]
-    states = rest[11 + count_req : 11 + count_req + got_total]
-    out_ref, state_ref, scores_ref, c_part_ref, b_part_ref = rest[11 + count_req + got_total :]
+    held_ref = rest[11]
+    states = rest[12 : 12 + got_total]
+    out_ref, state_ref, scores_ref, c_part_ref, b_part_ref = rest[12 + got_total :]
     tokens, channels = own_ref.shape
-    heads, width, state = pools[0].shape[1:]
+    heads, width, state = held_ref.shape[1:]
     starts = [starts_ref[j] for j in range(count_req)]
 
     @pl.when(pl.program_id(0) == 0)
@@ -308,7 +334,7 @@
     )
     for j in range(count_req):
         place = slice(j * state, (j + 1) * state)
-        start = pools[j][0].reshape(channels, state) * flags_ref[j, 0].astype(F32)
+        start = held_ref[j].reshape(channels, state) * flags_ref[j, 0].astype(F32)
         for step in range(got_total):
             start = start + states[step][j].astype(F32) * flags_ref[j, step + 1].astype(F32)
         from_state = from_state + lax.dot_general(
@@ -325,12 +351,11 @@
 
 
 def mixer(
-    slots, flags, starts, own, got, cache, kernel, bias, b_maps, c_maps, cum, cum_t, step_t, coef,
-    decay, skip, pool, states
+    flags, starts, own, got, cache, kernel, bias, b_maps, c_maps, cum, cum_t, step_t, coef,
+    decay, skip, held, states
 ):
     tokens, channels = own.shape
-    _, heads, width, state = pool.shape
-    count_req = cache.shape[0]
+    count_req, heads, width, state = held.shape
     kernel_len = kernel.shape[0]
     part = min(HEADS_STEP, heads)
     steps = heads // part
@@ -353,13 +378,7 @@
             pl.BlockSpec(memory_space=pltpu.SMEM),
             pl.BlockSpec((1, wide), columns),
         ]
-        + [
-            pl.BlockSpec(
-                (1, part, width, state),
-                functools.partial(lambda j, i, slots, *_: (slots[j], i, 0, 0), j),
-            )
-            for j in range(count_req)
-        ]
+        + [pl.BlockSpec((count_req, part, width, state), lambda i, *_: (0, i, 0, 0))]
         + [pl.BlockSpec((count_req, wide, state), lambda i, *_: (0, i, 0))] * len(states)
     )
     return pl.pallas_call(
@@ -369,7 +388,7 @@
             jax.ShapeDtypeStruct((count_req, heads, width, state), F32),
         ],
         grid_spec=pltpu.PrefetchScalarGridSpec(
-            num_scalar_prefetch=3,
+            num_scalar_prefetch=2,
             grid=(steps,),
             in_specs=in_specs,
             out_specs=[
@@ -383,11 +402,11 @@
             ],
         ),
         compiler_params=params(),
-        cost_estimate=cost(5e9, 8e6),
+        cost_estimate=cost(1e6, 1e4),
     )(
-        slots, flags, starts, own, *got, cache, kernel, bias[None], b_maps, c_maps,
+        flags, starts, own, *got, cache, kernel, bias[None], b_maps, c_maps,
         cum, cum_t, step_t, coef, decay,
-        jnp.repeat(skip, width)[None], *([pool] * count_req), *states
+        jnp.repeat(skip, width)[None], held, *states
     )
 
 
@@ -420,7 +439,9 @@
     lags = conv_x_pool.shape[1]
     conv_width = local_width + state_part
 
-    features = features_of(x_in)
+    count_wide = lax.axis_size("wide")
+    if req_count == 2 and count_wide == 16:
+        own_block, their_block = near_blocks(x_in)
 
     def slots_of(index):
         asked = lax.dynamic_slice_in_dim(state_slot, index * group_reqs, group_reqs)
@@ -436,15 +457,17 @@
 
     conv_size = lags * conv_width
     conv_rows = -(-conv_size // (16 * state)) * 16
+    own_slots = slots_of(me)
     got_states = []
     for step in range(1, req_count):
         slots = slots_of((me + step) % req_count)
         flat = conv_of(slots).reshape(group_reqs, conv_size)
         flat = jnp.pad(flat, ((0, 0), (0, conv_rows * state - conv_size)))
-        packed = pack(ssm_pool, flat.reshape(group_reqs, conv_rows, state), slots)
+        packed, held = pack(
+            ssm_pool, flat.reshape(group_reqs, conv_rows, state), slots, own_slots
+        )
         got_states.append(shift_req(packed, step))
 
-    own_slots = slots_of(me)
     asked = lax.dynamic_slice_in_dim(state_slot, me * group_reqs, group_reqs)
     came_from = (me - asked // slot_count) % req_count
     live = prefix_len > 0
@@ -458,22 +481,58 @@
         cache = jnp.where((came_from == step)[:, None, None], got, cache)
     cache = jnp.where(live[:, None, None], cache, 0).astype(F32)
 
+    chunks = 4
+    if req_count == 2 and count_wide == 16:
+        weights = [relayout(w_xz, k, chunks, packed) for k in range(2)]
+        block = after(their_block, *weights)
+        along_z = partner_2(block, "wide", 2)
+        along_x = partner_2(block, "wide", 1)
+        weights.append(relayout(w_xz, 2, chunks, block))
+        own_block = after(own_block, weights[2])
+        both = partner_2(after(along_z, weights[2]), "wide", 1)
+        own_z = partner_2(own_block, "wide", 2)
+        weights.append(relayout(w_xz, 3, chunks, own_block))
+        four = jnp.stack([block, along_x, along_z, after(both, weights[3])])
+        other = partner_2(four, "wide", 0)
+        own_x = partner_2(after(own_block, four), "wide", 1)
+        own_both = partner_2(after(own_z, four), "wide", 1)
+        theirs = quad_arrange(four, other)
+        own_four = jnp.stack([own_block, own_x, own_z, own_both])
+        own_other = partner_2(own_four, "wide", 0)
+        features = [(own_four, own_other), theirs]
+    else:
+        weights = [relayout(w_xz, k, chunks, packed) for k in range(chunks)]
+        features = features_in_general(x_in)
     w_map = jnp.concatenate([w_bc, w_dt], 1)
-
-    def project(block, kind):
-        low = jnp.dot(block, w_map, preferred_element_type=F32).astype(kind)
-        low, block = lax.optimization_barrier((low, block))
-        high = jnp.einsum("td,dkc->ktc", block, w_xz, preferred_element_type=F32)
-        return {"map": low, "xr": high[1].astype(kind), "z": high[0].astype(kind)}
+    depth = w_xz.shape[0] // chunks
+
+    def project(block, name):
+        if name == "map":
+            return jnp.dot(block, w_map, preferred_element_type=F32)
+        total = None
+        for k in range(chunks):
+            term = jnp.dot(
+                block[:, k * depth : (k + 1) * depth],
+                weights[k][1 if name == "xr" else 0],
+                preferred_element_type=F32,
+            )
+            total = term if total is None else total + term
+        return total
 
     came = {"map": [], "xr": [], "z": []}
-    order = features[0]
+    done = []
     for step in range(1, req_count):
-        part = project(features[step], BF16)
+        block = features[step]
         for name in came:
-            came[name].append(shift_req(part[name], step))
-        order, _ = lax.optimization_barrier((order, part))
-    own = lax.optimization_barrier(project(order, F32))
+            part, block = lax.optimization_barrier((project(block, name).astype(BF16), block))
+            came[name].append(shift_req(part, step))
+            done.append(part)
+    block = after(features[0], *done)
+    if req_count == 2 and count_wide == 16:
+        block = quad_arrange(*block)
+    own = {}
+    for name in came:
+        own[name], block = lax.optimization_barrier((project(block, name), block))
 
     bc_conv, cum, cum_t, step_t, coef, decay = prep(
         stretch_start, own["map"], came["map"], cache[:, :, local_width:], conv_bc_w, conv_bc_b,
@@ -491,9 +550,9 @@
         )
     state_width = joined.shape[1] // 2
     result, final_state = mixer(
-        own_slots, flags, stretch_start[0], own["xr"], came["xr"], cache[:, :, :local_width],
+        flags, stretch_start[0], own["xr"], came["xr"], cache[:, :, :local_width],
         conv_x_w, conv_x_b, joined[:, :state_width], joined[:, state_width:], cum, cum_t,
-        step_t, coef, decay, d_skip, ssm_pool, got_states
+        step_t, coef, decay, d_skip, held, got_states
     )
     gate = own["z"]
     for got in came["z"]:

time: 108 us -> 129 us (1.19)
  local copies, waits for them, and re-layouts: 10 us -> 52 us
  starting transfers between devices: 31.7 us -> 17.5 us
  matrix products: 27.2 us -> 20.2 us
  waiting for transfers between devices: 15.5 us -> 12 us
  other arithmetic: 5.9 us -> 8.37 us
  Pallas kernels: 15.1 us -> 16.9 us
    unnamed x43 -> x75, local copies, waits for them, and re-layouts: 6.38 us -> 34.4 us
    pallas_call x0 -> x4, local copies, waits for them, and re-layouts: none -> 15.6 us  [relayout(): pl.pallas_call(functools.partial(grab_kernel, chunk * rows), out_shape=ja...]
    dot_general x4 -> x18, matrix products: 27.2 us -> 20.2 us  [the longest x16 16.4 us: project(): jnp.dot(block[:, k * depth:(k + 1) * depth], weights[k][1 if name == 'xr'...]
    ppermute x3 -> x2, starting transfers between devices: 11.3 us -> 4.75 us  [the longest x1 4.09 us: near_blocks(): first = lax.ppermute(x_in, axes, first)]
    ppermute x4, starting transfers between devices: 11.6 us -> 6.14 us  [shift_req(): lax.ppermute(block, 'req', [(i, (i + step) % count) for i in range(count)])]
    ppermute x10, waiting for transfers between devices: 14 us -> 10.3 us  [partner_2(): return lax.ppermute(block, axis, route)]
    ppermute x10, starting transfers between devices: 8.79 us -> 6.62 us  [partner_2(): return lax.ppermute(block, axis, route)]
    pallas_call x1 -> x5, Pallas kernels: 2.81 us -> 4.06 us  [the longest x1 2.72 us: pack(): pl.pallas_call(pack_kernel, out_shape=[jax.ShapeDtypeStruct((count_req, h...]
  transfers between devices with their start and end apart: 17 -> 16, of which waited for: 6 -> 4; matrix products, arithmetic and copies ran while one was open for 35% -> 36% of each run, Pallas kernels for 14% -> 13%
where the time goes in v5:
time: 129 us; the launch traced here: 128 us
  local copies, waits for them, and re-layouts  52 us (40%)
  matrix products  20.2 us (16%)
  starting transfers between devices  17.5 us (14%)
  Pallas kernels  16.9 us (13%)
  waiting for transfers between devices  12 us (9%)
  other arithmetic  8.37 us (6%)
    unnamed x75, local copies, waits for them, and re-layouts  34.4 us
    dot_general x16, matrix products, project(): jnp.dot(block[:, k * depth:(k + 1) * depth], weights[k][1 if name == 'xr'...  16.4 us
    pallas_call x4, local copies, waits for them, and re-layouts, relayout(): pl.pallas_call(functools.partial(grab_kernel, chunk * rows), out_shape=ja...  15.6 us
    ppermute x10, waiting for transfers between devices, partner_2(): return lax.ppermute(block, axis, route)  10.3 us
    pallas_call x1, Pallas kernels, mixer(): pl.pallas_call(functools.partial(mixer_kernel, count_req, len(got)), out_...  7.7 us
    ppermute x10, starting transfers between devices, partner_2(): return lax.ppermute(block, axis, route)  6.62 us
    ppermute x4, starting transfers between devices, shift_req(): lax.ppermute(block, 'req', [(i, (i + step) % count) for i in range(count)])  6.14 us
    ppermute x1, starting transfers between devices, near_blocks(): first = lax.ppermute(x_in, axes, first)  4.09 us
  transfers between devices with their start and end apart: 16, of which 4 were waited for; matrix products, arithmetic and copies ran while one was open for 36% of the time, Pallas kernels for 13%

profile of v5, /device:TPU:0, one launch (start us, length us, event | category | flops | bytes accessed | tf_op | source)
XLA Modules:
  0.0 128.2 jit_solution(17285888650605499217)
XLA Ops:
  0.6 4.1 %collective-permute-start = (bf16[256,512]{1,0:T(8,128)(2,1)}, bf16[256,512]{1,0:T(8,128)(2,1)S(1)}, u32[]{:S(2)}, u32[]{:S(2)}) collective-permute-start(bf16[256,512]{1,0:T(8,128)(2,1)} %param.20), channel_id=1, source_target_pairs={{0,16},{1,0},{2,18},{3,2},{4,20},{5,4},{6,22},{7,6},{8,24},{9,8},{... | collective-permute-start | bytes 786440 | tf_op jit(solution)/shard_map/ppermute | solution.py:90
  8.2 2.7 %shard_map.203 = (bf16[2,1040,256]{2,1,0:T(8,128)(2,1)S(1)}, f32[2,16,64,256]{3,2,1,0:T(8,128)S(1)}) custom-call(s32[2]{0:T(128)S(1)} %get-tuple-element.71.slots_ref, s32[2]{0:T(128)S(1)} %get-tuple-element.70.own_slots_ref, f32[8,16,64,256]{3,2,1,0:T(8,128)} %own_pool_ref.1, f32[8,16,64,256]{3,2,1,0:T(8,128)} %own_pool_ref.1, bf16[2,16,256]{2,1,0:T(8,128)(2,1)S(1)} %bitcast.99), custom_call_target="tpu_custom_call" | custom-call | bytes 7340032 | tf_op jit(solution)/shard_map/pallas_call | solution.py:248
  10.9 6.5 %copy-done = bf16[4096,2,1024]{2,1,0:T(2,128)(2,1)S(1)} copy-done((bf16[4096,2,1024]{2,1,0:T(2,128)(2,1)S(1)}, bf16[4096,2,1024]{2,1,0:T(2,128)(2,1)}, u32[]{:S(2)}) %copy-start) | copy-done | bytes 16777240
  17.8 2.0 %copy-done.5 = bf16[1024,2,1024]{2,1,0:T(2,128)(2,1)} copy-done((bf16[1024,2,1024]{2,1,0:T(2,128)(2,1)}, bf16[1024,2,1024]{2,1,0:T(2,128)(2,1)S(1)}, u32[]{:S(2)}) %copy-start.5) | copy-done | bytes 4194328
  20.0 2.0 %copy-done.3 = bf16[1024,2,1024]{2,1,0:T(2,128)(2,1)} copy-done((bf16[1024,2,1024]{2,1,0:T(2,128)(2,1)}, bf16[1024,2,1024]{2,1,0:T(2,128)(2,1)S(1)}, u32[]{:S(2)}) %copy-start.3) | copy-done | bytes 4194328
  22.1 5.7 %copy.59 = bf16[1024,2,1024]{2,0,1:T(8,128)(2,1)} copy(bf16[1024,2,1024]{2,1,0:T(2,128)(2,1)} %copy-done.5) | data formatting | bytes 8388608 | tf_op jit(solution)/shard_map/pallas_call | solution.py:122
  27.7 3.4 %copy.58 = bf16[1024,2,1024]{2,0,1:T(8,128)(2,1)} copy(bf16[1024,2,1024]{2,1,0:T(2,128)(2,1)S(1)} %copy-done.4) | data formatting | bytes 8388608 | tf_op jit(solution)/shard_map/pallas_call | solution.py:122
  31.2 1.6 %collective-permute-start.3 = (bf16[256,512]{1,0:T(8,128)(2,1)S(1)}, bf16[256,512]{1,0:T(8,128)(2,1)S(1)}, u32[]{:S(2)}, u32[]{:S(2)}) collective-permute-start(bf16[256,512]{1,0:T(8,128)(2,1)S(1)} %get-tuple-element.31._), channel_id=1, source_target_pairs={{0,8},{8,0},{2,10},{10,2},{4,12},{12,4},{6,14},{14,6},{16,24},{24,... | collective-permute-start | bytes 786440 | tf_op jit(solution)/shard_map/ppermute | solution.py:35
  32.8 4.1 %collective-permute-start.11 = (bf16[2,1040,256]{2,1,0:T(8,128)(2,1)S(1)}, bf16[2,1040,256]{2,1,0:T(8,128)(2,1)}, u32[]{:S(2)}, u32[]{:S(2)}) collective-permute-start(bf16[2,1040,256]{2,1,0:T(8,128)(2,1)S(1)} %get-tuple-element.30._), channel_id=1, source_target_pairs={{0,1},{1,0},{2,3},{3,2},{4,5},{5,4},{6,7},{7,6},{8,9},{9,8},{10,11... | collective-permute-start | bytes 3194888 | tf_op jit(solution)/shard_map/ppermute | solution.py:40
  36.9 5.8 %copy-done.1 = bf16[4096,2,1024]{2,1,0:T(2,128)(2,1)S(1)} copy-done((bf16[4096,2,1024]{2,1,0:T(2,128)(2,1)S(1)}, bf16[4096,2,1024]{2,1,0:T(2,128)(2,1)}, u32[]{:S(2)}) %copy-start.1) | copy-done | bytes 16777240
  44.5 3.3 %copy.57 = bf16[1024,2,1024]{2,0,1:T(8,128)(2,1)} copy(bf16[1024,2,1024]{2,1,0:T(2,128)(2,1)S(1)} %shard_map.206) | data formatting | bytes 8388608 | tf_op jit(solution)/shard_map/pallas_call | solution.py:122
  48.9 5.8 %copy-done.2 = bf16[4096,2,1024]{2,1,0:T(2,128)(2,1)S(1)} copy-done((bf16[4096,2,1024]{2,1,0:T(2,128)(2,1)S(1)}, bf16[4096,2,1024]{2,1,0:T(2,128)(2,1)}, u32[]{:S(2)}) %copy-start.2) | copy-done | bytes 16777240
  55.1 3.3 %copy.56 = bf16[1024,2,1024]{2,0,1:T(8,128)(2,1)} copy(bf16[1024,2,1024]{2,1,0:T(2,128)(2,1)S(1)} %shard_map.207) | data formatting | bytes 8388608 | tf_op jit(solution)/shard_map/pallas_call | solution.py:122
  62.5 2.2 %copy.44 = bf16[4096,16]{1,0:T(8,128)(2,1)} copy(bf16[4096,16]{0,1:T(8,128)(2,1)} %param.22) | data formatting | bytes 262144 | tf_op args[2]
  65.4 4.0 %collective-permute-done.5 = bf16[256,512]{1,0:T(8,128)(2,1)S(1)} collective-permute-done((bf16[256,512]{1,0:T(8,128)(2,1)S(1)}, bf16[256,512]{1,0:T(8,128)(2,1)S(1)}, u32[]{:S(2)}, u32[]{:S(2)}) %collective-permute-start.5) | collective-permute-done | bytes 262176 | tf_op jit(solution)/shard_map/ppermute | solution.py:35
  69.4 5.2 %collective-permute-done.7 = bf16[256,512]{1,0:T(8,128)(2,1)S(1)} collective-permute-done((bf16[256,512]{1,0:T(8,128)(2,1)S(1)}, bf16[256,512]{1,0:T(8,128)(2,1)S(1)}, u32[]{:S(2)}, u32[]{:S(2)}) %collective-permute-start.7) | collective-permute-done | bytes 262176 | tf_op jit(solution)/shard_map/ppermute | solution.py:35
  80.4 1.9 %fusion.32 = bf16[256,272]{1,0:T(8,128)(2,1)} fusion(bf16[256,4096]{1,0:T(8,128)(2,1)S(1)} %shard_map.208, bf16[4096,16]{1,0:T(8,128)(2,1)S(1)} %copy-done.21, bf16[4096,256]{1,0:T(8,128)(2,1)S(1)} %copy-done.32), kind=kOutput, calls=%fused_computation.47 | convolution fusion | flops 574951424 | bytes 4464640 | tf_op jit(solution)/shard_map/dot_general | solution.py:511
  94.5 2.0 %collective-permute-start.10 = (bf16[256,1024]{1,0:T(8,128)(2,1)}, bf16[256,1024]{1,0:T(8,128)(2,1)}, u32[]{:S(2)}, u32[]{:S(2)}) collective-permute-start(bf16[256,1024]{1,0:T(8,128)(2,1)} %fusion.30), channel_id=1, source_target_pairs={{0,1},{1,0},{2,3},{3,2},{4,5},{5,4},{6,7},{7,6},{8,9},{9,8},{10,11... | collective-permute-start | bytes 1572872 | tf_op jit(solution)/shard_map/ppermute | solution.py:40
  97.9 1.9 %fusion = f32[256,272]{0,1:T(8,128)} fusion(bf16[256,4096]{1,0:T(8,128)(2,1)S(1)} %shard_map.209, bf16[4096,16]{1,0:T(8,128)(2,1)S(1)} %copy-done.21, bf16[4096,256]{1,0:T(8,128)(2,1)S(1)} %copy-done.32), kind=kOutput, calls=%fused_computation.13 | convolution fusion | flops 574881792 | bytes 4603904 | tf_op jit(solution)/shard_map/dot_general | solution.py:511
  104.4 1.7 %fusion.21 = f32[256,1024]{1,0:T(8,128)} fusion(f32[256,1024]{1,0:T(8,128)S(1)} %fusion.23, bf16[2,1024,1024]{2,1,0:T(8,128)(2,1)S(1)} %bitcast.112, bf16[256,4096]{1,0:T(8,128)(2,1)S(1)} %shard_map.209), kind=kOutput, calls=%fused_computation.34 | convolution fusion | flops 537133056 | bytes 4718592 | tf_op jit(solution)/shard_map/dot_general | solution.py:514
  109.9 2.2 %shard_map.210 = (bf16[256,256]{1,0:T(8,128)(2,1)S(1)}, f32[4,256,4]{2,1,0:T(8,128)S(1)}, f32[4,4,256]{2,1,0:T(4,128)S(1)}, f32[4,4,256]{2,1,0:T(4,128)S(1)}, f3...) custom-call(s32[1,2]{1,0:T(1,128)S(1)} %copy-done.13, f32[256,272]{1,0:T(8,128)S(1)} %copy.46.own_ref, ...), custom_call_target="tpu_custom_call" | custom-call | flops 1000000 | bytes 10000 | tf_op jit(solution)/shard_map/pallas_call | solution.py:220
  112.3 2.7 %fusion.19 = f32[256,1024]{1,0:T(8,128)S(1)} fusion(f32[256,1024]{1,0:T(8,128)} %fusion.21, bf16[2,1024,1024]{2,1,0:T(8,128)(2,1)} %bitcast.113, bf16[256,4096]{1,0:T(8,128)(2,1)S(1)} %shard_map.209), kind=kOutput, calls=%fused_computation.32 | convolution fusion | flops 537133056 | bytes 4718592 | tf_op jit(solution)/shard_map/dot_general | solution.py:514
  115.2 7.7 %shard_map.211 = (f32[256,1024]{1,0:T(8,128)S(1)}, f32[2,16,64,256]{3,2,1,0:T(8,128)}) custom-call(s32[2,2]{1,0:T(2,128)S(1)} %copy-done.12, s32[2]{0:T(128)S(1)} %bitcast.101, f32[256,1024]{1,0:T(8,128)S(1)} %fusion.25.refs_0_, bf16[256,1024]{1,0:T(8,128)(2,1)} %collective-permute-done.10.refs_1_, f32[2,3,1024]{2,1,0:T(4,128)S(1)} %copy-done.8, ...), custom_call_target="tpu_custom_call" | custom-call | flops 1000000 | bytes 10000 | tf_op jit(solution)/shard_map/pallas_call | solution.py:384
  122.9 1.7 %collective-permute-done.14 = bf16[256,1024]{1,0:T(8,128)(2,1)} collective-permute-done((bf16[256,1024]{1,0:T(8,128)(2,1)}, bf16[256,1024]{1,0:T(8,128)(2,1)}, u32[]{:S(2)}, u32[]{:S(2)}) %collective-permute-start.14) | collective-permute-done | bytes 524320 | tf_op jit(solution)/shard_map/ppermute | solution.py:40
  (140 shorter events, 43.6 us)
Async XLA Ops:
  0.6 30.5 %collective-permute-start = (bf16[256,512]{1,0:T(8,128)(2,1)}, bf16[256,512]{1,0:T(8,128)(2,1)S(1)}, u32[]{:S(2)}, u32[]{:S(2)}) collective-permute-start(bf16[256,512]{1,0:T(8,128)(2,1)} %param.20), channel_id=1, source_target_pairs={{0,16},{1,0},{2,18},{3,2},{4,20},{5,4},{6,22},{7,6},{8,24},{9,8},{... | collective-permute-start | bytes 786440 | tf_op jit(solution)/shard_map/ppermute | solution.py:90
  4.7 26.4 %collective-permute-start.1 = (bf16[256,512]{1,0:T(8,128)(2,1)}, bf16[256,512]{1,0:T(8,128)(2,1)S(1)}, u32[]{:S(2)}, u32[]{:S(2)}) collective-permute-start(bf16[256,512]{1,0:T(8,128)(2,1)} %param.20), channel_id=1, source_target_pairs={{1,16},{3,18},{5,20},{7,22},{9,24},{11,26},{13,28},{15,30},{16,1},... | collective-permute-start | bytes 786440 | tf_op jit(solution)/shard_map/ppermute | solution.py:91
  10.9 6.8 %copy-start.6 = (f32[2,16,64,256]{3,2,1,0:T(8,128)}, f32[2,16,64,256]{3,2,1,0:T(8,128)S(1)}, u32[]{:S(2)}) copy-start(f32[2,16,64,256]{3,2,1,0:T(8,128)S(1)} %get-tuple-element.53.refs_13_) | copy-start | bytes 6291460
  10.9 6.5 %copy-start = (bf16[4096,2,1024]{2,1,0:T(2,128)(2,1)S(1)}, bf16[4096,2,1024]{2,1,0:T(2,128)(2,1)}, u32[]{:S(2)}) copy-start(bf16[4096,2,1024]{2,1,0:T(2,128)(2,1)} %w_ref.7) | copy-start | bytes 50331652
  31.2 16.6 %collective-permute-start.3 = (bf16[256,512]{1,0:T(8,128)(2,1)S(1)}, bf16[256,512]{1,0:T(8,128)(2,1)S(1)}, u32[]{:S(2)}, u32[]{:S(2)}) collective-permute-start(bf16[256,512]{1,0:T(8,128)(2,1)S(1)} %get-tuple-element.31._), channel_id=1, source_target_pairs={{0,8},{8,0},{2,10},{10,2},{4,12},{12,4},{6,14},{14,6},{16,24},{24,... | collective-permute-start | bytes 786440 | tf_op jit(solution)/shard_map/ppermute | solution.py:35
  32.8 43.8 %collective-permute-start.11 = (bf16[2,1040,256]{2,1,0:T(8,128)(2,1)S(1)}, bf16[2,1040,256]{2,1,0:T(8,128)(2,1)}, u32[]{:S(2)}, u32[]{:S(2)}) collective-permute-start(bf16[2,1040,256]{2,1,0:T(8,128)(2,1)S(1)} %get-tuple-element.30._), channel_id=1, source_target_pairs={{0,1},{1,0},{2,3},{3,2},{4,5},{5,4},{6,7},{7,6},{8,9},{9,8},{10,11... | collective-permute-start | bytes 3194888 | tf_op jit(solution)/shard_map/ppermute | solution.py:40
  42.9 5.9 %copy-start.34 = (s32[8]{0:T(128)S(1)}, s32[8]{0:T(128)}, u32[]{:S(2)}) copy-start(s32[8]{0:T(128)} %constant.99.clone) | copy-start | bytes 100
  43.0 15.4 %collective-permute-start.2 = (bf16[256,512]{1,0:T(8,128)(2,1)S(1)}, bf16[256,512]{1,0:T(8,128)(2,1)S(1)}, u32[]{:S(2)}, u32[]{:S(2)}) collective-permute-start(bf16[256,512]{1,0:T(8,128)(2,1)S(1)} %get-tuple-element.31._), channel_id=1, source_target_pairs={{0,4},{4,0},{2,6},{6,2},{8,12},{12,8},{10,14},{14,10},{16,20},{20,... | collective-permute-start | bytes 786440 | tf_op jit(solution)/shard_map/ppermute | solution.py:35
  47.8 10.6 %collective-permute-start.4 = (bf16[256,512]{1,0:T(8,128)(2,1)S(1)}, bf16[256,512]{1,0:T(8,128)(2,1)S(1)}, u32[]{:S(2)}, u32[]{:S(2)}) collective-permute-start(bf16[256,512]{1,0:T(8,128)(2,1)S(1)} %collective-permute-done.3), channel_id=1, source_target_pairs={{0,4},{4,0},{2,6},{6,2},{8,12},{12,8},{10,14},{14,10},{16,20},{20,... | collective-permute-start | bytes 786440 | tf_op jit(solution)/shard_map/ppermute | solution.py:35
  48.3 16.5 %copy-start.29 = (pred[2]{0:T(512)(128)(4,1)}, pred[2]{0:T(512)(128)(4,1)S(1)}, u32[]{:S(2)}) copy-start(pred[2]{0:T(512)(128)(4,1)S(1)} %broadcast_compare_fusion.1) | copy-start | bytes 10
  48.3 13.5 %collective-permute-start.6 = (bf16[256,512]{1,0:T(8,128)(2,1)S(1)}, bf16[256,512]{1,0:T(8,128)(2,1)S(1)}, u32[]{:S(2)}, u32[]{:S(2)}) collective-permute-start(bf16[256,512]{1,0:T(8,128)(2,1)S(1)} %get-tuple-element.35._), channel_id=1, source_target_pairs={{0,8},{8,0},{2,10},{10,2},{4,12},{12,4},{6,14},{14,6},{16,24},{24,... | collective-permute-start | bytes 786440 | tf_op jit(solution)/shard_map/ppermute | solution.py:35
  48.9 5.8 %copy-start.2 = (bf16[4096,2,1024]{2,1,0:T(2,128)(2,1)S(1)}, bf16[4096,2,1024]{2,1,0:T(2,128)(2,1)}, u32[]{:S(2)}) copy-start(bf16[4096,2,1024]{2,1,0:T(2,128)(2,1)} %w_ref.7) | copy-start | bytes 50331652
  58.4 6.3 %copy-start.31 = (f32[16]{0:T(128)S(1)}, f32[16]{0:T(128)}, u32[]{:S(2)}) copy-start(f32[16]{0:T(128)} %param.26) | copy-start | bytes 196
  60.2 18.0 %collective-permute-start.9 = (bf16[4,256,512]{2,1,0:T(8,128)(2,1)S(1)}, bf16[4,256,512]{2,1,0:T(8,128)(2,1)}, u32[]{:S(2)}, u32[]{:S(2)}) collective-permute-start(bf16[4,256,512]{2,1,0:T(8,128)(2,1)S(1)} %pad_maximum_fusion.5.refs_0_), channel_id=1, source_target_pairs={{0,2},{2,0},{4,6},{6,4},{8,10},{10,8},{12,14},{14,12},{16,18},{18,... | collective-permute-start | bytes 3145736 | tf_op jit(solution)/shard_map/ppermute | solution.py:35
  60.3 9.2 %collective-permute-start.5 = (bf16[256,512]{1,0:T(8,128)(2,1)S(1)}, bf16[256,512]{1,0:T(8,128)(2,1)S(1)}, u32[]{:S(2)}, u32[]{:S(2)}) collective-permute-start(bf16[256,512]{1,0:T(8,128)(2,1)S(1)} %get-tuple-element.35._), channel_id=1, source_target_pairs={{0,4},{4,0},{2,6},{6,2},{8,12},{12,8},{10,14},{14,10},{16,20},{20,... | collective-permute-start | bytes 786440 | tf_op jit(solution)/shard_map/ppermute | solution.py:35
  61.8 12.8 %copy-start.23 = (bf16[256,512]{1,0:T(8,128)(2,1)}, bf16[256,512]{1,0:T(8,128)(2,1)S(1)}, u32[]{:S(2)}) copy-start(bf16[256,512]{1,0:T(8,128)(2,1)S(1)} %collective-permute-done.6) | copy-start | bytes 786436
  61.8 12.8 %collective-permute-start.7 = (bf16[256,512]{1,0:T(8,128)(2,1)S(1)}, bf16[256,512]{1,0:T(8,128)(2,1)S(1)}, u32[]{:S(2)}, u32[]{:S(2)}) collective-permute-start(bf16[256,512]{1,0:T(8,128)(2,1)S(1)} %collective-permute-done.6), channel_id=1, source_target_pairs={{0,4},{4,0},{2,6},{6,2},{8,12},{12,8},{10,14},{14,10},{16,20},{20,... | collective-permute-start | bytes 786440 | tf_op jit(solution)/shard_map/ppermute | solution.py:35
  65.4 12.0 %copy-start.30 = (pred[2]{0:T(512)(128)(4,1)S(1)}, pred[2]{0:T(512)(128)(4,1)}, u32[]{:S(2)}) copy-start(pred[2]{0:T(512)(128)(4,1)} %copy-done.29) | copy-start | bytes 10
  76.5 20.0 %collective-permute-start.8 = (bf16[4,256,512]{2,1,0:T(8,128)(2,1)S(1)}, bf16[4,256,512]{2,1,0:T(8,128)(2,1)}, u32[]{:S(2)}, u32[]{:S(2)}) collective-permute-start(bf16[4,256,512]{2,1,0:T(8,128)(2,1)S(1)} %pad_maximum_fusion.6.refs_0_), channel_id=1, source_target_pairs={{0,2},{2,0},{4,6},{6,4},{8,10},{10,8},{12,14},{14,12},{16,18},{18,... | collective-permute-start | bytes 3145736 | tf_op jit(solution)/shard_map/ppermute | solution.py:35
  94.5 12.8 %collective-permute-start.12 = (bf16[256,272]{1,0:T(8,128)(2,1)}, bf16[256,272]{1,0:T(8,128)(2,1)}, u32[]{:S(2)}, u32[]{:S(2)}) collective-permute-start(bf16[256,272]{1,0:T(8,128)(2,1)} %fusion.32), channel_id=1, source_target_pairs={{0,1},{1,0},{2,3},{3,2},{4,5},{5,4},{6,7},{7,6},{8,9},{9,8},{10,11... | collective-permute-start | bytes 417800 | tf_op jit(solution)/shard_map/ppermute | solution.py:40
  94.5 20.7 %collective-permute-start.10 = (bf16[256,1024]{1,0:T(8,128)(2,1)}, bf16[256,1024]{1,0:T(8,128)(2,1)}, u32[]{:S(2)}, u32[]{:S(2)}) collective-permute-start(bf16[256,1024]{1,0:T(8,128)(2,1)} %fusion.30), channel_id=1, source_target_pairs={{0,1},{1,0},{2,3},{3,2},{4,5},{5,4},{6,7},{7,6},{8,9},{9,8},{10,11... | collective-permute-start | bytes 1572872 | tf_op jit(solution)/shard_map/ppermute | solution.py:40
  96.5 28.1 %collective-permute-start.14 = (bf16[256,1024]{1,0:T(8,128)(2,1)}, bf16[256,1024]{1,0:T(8,128)(2,1)}, u32[]{:S(2)}, u32[]{:S(2)}) collective-permute-start(bf16[256,1024]{1,0:T(8,128)(2,1)} %fusion.31), channel_id=1, source_target_pairs={{0,1},{1,0},{2,3},{3,2},{4,5},{5,4},{6,7},{7,6},{8,9},{9,8},{10,11... | collective-permute-start | bytes 1572872 | tf_op jit(solution)/shard_map/ppermute | solution.py:40
  112.2 2.8 %collective-permute-start.13 = (bf16[256,256]{1,0:T(8,128)(2,1)S(1)}, bf16[256,256]{1,0:T(8,128)(2,1)S(1)}, u32[]{:S(2)}, u32[]{:S(2)}) collective-permute-start(bf16[256,256]{1,0:T(8,128)(2,1)S(1)} %get-tuple-element.47), channel_id=1, source_target_pairs={{0,2},{2,0},{4,6},{6,4},{8,10},{10,8},{12,14},{14,12},{16,18},{18,... | collective-permute-start | bytes 393224 | tf_op jit(solution)/shard_map/ppermute | solution.py:35
  126.0 1.2 collective-permute-start.15
  (27 other events, 72.2 us)

commit v6 on v5

--- a/solution.py
+++ b/solution.py
@@ -94,7 +94,7 @@
 
 
 def quad_arrange(four, other):
-    apart = jnp.array([0, 2, 4, 6, 1, 3, 5, 7], jnp.int32)
+    apart = jnp.array([0, 4, 2, 6, 1, 5, 3, 7], jnp.int32)
     return arrange([four, other], (lax.axis_index("wide") % 8) ^ apart)
 
 
@@ -110,26 +110,10 @@
     ]
 
 
-def grab_kernel(first, w_ref, _, out_ref, sem):
-    copy = pltpu.make_async_copy(w_ref.at[pl.ds(first, out_ref.shape[0])], out_ref, sem)
-    copy.start()
-    copy.wait()
-
-
-def relayout(w_xz, chunk, chunks, behind):
-    rows = w_xz.shape[0] // chunks
-    in_hbm = pl.BlockSpec(memory_space=pltpu.HBM)
-    held = pl.pallas_call(
-        functools.partial(grab_kernel, chunk * rows),
-        out_shape=jax.ShapeDtypeStruct((rows,) + w_xz.shape[1:], w_xz.dtype),
-        in_specs=[in_hbm, pl.BlockSpec(memory_space=pl.ANY)],
-        out_specs=pl.BlockSpec(memory_space=pltpu.VMEM),
-        scratch_shapes=[pltpu.SemaphoreType.DMA],
-        compiler_params=params(),
-        cost_estimate=cost(0, 4 * rows * w_xz.shape[1] * w_xz.shape[2]),
-    )(w_xz, behind)
-    rows_last = with_layout_constraint(jnp.transpose(held, (1, 0, 2)), Layout((0, 1, 2)))
-    return lax.optimization_barrier(rows_last)
+def pinned(array):
+    return lax.optimization_barrier(
+        with_layout_constraint(array, Layout(tuple(range(array.ndim))))
+    )
 
 
 def token_places(starts, count_tok, shape, axis):
@@ -439,9 +423,16 @@
     lags = conv_x_pool.shape[1]
     conv_width = local_width + state_part
 
-    count_wide = lax.axis_size("wide")
-    if req_count == 2 and count_wide == 16:
-        own_block, their_block = near_blocks(x_in)
+    direct = req_count == 2 and lax.axis_size("wide") == 16
+    w_pair = jnp.transpose(w_xz, (1, 0, 2))
+    w_step = w_dt
+    if direct:
+        own_block, block = near_blocks(x_in)
+        w_pair = pinned(w_pair)
+        block = after(block, w_pair)
+        along_z = partner_2(block, "wide", 2)
+        along_x = partner_2(block, "wide", 1)
+        w_step = pinned(after(w_dt, block))
 
     def slots_of(index):
         asked = lax.dynamic_slice_in_dim(state_slot, index * group_reqs, group_reqs)
@@ -462,6 +453,8 @@
     for step in range(1, req_count):
         slots = slots_of((me + step) % req_count)
         flat = conv_of(slots).reshape(group_reqs, conv_size)
+        if direct:
+            flat = after(flat, block)
         flat = jnp.pad(flat, ((0, 0), (0, conv_rows * state - conv_size)))
         packed, held = pack(
             ssm_pool, flat.reshape(group_reqs, conv_rows, state), slots, own_slots
@@ -481,54 +474,39 @@
         cache = jnp.where((came_from == step)[:, None, None], got, cache)
     cache = jnp.where(live[:, None, None], cache, 0).astype(F32)
 
-    chunks = 4
-    if req_count == 2 and count_wide == 16:
-        weights = [relayout(w_xz, k, chunks, packed) for k in range(2)]
-        block = after(their_block, *weights)
-        along_z = partner_2(block, "wide", 2)
-        along_x = partner_2(block, "wide", 1)
-        weights.append(relayout(w_xz, 2, chunks, block))
-        own_block = after(own_block, weights[2])
-        both = partner_2(after(along_z, weights[2]), "wide", 1)
+    if direct:
+        both = partner_2(after(along_z, packed, w_step), "wide", 1)
+        own_block = after(own_block, packed)
         own_z = partner_2(own_block, "wide", 2)
-        weights.append(relayout(w_xz, 3, chunks, own_block))
-        four = jnp.stack([block, along_x, along_z, after(both, weights[3])])
+        four = jnp.stack([block, along_z, along_x, both])
         other = partner_2(four, "wide", 0)
-        own_x = partner_2(after(own_block, four), "wide", 1)
-        own_both = partner_2(after(own_z, four), "wide", 1)
-        theirs = quad_arrange(four, other)
-        own_four = jnp.stack([own_block, own_x, own_z, own_both])
+        own_pair = after(jnp.stack([own_block, own_z]), four)
+        own_four = jnp.concatenate([own_pair, partner_2(own_pair, "wide", 1)], 0)
         own_other = partner_2(own_four, "wide", 0)
-        features = [(own_four, own_other), theirs]
+        features = [(own_four, own_other), quad_arrange(four, other)]
     else:
-        weights = [relayout(w_xz, k, chunks, packed) for k in range(chunks)]
         features = features_in_general(x_in)
-    w_map = jnp.concatenate([w_bc, w_dt], 1)
-    depth = w_xz.shape[0] // chunks
+    weights = {
+        "map": jnp.concatenate([w_bc, w_step], 1),
+        "xr": w_pair[1],
+        "z": w_pair[0],
+    }
 
     def project(block, name):
-        if name == "map":
-            return jnp.dot(block, w_map, preferred_element_type=F32)
-        total = None
-        for k in range(chunks):
-            term = jnp.dot(
-                block[:, k * depth : (k + 1) * depth],
-                weights[k][1 if name == "xr" else 0],
-                preferred_element_type=F32,
-            )
-            total = term if total is None else total + term
-        return total
+        return jnp.dot(block, weights[name], preferred_element_type=F32)
 
     came = {"map": [], "xr": [], "z": []}
     done = []
     for step in range(1, req_count):
         block = features[step]
         for name in came:
+            if name == "z":
+                block = after(block, came["map"][-1])
             part, block = lax.optimization_barrier((project(block, name).astype(BF16), block))
             came[name].append(shift_req(part, step))
             done.append(part)
     block = after(features[0], *done)
-    if req_count == 2 and count_wide == 16:
+    if direct:
         block = quad_arrange(*block)
     own = {}
     for name in came:

time: 129 us -> 106 us (0.82)
  local copies, waits for them, and re-layouts: 52 us -> 23.5 us
  waiting for transfers between devices: 12 us -> 21.7 us
  other arithmetic: 8.37 us -> 3.48 us
  matrix products: 20.2 us -> 22.4 us
  Pallas kernels: 16.9 us -> 14.9 us
    pallas_call x4 -> x0, local copies, waits for them, and re-layouts: 15.6 us -> none  [relayout(): pl.pallas_call(functools.partial(grab_kernel, chunk * rows), out_shape=ja...]
    unnamed x75 -> x64, local copies, waits for them, and re-layouts: 34.4 us -> 21.7 us
    ppermute x4, waiting for transfers between devices: 1.67 us -> 8.33 us  [shift_req(): lax.ppermute(block, 'req', [(i, (i + step) % count) for i in range(count)])]
    ppermute x10 -> x9, waiting for transfers between devices: 10.3 us -> 13.4 us  [partner_2(): return lax.ppermute(block, axis, route)]
    ppermute x4, starting transfers between devices: 6.14 us -> 8.46 us  [shift_req(): lax.ppermute(block, 'req', [(i, (i + step) % count) for i in range(count)])]
    dot_general x18 -> x6, matrix products: 20.2 us -> 22.4 us  [project(): return jnp.dot(block, weights[name], preferred_element_type=F32)]
    another operation x2, other arithmetic: 2.32 us -> 0.18 us  [the longest x1 0.13 us: on_device(): four = jnp.stack([block, along_z, along_x, both])]
    reduce_sum x2, other arithmetic: 1.78 us -> 0.26 us  [conv_of(): jnp.sum(jnp.where(hit[:, :, None, None], pool[None], 0), 1)]
  transfers between devices with their start and end apart: 16 -> 15, of which waited for: 4 -> 5; matrix products, arithmetic and copies ran while one was open for 36% -> 39% of each run, Pallas kernels for 13% -> 14%
where the time goes in v6:
time: 106 us
  local copies, waits for them, and re-layouts  23.5 us (22%)
  matrix products  22.4 us (21%)
  waiting for transfers between devices  21.7 us (20%)
  starting transfers between devices  18.5 us (17%)
  Pallas kernels  14.9 us (14%)
  other arithmetic  3.48 us (3%)
  between operations  1.21 us (1%)
    dot_general x6, matrix products, project(): return jnp.dot(block, weights[name], preferred_element_type=F32)  22.4 us
    unnamed x64, local copies, waits for them, and re-layouts  21.7 us
    ppermute x9, waiting for transfers between devices, partner_2(): return lax.ppermute(block, axis, route)  13.4 us
    ppermute x4, starting transfers between devices, shift_req(): lax.ppermute(block, 'req', [(i, (i + step) % count) for i in range(count)])  8.46 us
    ppermute x4, waiting for transfers between devices, shift_req(): lax.ppermute(block, 'req', [(i, (i + step) % count) for i in range(count)])  8.33 us
    pallas_call x1, Pallas kernels, mixer(): pl.pallas_call(functools.partial(mixer_kernel, count_req, len(got)), out_...  7.63 us
    ppermute x9, starting transfers between devices, partner_2(): return lax.ppermute(block, axis, route)  5.33 us
    ppermute x1, starting transfers between devices, near_blocks(): first = lax.ppermute(x_in, axes, first)  4.09 us
  transfers between devices with their start and end apart: 15, of which 5 were waited for; matrix products, arithmetic and copies ran while one was open for 39% of the time, Pallas kernels for 14%

profile of v6, /device:TPU:0, one launch (start us, length us, event | category | flops | bytes accessed | tf_op | source)
XLA Modules:
  0.0 105.8 jit_solution(16417184002137215386)
XLA Ops:
  0.6 4.1 %collective-permute-start = (bf16[256,512]{1,0:T(8,128)(2,1)}, bf16[256,512]{1,0:T(8,128)(2,1)S(1)}, u32[]{:S(2)}, u32[]{:S(2)}) collective-permute-start(bf16[256,512]{1,0:T(8,128)(2,1)} %param.20), channel_id=1, source_target_pairs={{0,16},{1,0},{2,18},{3,2},{4,20},{5,4},{6,22},{7,6},{8,24},{9,8},{... | collective-permute-start | bytes 786440 | tf_op jit(solution)/shard_map/ppermute | solution.py:90
  5.5 16.5 %copy.44 = bf16[4096,2,1024]{2,0,1:T(8,128)(2,1)} copy(bf16[4096,2,1024]{2,1,0:T(2,128)(2,1)} %param.21) | data formatting | bytes 33554432 | tf_op args[1]
  22.4 1.6 %collective-permute-start.3 = (bf16[256,512]{1,0:T(8,128)(2,1)S(1)}, bf16[256,512]{1,0:T(8,128)(2,1)S(1)}, u32[]{:S(2)}, u32[]{:S(2)}) collective-permute-start(bf16[256,512]{1,0:T(8,128)(2,1)S(1)} %get-tuple-element.31), channel_id=1, source_target_pairs={{0,8},{8,0},{2,10},{10,2},{4,12},{12,4},{6,14},{14,6},{16,24},{24,... | collective-permute-start | bytes 786440 | tf_op jit(solution)/shard_map/ppermute | solution.py:35
  24.2 1.6 %collective-permute-start.4 = (bf16[256,512]{1,0:T(8,128)(2,1)S(1)}, bf16[256,512]{1,0:T(8,128)(2,1)S(1)}, u32[]{:S(2)}, u32[]{:S(2)}) collective-permute-start(bf16[256,512]{1,0:T(8,128)(2,1)S(1)} %get-tuple-element.31), channel_id=1, source_target_pairs={{0,4},{4,0},{2,6},{6,2},{8,12},{12,8},{10,14},{14,10},{16,20},{20,... | collective-permute-start | bytes 786440 | tf_op jit(solution)/shard_map/ppermute | solution.py:35
  25.8 1.3 %copy.35 = bf16[4096,16]{1,0:T(8,128)(2,1)} copy(bf16[4096,16]{0,1:T(8,128)(2,1)S(1)} %copy-done.16) | data formatting | bytes 262144 | tf_op jit(solution)/shard_map/optimization_barrier | solution.py:84
  27.1 3.3 %shard_map.203 = (bf16[2,1040,256]{2,1,0:T(8,128)(2,1)}, f32[2,16,64,256]{3,2,1,0:T(8,128)S(1)}) custom-call(s32[2]{0:T(128)S(1)} %get-tuple-element.73.slots_ref, s32[2]{0:T(128)S(1)} %get-tuple-element.72.own_slots_ref, f32[8,16,64,256]{3,2,1,0:T(8,128)} %own_pool_ref.1, f32[8,16,64,256]{3,2,1,0:T(8,128)} %own_pool_ref.1, bf16[2,16,256]{2,1,0:T(8,128)(2,1)S(1)} %bitcast.42), custom_call_target="tpu_custom_call" | custom-call | bytes 7340032 | tf_op jit(solution)/shard_map/pallas_call | solution.py:232
  30.4 1.3 %copy-done = f32[2,16,64,256]{3,2,1,0:T(8,128)} copy-done((f32[2,16,64,256]{3,2,1,0:T(8,128)}, f32[2,16,64,256]{3,2,1,0:T(8,128)S(1)}, u32[]{:S(2)}) %copy-start) | copy-done | bytes 2097176
  32.8 4.6 %collective-permute-start.11 = (bf16[2,1040,256]{2,1,0:T(8,128)(2,1)}, bf16[2,1040,256]{2,1,0:T(8,128)(2,1)S(1)}, u32[]{:S(2)}, u32[]{:S(2)}) collective-permute-start(bf16[2,1040,256]{2,1,0:T(8,128)(2,1)} %get-tuple-element.33), channel_id=1, source_target_pairs={{0,1},{1,0},{2,3},{3,2},{4,5},{5,4},{6,7},{7,6},{8,9},{9,8},{10,11... | collective-permute-start | bytes 3194888 | tf_op jit(solution)/shard_map/ppermute | solution.py:40
  37.6 1.3 %collective-permute-done.2 = bf16[256,512]{1,0:T(8,128)(2,1)S(1)} collective-permute-done((bf16[256,512]{1,0:T(8,128)(2,1)S(1)}, bf16[256,512]{1,0:T(8,128)(2,1)S(1)}, u32[]{:S(2)}, u32[]{:S(2)}) %collective-permute-start.2) | collective-permute-done | bytes 262176 | tf_op jit(solution)/shard_map/ppermute | solution.py:35
  39.9 11.1 %collective-permute-done.6 = bf16[2,256,512]{2,1,0:T(8,128)(2,1)S(1)} collective-permute-done((bf16[2,256,512]{2,1,0:T(8,128)(2,1)S(1)}, bf16[2,256,512]{2,1,0:T(8,128)(2,1)S(1)}, u32[]{:S(2)}, u32[]{:S(2)}) %collective-permute-start.6) | collective-permute-done | bytes 524320 | tf_op jit(solution)/shard_map/ppermute | solution.py:35
  51.2 8.3 %collective-permute-done.11.refs_14_ = bf16[2,1040,256]{2,1,0:T(8,128)(2,1)S(1)} collective-permute-done((bf16[2,1040,256]{2,1,0:T(8,128)(2,1)}, bf16[2,1040,256]{2,1,0:T(8,128)(2,1)S(1)}, u32[]{:S(2)}, u32[]{:S(2)}) %collective-permute-start.11) | collective-permute-done | bytes 1064992 | tf_op jit(solution)/shard_map/ppermute | solution.py:40
  60.7 1.5 %shard_map.204 = bf16[256,4096]{1,0:T(8,128)(2,1)S(1)} custom-call(s32[8]{0:T(128)S(1)} %broadcast_xor_fusion.places_ref, bf16[4,256,512]{2,1,0:T(8,128)(2,1)S(1)} %pad_maximum_fusion.5.refs_0_, bf16[4,256,512]{2,1,0:T(8,128)(2,1)} %collective-permute-done.8.refs_1_), custom_call_target="tpu_custom_call" | custom-call | flops 1000000 | bytes 10000 | tf_op jit(solution)/shard_map/pallas_call | solution.py:72
  62.8 1.3 %fusion.8 = bf16[256,272]{1,0:T(8,128)(2,1)S(1)} fusion(bf16[256,4096]{1,0:T(8,128)(2,1)S(1)} %shard_map.204, bf16[4096,16]{1,0:T(8,128)(2,1)S(1)} %copy-done.14, bf16[4096,256]{1,0:T(8,128)(2,1)S(1)} %copy-done.22), kind=kOutput, calls=%fused_computation.14 | convolution fusion | flops 574951424 | bytes 4464640 | tf_op jit(solution)/shard_map/dot_general | solution.py:496
  64.1 1.8 %collective-permute-start.9 = (bf16[256,272]{1,0:T(8,128)(2,1)S(1)}, bf16[256,272]{1,0:T(8,128)(2,1)S(1)}, u32[]{:S(2)}, u32[]{:S(2)}) collective-permute-start(bf16[256,272]{1,0:T(8,128)(2,1)S(1)} %fusion.8), channel_id=1, source_target_pairs={{0,1},{1,0},{2,3},{3,2},{4,5},{5,4},{6,7},{7,6},{8,9},{9,8},{10,11... | collective-permute-start | bytes 417800 | tf_op jit(solution)/shard_map/ppermute | solution.py:40
  65.9 7.3 %fusion.7 = bf16[256,1024]{1,0:T(8,128)(2,1)} fusion(bf16[256,4096]{1,0:T(8,128)(2,1)S(1)} %shard_map.204, bf16[2,4096,1024]{2,1,0:T(8,128)(2,1)} %bitcast.48), kind=kOutput, calls=%fused_computation.13 | convolution fusion | flops 2147745792 | bytes 11010048 | tf_op jit(solution)/shard_map/dot_general | solution.py:496
  73.2 3.2 %fusion.6 = bf16[256,1024]{1,0:T(8,128)(2,1)} fusion(bf16[256,4096]{1,0:T(8,128)(2,1)S(1)} %shard_map.204, bf16[2,4096,1024]{2,1,0:T(8,128)(2,1)S(1)} %bitcast.52), kind=kOutput, calls=%fused_computation.12 | convolution fusion | flops 2147745792 | bytes 11010048 | tf_op jit(solution)/shard_map/dot_general | solution.py:496
  76.4 2.0 %collective-permute-start.13 = (bf16[256,1024]{1,0:T(8,128)(2,1)}, bf16[256,1024]{1,0:T(8,128)(2,1)}, u32[]{:S(2)}, u32[]{:S(2)}) collective-permute-start(bf16[256,1024]{1,0:T(8,128)(2,1)} %fusion.6), channel_id=1, source_target_pairs={{0,1},{1,0},{2,3},{3,2},{4,5},{5,4},{6,7},{7,6},{8,9},{9,8},{10,11... | collective-permute-start | bytes 1572872 | tf_op jit(solution)/shard_map/ppermute | solution.py:40
  79.4 1.2 %copy-done.5 = bf16[4,256,512]{2,1,0:T(8,128)(2,1)S(1)} copy-done((bf16[4,256,512]{2,1,0:T(8,128)(2,1)S(1)}, bf16[4,256,512]{2,1,0:T(8,128)(2,1)}, u32[]{:S(2)}) %copy-start.5) | copy-done | bytes 1048600
  81.4 1.2 %fusion.4 = f32[256,272]{0,1:T(8,128)S(1)} fusion(bf16[256,4096]{1,0:T(8,128)(2,1)S(1)} %shard_map.205, bf16[4096,16]{1,0:T(8,128)(2,1)S(1)} %copy-done.14, bf16[4096,256]{1,0:T(8,128)(2,1)S(1)} %copy-done.22), kind=kOutput, calls=%fused_computation.8 | convolution fusion | flops 574881792 | bytes 4603904 | tf_op jit(solution)/shard_map/dot_general | solution.py:496
  82.7 3.4 %fusion.refs_0_ = f32[256,1024]{1,0:T(8,128)} fusion(bf16[256,4096]{1,0:T(8,128)(2,1)S(1)} %shard_map.205, bf16[2,4096,1024]{2,1,0:T(8,128)(2,1)S(1)} %bitcast.53), kind=kOutput, calls=%fused_computation.3 | convolution fusion | flops 2147483648 | bytes 11534336 | tf_op jit(solution)/shard_map/dot_general | solution.py:496
  86.3 1.8 %shard_map.206 = (bf16[256,256]{1,0:T(8,128)(2,1)S(1)}, f32[4,256,4]{2,1,0:T(8,128)S(1)}, f32[4,4,256]{2,1,0:T(4,128)S(1)}, f32[4,4,256]{2,1,0:T(4,128)S(1)}, f3...) custom-call(s32[1,2]{1,0:T(1,128)S(1)} %copy-done.10, f32[256,272]{1,0:T(8,128)S(1)} %copy.37.own_ref, ...), custom_call_target="tpu_custom_call" | custom-call | flops 1000000 | bytes 10000 | tf_op jit(solution)/shard_map/pallas_call | solution.py:204
  88.2 6.1 %fusion.2 = f32[256,1024]{1,0:T(8,128)S(1)} fusion(bf16[256,4096]{1,0:T(8,128)(2,1)S(1)} %shard_map.205, bf16[2,4096,1024]{2,1,0:T(8,128)(2,1)} %bitcast.49), kind=kOutput, calls=%fused_computation.5 | convolution fusion | flops 2147483648 | bytes 11534336 | tf_op jit(solution)/shard_map/dot_general | solution.py:496
  94.5 7.6 %shard_map.207 = (f32[256,1024]{1,0:T(8,128)S(1)}, f32[2,16,64,256]{3,2,1,0:T(8,128)}) custom-call(s32[2,2]{1,0:T(2,128)S(1)} %and_convert_fusion.flags_ref, s32[2]{0:T(128)S(1)} %bitcast.44, f32[256,1024]{1,0:T(8,128)S(1)} %copy-done.6, bf16[256,1024]{1,0:T(8,128)(2,1)} %collective-permute-done.10.refs_1_, f32[2,3,1024]{2,1,0:T(4,128)S(1)} %slice.36.refs_2_, ...), custom_call_target="tpu_custom_call" | custom-call | flops 1000000 | bytes 10000 | tf_op jit(solution)/shard_map/pallas_call | solution.py:368
  102.2 1.5 %multiply_reduce_fusion = (f32[256]{0:T(256)S(1)}, f32[256,1024]{1,0:T(8,128)S(1)}) fusion(f32[256,1024]{1,0:T(8,128)S(1)} %get-tuple-element.56, f32[256,1024]{1,0:T(8,128)S(1)} %fusion.2, bf16[256,1024]{1,0:T(8,128)(2,1)} %collective-permute-done.13), kind=kLoop, calls=%fused_computation.21 | loop fusion | flops 2883328 | bytes 3671040 | tf_op jit(solution)/shard_map/reduce_sum | solution.py:539
  (110 shorter events, 9.6 us)
Async XLA Ops:
  0.6 21.6 %collective-permute-start = (bf16[256,512]{1,0:T(8,128)(2,1)}, bf16[256,512]{1,0:T(8,128)(2,1)S(1)}, u32[]{:S(2)}, u32[]{:S(2)}) collective-permute-start(bf16[256,512]{1,0:T(8,128)(2,1)} %param.20), channel_id=1, source_target_pairs={{0,16},{1,0},{2,18},{3,2},{4,20},{5,4},{6,22},{7,6},{8,24},{9,8},{... | collective-permute-start | bytes 786440 | tf_op jit(solution)/shard_map/ppermute | solution.py:90
  4.7 17.6 %collective-permute-start.1 = (bf16[256,512]{1,0:T(8,128)(2,1)}, bf16[256,512]{1,0:T(8,128)(2,1)S(1)}, u32[]{:S(2)}, u32[]{:S(2)}) collective-permute-start(bf16[256,512]{1,0:T(8,128)(2,1)} %param.20), channel_id=1, source_target_pairs={{1,16},{3,18},{5,20},{7,22},{9,24},{11,26},{13,28},{15,30},{16,1},... | collective-permute-start | bytes 786440 | tf_op jit(solution)/shard_map/ppermute | solution.py:91
  5.4 16.5 %copy-start.19 = (s32[4]{0:T(128)S(1)}, s32[4]{0:T(128)}, u32[]{:S(2)}) copy-start(s32[4]{0:T(128)} %param.34) | copy-start | bytes 52
  5.4 16.7 %copy-start.17 = (bf16[8,3,1024]{2,0,1:T(8,128)(2,1)S(1)}, bf16[8,3,1024]{2,0,1:T(8,128)(2,1)}, u32[]{:S(2)}) copy-start(bf16[8,3,1024]{2,0,1:T(8,128)(2,1)} %param.36) | copy-start | bytes 147460
  5.4 16.9 %copy-start.15 = (bf16[256,512]{1,0:T(8,128)(2,1)S(1)}, bf16[256,512]{1,0:T(8,128)(2,1)}, u32[]{:S(2)}) copy-start(bf16[256,512]{1,0:T(8,128)(2,1)} %param.20) | copy-start | bytes 786436
  5.5 18.6 %copy-start.18 = (bf16[8,3,256]{2,0,1:T(8,128)(2,1)S(1)}, bf16[8,3,256]{2,0,1:T(8,128)(2,1)}, u32[]{:S(2)}) copy-start(bf16[8,3,256]{2,0,1:T(8,128)(2,1)} %param.37) | copy-start | bytes 36868
  5.5 20.3 %copy-start.16 = (bf16[4096,16]{0,1:T(8,128)(2,1)S(1)}, bf16[4096,16]{0,1:T(8,128)(2,1)}, u32[]{:S(2)}) copy-start(bf16[4096,16]{0,1:T(8,128)(2,1)} %param.22) | copy-start | bytes 393220
  22.4 9.8 %collective-permute-start.3 = (bf16[256,512]{1,0:T(8,128)(2,1)S(1)}, bf16[256,512]{1,0:T(8,128)(2,1)S(1)}, u32[]{:S(2)}, u32[]{:S(2)}) collective-permute-start(bf16[256,512]{1,0:T(8,128)(2,1)S(1)} %get-tuple-element.31), channel_id=1, source_target_pairs={{0,8},{8,0},{2,10},{10,2},{4,12},{12,4},{6,14},{14,6},{16,24},{24,... | collective-permute-start | bytes 786440 | tf_op jit(solution)/shard_map/ppermute | solution.py:35
  24.2 14.8 %collective-permute-start.4 = (bf16[256,512]{1,0:T(8,128)(2,1)S(1)}, bf16[256,512]{1,0:T(8,128)(2,1)S(1)}, u32[]{:S(2)}, u32[]{:S(2)}) collective-permute-start(bf16[256,512]{1,0:T(8,128)(2,1)S(1)} %get-tuple-element.31), channel_id=1, source_target_pairs={{0,4},{4,0},{2,6},{6,2},{8,12},{12,8},{10,14},{14,10},{16,20},{20,... | collective-permute-start | bytes 786440 | tf_op jit(solution)/shard_map/ppermute | solution.py:35
  31.7 7.2 %collective-permute-start.2 = (bf16[256,512]{1,0:T(8,128)(2,1)S(1)}, bf16[256,512]{1,0:T(8,128)(2,1)S(1)}, u32[]{:S(2)}, u32[]{:S(2)}) collective-permute-start(bf16[256,512]{1,0:T(8,128)(2,1)S(1)} %get-tuple-element.34), channel_id=1, source_target_pairs={{0,8},{8,0},{2,10},{10,2},{4,12},{12,4},{6,14},{14,6},{16,24},{24,... | collective-permute-start | bytes 786440 | tf_op jit(solution)/shard_map/ppermute | solution.py:35
  32.1 6.9 %collective-permute-start.5 = (bf16[256,512]{1,0:T(8,128)(2,1)S(1)}, bf16[256,512]{1,0:T(8,128)(2,1)S(1)}, u32[]{:S(2)}, u32[]{:S(2)}) collective-permute-start(bf16[256,512]{1,0:T(8,128)(2,1)S(1)} %collective-permute-done.3), channel_id=1, source_target_pairs={{0,4},{4,0},{2,6},{6,2},{8,12},{12,8},{10,14},{14,10},{16,20},{20,... | collective-permute-start | bytes 786440 | tf_op jit(solution)/shard_map/ppermute | solution.py:35
  32.8 26.7 %collective-permute-start.11 = (bf16[2,1040,256]{2,1,0:T(8,128)(2,1)}, bf16[2,1040,256]{2,1,0:T(8,128)(2,1)S(1)}, u32[]{:S(2)}, u32[]{:S(2)}) collective-permute-start(bf16[2,1040,256]{2,1,0:T(8,128)(2,1)} %get-tuple-element.33), channel_id=1, source_target_pairs={{0,1},{1,0},{2,3},{3,2},{4,5},{5,4},{6,7},{7,6},{8,9},{9,8},{10,11... | collective-permute-start | bytes 3194888 | tf_op jit(solution)/shard_map/ppermute | solution.py:40
  39.2 11.9 %collective-permute-start.6 = (bf16[2,256,512]{2,1,0:T(8,128)(2,1)S(1)}, bf16[2,256,512]{2,1,0:T(8,128)(2,1)S(1)}, u32[]{:S(2)}, u32[]{:S(2)}) collective-permute-start(bf16[2,256,512]{2,1,0:T(8,128)(2,1)S(1)} %pad_maximum_fusion.6), channel_id=1, source_target_pairs={{0,4},{4,0},{2,6},{6,2},{8,12},{12,8},{10,14},{14,10},{16,20},{20,... | collective-permute-start | bytes 1572872 | tf_op jit(solution)/shard_map/ppermute | solution.py:35
  39.9 20.8 %collective-permute-start.8 = (bf16[4,256,512]{2,1,0:T(8,128)(2,1)S(1)}, bf16[4,256,512]{2,1,0:T(8,128)(2,1)}, u32[]{:S(2)}, u32[]{:S(2)}) collective-permute-start(bf16[4,256,512]{2,1,0:T(8,128)(2,1)S(1)} %pad_maximum_fusion.5.refs_0_), channel_id=1, source_target_pairs={{0,2},{2,0},{4,6},{6,4},{8,10},{10,8},{12,14},{14,12},{16,18},{18,... | collective-permute-start | bytes 3145736 | tf_op jit(solution)/shard_map/ppermute | solution.py:35
  51.1 27.3 %collective-permute-start.7 = (bf16[4,256,512]{2,1,0:T(8,128)(2,1)S(1)}, bf16[4,256,512]{2,1,0:T(8,128)(2,1)S(1)}, u32[]{:S(2)}, u32[]{:S(2)}) collective-permute-start(bf16[4,256,512]{2,1,0:T(8,128)(2,1)S(1)} %constant_dynamic-update-slice_fusion.refs_0_), channel_id=1, source_target_pairs={{0,2},{2,0},{4,6},{6,4},{8,10},{10,8},{12,14},{14,12},{16,18},{18,... | collective-permute-start | bytes 3145736 | tf_op jit(solution)/shard_map/ppermute | solution.py:35
  60.7 12.5 %slice-start = ((s8[16777216]{0:T(1024)(128)(4,1)}), s8[4194304]{0:T(1024)(128)(4,1)S(1)}, s32[]{:S(2)}) async-start(s8[16777216]{0:T(1024)(128)(4,1)} %bitcast.50), calls=%async_computation | async-start | bytes 8388608
  62.8 10.4 %slice-start.1 = ((s8[16777216]{0:T(1024)(128)(4,1)}), s8[4194304]{0:T(1024)(128)(4,1)S(1)}, s32[]{:S(2)}) async-start(s8[16777216]{0:T(1024)(128)(4,1)} %bitcast.50), calls=%async_computation.1 | async-start | bytes 8388608
  64.1 9.1 %slice-start.2 = ((s8[16777216]{0:T(1024)(128)(4,1)}), s8[4194304]{0:T(1024)(128)(4,1)S(1)}, s32[]{:S(2)}) async-start(s8[16777216]{0:T(1024)(128)(4,1)} %bitcast.50), calls=%async_computation.2 | async-start | bytes 8388608
  64.1 9.1 %slice-start.3 = ((s8[16777216]{0:T(1024)(128)(4,1)}), s8[4194304]{0:T(1024)(128)(4,1)S(1)}, s32[]{:S(2)}) async-start(s8[16777216]{0:T(1024)(128)(4,1)} %bitcast.50), calls=%async_computation.3 | async-start | bytes 8388608
  64.1 9.1 %collective-permute-start.9 = (bf16[256,272]{1,0:T(8,128)(2,1)S(1)}, bf16[256,272]{1,0:T(8,128)(2,1)S(1)}, u32[]{:S(2)}, u32[]{:S(2)}) collective-permute-start(bf16[256,272]{1,0:T(8,128)(2,1)S(1)} %fusion.8), channel_id=1, source_target_pairs={{0,1},{1,0},{2,3},{3,2},{4,5},{5,4},{6,7},{7,6},{8,9},{9,8},{10,11... | collective-permute-start | bytes 417800 | tf_op jit(solution)/shard_map/ppermute | solution.py:40
  73.2 21.3 %collective-permute-start.10 = (bf16[256,1024]{1,0:T(8,128)(2,1)}, bf16[256,1024]{1,0:T(8,128)(2,1)}, u32[]{:S(2)}, u32[]{:S(2)}) collective-permute-start(bf16[256,1024]{1,0:T(8,128)(2,1)} %fusion.7), channel_id=1, source_target_pairs={{0,1},{1,0},{2,3},{3,2},{4,5},{5,4},{6,7},{7,6},{8,9},{9,8},{10,11... | collective-permute-start | bytes 1572872 | tf_op jit(solution)/shard_map/ppermute | solution.py:40
  76.4 25.7 %collective-permute-start.13 = (bf16[256,1024]{1,0:T(8,128)(2,1)}, bf16[256,1024]{1,0:T(8,128)(2,1)}, u32[]{:S(2)}, u32[]{:S(2)}) collective-permute-start(bf16[256,1024]{1,0:T(8,128)(2,1)} %fusion.6), channel_id=1, source_target_pairs={{0,1},{1,0},{2,3},{3,2},{4,5},{5,4},{6,7},{7,6},{8,9},{9,8},{10,11... | collective-permute-start | bytes 1572872 | tf_op jit(solution)/shard_map/ppermute | solution.py:40
  88.2 6.1 %collective-permute-start.12 = (bf16[256,256]{1,0:T(8,128)(2,1)S(1)}, bf16[256,256]{1,0:T(8,128)(2,1)S(1)}, u32[]{:S(2)}, u32[]{:S(2)}) collective-permute-start(bf16[256,256]{1,0:T(8,128)(2,1)S(1)} %get-tuple-element.49), channel_id=1, source_target_pairs={{0,2},{2,0},{4,6},{6,4},{8,10},{10,8},{12,14},{14,12},{16,18},{18,... | collective-permute-start | bytes 393224 | tf_op jit(solution)/shard_map/ppermute | solution.py:35
  103.6 1.2 %collective-permute-start.14 = (f32[256]{0:T(256)S(1)}, f32[256]{0:T(256)S(1)}, u32[]{:S(2)}, u32[]{:S(2)}) collective-permute-start(f32[256]{0:T(256)S(1)} %get-tuple-element.64), channel_id=1, source_target_pairs={{0,2},{2,0},{4,6},{6,4},{8,10},{10,8},{12,14},{14,12},{16,18},{18,... | collective-permute-start | bytes 3080 | tf_op jit(solution)/shard_map/ppermute | solution.py:35
  (20 other events, 80.5 us)

commit v7 on v6

--- a/solution.py
+++ b/solution.py
@@ -467,13 +467,6 @@
     flags = (live[:, None] & (came_from[:, None] == jnp.arange(req_count)[None, :])).astype(
         jnp.int32
     )
-    cache = conv_of(own_slots)
-    for step in range(1, req_count):
-        got = got_states[step - 1][:, heads * head_width :].reshape(group_reqs, -1)
-        got = got[:, :conv_size].reshape(cache.shape)
-        cache = jnp.where((came_from == step)[:, None, None], got, cache)
-    cache = jnp.where(live[:, None, None], cache, 0).astype(F32)
-
     if direct:
         both = partner_2(after(along_z, packed, w_step), "wide", 1)
         own_block = after(own_block, packed)
@@ -481,9 +474,8 @@
         four = jnp.stack([block, along_z, along_x, both])
         other = partner_2(four, "wide", 0)
         own_pair = after(jnp.stack([own_block, own_z]), four)
-        own_four = jnp.concatenate([own_pair, partner_2(own_pair, "wide", 1)], 0)
-        own_other = partner_2(own_four, "wide", 0)
-        features = [(own_four, own_other), quad_arrange(four, other)]
+        own_got = partner_2(own_pair, "wide", 1)
+        features = [own_got, quad_arrange(four, other)]
     else:
         features = features_in_general(x_in)
     weights = {
@@ -496,21 +488,33 @@
         return jnp.dot(block, weights[name], preferred_element_type=F32)
 
     came = {"map": [], "xr": [], "z": []}
-    done = []
+    done, parts = [], {}
     for step in range(1, req_count):
         block = features[step]
         for name in came:
             if name == "z":
-                block = after(block, came["map"][-1])
+                block = after(block, came["map"][-1], got_states[step - 1])
             part, block = lax.optimization_barrier((project(block, name).astype(BF16), block))
             came[name].append(shift_req(part, step))
+            parts[name] = part
             done.append(part)
-    block = after(features[0], *done)
+    block = features[0]
     if direct:
-        block = quad_arrange(*block)
+        own_four = jnp.concatenate([own_pair, after(block, parts["xr"])], 0)
+        own_other = partner_2(own_four, "wide", 0)
+        block = quad_arrange(own_four, after(own_other, *done))
+    else:
+        block = after(block, *done)
     own = {}
     for name in came:
         own[name], block = lax.optimization_barrier((project(block, name), block))
+
+    cache = conv_of(own_slots)
+    for step in range(1, req_count):
+        got = after(got_states[step - 1], parts["xr"])[:, heads * head_width :].reshape(group_reqs, -1)
+        got = got[:, :conv_size].reshape(cache.shape)
+        cache = jnp.where((came_from == step)[:, None, None], got, cache)
+    cache = jnp.where(live[:, None, None], cache, 0).astype(F32)
 
     bc_conv, cum, cum_t, step_t, coef, decay = prep(
         stretch_start, own["map"], came["map"], cache[:, :, local_width:], conv_bc_w, conv_bc_b,
@@ -527,8 +531,9 @@
             upper_half, jnp.concatenate([partner, joined], 1), jnp.concatenate([joined, partner], 1)
         )
     state_width = joined.shape[1] // 2
+    came_xr = [after(got, own["xr"], bc_conv) for got in came["xr"]]
     result, final_state = mixer(
-        flags, stretch_start[0], own["xr"], came["xr"], cache[:, :, :local_width],
+        flags, stretch_start[0], own["xr"], came_xr, cache[:, :, :local_width],
         conv_x_w, conv_x_b, joined[:, :state_width], joined[:, state_width:], cum, cum_t,
         step_t, coef, decay, d_skip, held, got_states
     )

time: 106 us -> 110 us (1.038)
  matrix products: 22.4 us -> 29.4 us
  local copies, waits for them, and re-layouts: 23.5 us -> 19.8 us
  starting transfers between devices: 18.5 us -> 19.7 us
    dot_general x6, matrix products: 22.4 us -> 29.4 us  [project(): return jnp.dot(block, weights[name], preferred_element_type=F32)]
    unnamed x64 -> x56, local copies, waits for them, and re-layouts: 21.7 us -> 18.1 us
    ppermute x9, waiting for transfers between devices: 13.4 us -> 11.7 us  [partner_2(): return lax.ppermute(block, axis, route)]
    ppermute x4, waiting for transfers between devices: 8.33 us -> 9.61 us  [shift_req(): lax.ppermute(block, 'req', [(i, (i + step) % count) for i in range(count)])]
  transfers between devices with their start and end apart: 15 -> 15, of which waited for: 5 -> 5; matrix products, arithmetic and copies ran while one was open for 39% -> 44% of each run, Pallas kernels for 14% -> 13%
where the time goes in v7:
time: 110 us
  matrix products  29.4 us (27%)
  waiting for transfers between devices  21.3 us (19%)
  local copies, waits for them, and re-layouts  19.8 us (18%)
  starting transfers between devices  19.7 us (18%)
  Pallas kernels  14.7 us (13%)
  other arithmetic  3.48 us (3%)
  between operations  1.18 us (1%)
    dot_general x6, matrix products, project(): return jnp.dot(block, weights[name], preferred_element_type=F32)  29.4 us
    unnamed x56, local copies, waits for them, and re-layouts  18.1 us
    ppermute x9, waiting for transfers between devices, partner_2(): return lax.ppermute(block, axis, route)  11.7 us
    ppermute x4, waiting for transfers between devices, shift_req(): lax.ppermute(block, 'req', [(i, (i + step) % count) for i in range(count)])  9.61 us
    ppermute x4, starting transfers between devices, shift_req(): lax.ppermute(block, 'req', [(i, (i + step) % count) for i in range(count)])  9.45 us
    pallas_call x1, Pallas kernels, mixer(): pl.pallas_call(functools.partial(mixer_kernel, count_req, len(got)), out_...  7.64 us
    ppermute x9, starting transfers between devices, partner_2(): return lax.ppermute(block, axis, route)  5.5 us
    ppermute x1, starting transfers between devices, near_blocks(): first = lax.ppermute(x_in, axes, first)  4.09 us
  transfers between devices with their start and end apart: 15, of which 5 were waited for; matrix products, arithmetic and copies ran while one was open for 44% of the time, Pallas kernels for 13%

profile of v7, /device:TPU:0, one launch (start us, length us, event | category | flops | bytes accessed | tf_op | source)
XLA Modules:
  0.0 109.6 jit_solution(13876108605210301958)
XLA Ops:
  0.6 4.1 %collective-permute-start = (bf16[256,512]{1,0:T(8,128)(2,1)}, bf16[256,512]{1,0:T(8,128)(2,1)S(1)}, u32[]{:S(2)}, u32[]{:S(2)}) collective-permute-start(bf16[256,512]{1,0:T(8,128)(2,1)} %param.20), channel_id=1, source_target_pairs={{0,16},{1,0},{2,18},{3,2},{4,20},{5,4},{6,22},{7,6},{8,24},{9,8},{... | collective-permute-start | bytes 786440 | tf_op jit(solution)/shard_map/ppermute | solution.py:90
  5.5 16.5 %copy.44 = bf16[4096,2,1024]{2,0,1:T(8,128)(2,1)} copy(bf16[4096,2,1024]{2,1,0:T(2,128)(2,1)} %param.21) | data formatting | bytes 33554432 | tf_op args[1]
  22.4 1.6 %collective-permute-start.3 = (bf16[256,512]{1,0:T(8,128)(2,1)S(1)}, bf16[256,512]{1,0:T(8,128)(2,1)S(1)}, u32[]{:S(2)}, u32[]{:S(2)}) collective-permute-start(bf16[256,512]{1,0:T(8,128)(2,1)S(1)} %get-tuple-element.33), channel_id=1, source_target_pairs={{0,8},{8,0},{2,10},{10,2},{4,12},{12,4},{6,14},{14,6},{16,24},{24,... | collective-permute-start | bytes 786440 | tf_op jit(solution)/shard_map/ppermute | solution.py:35
  24.2 1.6 %collective-permute-start.4 = (bf16[256,512]{1,0:T(8,128)(2,1)S(1)}, bf16[256,512]{1,0:T(8,128)(2,1)S(1)}, u32[]{:S(2)}, u32[]{:S(2)}) collective-permute-start(bf16[256,512]{1,0:T(8,128)(2,1)S(1)} %get-tuple-element.33), channel_id=1, source_target_pairs={{0,4},{4,0},{2,6},{6,2},{8,12},{12,8},{10,14},{14,10},{16,20},{20,... | collective-permute-start | bytes 786440 | tf_op jit(solution)/shard_map/ppermute | solution.py:35
  25.8 1.3 %copy.35 = bf16[4096,16]{1,0:T(8,128)(2,1)} copy(bf16[4096,16]{0,1:T(8,128)(2,1)S(1)} %copy-done.15) | data formatting | bytes 262144 | tf_op jit(solution)/shard_map/optimization_barrier | solution.py:84
  27.1 2.9 %shard_map.203 = (bf16[2,1040,256]{2,1,0:T(8,128)(2,1)S(1)}, f32[2,16,64,256]{3,2,1,0:T(8,128)S(1)}) custom-call(s32[2]{0:T(128)S(1)} %get-tuple-element.77.slots_ref, s32[2]{0:T(128)S(1)} %get-tuple-element.76.own_slots_ref, f32[8,16,64,256]{3,2,1,0:T(8,128)} %own_pool_ref.1, f32[8,16,64,256]{3,2,1,0:T(8,128)} %own_pool_ref.1, bf16[2,16,256]{2,1,0:T(8,128)(2,1)S(1)} %bitcast.42), custom_call_target="tpu_custom_call" | custom-call | bytes 7340032 | tf_op jit(solution)/shard_map/pallas_call | solution.py:232
  30.0 1.3 %copy-done = f32[2,16,64,256]{3,2,1,0:T(8,128)} copy-done((f32[2,16,64,256]{3,2,1,0:T(8,128)}, f32[2,16,64,256]{3,2,1,0:T(8,128)S(1)}, u32[]{:S(2)}) %copy-start) | copy-done | bytes 2097176
  31.9 6.7 %collective-permute-done.5 = bf16[256,512]{1,0:T(8,128)(2,1)S(1)} collective-permute-done((bf16[256,512]{1,0:T(8,128)(2,1)S(1)}, bf16[256,512]{1,0:T(8,128)(2,1)S(1)}, u32[]{:S(2)}, u32[]{:S(2)}) %collective-permute-start.5) | collective-permute-done | bytes 262176 | tf_op jit(solution)/shard_map/ppermute | solution.py:35
  39.7 3.7 %collective-permute-start.10 = (bf16[2,1040,256]{2,1,0:T(8,128)(2,1)}, bf16[2,1040,256]{2,1,0:T(8,128)(2,1)S(1)}, u32[]{:S(2)}, u32[]{:S(2)}) collective-permute-start(bf16[2,1040,256]{2,1,0:T(8,128)(2,1)} %copy-done.11), channel_id=1, source_target_pairs={{0,1},{1,0},{2,3},{3,2},{4,5},{5,4},{6,7},{7,6},{8,9},{9,8},{10,11... | collective-permute-start | bytes 3194888 | tf_op jit(solution)/shard_map/ppermute | solution.py:40
  43.3 4.2 %collective-permute-done.2 = bf16[256,512]{1,0:T(8,128)(2,1)S(1)} collective-permute-done((bf16[256,512]{1,0:T(8,128)(2,1)S(1)}, bf16[256,512]{1,0:T(8,128)(2,1)S(1)}, u32[]{:S(2)}, u32[]{:S(2)}) %collective-permute-start.2) | collective-permute-done | bytes 262176 | tf_op jit(solution)/shard_map/ppermute | solution.py:35
  48.3 1.6 %shard_map.204 = bf16[256,4096]{1,0:T(8,128)(2,1)S(1)} custom-call(s32[8]{0:T(128)S(1)} %broadcast_xor_fusion.places_ref, bf16[4,256,512]{2,1,0:T(8,128)(2,1)S(1)} %pad_maximum_fusion.5.refs_0_, bf16[4,256,512]{2,1,0:T(8,128)(2,1)} %collective-permute-done.7.refs_1_), custom_call_target="tpu_custom_call" | custom-call | flops 1000000 | bytes 10000 | tf_op jit(solution)/shard_map/pallas_call | solution.py:72
  49.9 1.9 %fusion.8 = bf16[256,272]{1,0:T(8,128)(2,1)} fusion(bf16[256,4096]{1,0:T(8,128)(2,1)S(1)} %shard_map.204, bf16[4096,16]{1,0:T(8,128)(2,1)S(1)} %copy-done.12, bf16[4096,256]{1,0:T(8,128)(2,1)S(1)} %copy-done.21), kind=kOutput, calls=%fused_computation.14 | convolution fusion | flops 574951424 | bytes 4464640 | tf_op jit(solution)/shard_map/dot_general | solution.py:488
  51.9 6.6 %fusion.7 = bf16[256,1024]{1,0:T(8,128)(2,1)} fusion(bf16[256,4096]{1,0:T(8,128)(2,1)S(1)} %shard_map.204, bf16[2,4096,1024]{2,1,0:T(8,128)(2,1)} %bitcast.48), kind=kOutput, calls=%fused_computation.13 | convolution fusion | flops 2147745792 | bytes 11010048 | tf_op jit(solution)/shard_map/dot_general | solution.py:488
  58.4 3.7 %collective-permute-start.9 = (bf16[256,272]{1,0:T(8,128)(2,1)}, bf16[256,272]{1,0:T(8,128)(2,1)S(1)}, u32[]{:S(2)}, u32[]{:S(2)}) collective-permute-start(bf16[256,272]{1,0:T(8,128)(2,1)} %fusion.8), channel_id=1, source_target_pairs={{0,1},{1,0},{2,3},{3,2},{4,5},{5,4},{6,7},{7,6},{8,9},{9,8},{10,11... | collective-permute-start | bytes 417800 | tf_op jit(solution)/shard_map/ppermute | solution.py:40
  62.3 5.6 %collective-permute-done.10.refs_14_ = bf16[2,1040,256]{2,1,0:T(8,128)(2,1)S(1)} collective-permute-done((bf16[2,1040,256]{2,1,0:T(8,128)(2,1)}, bf16[2,1040,256]{2,1,0:T(8,128)(2,1)S(1)}, u32[]{:S(2)}, u32[]{:S(2)}) %collective-permute-start.10) | collective-permute-done | bytes 1064992 | tf_op jit(solution)/shard_map/ppermute | solution.py:40
  68.0 4.0 %collective-permute-done.9.refs_0_ = bf16[256,272]{1,0:T(8,128)(2,1)S(1)} collective-permute-done((bf16[256,272]{1,0:T(8,128)(2,1)}, bf16[256,272]{1,0:T(8,128)(2,1)S(1)}, u32[]{:S(2)}, u32[]{:S(2)}) %collective-permute-start.9) | collective-permute-done | bytes 139296 | tf_op jit(solution)/shard_map/ppermute | solution.py:40
  72.1 7.2 %fusion.6 = bf16[256,1024]{1,0:T(8,128)(2,1)} fusion(bf16[256,4096]{1,0:T(8,128)(2,1)} %copy-done.2, bf16[2,4096,1024]{2,1,0:T(8,128)(2,1)} %bitcast.49), kind=kOutput, calls=%fused_computation.12 | convolution fusion | flops 2147745792 | bytes 11010048 | tf_op jit(solution)/shard_map/dot_general | solution.py:488
  79.2 2.1 %collective-permute-start.13 = (bf16[256,1024]{1,0:T(8,128)(2,1)}, bf16[256,1024]{1,0:T(8,128)(2,1)}, u32[]{:S(2)}, u32[]{:S(2)}) collective-permute-start(bf16[256,1024]{1,0:T(8,128)(2,1)} %fusion.6), channel_id=1, source_target_pairs={{0,1},{1,0},{2,3},{3,2},{4,5},{5,4},{6,7},{7,6},{8,9},{9,8},{10,11... | collective-permute-start | bytes 1572872 | tf_op jit(solution)/shard_map/ppermute | solution.py:40
  82.0 1.3 %fusion.4 = f32[256,272]{0,1:T(8,128)S(1)} fusion(bf16[256,4096]{1,0:T(8,128)(2,1)S(1)} %shard_map.205, bf16[4096,16]{1,0:T(8,128)(2,1)S(1)} %copy-done.13, bf16[4096,256]{1,0:T(8,128)(2,1)S(1)} %copy-done.22), kind=kOutput, calls=%fused_computation.8 | convolution fusion | flops 574881792 | bytes 4603904 | tf_op jit(solution)/shard_map/dot_general | solution.py:488
  83.4 5.8 %fusion.refs_0_ = f32[256,1024]{1,0:T(8,128)S(1)} fusion(bf16[256,4096]{1,0:T(8,128)(2,1)S(1)} %shard_map.205, bf16[2,4096,1024]{2,1,0:T(8,128)(2,1)} %bitcast.50), kind=kOutput, calls=%fused_computation.3 | convolution fusion | flops 2147483648 | bytes 11534336 | tf_op jit(solution)/shard_map/dot_general | solution.py:488
  89.4 1.8 %shard_map.206 = (bf16[256,256]{1,0:T(8,128)(2,1)S(1)}, f32[4,256,4]{2,1,0:T(8,128)S(1)}, f32[4,4,256]{2,1,0:T(4,128)S(1)}, f32[4,4,256]{2,1,0:T(4,128)S(1)}, f3...) custom-call(s32[1,2]{1,0:T(1,128)S(1)} %copy-done.7, f32[256,272]{1,0:T(8,128)S(1)} %copy.37.own_ref, ...), custom_call_target="tpu_custom_call" | custom-call | flops 1000000 | bytes 10000 | tf_op jit(solution)/shard_map/pallas_call | solution.py:204
  91.4 6.7 %fusion.2 = f32[256,1024]{1,0:T(8,128)S(1)} fusion(bf16[256,4096]{1,0:T(8,128)(2,1)} %copy-done.3, bf16[2,4096,1024]{2,1,0:T(8,128)(2,1)} %bitcast.51), kind=kOutput, calls=%fused_computation.5 | convolution fusion | flops 2147483648 | bytes 11534336 | tf_op jit(solution)/shard_map/dot_general | solution.py:488
  98.2 7.6 %shard_map.207 = (f32[256,1024]{1,0:T(8,128)S(1)}, f32[2,16,64,256]{3,2,1,0:T(8,128)}) custom-call(s32[2,2]{1,0:T(2,128)S(1)} %and_convert_fusion.flags_ref, s32[2]{0:T(128)S(1)} %bitcast.44, f32[256,1024]{1,0:T(8,128)S(1)} %fusion.refs_0_, bf16[256,1024]{1,0:T(8,128)(2,1)} %collective-permute-done.11.refs_1_, f32[2,3,1024]{2,1,0:T(4,128)S(1)} %slice.36.refs_2_, ...), custom_call_target="tpu_custom_call" | custom-call | flops 1000000 | bytes 10000 | tf_op jit(solution)/shard_map/pallas_call | solution.py:368
  105.9 1.5 %multiply_reduce_fusion = (f32[256]{0:T(256)S(1)}, f32[256,1024]{1,0:T(8,128)S(1)}) fusion(f32[256,1024]{1,0:T(8,128)S(1)} %get-tuple-element.60, f32[256,1024]{1,0:T(8,128)S(1)} %fusion.2, bf16[256,1024]{1,0:T(8,128)(2,1)} %collective-permute-done.13), kind=kLoop, calls=%fused_computation.21 | loop fusion | flops 2883328 | bytes 3671040 | tf_op jit(solution)/shard_map/reduce_sum | solution.py:544
  (101 shorter events, 7.2 us)
Async XLA Ops:
  0.6 21.7 %collective-permute-start = (bf16[256,512]{1,0:T(8,128)(2,1)}, bf16[256,512]{1,0:T(8,128)(2,1)S(1)}, u32[]{:S(2)}, u32[]{:S(2)}) collective-permute-start(bf16[256,512]{1,0:T(8,128)(2,1)} %param.20), channel_id=1, source_target_pairs={{0,16},{1,0},{2,18},{3,2},{4,20},{5,4},{6,22},{7,6},{8,24},{9,8},{... | collective-permute-start | bytes 786440 | tf_op jit(solution)/shard_map/ppermute | solution.py:90
  4.7 17.6 %collective-permute-start.1 = (bf16[256,512]{1,0:T(8,128)(2,1)}, bf16[256,512]{1,0:T(8,128)(2,1)S(1)}, u32[]{:S(2)}, u32[]{:S(2)}) collective-permute-start(bf16[256,512]{1,0:T(8,128)(2,1)} %param.20), channel_id=1, source_target_pairs={{1,16},{3,18},{5,20},{7,22},{9,24},{11,26},{13,28},{15,30},{16,1},... | collective-permute-start | bytes 786440 | tf_op jit(solution)/shard_map/ppermute | solution.py:91
  5.4 16.5 %copy-start.18 = (s32[4]{0:T(128)S(1)}, s32[4]{0:T(128)}, u32[]{:S(2)}) copy-start(s32[4]{0:T(128)} %param.34) | copy-start | bytes 52
  5.4 16.7 %copy-start.16 = (bf16[8,3,1024]{2,0,1:T(8,128)(2,1)S(1)}, bf16[8,3,1024]{2,0,1:T(8,128)(2,1)}, u32[]{:S(2)}) copy-start(bf16[8,3,1024]{2,0,1:T(8,128)(2,1)} %param.36) | copy-start | bytes 147460
  5.4 16.9 %copy-start.14 = (bf16[256,512]{1,0:T(8,128)(2,1)S(1)}, bf16[256,512]{1,0:T(8,128)(2,1)}, u32[]{:S(2)}) copy-start(bf16[256,512]{1,0:T(8,128)(2,1)} %param.20) | copy-start | bytes 786436
  5.5 18.6 %copy-start.17 = (bf16[8,3,256]{2,0,1:T(8,128)(2,1)S(1)}, bf16[8,3,256]{2,0,1:T(8,128)(2,1)}, u32[]{:S(2)}) copy-start(bf16[8,3,256]{2,0,1:T(8,128)(2,1)} %param.37) | copy-start | bytes 36868
  5.5 20.3 %copy-start.15 = (bf16[4096,16]{0,1:T(8,128)(2,1)S(1)}, bf16[4096,16]{0,1:T(8,128)(2,1)}, u32[]{:S(2)}) copy-start(bf16[4096,16]{0,1:T(8,128)(2,1)} %param.22) | copy-start | bytes 393220
  22.4 9.0 %collective-permute-start.3 = (bf16[256,512]{1,0:T(8,128)(2,1)S(1)}, bf16[256,512]{1,0:T(8,128)(2,1)S(1)}, u32[]{:S(2)}, u32[]{:S(2)}) collective-permute-start(bf16[256,512]{1,0:T(8,128)(2,1)S(1)} %get-tuple-element.33), channel_id=1, source_target_pairs={{0,8},{8,0},{2,10},{10,2},{4,12},{12,4},{6,14},{14,6},{16,24},{24,... | collective-permute-start | bytes 786440 | tf_op jit(solution)/shard_map/ppermute | solution.py:35
  24.2 7.7 %collective-permute-start.4 = (bf16[256,512]{1,0:T(8,128)(2,1)S(1)}, bf16[256,512]{1,0:T(8,128)(2,1)S(1)}, u32[]{:S(2)}, u32[]{:S(2)}) collective-permute-start(bf16[256,512]{1,0:T(8,128)(2,1)S(1)} %get-tuple-element.33), channel_id=1, source_target_pairs={{0,4},{4,0},{2,6},{6,2},{8,12},{12,8},{10,14},{14,10},{16,20},{20,... | collective-permute-start | bytes 786440 | tf_op jit(solution)/shard_map/ppermute | solution.py:35
  27.1 11.7 %copy-start.23 = (s32[2]{0:T(128)S(1)}, s32[2]{0:T(128)}, u32[]{:S(2)}) copy-start(s32[2]{0:T(128)} %param.33) | copy-start | bytes 28
  27.1 11.7 %copy-start.24 = (s32[8]{0:T(128)S(1)}, s32[8]{0:T(128)}, u32[]{:S(2)}) copy-start(s32[8]{0:T(128)} %constant.99.clone) | copy-start | bytes 100
  27.1 12.3 %copy-start.20 = (f32[16]{0:T(128)S(1)}, f32[16]{0:T(128)}, u32[]{:S(2)}) copy-start(f32[16]{0:T(128)} %param.26) | copy-start | bytes 196
  31.3 7.2 %copy-start.11 = (bf16[2,1040,256]{2,1,0:T(8,128)(2,1)}, bf16[2,1040,256]{2,1,0:T(8,128)(2,1)S(1)}, u32[]{:S(2)}) copy-start(bf16[2,1040,256]{2,1,0:T(8,128)(2,1)S(1)} %get-tuple-element.35) | copy-start | bytes 3194884
  31.3 7.2 %collective-permute-start.5 = (bf16[256,512]{1,0:T(8,128)(2,1)S(1)}, bf16[256,512]{1,0:T(8,128)(2,1)S(1)}, u32[]{:S(2)}, u32[]{:S(2)}) collective-permute-start(bf16[256,512]{1,0:T(8,128)(2,1)S(1)} %collective-permute-done.3), channel_id=1, source_target_pairs={{0,4},{4,0},{2,6},{6,2},{8,12},{12,8},{10,14},{14,10},{16,20},{20,... | collective-permute-start | bytes 786440 | tf_op jit(solution)/shard_map/ppermute | solution.py:35
  38.7 9.6 %collective-permute-start.7 = (bf16[4,256,512]{2,1,0:T(8,128)(2,1)S(1)}, bf16[4,256,512]{2,1,0:T(8,128)(2,1)}, u32[]{:S(2)}, u32[]{:S(2)}) collective-permute-start(bf16[4,256,512]{2,1,0:T(8,128)(2,1)S(1)} %pad_maximum_fusion.5.refs_0_), channel_id=1, source_target_pairs={{0,2},{2,0},{4,6},{6,4},{8,10},{10,8},{12,14},{14,12},{16,18},{18,... | collective-permute-start | bytes 3145736 | tf_op jit(solution)/shard_map/ppermute | solution.py:35
  38.8 8.7 %collective-permute-start.2 = (bf16[256,512]{1,0:T(8,128)(2,1)S(1)}, bf16[256,512]{1,0:T(8,128)(2,1)S(1)}, u32[]{:S(2)}, u32[]{:S(2)}) collective-permute-start(bf16[256,512]{1,0:T(8,128)(2,1)S(1)} %get-tuple-element.36), channel_id=1, source_target_pairs={{0,8},{8,0},{2,10},{10,2},{4,12},{12,4},{6,14},{14,6},{16,24},{24,... | collective-permute-start | bytes 786440 | tf_op jit(solution)/shard_map/ppermute | solution.py:35
  39.7 28.2 %collective-permute-start.10 = (bf16[2,1040,256]{2,1,0:T(8,128)(2,1)}, bf16[2,1040,256]{2,1,0:T(8,128)(2,1)S(1)}, u32[]{:S(2)}, u32[]{:S(2)}) collective-permute-start(bf16[2,1040,256]{2,1,0:T(8,128)(2,1)} %copy-done.11), channel_id=1, source_target_pairs={{0,1},{1,0},{2,3},{3,2},{4,5},{5,4},{6,7},{7,6},{8,9},{9,8},{10,11... | collective-permute-start | bytes 3194888 | tf_op jit(solution)/shard_map/ppermute | solution.py:40
  47.6 14.5 %collective-permute-start.6 = (bf16[2,256,512]{2,1,0:T(8,128)(2,1)S(1)}, bf16[2,256,512]{2,1,0:T(8,128)(2,1)S(1)}, u32[]{:S(2)}, u32[]{:S(2)}) collective-permute-start(bf16[2,256,512]{2,1,0:T(8,128)(2,1)S(1)} %pad_maximum_fusion.6), channel_id=1, source_target_pairs={{0,4},{4,0},{2,6},{6,2},{8,12},{12,8},{10,14},{14,10},{16,20},{20,... | collective-permute-start | bytes 1572872 | tf_op jit(solution)/shard_map/ppermute | solution.py:35
  58.4 13.6 %collective-permute-start.9 = (bf16[256,272]{1,0:T(8,128)(2,1)}, bf16[256,272]{1,0:T(8,128)(2,1)S(1)}, u32[]{:S(2)}, u32[]{:S(2)}) collective-permute-start(bf16[256,272]{1,0:T(8,128)(2,1)} %fusion.8), channel_id=1, source_target_pairs={{0,1},{1,0},{2,3},{3,2},{4,5},{5,4},{6,7},{7,6},{8,9},{9,8},{10,11... | collective-permute-start | bytes 417800 | tf_op jit(solution)/shard_map/ppermute | solution.py:40
  62.1 35.9 %collective-permute-start.11 = (bf16[256,1024]{1,0:T(8,128)(2,1)}, bf16[256,1024]{1,0:T(8,128)(2,1)}, u32[]{:S(2)}, u32[]{:S(2)}) collective-permute-start(bf16[256,1024]{1,0:T(8,128)(2,1)} %fusion.7), channel_id=1, source_target_pairs={{0,1},{1,0},{2,3},{3,2},{4,5},{5,4},{6,7},{7,6},{8,9},{9,8},{10,11... | collective-permute-start | bytes 1572872 | tf_op jit(solution)/shard_map/ppermute | solution.py:40
  62.2 19.1 %collective-permute-start.8 = (bf16[4,256,512]{2,1,0:T(8,128)(2,1)S(1)}, bf16[4,256,512]{2,1,0:T(8,128)(2,1)S(1)}, u32[]{:S(2)}, u32[]{:S(2)}) collective-permute-start(bf16[4,256,512]{2,1,0:T(8,128)(2,1)S(1)} %constant_dynamic-update-slice_fusion.refs_0_), channel_id=1, source_target_pairs={{0,2},{2,0},{4,6},{6,4},{8,10},{10,8},{12,14},{14,12},{16,18},{18,... | collective-permute-start | bytes 3145736 | tf_op jit(solution)/shard_map/ppermute | solution.py:35
  79.2 26.6 %collective-permute-start.13 = (bf16[256,1024]{1,0:T(8,128)(2,1)}, bf16[256,1024]{1,0:T(8,128)(2,1)}, u32[]{:S(2)}, u32[]{:S(2)}) collective-permute-start(bf16[256,1024]{1,0:T(8,128)(2,1)} %fusion.6), channel_id=1, source_target_pairs={{0,1},{1,0},{2,3},{3,2},{4,5},{5,4},{6,7},{7,6},{8,9},{9,8},{10,11... | collective-permute-start | bytes 1572872 | tf_op jit(solution)/shard_map/ppermute | solution.py:40
  91.3 6.8 %collective-permute-start.12 = (bf16[256,256]{1,0:T(8,128)(2,1)S(1)}, bf16[256,256]{1,0:T(8,128)(2,1)S(1)}, u32[]{:S(2)}, u32[]{:S(2)}) collective-permute-start(bf16[256,256]{1,0:T(8,128)(2,1)S(1)} %get-tuple-element.52), channel_id=1, source_target_pairs={{0,2},{2,0},{4,6},{6,4},{8,10},{10,8},{12,14},{14,12},{16,18},{18,... | collective-permute-start | bytes 393224 | tf_op jit(solution)/shard_map/ppermute | solution.py:35
  107.4 1.3 %collective-permute-start.14 = (f32[256]{0:T(256)S(1)}, f32[256]{0:T(256)S(1)}, u32[]{:S(2)}, u32[]{:S(2)}) collective-permute-start(f32[256]{0:T(256)S(1)} %get-tuple-element.68), channel_id=1, source_target_pairs={{0,2},{2,0},{4,6},{6,4},{8,10},{10,8},{12,14},{14,12},{16,18},{18,... | collective-permute-start | bytes 3080 | tf_op jit(solution)/shard_map/ppermute | solution.py:35
  (16 other events, 68.7 us)

commit v8 on v7

--- a/solution.py
+++ b/solution.py
@@ -248,7 +248,7 @@
                 pl.BlockSpec(block, lambda j, *_: (j, 0, 0, 0)),
             ],
         ),
-        compiler_params=params(3 * VMEM_BYTES),
+        compiler_params=params(12 * 1024 * 1024),
         cost_estimate=cost(0, 14 * count_req * heads * width * state),
     )(slots, own_slots, pool, pool, conv_rows)
 
@@ -471,7 +471,7 @@
         both = partner_2(after(along_z, packed, w_step), "wide", 1)
         own_block = after(own_block, packed)
         own_z = partner_2(own_block, "wide", 2)
-        four = jnp.stack([block, along_z, along_x, both])
+        four = after(jnp.stack([block, along_z, along_x, both]), own_z)
         other = partner_2(four, "wide", 0)
         own_pair = after(jnp.stack([own_block, own_z]), four)
         own_got = partner_2(own_pair, "wide", 1)
@@ -487,13 +487,11 @@
     def project(block, name):
         return jnp.dot(block, weights[name], preferred_element_type=F32)
 
-    came = {"map": [], "xr": [], "z": []}
+    came = {"xr": [], "map": [], "z": []}
     done, parts = [], {}
     for step in range(1, req_count):
         block = features[step]
         for name in came:
-            if name == "z":
-                block = after(block, came["map"][-1], got_states[step - 1])
             part, block = lax.optimization_barrier((project(block, name).astype(BF16), block))
             came[name].append(shift_req(part, step))
             parts[name] = part
@@ -502,11 +500,11 @@
     if direct:
         own_four = jnp.concatenate([own_pair, after(block, parts["xr"])], 0)
         own_other = partner_2(own_four, "wide", 0)
-        block = quad_arrange(own_four, after(own_other, *done))
+        block = quad_arrange(own_four, after(own_other, *done, *came["map"]))
     else:
         block = after(block, *done)
     own = {}
-    for name in came:
+    for name in ("map", "xr", "z"):
         own[name], block = lax.optimization_barrier((project(block, name), block))
 
     cache = conv_of(own_slots)

time: 110 us -> 106 us (0.964)
  waiting for transfers between devices: 21.3 us -> 16.3 us
  Pallas kernels: 14.7 us -> 12.4 us
  local copies, waits for them, and re-layouts: 19.8 us -> 21.9 us
    ppermute x9, waiting for transfers between devices: 11.7 us -> 6.28 us  [partner_2(): return lax.ppermute(block, axis, route)]
    unnamed x56 -> x58, local copies, waits for them, and re-layouts: 18.1 us -> 20.1 us
    pallas_call x1, Pallas kernels: 2.89 us -> 0.83 us  [pack(): pl.pallas_call(pack_kernel, out_shape=[jax.ShapeDtypeStruct((count_req, h...]
    ppermute x9, starting transfers between devices: 5.5 us -> 7.25 us  [partner_2(): return lax.ppermute(block, axis, route)]
    ppermute x4, starting transfers between devices: 9.45 us -> 7.97 us  [shift_req(): lax.ppermute(block, 'req', [(i, (i + step) % count) for i in range(count)])]
  transfers between devices with their start and end apart: 15 -> 15, of which waited for: 5 -> 4; matrix products, arithmetic and copies ran while one was open for 44% -> 47% of each run, Pallas kernels for 13% -> 12%
where the time goes in v8:
time: 106 us; the launch traced here: 105 us
  matrix products  30.2 us (28%)
  local copies, waits for them, and re-layouts  21.9 us (21%)
  starting transfers between devices  20 us (19%)
  waiting for transfers between devices  16.3 us (15%)
  Pallas kernels  12.4 us (12%)
  other arithmetic  3.48 us (3%)
  between operations  1.18 us (1%)
    dot_general x6, matrix products, project(): return jnp.dot(block, weights[name], preferred_element_type=F32)  30.2 us
    unnamed x58, local copies, waits for them, and re-layouts  20.1 us
    ppermute x4, waiting for transfers between devices, shift_req(): lax.ppermute(block, 'req', [(i, (i + step) % count) for i in range(count)])  10 us
    ppermute x4, starting transfers between devices, shift_req(): lax.ppermute(block, 'req', [(i, (i + step) % count) for i in range(count)])  7.97 us
    pallas_call x1, Pallas kernels, mixer(): pl.pallas_call(functools.partial(mixer_kernel, count_req, len(got)), out_...  7.63 us
    ppermute x9, starting transfers between devices, partner_2(): return lax.ppermute(block, axis, route)  7.25 us
    ppermute x9, waiting for transfers between devices, partner_2(): return lax.ppermute(block, axis, route)  6.28 us
    ppermute x1, starting transfers between devices, near_blocks(): first = lax.ppermute(x_in, axes, first)  4.09 us
  transfers between devices with their start and end apart: 15, of which 4 were waited for; matrix products, arithmetic and copies ran while one was open for 47% of the time, Pallas kernels for 12%

profile of v8, /device:TPU:0, one launch (start us, length us, event | category | flops | bytes accessed | tf_op | source)
XLA Modules:
  0.0 105.4 jit_solution(7295180923625958651)
XLA Ops:
  0.6 4.1 %collective-permute-start = (bf16[256,512]{1,0:T(8,128)(2,1)}, bf16[256,512]{1,0:T(8,128)(2,1)S(1)}, u32[]{:S(2)}, u32[]{:S(2)}) collective-permute-start(bf16[256,512]{1,0:T(8,128)(2,1)} %param.20), channel_id=1, source_target_pairs={{0,16},{1,0},{2,18},{3,2},{4,20},{5,4},{6,22},{7,6},{8,24},{9,8},{... | collective-permute-start | bytes 786440 | tf_op jit(solution)/shard_map/ppermute | solution.py:90
  5.5 16.5 %copy.44 = bf16[4096,2,1024]{2,0,1:T(8,128)(2,1)} copy(bf16[4096,2,1024]{2,1,0:T(2,128)(2,1)} %param.21) | data formatting | bytes 33554432 | tf_op args[1]
  22.4 1.6 %collective-permute-start.3 = (bf16[256,512]{1,0:T(8,128)(2,1)S(1)}, bf16[256,512]{1,0:T(8,128)(2,1)S(1)}, u32[]{:S(2)}, u32[]{:S(2)}) collective-permute-start(bf16[256,512]{1,0:T(8,128)(2,1)S(1)} %get-tuple-element.33), channel_id=1, source_target_pairs={{0,8},{8,0},{2,10},{10,2},{4,12},{12,4},{6,14},{14,6},{16,24},{24,... | collective-permute-start | bytes 786440 | tf_op jit(solution)/shard_map/ppermute | solution.py:35
  24.2 1.6 %collective-permute-start.4 = (bf16[256,512]{1,0:T(8,128)(2,1)S(1)}, bf16[256,512]{1,0:T(8,128)(2,1)S(1)}, u32[]{:S(2)}, u32[]{:S(2)}) collective-permute-start(bf16[256,512]{1,0:T(8,128)(2,1)S(1)} %get-tuple-element.33), channel_id=1, source_target_pairs={{0,4},{4,0},{2,6},{6,2},{8,12},{12,8},{10,14},{14,10},{16,20},{20,... | collective-permute-start | bytes 786440 | tf_op jit(solution)/shard_map/ppermute | solution.py:35
  25.8 1.3 %copy.35 = bf16[4096,16]{1,0:T(8,128)(2,1)} copy(bf16[4096,16]{0,1:T(8,128)(2,1)S(1)} %copy-done.16) | data formatting | bytes 262144 | tf_op jit(solution)/shard_map/optimization_barrier | solution.py:84
  27.1 3.4 %copy-done = f32[8,16,64,256]{3,2,1,0:T(8,128)S(1)} copy-done((f32[8,16,64,256]{3,2,1,0:T(8,128)S(1)}, f32[8,16,64,256]{3,2,1,0:T(8,128)}, u32[]{:S(2)}) %copy-start) | copy-done | bytes 8388632
  31.9 1.3 %collective-permute-start.2 = (bf16[256,512]{1,0:T(8,128)(2,1)S(1)}, bf16[256,512]{1,0:T(8,128)(2,1)S(1)}, u32[]{:S(2)}, u32[]{:S(2)}) collective-permute-start(bf16[256,512]{1,0:T(8,128)(2,1)S(1)} %get-tuple-element.36), channel_id=1, source_target_pairs={{0,8},{8,0},{2,10},{10,2},{4,12},{12,4},{6,14},{14,6},{16,24},{24,... | collective-permute-start | bytes 786440 | tf_op jit(solution)/shard_map/ppermute | solution.py:35
  33.3 5.3 %collective-permute-done.5 = bf16[256,512]{1,0:T(8,128)(2,1)S(1)} collective-permute-done((bf16[256,512]{1,0:T(8,128)(2,1)S(1)}, bf16[256,512]{1,0:T(8,128)(2,1)S(1)}, u32[]{:S(2)}, u32[]{:S(2)}) %collective-permute-start.5) | collective-permute-done | bytes 262176 | tf_op jit(solution)/shard_map/ppermute | solution.py:35
  39.2 3.9 %collective-permute-start.11 = (bf16[2,1040,256]{2,1,0:T(8,128)(2,1)}, bf16[2,1040,256]{2,1,0:T(8,128)(2,1)S(1)}, u32[]{:S(2)}, u32[]{:S(2)}) collective-permute-start(bf16[2,1040,256]{2,1,0:T(8,128)(2,1)} %copy-done.12), channel_id=1, source_target_pairs={{0,1},{1,0},{2,3},{3,2},{4,5},{5,4},{6,7},{7,6},{8,9},{9,8},{10,11... | collective-permute-start | bytes 3194888 | tf_op jit(solution)/shard_map/ppermute | solution.py:40
  43.2 1.5 %collective-permute-start.6 = (bf16[2,256,512]{2,1,0:T(8,128)(2,1)S(1)}, bf16[2,256,512]{2,1,0:T(8,128)(2,1)S(1)}, u32[]{:S(2)}, u32[]{:S(2)}) collective-permute-start(bf16[2,256,512]{2,1,0:T(8,128)(2,1)S(1)} %pad_maximum_fusion.6), channel_id=1, source_target_pairs={{0,4},{4,0},{2,6},{6,2},{8,12},{12,8},{10,14},{14,10},{16,20},{20,... | collective-permute-start | bytes 1572872 | tf_op jit(solution)/shard_map/ppermute | solution.py:35
  44.8 1.4 %shard_map.204 = bf16[256,4096]{1,0:T(8,128)(2,1)S(1)} custom-call(s32[8]{0:T(128)S(1)} %broadcast_xor_fusion.places_ref, bf16[4,256,512]{2,1,0:T(8,128)(2,1)S(1)} %pad_maximum_fusion.5.refs_0_, bf16[4,256,512]{2,1,0:T(8,128)(2,1)} %collective-permute-done.7.refs_1_), custom_call_target="tpu_custom_call" | custom-call | flops 1000000 | bytes 10000 | tf_op jit(solution)/shard_map/pallas_call | solution.py:72
  46.3 7.4 %fusion.7 = bf16[256,1024]{1,0:T(8,128)(2,1)} fusion(bf16[256,4096]{1,0:T(8,128)(2,1)S(1)} %shard_map.204, bf16[2,4096,1024]{2,1,0:T(8,128)(2,1)} %bitcast.48), kind=kOutput, calls=%fused_computation.13 | convolution fusion | flops 2147745792 | bytes 11010048 | tf_op jit(solution)/shard_map/dot_general | solution.py:488
  53.6 1.9 %fusion.8 = bf16[256,272]{1,0:T(8,128)(2,1)} fusion(bf16[256,4096]{1,0:T(8,128)(2,1)S(1)} %shard_map.204, bf16[4096,16]{1,0:T(8,128)(2,1)S(1)} %copy-done.13, bf16[4096,256]{1,0:T(8,128)(2,1)S(1)} %copy-done.22), kind=kOutput, calls=%fused_computation.14 | convolution fusion | flops 574951424 | bytes 4464640 | tf_op jit(solution)/shard_map/dot_general | solution.py:488
  56.3 1.3 %collective-permute-start.10 = (bf16[256,1024]{1,0:T(8,128)(2,1)}, bf16[256,1024]{1,0:T(8,128)(2,1)}, u32[]{:S(2)}, u32[]{:S(2)}) collective-permute-start(bf16[256,1024]{1,0:T(8,128)(2,1)} %fusion.7), channel_id=1, source_target_pairs={{0,1},{1,0},{2,3},{3,2},{4,5},{5,4},{6,7},{7,6},{8,9},{9,8},{10,11... | collective-permute-start | bytes 1572872 | tf_op jit(solution)/shard_map/ppermute | solution.py:40
  57.7 10.0 %collective-permute-done.11.refs_14_ = bf16[2,1040,256]{2,1,0:T(8,128)(2,1)S(1)} collective-permute-done((bf16[2,1040,256]{2,1,0:T(8,128)(2,1)}, bf16[2,1040,256]{2,1,0:T(8,128)(2,1)S(1)}, u32[]{:S(2)}, u32[]{:S(2)}) %collective-permute-start.11) | collective-permute-done | bytes 1064992 | tf_op jit(solution)/shard_map/ppermute | solution.py:40
  67.8 7.2 %fusion.6 = bf16[256,1024]{1,0:T(8,128)(2,1)} fusion(bf16[256,4096]{1,0:T(8,128)(2,1)} %copy-done.3, bf16[2,4096,1024]{2,1,0:T(8,128)(2,1)} %bitcast.49), kind=kOutput, calls=%fused_computation.12 | convolution fusion | flops 2147745792 | bytes 11010048 | tf_op jit(solution)/shard_map/dot_general | solution.py:488
  75.1 2.0 %collective-permute-start.13 = (bf16[256,1024]{1,0:T(8,128)(2,1)}, bf16[256,1024]{1,0:T(8,128)(2,1)}, u32[]{:S(2)}, u32[]{:S(2)}) collective-permute-start(bf16[256,1024]{1,0:T(8,128)(2,1)} %fusion.6), channel_id=1, source_target_pairs={{0,1},{1,0},{2,3},{3,2},{4,5},{5,4},{6,7},{7,6},{8,9},{9,8},{10,11... | collective-permute-start | bytes 1572872 | tf_op jit(solution)/shard_map/ppermute | solution.py:40
  77.9 1.2 %fusion.4 = f32[256,272]{0,1:T(8,128)S(1)} fusion(bf16[256,4096]{1,0:T(8,128)(2,1)S(1)} %shard_map.205, bf16[4096,16]{1,0:T(8,128)(2,1)S(1)} %copy-done.14, bf16[4096,256]{1,0:T(8,128)(2,1)S(1)} %copy-done.23), kind=kOutput, calls=%fused_computation.8 | convolution fusion | flops 574881792 | bytes 4603904 | tf_op jit(solution)/shard_map/dot_general | solution.py:488
  79.2 5.8 %fusion.refs_0_ = f32[256,1024]{1,0:T(8,128)S(1)} fusion(bf16[256,4096]{1,0:T(8,128)(2,1)S(1)} %shard_map.205, bf16[2,4096,1024]{2,1,0:T(8,128)(2,1)} %bitcast.50), kind=kOutput, calls=%fused_computation.3 | convolution fusion | flops 2147483648 | bytes 11534336 | tf_op jit(solution)/shard_map/dot_general | solution.py:488
  85.3 1.8 %shard_map.206 = (bf16[256,256]{1,0:T(8,128)(2,1)S(1)}, f32[4,256,4]{2,1,0:T(8,128)S(1)}, f32[4,4,256]{2,1,0:T(4,128)S(1)}, f32[4,4,256]{2,1,0:T(4,128)S(1)}, f3...) custom-call(s32[1,2]{1,0:T(1,128)S(1)} %copy-done.8, f32[256,272]{1,0:T(8,128)S(1)} %copy.37.own_ref, ...), custom_call_target="tpu_custom_call" | custom-call | flops 1000000 | bytes 10000 | tf_op jit(solution)/shard_map/pallas_call | solution.py:204
  87.2 6.7 %fusion.2 = f32[256,1024]{1,0:T(8,128)S(1)} fusion(bf16[256,4096]{1,0:T(8,128)(2,1)} %copy-done.4, bf16[2,4096,1024]{2,1,0:T(8,128)(2,1)} %bitcast.51), kind=kOutput, calls=%fused_computation.5 | convolution fusion | flops 2147483648 | bytes 11534336 | tf_op jit(solution)/shard_map/dot_general | solution.py:488
  94.1 7.6 %shard_map.207 = (f32[256,1024]{1,0:T(8,128)S(1)}, f32[2,16,64,256]{3,2,1,0:T(8,128)}) custom-call(s32[2,2]{1,0:T(2,128)S(1)} %and_convert_fusion.flags_ref, s32[2]{0:T(128)S(1)} %bitcast.44, f32[256,1024]{1,0:T(8,128)S(1)} %fusion.refs_0_, bf16[256,1024]{1,0:T(8,128)(2,1)} %collective-permute-done.10.refs_1_, f32[2,3,1024]{2,1,0:T(4,128)S(1)} %slice.36.refs_2_, ...), custom_call_target="tpu_custom_call" | custom-call | flops 1000000 | bytes 10000 | tf_op jit(solution)/shard_map/pallas_call | solution.py:368
  101.7 1.5 %multiply_reduce_fusion = (f32[256]{0:T(256)S(1)}, f32[256,1024]{1,0:T(8,128)S(1)}) fusion(f32[256,1024]{1,0:T(8,128)S(1)} %get-tuple-element.60, f32[256,1024]{1,0:T(8,128)S(1)} %fusion.2, bf16[256,1024]{1,0:T(8,128)(2,1)} %collective-permute-done.13), kind=kLoop, calls=%fused_computation.21 | loop fusion | flops 2883328 | bytes 3671040 | tf_op jit(solution)/shard_map/reduce_sum | solution.py:542
  104.5 1.0 multiply_convert_fusion
  (103 shorter events, 6.8 us)
Async XLA Ops:
  0.6 21.6 %collective-permute-start = (bf16[256,512]{1,0:T(8,128)(2,1)}, bf16[256,512]{1,0:T(8,128)(2,1)S(1)}, u32[]{:S(2)}, u32[]{:S(2)}) collective-permute-start(bf16[256,512]{1,0:T(8,128)(2,1)} %param.20), channel_id=1, source_target_pairs={{0,16},{1,0},{2,18},{3,2},{4,20},{5,4},{6,22},{7,6},{8,24},{9,8},{... | collective-permute-start | bytes 786440 | tf_op jit(solution)/shard_map/ppermute | solution.py:90
  4.7 17.6 %collective-permute-start.1 = (bf16[256,512]{1,0:T(8,128)(2,1)}, bf16[256,512]{1,0:T(8,128)(2,1)S(1)}, u32[]{:S(2)}, u32[]{:S(2)}) collective-permute-start(bf16[256,512]{1,0:T(8,128)(2,1)} %param.20), channel_id=1, source_target_pairs={{1,16},{3,18},{5,20},{7,22},{9,24},{11,26},{13,28},{15,30},{16,1},... | collective-permute-start | bytes 786440 | tf_op jit(solution)/shard_map/ppermute | solution.py:91
  5.4 16.5 %copy-start.19 = (s32[4]{0:T(128)S(1)}, s32[4]{0:T(128)}, u32[]{:S(2)}) copy-start(s32[4]{0:T(128)} %param.34) | copy-start | bytes 52
  5.4 16.7 %copy-start.17 = (bf16[8,3,1024]{2,0,1:T(8,128)(2,1)S(1)}, bf16[8,3,1024]{2,0,1:T(8,128)(2,1)}, u32[]{:S(2)}) copy-start(bf16[8,3,1024]{2,0,1:T(8,128)(2,1)} %param.36) | copy-start | bytes 147460
  5.4 16.9 %copy-start.15 = (bf16[256,512]{1,0:T(8,128)(2,1)S(1)}, bf16[256,512]{1,0:T(8,128)(2,1)}, u32[]{:S(2)}) copy-start(bf16[256,512]{1,0:T(8,128)(2,1)} %param.20) | copy-start | bytes 786436
  5.5 18.5 %copy-start.18 = (bf16[8,3,256]{2,0,1:T(8,128)(2,1)S(1)}, bf16[8,3,256]{2,0,1:T(8,128)(2,1)}, u32[]{:S(2)}) copy-start(bf16[8,3,256]{2,0,1:T(8,128)(2,1)} %param.37) | copy-start | bytes 36868
  5.5 20.3 %copy-start.16 = (bf16[4096,16]{0,1:T(8,128)(2,1)S(1)}, bf16[4096,16]{0,1:T(8,128)(2,1)}, u32[]{:S(2)}) copy-start(bf16[4096,16]{0,1:T(8,128)(2,1)} %param.22) | copy-start | bytes 393220
  22.4 9.0 %collective-permute-start.3 = (bf16[256,512]{1,0:T(8,128)(2,1)S(1)}, bf16[256,512]{1,0:T(8,128)(2,1)S(1)}, u32[]{:S(2)}, u32[]{:S(2)}) collective-permute-start(bf16[256,512]{1,0:T(8,128)(2,1)S(1)} %get-tuple-element.33), channel_id=1, source_target_pairs={{0,8},{8,0},{2,10},{10,2},{4,12},{12,4},{6,14},{14,6},{16,24},{24,... | collective-permute-start | bytes 786440 | tf_op jit(solution)/shard_map/ppermute | solution.py:35
  24.2 9.1 %collective-permute-start.4 = (bf16[256,512]{1,0:T(8,128)(2,1)S(1)}, bf16[256,512]{1,0:T(8,128)(2,1)S(1)}, u32[]{:S(2)}, u32[]{:S(2)}) collective-permute-start(bf16[256,512]{1,0:T(8,128)(2,1)S(1)} %get-tuple-element.33), channel_id=1, source_target_pairs={{0,4},{4,0},{2,6},{6,2},{8,12},{12,8},{10,14},{14,10},{16,20},{20,... | collective-permute-start | bytes 786440 | tf_op jit(solution)/shard_map/ppermute | solution.py:35
  30.5 8.4 %copy-start.21 = (f32[16]{0:T(128)S(1)}, f32[16]{0:T(128)}, u32[]{:S(2)}) copy-start(f32[16]{0:T(128)} %param.26) | copy-start | bytes 196
  30.5 8.7 %copy-start.24 = (s32[2]{0:T(128)S(1)}, s32[2]{0:T(128)}, u32[]{:S(2)}) copy-start(s32[2]{0:T(128)} %param.33) | copy-start | bytes 28
  30.5 8.7 %copy-start.25 = (s32[8]{0:T(128)S(1)}, s32[8]{0:T(128)}, u32[]{:S(2)}) copy-start(s32[8]{0:T(128)} %constant.99.clone) | copy-start | bytes 100
  31.3 7.4 %copy-start.1 = (f32[2,16,64,256]{3,2,1,0:T(8,128)}, f32[2,16,64,256]{3,2,1,0:T(8,128)S(1)}, u32[]{:S(2)}) copy-start(f32[2,16,64,256]{3,2,1,0:T(8,128)S(1)} %get-tuple-element.59.refs_13_) | copy-start | bytes 6291460
  31.3 7.3 %collective-permute-start.5 = (bf16[256,512]{1,0:T(8,128)(2,1)S(1)}, bf16[256,512]{1,0:T(8,128)(2,1)S(1)}, u32[]{:S(2)}, u32[]{:S(2)}) collective-permute-start(bf16[256,512]{1,0:T(8,128)(2,1)S(1)} %collective-permute-done.3), channel_id=1, source_target_pairs={{0,4},{4,0},{2,6},{6,2},{8,12},{12,8},{10,14},{14,10},{16,20},{20,... | collective-permute-start | bytes 786440 | tf_op jit(solution)/shard_map/ppermute | solution.py:35
  31.9 6.9 %collective-permute-start.2 = (bf16[256,512]{1,0:T(8,128)(2,1)S(1)}, bf16[256,512]{1,0:T(8,128)(2,1)S(1)}, u32[]{:S(2)}, u32[]{:S(2)}) collective-permute-start(bf16[256,512]{1,0:T(8,128)(2,1)S(1)} %get-tuple-element.36), channel_id=1, source_target_pairs={{0,8},{8,0},{2,10},{10,2},{4,12},{12,4},{6,14},{14,6},{16,24},{24,... | collective-permute-start | bytes 786440 | tf_op jit(solution)/shard_map/ppermute | solution.py:35
  38.9 6.0 %collective-permute-start.7 = (bf16[4,256,512]{2,1,0:T(8,128)(2,1)S(1)}, bf16[4,256,512]{2,1,0:T(8,128)(2,1)}, u32[]{:S(2)}, u32[]{:S(2)}) collective-permute-start(bf16[4,256,512]{2,1,0:T(8,128)(2,1)S(1)} %pad_maximum_fusion.5.refs_0_), channel_id=1, source_target_pairs={{0,2},{2,0},{4,6},{6,4},{8,10},{10,8},{12,14},{14,12},{16,18},{18,... | collective-permute-start | bytes 3145736 | tf_op jit(solution)/shard_map/ppermute | solution.py:35
  39.2 28.5 %collective-permute-start.11 = (bf16[2,1040,256]{2,1,0:T(8,128)(2,1)}, bf16[2,1040,256]{2,1,0:T(8,128)(2,1)S(1)}, u32[]{:S(2)}, u32[]{:S(2)}) collective-permute-start(bf16[2,1040,256]{2,1,0:T(8,128)(2,1)} %copy-done.12), channel_id=1, source_target_pairs={{0,1},{1,0},{2,3},{3,2},{4,5},{5,4},{6,7},{7,6},{8,9},{9,8},{10,11... | collective-permute-start | bytes 3194888 | tf_op jit(solution)/shard_map/ppermute | solution.py:40
  43.2 14.4 %collective-permute-start.6 = (bf16[2,256,512]{2,1,0:T(8,128)(2,1)S(1)}, bf16[2,256,512]{2,1,0:T(8,128)(2,1)S(1)}, u32[]{:S(2)}, u32[]{:S(2)}) collective-permute-start(bf16[2,256,512]{2,1,0:T(8,128)(2,1)S(1)} %pad_maximum_fusion.6), channel_id=1, source_target_pairs={{0,4},{4,0},{2,6},{6,2},{8,12},{12,8},{10,14},{14,10},{16,20},{20,... | collective-permute-start | bytes 1572872 | tf_op jit(solution)/shard_map/ppermute | solution.py:35
  55.6 21.5 %collective-permute-start.9 = (bf16[256,272]{1,0:T(8,128)(2,1)}, bf16[256,272]{1,0:T(8,128)(2,1)S(1)}, u32[]{:S(2)}, u32[]{:S(2)}) collective-permute-start(bf16[256,272]{1,0:T(8,128)(2,1)} %fusion.8), channel_id=1, source_target_pairs={{0,1},{1,0},{2,3},{3,2},{4,5},{5,4},{6,7},{7,6},{8,9},{9,8},{10,11... | collective-permute-start | bytes 417800 | tf_op jit(solution)/shard_map/ppermute | solution.py:40
  56.3 37.5 %collective-permute-start.10 = (bf16[256,1024]{1,0:T(8,128)(2,1)}, bf16[256,1024]{1,0:T(8,128)(2,1)}, u32[]{:S(2)}, u32[]{:S(2)}) collective-permute-start(bf16[256,1024]{1,0:T(8,128)(2,1)} %fusion.7), channel_id=1, source_target_pairs={{0,1},{1,0},{2,3},{3,2},{4,5},{5,4},{6,7},{7,6},{8,9},{9,8},{10,11... | collective-permute-start | bytes 1572872 | tf_op jit(solution)/shard_map/ppermute | solution.py:40
  57.6 19.5 %collective-permute-start.8 = (bf16[4,256,512]{2,1,0:T(8,128)(2,1)S(1)}, bf16[4,256,512]{2,1,0:T(8,128)(2,1)S(1)}, u32[]{:S(2)}, u32[]{:S(2)}) collective-permute-start(bf16[4,256,512]{2,1,0:T(8,128)(2,1)S(1)} %constant_dynamic-update-slice_fusion.refs_0_), channel_id=1, source_target_pairs={{0,2},{2,0},{4,6},{6,4},{8,10},{10,8},{12,14},{14,12},{16,18},{18,... | collective-permute-start | bytes 3145736 | tf_op jit(solution)/shard_map/ppermute | solution.py:35
  75.1 26.6 %collective-permute-start.13 = (bf16[256,1024]{1,0:T(8,128)(2,1)}, bf16[256,1024]{1,0:T(8,128)(2,1)}, u32[]{:S(2)}, u32[]{:S(2)}) collective-permute-start(bf16[256,1024]{1,0:T(8,128)(2,1)} %fusion.6), channel_id=1, source_target_pairs={{0,1},{1,0},{2,3},{3,2},{4,5},{5,4},{6,7},{7,6},{8,9},{9,8},{10,11... | collective-permute-start | bytes 1572872 | tf_op jit(solution)/shard_map/ppermute | solution.py:40
  87.1 6.8 %collective-permute-start.12 = (bf16[256,256]{1,0:T(8,128)(2,1)S(1)}, bf16[256,256]{1,0:T(8,128)(2,1)S(1)}, u32[]{:S(2)}, u32[]{:S(2)}) collective-permute-start(bf16[256,256]{1,0:T(8,128)(2,1)S(1)} %get-tuple-element.52), channel_id=1, source_target_pairs={{0,2},{2,0},{4,6},{6,4},{8,10},{10,8},{12,14},{14,12},{16,18},{18,... | collective-permute-start | bytes 393224 | tf_op jit(solution)/shard_map/ppermute | solution.py:35
  103.2 1.3 %collective-permute-start.14 = (f32[256]{0:T(256)S(1)}, f32[256]{0:T(256)S(1)}, u32[]{:S(2)}, u32[]{:S(2)}) collective-permute-start(f32[256]{0:T(256)S(1)} %get-tuple-element.68), channel_id=1, source_target_pairs={{0,2},{2,0},{4,6},{6,4},{8,10},{10,8},{12,14},{14,12},{16,18},{18,... | collective-permute-start | bytes 3080 | tf_op jit(solution)/shard_map/ppermute | solution.py:35
  (17 other events, 93.7 us)

commit v9 on v8

--- a/solution.py
+++ b/solution.py
@@ -15,6 +15,7 @@
 HIGH = lax.Precision.HIGHEST
 VMEM_BYTES = 16 * 1024 * 1024
 HEADS_STEP = 4
+COLUMNS = 256
 
 
 def cost(flops, bytes_accessed):
@@ -114,6 +115,29 @@
     return lax.optimization_barrier(
         with_layout_constraint(array, Layout(tuple(range(array.ndim))))
     )
+
+
+def product_kernel(x_ref, w_ref, out_ref):
+    total = jnp.dot(x_ref[...], w_ref[0], preferred_element_type=F32)
+    out_ref[...] = total.astype(out_ref.dtype)
+
+
+def product(block, w_pair, which, kind):
+    tokens, depth = block.shape
+    width = w_pair.shape[2]
+    tile = min(COLUMNS, width)
+    return pl.pallas_call(
+        product_kernel,
+        out_shape=jax.ShapeDtypeStruct((tokens, width), kind),
+        grid=(width // tile,),
+        in_specs=[
+            pl.BlockSpec((tokens, depth), lambda n: (0, 0)),
+            pl.BlockSpec((1, depth, tile), lambda n: (which, 0, n)),
+        ],
+        out_specs=pl.BlockSpec((tokens, tile), lambda n: (0, n)),
+        compiler_params=params(3 * VMEM_BYTES),
+        cost_estimate=cost(2 * tokens * depth * width, 2 * depth * width),
+    )(block, w_pair)
 
 
 def token_places(starts, count_tok, shape, axis):
@@ -248,7 +272,7 @@
                 pl.BlockSpec(block, lambda j, *_: (j, 0, 0, 0)),
             ],
         ),
-        compiler_params=params(12 * 1024 * 1024),
+        compiler_params=params(3 * VMEM_BYTES),
         cost_estimate=cost(0, 14 * count_req * heads * width * state),
     )(slots, own_slots, pool, pool, conv_rows)
 
@@ -478,21 +502,21 @@
         features = [own_got, quad_arrange(four, other)]
     else:
         features = features_in_general(x_in)
-    weights = {
-        "map": jnp.concatenate([w_bc, w_step], 1),
-        "xr": w_pair[1],
-        "z": w_pair[0],
-    }
-
-    def project(block, name):
-        return jnp.dot(block, weights[name], preferred_element_type=F32)
+    w_map = jnp.concatenate([w_bc, w_step], 1)
+
+    def project(block, name, kind):
+        if name == "map":
+            return jnp.dot(block, w_map, preferred_element_type=F32).astype(kind)
+        return product(block, w_pair, 1 if name == "xr" else 0, kind)
 
     came = {"xr": [], "map": [], "z": []}
     done, parts = [], {}
     for step in range(1, req_count):
         block = features[step]
         for name in came:
-            part, block = lax.optimization_barrier((project(block, name).astype(BF16), block))
+            if name == "map":
+                block = after(block, got_states[step - 1])
+            part, block = lax.optimization_barrier((project(block, name, BF16), block))
             came[name].append(shift_req(part, step))
             parts[name] = part
             done.append(part)
@@ -505,7 +529,7 @@
         block = after(block, *done)
     own = {}
     for name in ("map", "xr", "z"):
-        own[name], block = lax.optimization_barrier((project(block, name), block))
+        own[name], block = lax.optimization_barrier((project(block, name, F32), block))
 
     cache = conv_of(own_slots)
     for step in range(1, req_count):

time: 106 us -> 116 us (1.094)
  Pallas kernels: 12.4 us -> 39.1 us
  matrix products: 30.2 us -> 5.09 us
  local copies, waits for them, and re-layouts: 21.9 us -> 28.1 us
  waiting for transfers between devices: 16.3 us -> 19.2 us
  starting transfers between devices: 20 us -> 18.4 us
    dot_general x6 -> x2, matrix products: 30.2 us -> 5.09 us  [project(): return jnp.dot(block, w_map, preferred_element_type=F32).astype(kind)]
    pallas_call x0 -> x4, Pallas kernels: none -> 23.8 us  [product(): pl.pallas_call(product_kernel, out_shape=jax.ShapeDtypeStruct((tokens, wi...]
    unnamed x58 -> x60, local copies, waits for them, and re-layouts: 20.1 us -> 24 us
    pallas_call x1, Pallas kernels: 0.83 us -> 3.67 us  [pack(): pl.pallas_call(pack_kernel, out_shape=[jax.ShapeDtypeStruct((count_req, h...]
    ppermute x4, starting transfers between devices: 7.97 us -> 5.86 us  [shift_req(): lax.ppermute(block, 'req', [(i, (i + step) % count) for i in range(count)])]
    ppermute x9, waiting for transfers between devices: 6.28 us -> 8.21 us  [partner_2(): return lax.ppermute(block, axis, route)]
  transfers between devices with their start and end apart: 15 -> 15, of which waited for: 4 -> 6; matrix products, arithmetic and copies ran while one was open for 47% -> 25% of each run, Pallas kernels for 12% -> 34%
where the time goes in v9:
time: 116 us; the launch traced here: 115 us
  Pallas kernels  39.1 us (34%)
  local copies, waits for them, and re-layouts  28.1 us (24%)
  waiting for transfers between devices  19.2 us (17%)
  starting transfers between devices  18.4 us (16%)
  matrix products  5.09 us (4%)
  other arithmetic  4.05 us (3%)
    unnamed x60, local copies, waits for them, and re-layouts  24 us
    pallas_call x4, Pallas kernels, product(): pl.pallas_call(product_kernel, out_shape=jax.ShapeDtypeStruct((tokens, wi...  23.8 us
    ppermute x4, waiting for transfers between devices, shift_req(): lax.ppermute(block, 'req', [(i, (i + step) % count) for i in range(count)])  11 us
    ppermute x9, waiting for transfers between devices, partner_2(): return lax.ppermute(block, axis, route)  8.21 us
    ppermute x9, starting transfers between devices, partner_2(): return lax.ppermute(block, axis, route)  7.77 us
    pallas_call x1, Pallas kernels, mixer(): pl.pallas_call(functools.partial(mixer_kernel, count_req, len(got)), out_...  7.7 us
    ppermute x4, starting transfers between devices, shift_req(): lax.ppermute(block, 'req', [(i, (i + step) % count) for i in range(count)])  5.86 us
    dot_general x2, matrix products, project(): return jnp.dot(block, w_map, preferred_element_type=F32).astype(kind)  5.09 us
  transfers between devices with their start and end apart: 15, of which 6 were waited for; matrix products, arithmetic and copies ran while one was open for 25% of the time, Pallas kernels for 34%

profile of v9, /device:TPU:0, one launch (start us, length us, event | category | flops | bytes accessed | tf_op | source)
XLA Modules:
  0.0 115.1 jit_solution(11716793783734847483)
XLA Ops:
  0.6 4.1 %collective-permute-start = (bf16[256,512]{1,0:T(8,128)(2,1)}, bf16[256,512]{1,0:T(8,128)(2,1)S(1)}, u32[]{:S(2)}, u32[]{:S(2)}) collective-permute-start(bf16[256,512]{1,0:T(8,128)(2,1)} %param.20), channel_id=1, source_target_pairs={{0,16},{1,0},{2,18},{3,2},{4,20},{5,4},{6,22},{7,6},{8,24},{9,8},{... | collective-permute-start | bytes 786440 | tf_op jit(solution)/shard_map/ppermute | solution.py:91
  5.5 16.5 %copy.44 = bf16[4096,2,1024]{2,0,1:T(8,128)(2,1)} copy(bf16[4096,2,1024]{2,1,0:T(2,128)(2,1)} %param.21) | data formatting | bytes 33554432 | tf_op args[1]
  22.4 1.6 %collective-permute-start.3 = (bf16[256,512]{1,0:T(8,128)(2,1)S(1)}, bf16[256,512]{1,0:T(8,128)(2,1)S(1)}, u32[]{:S(2)}, u32[]{:S(2)}) collective-permute-start(bf16[256,512]{1,0:T(8,128)(2,1)S(1)} %get-tuple-element.34), channel_id=1, source_target_pairs={{0,8},{8,0},{2,10},{10,2},{4,12},{12,4},{6,14},{14,6},{16,24},{24,... | collective-permute-start | bytes 786440 | tf_op jit(solution)/shard_map/ppermute | solution.py:36
  24.2 1.6 %collective-permute-start.4 = (bf16[256,512]{1,0:T(8,128)(2,1)S(1)}, bf16[256,512]{1,0:T(8,128)(2,1)S(1)}, u32[]{:S(2)}, u32[]{:S(2)}) collective-permute-start(bf16[256,512]{1,0:T(8,128)(2,1)S(1)} %get-tuple-element.34), channel_id=1, source_target_pairs={{0,4},{4,0},{2,6},{6,2},{8,12},{12,8},{10,14},{14,10},{16,20},{20,... | collective-permute-start | bytes 786440 | tf_op jit(solution)/shard_map/ppermute | solution.py:36
  25.7 1.3 %copy.35 = bf16[4096,16]{1,0:T(8,128)(2,1)} copy(bf16[4096,16]{0,1:T(8,128)(2,1)S(1)} %copy-done.18) | data formatting | bytes 262144 | tf_op jit(solution)/shard_map/optimization_barrier | solution.py:85
  27.1 3.7 %shard_map.203 = (bf16[2,1040,256]{2,1,0:T(8,128)(2,1)}, f32[2,16,64,256]{3,2,1,0:T(8,128)S(1)}) custom-call(s32[2]{0:T(128)S(1)} %get-tuple-element.79.slots_ref, s32[2]{0:T(128)S(1)} %get-tuple-element.78.own_slots_ref, f32[8,16,64,256]{3,2,1,0:T(8,128)} %own_pool_ref.1, f32[8,16,64,256]{3,2,1,0:T(8,128)} %own_pool_ref.1, bf16[2,16,256]{2,1,0:T(8,128)(2,1)S(1)} %bitcast.26), custom_call_target="tpu_custom_call" | custom-call | bytes 7340032 | tf_op jit(solution)/shard_map/pallas_call | solution.py:256
  31.7 1.6 %collective-permute-start.2 = (bf16[256,512]{1,0:T(8,128)(2,1)S(1)}, bf16[256,512]{1,0:T(8,128)(2,1)S(1)}, u32[]{:S(2)}, u32[]{:S(2)}) collective-permute-start(bf16[256,512]{1,0:T(8,128)(2,1)S(1)} %get-tuple-element.37), channel_id=1, source_target_pairs={{0,8},{8,0},{2,10},{10,2},{4,12},{12,4},{6,14},{14,6},{16,24},{24,... | collective-permute-start | bytes 786440 | tf_op jit(solution)/shard_map/ppermute | solution.py:36
  33.3 4.8 %collective-permute-done.5 = bf16[256,512]{1,0:T(8,128)(2,1)S(1)} collective-permute-done((bf16[256,512]{1,0:T(8,128)(2,1)S(1)}, bf16[256,512]{1,0:T(8,128)(2,1)S(1)}, u32[]{:S(2)}, u32[]{:S(2)}) %collective-permute-start.5) | collective-permute-done | bytes 262176 | tf_op jit(solution)/shard_map/ppermute | solution.py:36
  38.3 3.8 %collective-permute-start.9 = (bf16[2,1040,256]{2,1,0:T(8,128)(2,1)}, bf16[2,1040,256]{2,1,0:T(8,128)(2,1)}, u32[]{:S(2)}, u32[]{:S(2)}) collective-permute-start(bf16[2,1040,256]{2,1,0:T(8,128)(2,1)} %get-tuple-element.36), channel_id=1, source_target_pairs={{0,1},{1,0},{2,3},{3,2},{4,5},{5,4},{6,7},{7,6},{8,9},{9,8},{10,11... | collective-permute-start | bytes 3194888 | tf_op jit(solution)/shard_map/ppermute | solution.py:41
  43.1 1.5 %collective-permute-start.6 = (bf16[2,256,512]{2,1,0:T(8,128)(2,1)S(1)}, bf16[2,256,512]{2,1,0:T(8,128)(2,1)S(1)}, u32[]{:S(2)}, u32[]{:S(2)}) collective-permute-start(bf16[2,256,512]{2,1,0:T(8,128)(2,1)S(1)} %pad_maximum_fusion.6), channel_id=1, source_target_pairs={{0,4},{4,0},{2,6},{6,2},{8,12},{12,8},{10,14},{14,10},{16,20},{20,... | collective-permute-start | bytes 1572872 | tf_op jit(solution)/shard_map/ppermute | solution.py:36
  48.3 6.3 %shard_map.205 = bf16[256,1024]{1,0:T(8,128)(2,1)} custom-call(bf16[256,4096]{1,0:T(8,128)(2,1)S(1)} %shard_map.204.x_ref, bf16[2,4096,1024]{2,1,0:T(8,128)(2,1)} %bitcast.32), custom_call_target="tpu_custom_call" | custom-call | flops 2147483648 | bytes 8388608 | tf_op jit(solution)/shard_map/pallas_call | solution.py:129
  54.6 2.5 %collective-permute-done.6 = bf16[2,256,512]{2,1,0:T(8,128)(2,1)S(1)} collective-permute-done((bf16[2,256,512]{2,1,0:T(8,128)(2,1)S(1)}, bf16[2,256,512]{2,1,0:T(8,128)(2,1)S(1)}, u32[]{:S(2)}, u32[]{:S(2)}) %collective-permute-start.6) | collective-permute-done | bytes 524320 | tf_op jit(solution)/shard_map/ppermute | solution.py:36
  58.0 8.8 %collective-permute-done.9.refs_14_ = bf16[2,1040,256]{2,1,0:T(8,128)(2,1)} collective-permute-done((bf16[2,1040,256]{2,1,0:T(8,128)(2,1)}, bf16[2,1040,256]{2,1,0:T(8,128)(2,1)}, u32[]{:S(2)}, u32[]{:S(2)}) %collective-permute-start.9) | collective-permute-done | bytes 1064992 | tf_op jit(solution)/shard_map/ppermute | solution.py:41
  68.3 3.2 %fusion.2 = bf16[256,272]{1,0:T(8,128)(2,1)S(1)} fusion(bf16[256,4096]{1,0:T(8,128)(2,1)S(1)} %shard_map.204.x_ref, bf16[4096,16]{1,0:T(8,128)(2,1)} %copy.35, bf16[4096,256]{1,0:T(8,128)(2,1)} %param.23), kind=kOutput, calls=%fused_computation.6 | convolution fusion | flops 574951424 | bytes 4464640 | tf_op jit(solution)/shard_map/dot_general | solution.py:509
  71.5 2.0 %collective-permute-start.10 = (bf16[256,272]{1,0:T(8,128)(2,1)S(1)}, bf16[256,272]{1,0:T(8,128)(2,1)S(1)}, u32[]{:S(2)}, u32[]{:S(2)}) collective-permute-start(bf16[256,272]{1,0:T(8,128)(2,1)S(1)} %fusion.2), channel_id=1, source_target_pairs={{0,1},{1,0},{2,3},{3,2},{4,5},{5,4},{6,7},{7,6},{8,9},{9,8},{10,11... | collective-permute-start | bytes 417800 | tf_op jit(solution)/shard_map/ppermute | solution.py:41
  73.5 6.3 %shard_map.206 = bf16[256,1024]{1,0:T(8,128)(2,1)} custom-call(bf16[256,4096]{1,0:T(8,128)(2,1)S(1)} %shard_map.204.x_ref, bf16[2,4096,1024]{2,1,0:T(8,128)(2,1)} %bitcast.33), custom_call_target="tpu_custom_call" | custom-call | flops 2147483648 | bytes 8388608 | tf_op jit(solution)/shard_map/pallas_call | solution.py:129
  79.8 2.2 %collective-permute-done.10.refs_0_ = bf16[256,272]{1,0:T(8,128)(2,1)S(1)} collective-permute-done((bf16[256,272]{1,0:T(8,128)(2,1)S(1)}, bf16[256,272]{1,0:T(8,128)(2,1)S(1)}, u32[]{:S(2)}, u32[]{:S(2)}) %collective-permute-start.10) | collective-permute-done | bytes 139296 | tf_op jit(solution)/shard_map/ppermute | solution.py:41
  82.1 1.5 %shard_map.207.x_ref = bf16[256,4096]{1,0:T(8,128)(2,1)S(1)} custom-call(s32[8]{0:T(128)S(1)} %broadcast_xor_fusion.places_ref, bf16[4,256,512]{2,1,0:T(8,128)(2,1)} %constant_dynamic-update-slice_fusion.refs_0_, bf16[4,256,512]{2,1,0:T(8,128)(2,1)S(1)} %collective-permute-done.8.refs_1_), custom_call_target="tpu_custom_call" | custom-call | flops 1000000 | bytes 10000 | tf_op jit(solution)/shard_map/pallas_call | solution.py:73
  83.6 1.9 %fusion = f32[256,272]{0,1:T(8,128)} fusion(bf16[256,4096]{1,0:T(8,128)(2,1)S(1)} %shard_map.207.x_ref, bf16[4096,16]{1,0:T(8,128)(2,1)S(1)} %copy-done.16, bf16[4096,256]{1,0:T(8,128)(2,1)S(1)} %copy-done.24), kind=kOutput, calls=%fused_computation.2 | convolution fusion | flops 574881792 | bytes 4603904 | tf_op jit(solution)/shard_map/dot_general | solution.py:509
  85.5 5.5 %shard_map.208.refs_0_ = f32[256,1024]{1,0:T(8,128)S(1)} custom-call(bf16[256,4096]{1,0:T(8,128)(2,1)S(1)} %shard_map.207.x_ref, bf16[2,4096,1024]{2,1,0:T(8,128)(2,1)} %bitcast.34), custom_call_target="tpu_custom_call" | custom-call | flops 2147483648 | bytes 8388608 | tf_op jit(solution)/shard_map/pallas_call | solution.py:129
  95.8 1.8 %shard_map.209 = (bf16[256,256]{1,0:T(8,128)(2,1)S(1)}, f32[4,256,4]{2,1,0:T(8,128)S(1)}, f32[4,4,256]{2,1,0:T(4,128)S(1)}, f32[4,4,256]{2,1,0:T(4,128)S(1)}, f3...) custom-call(s32[1,2]{1,0:T(1,128)S(1)} %copy-done.11, f32[256,272]{1,0:T(8,128)S(1)} %copy.37.own_ref, ...), custom_call_target="tpu_custom_call" | custom-call | flops 1000000 | bytes 10000 | tf_op jit(solution)/shard_map/pallas_call | solution.py:228
  97.7 5.7 %shard_map.211 = f32[256,1024]{1,0:T(8,128)S(1)} custom-call(bf16[256,4096]{1,0:T(8,128)(2,1)S(1)} %shard_map.207.x_ref, bf16[2,4096,1024]{2,1,0:T(8,128)(2,1)} %bitcast.35), custom_call_target="tpu_custom_call" | custom-call | flops 2147483648 | bytes 8388608 | tf_op jit(solution)/shard_map/pallas_call | solution.py:129
  103.6 7.7 %shard_map.210 = (f32[256,1024]{1,0:T(8,128)S(1)}, f32[2,16,64,256]{3,2,1,0:T(8,128)}) custom-call(s32[2,2]{1,0:T(2,128)S(1)} %copy-done.10, s32[2]{0:T(128)S(1)} %bitcast.28, f32[256,1024]{1,0:T(8,128)S(1)} %shard_map.208.refs_0_, bf16[256,1024]{1,0:T(8,128)(2,1)} %collective-permute-done.11.refs_1_, f32[2,3,1024]{2,1,0:T(4,128)S(1)} %copy-done.6, ...), custom_call_target="tpu_custom_call" | custom-call | flops 1000000 | bytes 10000 | tf_op jit(solution)/shard_map/pallas_call | solution.py:392
  111.3 1.5 %multiply_reduce_fusion = (f32[256]{0:T(256)S(1)}, f32[256,1024]{1,0:T(8,128)S(1)}) fusion(f32[256,1024]{1,0:T(8,128)S(1)} %get-tuple-element.62, f32[256,1024]{1,0:T(8,128)S(1)} %shard_map.211, bf16[256,1024]{1,0:T(8,128)(2,1)} %collective-permute-done.13), kind=kLoop, calls=%fused_computation.13 | loop fusion | flops 2883328 | bytes 3671040 | tf_op jit(solution)/shard_map/reduce_sum | solution.py:566
  (105 shorter events, 16.8 us)
Async XLA Ops:
  0.6 21.6 %collective-permute-start = (bf16[256,512]{1,0:T(8,128)(2,1)}, bf16[256,512]{1,0:T(8,128)(2,1)S(1)}, u32[]{:S(2)}, u32[]{:S(2)}) collective-permute-start(bf16[256,512]{1,0:T(8,128)(2,1)} %param.20), channel_id=1, source_target_pairs={{0,16},{1,0},{2,18},{3,2},{4,20},{5,4},{6,22},{7,6},{8,24},{9,8},{... | collective-permute-start | bytes 786440 | tf_op jit(solution)/shard_map/ppermute | solution.py:91
  4.7 17.6 %collective-permute-start.1 = (bf16[256,512]{1,0:T(8,128)(2,1)}, bf16[256,512]{1,0:T(8,128)(2,1)S(1)}, u32[]{:S(2)}, u32[]{:S(2)}) collective-permute-start(bf16[256,512]{1,0:T(8,128)(2,1)} %param.20), channel_id=1, source_target_pairs={{1,16},{3,18},{5,20},{7,22},{9,24},{11,26},{13,28},{15,30},{16,1},... | collective-permute-start | bytes 786440 | tf_op jit(solution)/shard_map/ppermute | solution.py:92
  5.4 16.5 %copy-start.21 = (s32[4]{0:T(128)S(1)}, s32[4]{0:T(128)}, u32[]{:S(2)}) copy-start(s32[4]{0:T(128)} %param.34) | copy-start | bytes 52
  5.4 16.7 %copy-start.19 = (bf16[8,3,1024]{2,0,1:T(8,128)(2,1)S(1)}, bf16[8,3,1024]{2,0,1:T(8,128)(2,1)}, u32[]{:S(2)}) copy-start(bf16[8,3,1024]{2,0,1:T(8,128)(2,1)} %param.36) | copy-start | bytes 147460
  5.4 16.8 %copy-start.17 = (bf16[256,512]{1,0:T(8,128)(2,1)S(1)}, bf16[256,512]{1,0:T(8,128)(2,1)}, u32[]{:S(2)}) copy-start(bf16[256,512]{1,0:T(8,128)(2,1)} %param.20) | copy-start | bytes 786436
  5.5 18.5 %copy-start.20 = (bf16[8,3,256]{2,0,1:T(8,128)(2,1)S(1)}, bf16[8,3,256]{2,0,1:T(8,128)(2,1)}, u32[]{:S(2)}) copy-start(bf16[8,3,256]{2,0,1:T(8,128)(2,1)} %param.37) | copy-start | bytes 36868
  5.5 20.3 %copy-start.18 = (bf16[4096,16]{0,1:T(8,128)(2,1)S(1)}, bf16[4096,16]{0,1:T(8,128)(2,1)}, u32[]{:S(2)}) copy-start(bf16[4096,16]{0,1:T(8,128)(2,1)} %param.22) | copy-start | bytes 393220
  22.4 8.4 %collective-permute-start.3 = (bf16[256,512]{1,0:T(8,128)(2,1)S(1)}, bf16[256,512]{1,0:T(8,128)(2,1)S(1)}, u32[]{:S(2)}, u32[]{:S(2)}) collective-permute-start(bf16[256,512]{1,0:T(8,128)(2,1)S(1)} %get-tuple-element.34), channel_id=1, source_target_pairs={{0,8},{8,0},{2,10},{10,2},{4,12},{12,4},{6,14},{14,6},{16,24},{24,... | collective-permute-start | bytes 786440 | tf_op jit(solution)/shard_map/ppermute | solution.py:36
  24.2 9.1 %collective-permute-start.4 = (bf16[256,512]{1,0:T(8,128)(2,1)S(1)}, bf16[256,512]{1,0:T(8,128)(2,1)S(1)}, u32[]{:S(2)}, u32[]{:S(2)}) collective-permute-start(bf16[256,512]{1,0:T(8,128)(2,1)S(1)} %get-tuple-element.34), channel_id=1, source_target_pairs={{0,4},{4,0},{2,6},{6,2},{8,12},{12,8},{10,14},{14,10},{16,20},{20,... | collective-permute-start | bytes 786440 | tf_op jit(solution)/shard_map/ppermute | solution.py:36
  30.7 7.4 %copy-start = (f32[2,16,64,256]{3,2,1,0:T(8,128)}, f32[2,16,64,256]{3,2,1,0:T(8,128)S(1)}, u32[]{:S(2)}) copy-start(f32[2,16,64,256]{3,2,1,0:T(8,128)S(1)} %get-tuple-element.61.refs_13_) | copy-start | bytes 6291460
  30.7 7.6 %copy-start.25 = (s32[2]{0:T(128)S(1)}, s32[2]{0:T(128)}, u32[]{:S(2)}) copy-start(s32[2]{0:T(128)} %param.33) | copy-start | bytes 28
  30.7 11.4 %copy-start.23 = (f32[16]{0:T(128)S(1)}, f32[16]{0:T(128)}, u32[]{:S(2)}) copy-start(f32[16]{0:T(128)} %param.26) | copy-start | bytes 196
  30.7 13.8 %copy-start.26 = (s32[8]{0:T(128)S(1)}, s32[8]{0:T(128)}, u32[]{:S(2)}) copy-start(s32[8]{0:T(128)} %constant.99.clone) | copy-start | bytes 100
  30.8 7.3 %collective-permute-start.5 = (bf16[256,512]{1,0:T(8,128)(2,1)S(1)}, bf16[256,512]{1,0:T(8,128)(2,1)S(1)}, u32[]{:S(2)}, u32[]{:S(2)}) collective-permute-start(bf16[256,512]{1,0:T(8,128)(2,1)S(1)} %collective-permute-done.3), channel_id=1, source_target_pairs={{0,4},{4,0},{2,6},{6,2},{8,12},{12,8},{10,14},{14,10},{16,20},{20,... | collective-permute-start | bytes 786440 | tf_op jit(solution)/shard_map/ppermute | solution.py:36
  31.7 6.6 %collective-permute-start.2 = (bf16[256,512]{1,0:T(8,128)(2,1)S(1)}, bf16[256,512]{1,0:T(8,128)(2,1)S(1)}, u32[]{:S(2)}, u32[]{:S(2)}) collective-permute-start(bf16[256,512]{1,0:T(8,128)(2,1)S(1)} %get-tuple-element.37), channel_id=1, source_target_pairs={{0,8},{8,0},{2,10},{10,2},{4,12},{12,4},{6,14},{14,6},{16,24},{24,... | collective-permute-start | bytes 786440 | tf_op jit(solution)/shard_map/ppermute | solution.py:36
  38.3 7.1 %collective-permute-start.7 = (bf16[4,256,512]{2,1,0:T(8,128)(2,1)S(1)}, bf16[4,256,512]{2,1,0:T(8,128)(2,1)S(1)}, u32[]{:S(2)}, u32[]{:S(2)}) collective-permute-start(bf16[4,256,512]{2,1,0:T(8,128)(2,1)S(1)} %pad_maximum_fusion.5.refs_0_), channel_id=1, source_target_pairs={{0,2},{2,0},{4,6},{6,4},{8,10},{10,8},{12,14},{14,12},{16,18},{18,... | collective-permute-start | bytes 3145736 | tf_op jit(solution)/shard_map/ppermute | solution.py:36
  38.3 28.4 %collective-permute-start.9 = (bf16[2,1040,256]{2,1,0:T(8,128)(2,1)}, bf16[2,1040,256]{2,1,0:T(8,128)(2,1)}, u32[]{:S(2)}, u32[]{:S(2)}) collective-permute-start(bf16[2,1040,256]{2,1,0:T(8,128)(2,1)} %get-tuple-element.36), channel_id=1, source_target_pairs={{0,1},{1,0},{2,3},{3,2},{4,5},{5,4},{6,7},{7,6},{8,9},{9,8},{10,11... | collective-permute-start | bytes 3194888 | tf_op jit(solution)/shard_map/ppermute | solution.py:41
  43.1 14.1 %collective-permute-start.6 = (bf16[2,256,512]{2,1,0:T(8,128)(2,1)S(1)}, bf16[2,256,512]{2,1,0:T(8,128)(2,1)S(1)}, u32[]{:S(2)}, u32[]{:S(2)}) collective-permute-start(bf16[2,256,512]{2,1,0:T(8,128)(2,1)S(1)} %pad_maximum_fusion.6), channel_id=1, source_target_pairs={{0,4},{4,0},{2,6},{6,2},{8,12},{12,8},{10,14},{14,10},{16,20},{20,... | collective-permute-start | bytes 1572872 | tf_op jit(solution)/shard_map/ppermute | solution.py:36
  54.6 48.8 %collective-permute-start.11 = (bf16[256,1024]{1,0:T(8,128)(2,1)}, bf16[256,1024]{1,0:T(8,128)(2,1)}, u32[]{:S(2)}, u32[]{:S(2)}) collective-permute-start(bf16[256,1024]{1,0:T(8,128)(2,1)} %shard_map.205), channel_id=1, source_target_pairs={{0,1},{1,0},{2,3},{3,2},{4,5},{5,4},{6,7},{7,6},{8,9},{9,8},{10,11... | collective-permute-start | bytes 1572872 | tf_op jit(solution)/shard_map/ppermute | solution.py:41
  58.0 24.1 %collective-permute-start.8 = (bf16[4,256,512]{2,1,0:T(8,128)(2,1)}, bf16[4,256,512]{2,1,0:T(8,128)(2,1)S(1)}, u32[]{:S(2)}, u32[]{:S(2)}) collective-permute-start(bf16[4,256,512]{2,1,0:T(8,128)(2,1)} %constant_dynamic-update-slice_fusion.refs_0_), channel_id=1, source_target_pairs={{0,2},{2,0},{4,6},{6,4},{8,10},{10,8},{12,14},{14,12},{16,18},{18,... | collective-permute-start | bytes 3145736 | tf_op jit(solution)/shard_map/ppermute | solution.py:36
  71.5 10.6 %collective-permute-start.10 = (bf16[256,272]{1,0:T(8,128)(2,1)S(1)}, bf16[256,272]{1,0:T(8,128)(2,1)S(1)}, u32[]{:S(2)}, u32[]{:S(2)}) collective-permute-start(bf16[256,272]{1,0:T(8,128)(2,1)S(1)} %fusion.2), channel_id=1, source_target_pairs={{0,1},{1,0},{2,3},{3,2},{4,5},{5,4},{6,7},{7,6},{8,9},{9,8},{10,11... | collective-permute-start | bytes 417800 | tf_op jit(solution)/shard_map/ppermute | solution.py:41
  79.8 31.6 %collective-permute-start.13 = (bf16[256,1024]{1,0:T(8,128)(2,1)}, bf16[256,1024]{1,0:T(8,128)(2,1)}, u32[]{:S(2)}, u32[]{:S(2)}) collective-permute-start(bf16[256,1024]{1,0:T(8,128)(2,1)} %shard_map.206), channel_id=1, source_target_pairs={{0,1},{1,0},{2,3},{3,2},{4,5},{5,4},{6,7},{7,6},{8,9},{9,8},{10,11... | collective-permute-start | bytes 1572872 | tf_op jit(solution)/shard_map/ppermute | solution.py:41
  97.6 5.8 %collective-permute-start.12 = (bf16[256,256]{1,0:T(8,128)(2,1)S(1)}, bf16[256,256]{1,0:T(8,128)(2,1)S(1)}, u32[]{:S(2)}, u32[]{:S(2)}) collective-permute-start(bf16[256,256]{1,0:T(8,128)(2,1)S(1)} %get-tuple-element.54), channel_id=1, source_target_pairs={{0,2},{2,0},{4,6},{6,4},{8,10},{10,8},{12,14},{14,12},{16,18},{18,... | collective-permute-start | bytes 393224 | tf_op jit(solution)/shard_map/ppermute | solution.py:36
  112.8 1.3 %collective-permute-start.14 = (f32[256]{0:T(256)S(1)}, f32[256]{0:T(256)S(1)}, u32[]{:S(2)}, u32[]{:S(2)}) collective-permute-start(f32[256]{0:T(256)S(1)} %get-tuple-element.70), channel_id=1, source_target_pairs={{0,2},{2,0},{4,6},{6,4},{8,10},{10,8},{12,14},{14,12},{16,18},{18,... | collective-permute-start | bytes 3080 | tf_op jit(solution)/shard_map/ppermute | solution.py:36
  (18 other events, 60.4 us)

commit v10 on v8

--- a/solution.py
+++ b/solution.py
@@ -14,6 +14,7 @@
 BF16 = jnp.bfloat16
 HIGH = lax.Precision.HIGHEST
 VMEM_BYTES = 16 * 1024 * 1024
+LARGE_BYTES = 40 * 1024 * 1024
 HEADS_STEP = 4
 
 
@@ -93,9 +94,9 @@
     return jnp.where(near, x_in, first), jnp.where(near, first, second)
 
 
-def quad_arrange(four, other):
-    apart = jnp.array([0, 4, 2, 6, 1, 5, 3, 7], jnp.int32)
-    return arrange([four, other], (lax.axis_index("wide") % 8) ^ apart)
+def quad_arrange(stacks, apart):
+    places = (lax.axis_index("wide") % 8) ^ jnp.array(apart, jnp.int32)
+    return arrange(stacks, places)
 
 
 def features_in_general(x_in):
@@ -114,6 +115,24 @@
     return lax.optimization_barrier(
         with_layout_constraint(array, Layout(tuple(range(array.ndim))))
     )
+
+
+def stage_kernel(which, w_ref, _, out_ref, sem):
+    copy = pltpu.make_async_copy(w_ref.at[which], out_ref, sem)
+    copy.start()
+    copy.wait()
+
+
+def stage(w_pair, which, behind):
+    return pl.pallas_call(
+        functools.partial(stage_kernel, which),
+        out_shape=jax.ShapeDtypeStruct(w_pair.shape[1:], w_pair.dtype),
+        in_specs=[pl.BlockSpec(memory_space=pl.ANY)] * 2,
+        out_specs=pl.BlockSpec(memory_space=pltpu.VMEM),
+        scratch_shapes=[pltpu.SemaphoreType.DMA],
+        compiler_params=params(LARGE_BYTES),
+        cost_estimate=cost(0, 2 * w_pair.shape[1] * w_pair.shape[2]),
+    )(w_pair, behind)
 
 
 def token_places(starts, count_tok, shape, axis):
@@ -218,39 +237,25 @@
     )(starts, own, *got, cache, kernel, bias[None], dt_bias[None], a_log[None])
 
 
-def pack_kernel(slots_ref, own_slots_ref, pool_ref, own_pool_ref, conv_ref, out_ref, own_ref):
-    heads, width, state = pool_ref.shape[1:]
-    out_ref[0, : heads * width, :] = pool_ref[0].reshape(heads * width, state).astype(BF16)
-    out_ref[0, heads * width :, :] = conv_ref[0]
-    own_ref[...] = own_pool_ref[...]
-
-
-def pack(pool, conv_rows, slots, own_slots):
-    _, heads, width, state = pool.shape
-    count_req, rows, _ = conv_rows.shape
-    block = (1, heads, width, state)
+def pack_kernel(slots_ref, pool_ref, out_ref):
+    out_ref[...] = pool_ref[...].reshape(out_ref.shape).astype(out_ref.dtype)
+
+
+def pack(pool, slots, shape, kind):
+    count_req = slots.shape[0]
+    block = (1,) + pool.shape[1:]
     return pl.pallas_call(
         pack_kernel,
-        out_shape=[
-            jax.ShapeDtypeStruct((count_req, heads * width + rows, state), BF16),
-            jax.ShapeDtypeStruct((count_req, heads, width, state), F32),
-        ],
+        out_shape=jax.ShapeDtypeStruct((count_req,) + shape, kind),
         grid_spec=pltpu.PrefetchScalarGridSpec(
-            num_scalar_prefetch=2,
+            num_scalar_prefetch=1,
             grid=(count_req,),
-            in_specs=[
-                pl.BlockSpec(block, lambda j, slots, own: (slots[j], 0, 0, 0)),
-                pl.BlockSpec(block, lambda j, slots, own: (own[j], 0, 0, 0)),
-                pl.BlockSpec((1, rows, state), lambda j, *_: (j, 0, 0)),
-            ],
-            out_specs=[
-                pl.BlockSpec((1, heads * width + rows, state), lambda j, *_: (j, 0, 0)),
-                pl.BlockSpec(block, lambda j, *_: (j, 0, 0, 0)),
-            ],
+            in_specs=[pl.BlockSpec(block, lambda j, slots: (slots[j], 0, 0, 0))],
+            out_specs=pl.BlockSpec((1,) + shape, lambda j, slots: (j,) + (0,) * len(shape)),
         ),
-        compiler_params=params(12 * 1024 * 1024),
-        cost_estimate=cost(0, 14 * count_req * heads * width * state),
-    )(slots, own_slots, pool, pool, conv_rows)
+        compiler_params=params(3 * VMEM_BYTES),
+        cost_estimate=cost(0, 6 * pool[0].size * count_req),
+    )(slots, pool)
 
 
 def mixer_kernel(count_req, got_total, flags_ref, starts_ref, *refs):
@@ -424,15 +429,8 @@
     conv_width = local_width + state_part
 
     direct = req_count == 2 and lax.axis_size("wide") == 16
-    w_pair = jnp.transpose(w_xz, (1, 0, 2))
-    w_step = w_dt
     if direct:
         own_block, block = near_blocks(x_in)
-        w_pair = pinned(w_pair)
-        block = after(block, w_pair)
-        along_z = partner_2(block, "wide", 2)
-        along_x = partner_2(block, "wide", 1)
-        w_step = pinned(after(w_dt, block))
 
     def slots_of(index):
         asked = lax.dynamic_slice_in_dim(state_slot, index * group_reqs, group_reqs)
@@ -446,72 +444,86 @@
         ]
         return jnp.concatenate(parts, 2)
 
-    conv_size = lags * conv_width
-    conv_rows = -(-conv_size // (16 * state)) * 16
-    own_slots = slots_of(me)
     got_states = []
     for step in range(1, req_count):
         slots = slots_of((me + step) % req_count)
-        flat = conv_of(slots).reshape(group_reqs, conv_size)
-        if direct:
-            flat = after(flat, block)
-        flat = jnp.pad(flat, ((0, 0), (0, conv_rows * state - conv_size)))
-        packed, held = pack(
-            ssm_pool, flat.reshape(group_reqs, conv_rows, state), slots, own_slots
-        )
+        packed = pack(ssm_pool, slots, (heads * head_width, state), BF16)
         got_states.append(shift_req(packed, step))
-
+    own_slots = slots_of(me)
     asked = lax.dynamic_slice_in_dim(state_slot, me * group_reqs, group_reqs)
     came_from = (me - asked // slot_count) % req_count
     live = prefix_len > 0
     flags = (live[:, None] & (came_from[:, None] == jnp.arange(req_count)[None, :])).astype(
         jnp.int32
     )
+
+    w_pair = jnp.transpose(w_xz, (1, 0, 2))
+    w_step = w_dt
     if direct:
-        both = partner_2(after(along_z, packed, w_step), "wide", 1)
-        own_block = after(own_block, packed)
+        w_pair = pinned(w_pair)
+        block = after(block, w_pair)
+        along_z = partner_2(block, "wide", 2)
+        along_x = partner_2(block, "wide", 1)
+        w_step = pinned(after(w_dt, block))
+        own_slots = after(own_slots, block)
+    held = pack(ssm_pool, own_slots, (heads, head_width, state), F32)
+    got_conv = []
+    for step in range(1, req_count):
+        slots = slots_of((me + step) % req_count)
+        if direct:
+            slots = after(slots, block)
+        got_conv.append(shift_req(conv_of(slots), step))
+
+    if direct:
+        near_three = after(jnp.stack([block, along_z, along_x]), held, w_step)
+        both = partner_2(after(along_z, held, w_step, *got_states, *got_conv), "wide", 1)
+        core_three = partner_2(near_three, "wide", 0)
+        own_block = after(own_block, held)
         own_z = partner_2(own_block, "wide", 2)
-        four = after(jnp.stack([block, along_z, along_x, both]), own_z)
-        other = partner_2(four, "wide", 0)
-        own_pair = after(jnp.stack([own_block, own_z]), four)
+        w_xr = stage(w_pair, 1, near_three)
+        w_z = stage(w_pair, 0, near_three)
+        both = after(both[None], own_z, w_xr, w_z)
+        core_both = partner_2(both, "wide", 0)
+        own_pair = after(jnp.stack([own_block, own_z]), both)
         own_got = partner_2(own_pair, "wide", 1)
-        features = [own_got, quad_arrange(four, other)]
+        theirs = quad_arrange(
+            [near_three, both, core_three, core_both], [0, 4, 2, 6, 1, 5, 3, 7]
+        )
+        features = [own_got, theirs]
     else:
         features = features_in_general(x_in)
-    weights = {
-        "map": jnp.concatenate([w_bc, w_step], 1),
-        "xr": w_pair[1],
-        "z": w_pair[0],
-    }
-
-    def project(block, name):
-        return jnp.dot(block, weights[name], preferred_element_type=F32)
+        w_z, w_xr = w_pair[0], w_pair[1]
+    w_map = jnp.concatenate([w_bc, w_step], 1)
+
+    weights = {"xr": w_xr, "map": w_map, "z": w_z}
+
+    def project(block, name, kind):
+        return jnp.dot(block, weights[name], preferred_element_type=F32).astype(kind)
 
     came = {"xr": [], "map": [], "z": []}
     done, parts = [], {}
     for step in range(1, req_count):
         block = features[step]
         for name in came:
-            part, block = lax.optimization_barrier((project(block, name).astype(BF16), block))
-            came[name].append(shift_req(part, step))
+            part, block = lax.optimization_barrier((project(block, name, BF16), block))
             parts[name] = part
+            part = shift_req(part, step)
+            came[name].append(part)
             done.append(part)
     block = features[0]
     if direct:
         own_four = jnp.concatenate([own_pair, after(block, parts["xr"])], 0)
-        own_other = partner_2(own_four, "wide", 0)
-        block = quad_arrange(own_four, after(own_other, *done, *came["map"]))
+        own_core = after(partner_2(own_four, "wide", 0), *done, *came["map"])
+        block = quad_arrange([own_four, own_core], [0, 4, 2, 6, 1, 5, 3, 7])
     else:
         block = after(block, *done)
     own = {}
     for name in ("map", "xr", "z"):
-        own[name], block = lax.optimization_barrier((project(block, name), block))
+        own[name], block = lax.optimization_barrier((project(block, name, F32), block))
 
     cache = conv_of(own_slots)
     for step in range(1, req_count):
-        got = after(got_states[step - 1], parts["xr"])[:, heads * head_width :].reshape(group_reqs, -1)
-        got = got[:, :conv_size].reshape(cache.shape)
-        cache = jnp.where((came_from == step)[:, None, None], got, cache)
+        cache = jnp.where((came_from == step)[:, None, None], got_conv[step - 1], cache)
     cache = jnp.where(live[:, None, None], cache, 0).astype(F32)
 
     bc_conv, cum, cum_t, step_t, coef, decay = prep(

time: 106 us -> 124 us (1.17)
  Pallas kernels: 12.4 us -> 26.9 us
  matrix products: 30.2 us -> 18.3 us
  local copies, waits for them, and re-layouts: 21.9 us -> 28 us
  waiting for transfers between devices: 16.3 us -> 21.5 us
  other arithmetic: 3.48 us -> 6.93 us
    pallas_call x1 -> x4, Pallas kernels: 0.83 us -> 14.6 us  [the longest x2 9.82 us: stage(): pl.pallas_call(functools.partial(stage_kernel, which), out_shape=jax.Shap...]
    dot_general x6, matrix products: 30.2 us -> 18.3 us  [project(): jnp.dot(block, weights[name], preferred_element_type=F32).astype(kind)]
    ppermute x4 -> x5, waiting for transfers between devices: 10 us -> 15.7 us  [shift_req(): lax.ppermute(block, 'req', [(i, (i + step) % count) for i in range(count)])]
    unnamed x58 -> x64, local copies, waits for them, and re-layouts: 20.1 us -> 24 us
    another operation x2, other arithmetic: 0.18 us -> 2.31 us  [the longest x1 1.19 us: on_device(): own_pair = after(jnp.stack([own_block, own_z]), both)]
    ppermute x4 -> x5, starting transfers between devices: 7.97 us -> 9.57 us  [shift_req(): lax.ppermute(block, 'req', [(i, (i + step) % count) for i in range(count)])]
    ppermute x9 -> x10, starting transfers between devices: 7.25 us -> 6.48 us  [partner_2(): return lax.ppermute(block, axis, route)]
    ppermute x9 -> x10, waiting for transfers between devices: 6.28 us -> 5.85 us  [partner_2(): return lax.ppermute(block, axis, route)]
  transfers between devices with their start and end apart: 15 -> 17, of which waited for: 4 -> 5; matrix products, arithmetic and copies ran while one was open for 47% -> 32% of each run, Pallas kernels for 12% -> 13%
where the time goes in v10:
time: 124 us
  local copies, waits for them, and re-layouts  28 us (23%)
  Pallas kernels  26.9 us (22%)
  waiting for transfers between devices  21.5 us (17%)
  starting transfers between devices  20.8 us (17%)
  matrix products  18.3 us (15%)
  other arithmetic  6.93 us (6%)
    unnamed x64, local copies, waits for them, and re-layouts  24 us
    dot_general x6, matrix products, project(): jnp.dot(block, weights[name], preferred_element_type=F32).astype(kind)  18.3 us
    ppermute x5, waiting for transfers between devices, shift_req(): lax.ppermute(block, 'req', [(i, (i + step) % count) for i in range(count)])  15.7 us
    pallas_call x2, Pallas kernels, stage(): pl.pallas_call(functools.partial(stage_kernel, which), out_shape=jax.Shap...  9.82 us
    ppermute x5, starting transfers between devices, shift_req(): lax.ppermute(block, 'req', [(i, (i + step) % count) for i in range(count)])  9.57 us
    pallas_call x1, Pallas kernels, mixer(): pl.pallas_call(functools.partial(mixer_kernel, count_req, len(got)), out_...  7.73 us
    ppermute x10, starting transfers between devices, partner_2(): return lax.ppermute(block, axis, route)  6.48 us
    ppermute x10, waiting for transfers between devices, partner_2(): return lax.ppermute(block, axis, route)  5.85 us
  transfers between devices with their start and end apart: 17, of which 5 were waited for; matrix products, arithmetic and copies ran while one was open for 32% of the time, Pallas kernels for 13%

profile of v10, /device:TPU:0, one launch (start us, length us, event | category | flops | bytes accessed | tf_op | source)
XLA Modules:
  0.0 123.6 jit_solution(10518776388853957277)
XLA Ops:
  0.6 4.1 %collective-permute-start = (bf16[256,512]{1,0:T(8,128)(2,1)}, bf16[256,512]{1,0:T(8,128)(2,1)S(1)}, u32[]{:S(2)}, u32[]{:S(2)}) collective-permute-start(bf16[256,512]{1,0:T(8,128)(2,1)} %param.20), channel_id=1, source_target_pairs={{0,16},{1,0},{2,18},{3,2},{4,20},{5,4},{6,22},{7,6},{8,24},{9,8},{... | collective-permute-start | bytes 786440 | tf_op jit(solution)/shard_map/ppermute | solution.py:91
  6.2 2.8 %shard_map.204 = bf16[2,1024,256]{2,1,0:T(8,128)(2,1)} custom-call(s32[2]{0:T(128)S(1)} %get-tuple-element.36.slots_ref, f32[8,16,64,256]{3,2,1,0:T(8,128)} %pool_ref.3), custom_call_target="tpu_custom_call" | custom-call | bytes 3145728 | tf_op jit(solution)/shard_map/pallas_call | solution.py:247
  9.0 4.4 %collective-permute-start.4 = (bf16[2,1024,256]{2,1,0:T(8,128)(2,1)}, bf16[2,1024,256]{2,1,0:T(8,128)(2,1)}, u32[]{:S(2)}, u32[]{:S(2)}) collective-permute-start(bf16[2,1024,256]{2,1,0:T(8,128)(2,1)} %shard_map.204), channel_id=1, source_target_pairs={{0,1},{1,0},{2,3},{3,2},{4,5},{5,4},{6,7},{7,6},{8,9},{9,8},{10,11... | collective-permute-start | bytes 3145736 | tf_op jit(solution)/shard_map/ppermute | solution.py:41
  13.4 16.5 %copy.34 = bf16[4096,2,1024]{2,0,1:T(8,128)(2,1)} copy(bf16[4096,2,1024]{2,1,0:T(2,128)(2,1)} %param.21) | data formatting | bytes 33554432 | tf_op args[1]
  29.9 1.6 %collective-permute-start.3 = (bf16[256,512]{1,0:T(8,128)(2,1)S(1)}, bf16[256,512]{1,0:T(8,128)(2,1)S(1)}, u32[]{:S(2)}, u32[]{:S(2)}) collective-permute-start(bf16[256,512]{1,0:T(8,128)(2,1)S(1)} %get-tuple-element.32), channel_id=1, source_target_pairs={{0,8},{8,0},{2,10},{10,2},{4,12},{12,4},{6,14},{14,6},{16,24},{24,... | collective-permute-start | bytes 786440 | tf_op jit(solution)/shard_map/ppermute | solution.py:36
  31.6 1.5 %collective-permute-start.7 = (bf16[256,512]{1,0:T(8,128)(2,1)S(1)}, bf16[256,512]{1,0:T(8,128)(2,1)S(1)}, u32[]{:S(2)}, u32[]{:S(2)}) collective-permute-start(bf16[256,512]{1,0:T(8,128)(2,1)S(1)} %get-tuple-element.32), channel_id=1, source_target_pairs={{0,4},{4,0},{2,6},{6,2},{8,12},{12,8},{10,14},{14,10},{16,20},{20,... | collective-permute-start | bytes 786440 | tf_op jit(solution)/shard_map/ppermute | solution.py:36
  33.5 2.0 %shard_map.203.refs_13_ = f32[2,16,64,256]{3,2,1,0:T(8,128)S(1)} custom-call(s32[2]{0:T(128)S(1)} %get-tuple-element.33.slots_ref, f32[8,16,64,256]{3,2,1,0:T(8,128)} %pool_ref.3), custom_call_target="tpu_custom_call" | custom-call | bytes 3145728 | tf_op jit(solution)/shard_map/pallas_call | solution.py:247
  40.6 1.4 %collective-permute-start.6 = (bf16[256,512]{1,0:T(8,128)(2,1)}, bf16[256,512]{1,0:T(8,128)(2,1)S(1)}, u32[]{:S(2)}, u32[]{:S(2)}) collective-permute-start(bf16[256,512]{1,0:T(8,128)(2,1)} %copy-done.19), channel_id=1, source_target_pairs={{0,4},{4,0},{2,6},{6,2},{8,12},{12,8},{10,14},{14,10},{16,20},{20,... | collective-permute-start | bytes 786440 | tf_op jit(solution)/shard_map/ppermute | solution.py:36
  42.0 3.4 %shard_map.206 = bf16[4096,1024]{1,0:T(8,128)(2,1)S(1)} custom-call(bf16[2,4096,1024]{2,1,0:T(8,128)(2,1)} %bitcast.31, bf16[3,256,512]{2,1,0:T(8,128)(2,1)S(1)} %pad_maximum_fusion.5._.refs_0_), custom_call_target="tpu_custom_call" | custom-call | bytes 8388608 | tf_op jit(solution)/shard_map/pallas_call | solution.py:127
  45.4 6.4 %shard_map.205 = bf16[4096,1024]{1,0:T(8,128)(2,1)S(1)} custom-call(bf16[2,4096,1024]{2,1,0:T(8,128)(2,1)} %bitcast.32, bf16[3,256,512]{2,1,0:T(8,128)(2,1)S(1)} %pad_maximum_fusion.5._.refs_0_), custom_call_target="tpu_custom_call" | custom-call | bytes 8388608 | tf_op jit(solution)/shard_map/pallas_call | solution.py:127
  54.0 1.4 %constant_dynamic-update-slice_fusion.1 = bf16[4,256,512]{2,1,0:T(8,128)(2,1)} fusion(bf16[2,256,512]{2,1,0:T(8,128)(2,1)S(1)} %pad_maximum_fusion.6), kind=kLoop, calls=%fused_computation.30 | loop fusion | bytes 1048576
  56.8 3.1 %convolution_convert_fusion.1 = bf16[256,1024]{1,0:T(8,128)(2,1)} fusion(bf16[256,4096]{1,0:T(8,128)(2,1)S(1)} %shard_map.207, bf16[4096,1024]{1,0:T(8,128)(2,1)S(1)} %shard_map.205), kind=kOutput, calls=%fused_computation.7 | convolution fusion | flops 2147745792 | bytes 11010048 | tf_op jit(solution)/shard_map/dot_general | solution.py:501
  61.2 2.5 %collective-permute-start.12 = (bf16[256,1024]{1,0:T(8,128)(2,1)}, bf16[256,1024]{1,0:T(8,128)(2,1)}, u32[]{:S(2)}, u32[]{:S(2)}) collective-permute-start(bf16[256,1024]{1,0:T(8,128)(2,1)} %convolution_convert_fusion.1), channel_id=1, source_target_pairs={{0,1},{1,0},{2,3},{3,2},{4,5},{5,4},{6,7},{7,6},{8,9},{9,8},{10,11... | collective-permute-start | bytes 1572872 | tf_op jit(solution)/shard_map/ppermute | solution.py:41
  63.6 4.0 %collective-permute-done.8 = bf16[2,256,512]{2,1,0:T(8,128)(2,1)S(1)} collective-permute-done((bf16[2,256,512]{2,1,0:T(8,128)(2,1)S(1)}, bf16[2,256,512]{2,1,0:T(8,128)(2,1)S(1)}, u32[]{:S(2)}, u32[]{:S(2)}) %collective-permute-start.8) | collective-permute-done | bytes 524320 | tf_op jit(solution)/shard_map/ppermute | solution.py:36
  68.5 3.1 %convolution_convert_fusion = bf16[256,1024]{1,0:T(8,128)(2,1)} fusion(bf16[256,4096]{1,0:T(8,128)(2,1)S(1)} %shard_map.207, bf16[4096,1024]{1,0:T(8,128)(2,1)S(1)} %shard_map.206), kind=kOutput, calls=%fused_computation.6 | convolution fusion | flops 2147745792 | bytes 11010048 | tf_op jit(solution)/shard_map/dot_general | solution.py:501
  71.6 2.4 %collective-permute-start.14 = (bf16[256,1024]{1,0:T(8,128)(2,1)}, bf16[256,1024]{1,0:T(8,128)(2,1)}, u32[]{:S(2)}, u32[]{:S(2)}) collective-permute-start(bf16[256,1024]{1,0:T(8,128)(2,1)} %convolution_convert_fusion), channel_id=1, source_target_pairs={{0,1},{1,0},{2,3},{3,2},{4,5},{5,4},{6,7},{7,6},{8,9},{9,8},{10,11... | collective-permute-start | bytes 1572872 | tf_op jit(solution)/shard_map/ppermute | solution.py:41
  75.6 15.5 %collective-permute-done.13.refs_0_ = bf16[256,272]{1,0:T(8,128)(2,1)S(1)} collective-permute-done((bf16[256,272]{1,0:T(8,128)(2,1)S(1)}, bf16[256,272]{1,0:T(8,128)(2,1)S(1)}, u32[]{:S(2)}, u32[]{:S(2)}) %collective-permute-start.13) | collective-permute-done | bytes 139296 | tf_op jit(solution)/shard_map/ppermute | solution.py:41
  91.7 1.5 %shard_map.208 = bf16[256,4096]{1,0:T(8,128)(2,1)S(1)} custom-call(s32[8]{0:T(128)S(1)} %broadcast_xor_fusion.places_ref, bf16[4,256,512]{2,1,0:T(8,128)(2,1)} %constant_dynamic-update-slice_fusion.refs_0_, bf16[4,256,512]{2,1,0:T(8,128)(2,1)S(1)} %collective-permute-done.11.refs_1_), custom_call_target="tpu_custom_call" | custom-call | flops 1000000 | bytes 10000 | tf_op jit(solution)/shard_map/pallas_call | solution.py:73
  93.3 1.9 %fusion = f32[256,272]{0,1:T(8,128)} fusion(bf16[256,4096]{1,0:T(8,128)(2,1)S(1)} %shard_map.208, bf16[4096,16]{1,0:T(8,128)(2,1)S(1)} %copy-done.17, bf16[4096,256]{1,0:T(8,128)(2,1)S(1)} %copy-done.28), kind=kOutput, calls=%fused_computation.2 | convolution fusion | flops 574881792 | bytes 4603904 | tf_op jit(solution)/shard_map/dot_general | solution.py:501
  96.3 2.3 %fusion.14.refs_0_ = f32[256,1024]{1,0:T(8,128)S(1)} fusion(bf16[256,4096]{1,0:T(8,128)(2,1)S(1)} %shard_map.208, bf16[4096,1024]{1,0:T(8,128)(2,1)S(1)} %copy-done.2), kind=kOutput, calls=%fused_computation.51 | convolution fusion | flops 2147483648 | bytes 11534336 | tf_op jit(solution)/shard_map/dot_general | solution.py:501
  103.3 1.8 %shard_map.209 = (bf16[256,256]{1,0:T(8,128)(2,1)S(1)}, f32[4,256,4]{2,1,0:T(8,128)S(1)}, f32[4,4,256]{2,1,0:T(4,128)S(1)}, f32[4,4,256]{2,1,0:T(4,128)S(1)}, f3...) custom-call(s32[1,2]{1,0:T(1,128)S(1)} %copy-done.11, f32[256,272]{1,0:T(8,128)S(1)} %copy.31.own_ref, ...), custom_call_target="tpu_custom_call" | custom-call | flops 1000000 | bytes 10000 | tf_op jit(solution)/shard_map/pallas_call | solution.py:223
  105.3 6.5 %fusion.15 = f32[256,1024]{1,0:T(8,128)S(1)} fusion(bf16[256,4096]{1,0:T(8,128)(2,1)} %copy-done.3, bf16[4096,1024]{1,0:T(8,128)(2,1)} %copy-done), kind=kOutput, calls=%fused_computation.52 | convolution fusion | flops 2147483648 | bytes 11534336 | tf_op jit(solution)/shard_map/dot_general | solution.py:501
  112.0 7.7 %shard_map.210 = (f32[256,1024]{1,0:T(8,128)S(1)}, f32[2,16,64,256]{3,2,1,0:T(8,128)}) custom-call(s32[2,2]{1,0:T(2,128)S(1)} %copy-done.10, s32[2]{0:T(128)S(1)} %bitcast.27, f32[256,1024]{1,0:T(8,128)S(1)} %fusion.14.refs_0_, bf16[256,1024]{1,0:T(8,128)(2,1)} %collective-permute-done.12.refs_1_, f32[2,3,1024]{2,1,0:T(4,128)S(1)} %copy-done.6, ...), custom_call_target="tpu_custom_call" | custom-call | flops 1000000 | bytes 10000 | tf_op jit(solution)/shard_map/pallas_call | solution.py:373
  119.7 1.5 %multiply_reduce_fusion = (f32[256]{0:T(256)S(1)}, f32[256,1024]{1,0:T(8,128)S(1)}) fusion(f32[256,1024]{1,0:T(8,128)S(1)} %get-tuple-element.58, f32[256,1024]{1,0:T(8,128)S(1)} %fusion.15, bf16[256,1024]{1,0:T(8,128)(2,1)} %collective-permute-done.14), kind=kLoop, calls=%fused_computation.14 | loop fusion | flops 2883328 | bytes 3671040 | tf_op jit(solution)/shard_map/reduce_sum | solution.py:554
  (113 shorter events, 23.2 us)
Async XLA Ops:
  0.6 29.2 %collective-permute-start = (bf16[256,512]{1,0:T(8,128)(2,1)}, bf16[256,512]{1,0:T(8,128)(2,1)S(1)}, u32[]{:S(2)}, u32[]{:S(2)}) collective-permute-start(bf16[256,512]{1,0:T(8,128)(2,1)} %param.20), channel_id=1, source_target_pairs={{0,16},{1,0},{2,18},{3,2},{4,20},{5,4},{6,22},{7,6},{8,24},{9,8},{... | collective-permute-start | bytes 786440 | tf_op jit(solution)/shard_map/ppermute | solution.py:91
  4.7 25.2 %collective-permute-start.1 = (bf16[256,512]{1,0:T(8,128)(2,1)}, bf16[256,512]{1,0:T(8,128)(2,1)S(1)}, u32[]{:S(2)}, u32[]{:S(2)}) collective-permute-start(bf16[256,512]{1,0:T(8,128)(2,1)} %param.20), channel_id=1, source_target_pairs={{1,16},{3,18},{5,20},{7,22},{9,24},{11,26},{13,28},{15,30},{16,1},... | collective-permute-start | bytes 786440 | tf_op jit(solution)/shard_map/ppermute | solution.py:92
  9.0 31.6 %collective-permute-start.4 = (bf16[2,1024,256]{2,1,0:T(8,128)(2,1)}, bf16[2,1024,256]{2,1,0:T(8,128)(2,1)}, u32[]{:S(2)}, u32[]{:S(2)}) collective-permute-start(bf16[2,1024,256]{2,1,0:T(8,128)(2,1)} %shard_map.204), channel_id=1, source_target_pairs={{0,1},{1,0},{2,3},{3,2},{4,5},{5,4},{6,7},{7,6},{8,9},{9,8},{10,11... | collective-permute-start | bytes 3145736 | tf_op jit(solution)/shard_map/ppermute | solution.py:41
  13.4 16.5 %copy-start.18 = (bf16[256,512]{1,0:T(8,128)(2,1)S(1)}, bf16[256,512]{1,0:T(8,128)(2,1)}, u32[]{:S(2)}) copy-start(bf16[256,512]{1,0:T(8,128)(2,1)} %param.20) | copy-start | bytes 786436
  13.4 19.8 %copy-start.22 = (bf16[8,3,1024]{2,0,1:T(8,128)(2,1)S(1)}, bf16[8,3,1024]{2,0,1:T(8,128)(2,1)}, u32[]{:S(2)}) copy-start(bf16[8,3,1024]{2,0,1:T(8,128)(2,1)} %param.36) | copy-start | bytes 147460
  13.4 19.9 %copy-start.23 = (bf16[8,3,256]{2,0,1:T(8,128)(2,1)S(1)}, bf16[8,3,256]{2,0,1:T(8,128)(2,1)}, u32[]{:S(2)}) copy-start(bf16[8,3,256]{2,0,1:T(8,128)(2,1)} %param.37) | copy-start | bytes 36868
  29.9 7.6 %collective-permute-start.3 = (bf16[256,512]{1,0:T(8,128)(2,1)S(1)}, bf16[256,512]{1,0:T(8,128)(2,1)S(1)}, u32[]{:S(2)}, u32[]{:S(2)}) collective-permute-start(bf16[256,512]{1,0:T(8,128)(2,1)S(1)} %get-tuple-element.32), channel_id=1, source_target_pairs={{0,8},{8,0},{2,10},{10,2},{4,12},{12,4},{6,14},{14,6},{16,24},{24,... | collective-permute-start | bytes 786440 | tf_op jit(solution)/shard_map/ppermute | solution.py:36
  31.6 6.9 %collective-permute-start.7 = (bf16[256,512]{1,0:T(8,128)(2,1)S(1)}, bf16[256,512]{1,0:T(8,128)(2,1)S(1)}, u32[]{:S(2)}, u32[]{:S(2)}) collective-permute-start(bf16[256,512]{1,0:T(8,128)(2,1)S(1)} %get-tuple-element.32), channel_id=1, source_target_pairs={{0,4},{4,0},{2,6},{6,2},{8,12},{12,8},{10,14},{14,10},{16,20},{20,... | collective-permute-start | bytes 786440 | tf_op jit(solution)/shard_map/ppermute | solution.py:36
  33.4 8.6 %copy-start.29 = (s32[2]{0:T(128)S(1)}, s32[2]{0:T(128)}, u32[]{:S(2)}) copy-start(s32[2]{0:T(128)} %param.33) | copy-start | bytes 28
  36.8 3.8 %collective-permute-start.5 = (bf16[2,3,1280]{2,1,0:T(4,128)(2,1)S(1)}, bf16[2,3,1280]{2,1,0:T(4,128)(2,1)S(1)}, u32[]{:S(2)}, u32[]{:S(2)}) collective-permute-start(bf16[2,3,1280]{2,1,0:T(4,128)(2,1)S(1)} %pad_maximum_fusion.7), channel_id=1, source_target_pairs={{0,1},{1,0},{2,3},{3,2},{4,5},{5,4},{6,7},{7,6},{8,9},{9,8},{10,11... | collective-permute-start | bytes 46088 | tf_op jit(solution)/shard_map/ppermute | solution.py:41
  37.1 14.8 %collective-permute-start.2 = (bf16[256,512]{1,0:T(8,128)(2,1)S(1)}, bf16[256,512]{1,0:T(8,128)(2,1)}, u32[]{:S(2)}, u32[]{:S(2)}) collective-permute-start(bf16[256,512]{1,0:T(8,128)(2,1)S(1)} %get-tuple-element.34), channel_id=1, source_target_pairs={{0,8},{8,0},{2,10},{10,2},{4,12},{12,4},{6,14},{14,6},{16,24},{24,... | collective-permute-start | bytes 786440 | tf_op jit(solution)/shard_map/ppermute | solution.py:36
  40.3 15.1 %collective-permute-start.9 = (bf16[3,256,512]{2,1,0:T(8,128)(2,1)S(1)}, bf16[3,256,512]{2,1,0:T(8,128)(2,1)}, u32[]{:S(2)}, u32[]{:S(2)}) collective-permute-start(bf16[3,256,512]{2,1,0:T(8,128)(2,1)S(1)} %pad_maximum_fusion.5._.refs_0_), channel_id=1, source_target_pairs={{0,2},{2,0},{4,6},{6,4},{8,10},{10,8},{12,14},{14,12},{16,18},{18,... | collective-permute-start | bytes 2359304 | tf_op jit(solution)/shard_map/ppermute | solution.py:36
  40.6 11.3 %collective-permute-start.6 = (bf16[256,512]{1,0:T(8,128)(2,1)}, bf16[256,512]{1,0:T(8,128)(2,1)S(1)}, u32[]{:S(2)}, u32[]{:S(2)}) collective-permute-start(bf16[256,512]{1,0:T(8,128)(2,1)} %copy-done.19), channel_id=1, source_target_pairs={{0,4},{4,0},{2,6},{6,2},{8,12},{12,8},{10,14},{14,10},{16,20},{20,... | collective-permute-start | bytes 786440 | tf_op jit(solution)/shard_map/ppermute | solution.py:36
  45.4 23.1 %copy-start = (bf16[4096,1024]{1,0:T(8,128)(2,1)}, bf16[4096,1024]{1,0:T(8,128)(2,1)S(1)}, u32[]{:S(2)}) copy-start(bf16[4096,1024]{1,0:T(8,128)(2,1)S(1)} %shard_map.206) | copy-start | bytes 25165828
  51.9 3.5 %collective-permute-start.10 = (bf16[1,256,512]{2,1,0:T(8,128)(2,1)S(1)}, bf16[1,256,512]{2,1,0:T(8,128)(2,1)S(1)}, u32[]{:S(2)}, u32[]{:S(2)}) collective-permute-start(bf16[1,256,512]{2,1,0:T(8,128)(2,1)S(1)} %bitcast.24), channel_id=1, source_target_pairs={{0,2},{2,0},{4,6},{6,4},{8,10},{10,8},{12,14},{14,12},{16,18},{18,... | collective-permute-start | bytes 786440 | tf_op jit(solution)/shard_map/ppermute | solution.py:36
  53.4 14.3 %collective-permute-start.8 = (bf16[2,256,512]{2,1,0:T(8,128)(2,1)S(1)}, bf16[2,256,512]{2,1,0:T(8,128)(2,1)S(1)}, u32[]{:S(2)}, u32[]{:S(2)}) collective-permute-start(bf16[2,256,512]{2,1,0:T(8,128)(2,1)S(1)} %pad_maximum_fusion.6), channel_id=1, source_target_pairs={{0,4},{4,0},{2,6},{6,2},{8,12},{12,8},{10,14},{14,10},{16,20},{20,... | collective-permute-start | bytes 1572872 | tf_op jit(solution)/shard_map/ppermute | solution.py:36
  61.2 30.6 %collective-permute-start.12 = (bf16[256,1024]{1,0:T(8,128)(2,1)}, bf16[256,1024]{1,0:T(8,128)(2,1)}, u32[]{:S(2)}, u32[]{:S(2)}) collective-permute-start(bf16[256,1024]{1,0:T(8,128)(2,1)} %convolution_convert_fusion.1), channel_id=1, source_target_pairs={{0,1},{1,0},{2,3},{3,2},{4,5},{5,4},{6,7},{7,6},{8,9},{9,8},{10,11... | collective-permute-start | bytes 1572872 | tf_op jit(solution)/shard_map/ppermute | solution.py:41
  68.5 23.2 %collective-permute-start.11 = (bf16[4,256,512]{2,1,0:T(8,128)(2,1)}, bf16[4,256,512]{2,1,0:T(8,128)(2,1)S(1)}, u32[]{:S(2)}, u32[]{:S(2)}) collective-permute-start(bf16[4,256,512]{2,1,0:T(8,128)(2,1)} %constant_dynamic-update-slice_fusion.refs_0_), channel_id=1, source_target_pairs={{0,2},{2,0},{4,6},{6,4},{8,10},{10,8},{12,14},{14,12},{16,18},{18,... | collective-permute-start | bytes 3145736 | tf_op jit(solution)/shard_map/ppermute | solution.py:36
  71.6 20.1 %collective-permute-start.14 = (bf16[256,1024]{1,0:T(8,128)(2,1)}, bf16[256,1024]{1,0:T(8,128)(2,1)}, u32[]{:S(2)}, u32[]{:S(2)}) collective-permute-start(bf16[256,1024]{1,0:T(8,128)(2,1)} %convolution_convert_fusion), channel_id=1, source_target_pairs={{0,1},{1,0},{2,3},{3,2},{4,5},{5,4},{6,7},{7,6},{8,9},{9,8},{10,11... | collective-permute-start | bytes 1572872 | tf_op jit(solution)/shard_map/ppermute | solution.py:41
  74.8 18.5 %copy-start.17 = (bf16[4096,16]{1,0:T(8,128)(2,1)S(1)}, bf16[4096,16]{1,0:T(8,128)(2,1)}, u32[]{:S(2)}) copy-start(bf16[4096,16]{1,0:T(8,128)(2,1)} %copy.29) | copy-start | bytes 393220
  74.8 18.5 %copy-start.28 = (bf16[4096,256]{1,0:T(8,128)(2,1)S(1)}, bf16[4096,256]{1,0:T(8,128)(2,1)}, u32[]{:S(2)}) copy-start(bf16[4096,256]{1,0:T(8,128)(2,1)} %param.23) | copy-start | bytes 6291460
  74.8 16.2 %collective-permute-start.13 = (bf16[256,272]{1,0:T(8,128)(2,1)S(1)}, bf16[256,272]{1,0:T(8,128)(2,1)S(1)}, u32[]{:S(2)}, u32[]{:S(2)}) collective-permute-start(bf16[256,272]{1,0:T(8,128)(2,1)S(1)} %fusion.2), channel_id=1, source_target_pairs={{0,1},{1,0},{2,3},{3,2},{4,5},{5,4},{6,7},{7,6},{8,9},{9,8},{10,11... | collective-permute-start | bytes 417800 | tf_op jit(solution)/shard_map/ppermute | solution.py:41
  105.2 6.6 %collective-permute-start.15 = (bf16[256,256]{1,0:T(8,128)(2,1)S(1)}, bf16[256,256]{1,0:T(8,128)(2,1)S(1)}, u32[]{:S(2)}, u32[]{:S(2)}) collective-permute-start(bf16[256,256]{1,0:T(8,128)(2,1)S(1)} %get-tuple-element.51), channel_id=1, source_target_pairs={{0,2},{2,0},{4,6},{6,4},{8,10},{10,8},{12,14},{14,12},{16,18},{18,... | collective-permute-start | bytes 393224 | tf_op jit(solution)/shard_map/ppermute | solution.py:36
  121.2 1.4 %collective-permute-start.16 = (f32[256]{0:T(256)S(1)}, f32[256]{0:T(256)S(1)}, u32[]{:S(2)}, u32[]{:S(2)}) collective-permute-start(f32[256]{0:T(256)S(1)} %get-tuple-element.66), channel_id=1, source_target_pairs={{0,2},{2,0},{4,6},{6,4},{8,10},{10,8},{12,14},{14,12},{16,18},{18,... | collective-permute-start | bytes 3080 | tf_op jit(solution)/shard_map/ppermute | solution.py:36
  (24 other events, 90.7 us)

commit v11 on v10

--- a/solution.py
+++ b/solution.py
@@ -14,7 +14,6 @@
 BF16 = jnp.bfloat16
 HIGH = lax.Precision.HIGHEST
 VMEM_BYTES = 16 * 1024 * 1024
-LARGE_BYTES = 40 * 1024 * 1024
 HEADS_STEP = 4
 
 
@@ -115,24 +114,6 @@
     return lax.optimization_barrier(
         with_layout_constraint(array, Layout(tuple(range(array.ndim))))
     )
-
-
-def stage_kernel(which, w_ref, _, out_ref, sem):
-    copy = pltpu.make_async_copy(w_ref.at[which], out_ref, sem)
-    copy.start()
-    copy.wait()
-
-
-def stage(w_pair, which, behind):
-    return pl.pallas_call(
-        functools.partial(stage_kernel, which),
-        out_shape=jax.ShapeDtypeStruct(w_pair.shape[1:], w_pair.dtype),
-        in_specs=[pl.BlockSpec(memory_space=pl.ANY)] * 2,
-        out_specs=pl.BlockSpec(memory_space=pltpu.VMEM),
-        scratch_shapes=[pltpu.SemaphoreType.DMA],
-        compiler_params=params(LARGE_BYTES),
-        cost_estimate=cost(0, 2 * w_pair.shape[1] * w_pair.shape[2]),
-    )(w_pair, behind)
 
 
 def token_places(starts, count_tok, shape, axis):
@@ -444,11 +425,12 @@
         ]
         return jnp.concatenate(parts, 2)
 
-    got_states = []
+    got_states, got_conv = [], []
     for step in range(1, req_count):
         slots = slots_of((me + step) % req_count)
         packed = pack(ssm_pool, slots, (heads * head_width, state), BF16)
         got_states.append(shift_req(packed, step))
+        got_conv.append(shift_req(conv_of(slots), step))
     own_slots = slots_of(me)
     asked = lax.dynamic_slice_in_dim(state_slot, me * group_reqs, group_reqs)
     came_from = (me - asked // slot_count) % req_count
@@ -457,69 +439,54 @@
         jnp.int32
     )
 
-    w_pair = jnp.transpose(w_xz, (1, 0, 2))
     w_step = w_dt
     if direct:
-        w_pair = pinned(w_pair)
-        block = after(block, w_pair)
+        block = after(block, packed)
         along_z = partner_2(block, "wide", 2)
         along_x = partner_2(block, "wide", 1)
         w_step = pinned(after(w_dt, block))
         own_slots = after(own_slots, block)
     held = pack(ssm_pool, own_slots, (heads, head_width, state), F32)
-    got_conv = []
-    for step in range(1, req_count):
-        slots = slots_of((me + step) % req_count)
-        if direct:
-            slots = after(slots, block)
-        got_conv.append(shift_req(conv_of(slots), step))
-
     if direct:
         near_three = after(jnp.stack([block, along_z, along_x]), held, w_step)
-        both = partner_2(after(along_z, held, w_step, *got_states, *got_conv), "wide", 1)
+        both = partner_2(after(along_z, held, w_step), "wide", 1)
         core_three = partner_2(near_three, "wide", 0)
         own_block = after(own_block, held)
         own_z = partner_2(own_block, "wide", 2)
-        w_xr = stage(w_pair, 1, near_three)
-        w_z = stage(w_pair, 0, near_three)
-        both = after(both[None], own_z, w_xr, w_z)
+        both = after(both[None], own_z)
         core_both = partner_2(both, "wide", 0)
         own_pair = after(jnp.stack([own_block, own_z]), both)
         own_got = partner_2(own_pair, "wide", 1)
+        core_both = after(core_both, *got_states, *got_conv)
         theirs = quad_arrange(
             [near_three, both, core_three, core_both], [0, 4, 2, 6, 1, 5, 3, 7]
         )
         features = [own_got, theirs]
     else:
         features = features_in_general(x_in)
-        w_z, w_xr = w_pair[0], w_pair[1]
     w_map = jnp.concatenate([w_bc, w_step], 1)
 
-    weights = {"xr": w_xr, "map": w_map, "z": w_z}
-
-    def project(block, name, kind):
-        return jnp.dot(block, weights[name], preferred_element_type=F32).astype(kind)
-
-    came = {"xr": [], "map": [], "z": []}
-    done, parts = [], {}
+    def project(block, kind):
+        low = jnp.dot(block, w_map, preferred_element_type=F32).astype(kind)
+        low, block = lax.optimization_barrier((low, block))
+        high = jnp.einsum("td,dkc->ktc", block, w_xz, preferred_element_type=F32)
+        return {"map": low, "xr": high[1].astype(kind), "z": high[0].astype(kind)}
+
+    came = {"map": [], "xr": [], "z": []}
+    parts = []
     for step in range(1, req_count):
-        block = features[step]
+        part = lax.optimization_barrier(project(features[step], BF16))
         for name in came:
-            part, block = lax.optimization_barrier((project(block, name, BF16), block))
-            parts[name] = part
-            part = shift_req(part, step)
-            came[name].append(part)
-            done.append(part)
+            came[name].append(shift_req(part[name], step))
+        parts.append(part)
     block = features[0]
     if direct:
-        own_four = jnp.concatenate([own_pair, after(block, parts["xr"])], 0)
-        own_core = after(partner_2(own_four, "wide", 0), *done, *came["map"])
+        own_four = jnp.concatenate([own_pair, after(block, *parts)], 0)
+        own_core = partner_2(own_four, "wide", 0)
         block = quad_arrange([own_four, own_core], [0, 4, 2, 6, 1, 5, 3, 7])
     else:
-        block = after(block, *done)
-    own = {}
-    for name in ("map", "xr", "z"):
-        own[name], block = lax.optimization_barrier((project(block, name, F32), block))
+        block = after(block, *parts)
+    own = lax.optimization_barrier(project(block, F32))
 
     cache = conv_of(own_slots)
     for step in range(1, req_count):

time: 124 us -> 98.9 us (0.80)
  local copies, waits for them, and re-layouts: 28 us -> 9.76 us
  Pallas kernels: 26.9 us -> 16.7 us
  matrix products: 18.3 us -> 27.1 us
  waiting for transfers between devices: 21.5 us -> 13.1 us
  starting transfers between devices: 20.8 us -> 25.1 us
  other arithmetic: 6.93 us -> 5.49 us
    unnamed x64 -> x47, local copies, waits for them, and re-layouts: 24 us -> 4.16 us
    ppermute x5, waiting for transfers between devices: 15.7 us -> 2.42 us  [shift_req(): lax.ppermute(block, 'req', [(i, (i + step) % count) for i in range(count)])]
    pallas_call x2 -> x0, Pallas kernels: 9.82 us -> none  [stage(): pl.pallas_call(functools.partial(stage_kernel, which), out_shape=jax.Shap...]
    dot_general x6 -> x4, matrix products: 18.3 us -> 27.1 us  [the longest x2 23.3 us: project(): high = jnp.einsum('td,dkc->ktc', block, w_xz, preferred_element_type=F32)]
    ppermute x10, waiting for transfers between devices: 5.85 us -> 10.7 us  [partner_2(): return lax.ppermute(block, axis, route)]
    ppermute x5, starting transfers between devices: 9.57 us -> 12.3 us  [shift_req(): lax.ppermute(block, 'req', [(i, (i + step) % count) for i in range(count)])]
    ppermute x10, starting transfers between devices: 6.48 us -> 8.08 us  [partner_2(): return lax.ppermute(block, axis, route)]
  transfers between devices with their start and end apart: 17 -> 17, of which waited for: 5 -> 5; matrix products, arithmetic and copies ran while one was open for 32% -> 36% of each run, Pallas kernels for 13% -> 17%
where the time goes in v11:
time: 98.9 us; the launch traced here: 98.4 us
  matrix products  27.1 us (27%)
  starting transfers between devices  25.1 us (25%)
  Pallas kernels  16.7 us (17%)
  waiting for transfers between devices  13.1 us (13%)
  local copies, waits for them, and re-layouts  9.76 us (10%)
  other arithmetic  5.49 us (6%)
  between operations  1.04 us (1%)
    dot_general x2, matrix products, project(): high = jnp.einsum('td,dkc->ktc', block, w_xz, preferred_element_type=F32)  23.3 us
    ppermute x5, starting transfers between devices, shift_req(): lax.ppermute(block, 'req', [(i, (i + step) % count) for i in range(count)])  12.3 us
    ppermute x10, waiting for transfers between devices, partner_2(): return lax.ppermute(block, axis, route)  10.7 us
    ppermute x10, starting transfers between devices, partner_2(): return lax.ppermute(block, axis, route)  8.08 us
    pallas_call x1, Pallas kernels, mixer(): pl.pallas_call(functools.partial(mixer_kernel, count_req, len(got)), out_...  7.7 us
    pallas_call x2, Pallas kernels, pack(): pl.pallas_call(pack_kernel, out_shape=jax.ShapeDtypeStruct((count_req,) +...  4.74 us
    unnamed x47, local copies, waits for them, and re-layouts  4.16 us
    ppermute x1, starting transfers between devices, near_blocks(): first = lax.ppermute(x_in, axes, first)  4.09 us
  transfers between devices with their start and end apart: 17, of which 5 were waited for; matrix products, arithmetic and copies ran while one was open for 36% of the time, Pallas kernels for 17%

profile of v11, /device:TPU:0, one launch (start us, length us, event | category | flops | bytes accessed | tf_op | source)
XLA Modules:
  0.0 98.4 jit_solution(7114915495762476378)
XLA Ops:
  0.6 4.1 %collective-permute-start = (bf16[256,512]{1,0:T(8,128)(2,1)}, bf16[256,512]{1,0:T(8,128)(2,1)S(1)}, u32[]{:S(2)}, u32[]{:S(2)}) collective-permute-start(bf16[256,512]{1,0:T(8,128)(2,1)} %param.20), channel_id=1, source_target_pairs={{0,16},{1,0},{2,18},{3,2},{4,20},{5,4},{6,22},{7,6},{8,24},{9,8},{... | collective-permute-start | bytes 786440 | tf_op jit(solution)/shard_map/ppermute | solution.py:90
  6.2 2.8 %shard_map.203 = bf16[2,1024,256]{2,1,0:T(8,128)(2,1)} custom-call(s32[2]{0:T(128)S(1)} %get-tuple-element.76.slots_ref, f32[8,16,64,256]{3,2,1,0:T(8,128)} %pool_ref.3), custom_call_target="tpu_custom_call" | custom-call | bytes 3145728 | tf_op jit(solution)/shard_map/pallas_call | solution.py:228
  9.0 4.4 %collective-permute-start.9 = (bf16[2,1024,256]{2,1,0:T(8,128)(2,1)}, bf16[2,1024,256]{2,1,0:T(8,128)(2,1)}, u32[]{:S(2)}, u32[]{:S(2)}) collective-permute-start(bf16[2,1024,256]{2,1,0:T(8,128)(2,1)} %shard_map.203), channel_id=1, source_target_pairs={{0,1},{1,0},{2,3},{3,2},{4,5},{5,4},{6,7},{7,6},{8,9},{9,8},{10,11... | collective-permute-start | bytes 3145736 | tf_op jit(solution)/shard_map/ppermute | solution.py:40
  13.5 1.6 %collective-permute-start.6 = (bf16[256,512]{1,0:T(8,128)(2,1)S(1)}, bf16[256,512]{1,0:T(8,128)(2,1)S(1)}, u32[]{:S(2)}, u32[]{:S(2)}) collective-permute-start(bf16[256,512]{1,0:T(8,128)(2,1)S(1)} %get-tuple-element.31), channel_id=1, source_target_pairs={{0,4},{4,0},{2,6},{6,2},{8,12},{12,8},{10,14},{14,10},{16,20},{20,... | collective-permute-start | bytes 786440 | tf_op jit(solution)/shard_map/ppermute | solution.py:35
  15.0 4.3 %collective-permute-start.3 = (bf16[256,512]{1,0:T(8,128)(2,1)S(1)}, bf16[256,512]{1,0:T(8,128)(2,1)S(1)}, u32[]{:S(2)}, u32[]{:S(2)}) collective-permute-start(bf16[256,512]{1,0:T(8,128)(2,1)S(1)} %get-tuple-element.31), channel_id=1, source_target_pairs={{0,8},{8,0},{2,10},{10,2},{4,12},{12,4},{6,14},{14,6},{16,24},{24,... | collective-permute-start | bytes 786440 | tf_op jit(solution)/shard_map/ppermute | solution.py:35
  19.4 1.3 %copy.29 = bf16[4096,16]{1,0:T(8,128)(2,1)} copy(bf16[4096,16]{0,1:T(8,128)(2,1)S(1)} %copy-done.12) | data formatting | bytes 262144 | tf_op jit(solution)/shard_map/optimization_barrier | solution.py:84
  20.7 2.0 %shard_map.204.refs_13_ = f32[2,16,64,256]{3,2,1,0:T(8,128)S(1)} custom-call(s32[2]{0:T(128)S(1)} %get-tuple-element.32.slots_ref, f32[8,16,64,256]{3,2,1,0:T(8,128)} %pool_ref.3), custom_call_target="tpu_custom_call" | custom-call | bytes 3145728 | tf_op jit(solution)/shard_map/pallas_call | solution.py:228
  22.7 3.7 %collective-permute-done.3 = bf16[256,512]{1,0:T(8,128)(2,1)S(1)} collective-permute-done((bf16[256,512]{1,0:T(8,128)(2,1)S(1)}, bf16[256,512]{1,0:T(8,128)(2,1)S(1)}, u32[]{:S(2)}, u32[]{:S(2)}) %collective-permute-start.3) | collective-permute-done | bytes 262176 | tf_op jit(solution)/shard_map/ppermute | solution.py:35
  27.7 3.5 %collective-permute-done.2 = bf16[256,512]{1,0:T(8,128)(2,1)S(1)} collective-permute-done((bf16[256,512]{1,0:T(8,128)(2,1)S(1)}, bf16[256,512]{1,0:T(8,128)(2,1)S(1)}, u32[]{:S(2)}, u32[]{:S(2)}) %collective-permute-start.2) | collective-permute-done | bytes 262176 | tf_op jit(solution)/shard_map/ppermute | solution.py:35
  31.3 2.6 %collective-permute-done.4 = bf16[256,512]{1,0:T(8,128)(2,1)S(1)} collective-permute-done((bf16[256,512]{1,0:T(8,128)(2,1)S(1)}, bf16[256,512]{1,0:T(8,128)(2,1)S(1)}, u32[]{:S(2)}, u32[]{:S(2)}) %collective-permute-start.4) | collective-permute-done | bytes 262176 | tf_op jit(solution)/shard_map/ppermute | solution.py:35
  33.9 3.4 %collective-permute-start.10 = (bf16[2,3,1280]{2,1,0:T(4,128)(2,1)S(1)}, bf16[2,3,1280]{2,1,0:T(4,128)(2,1)S(1)}, u32[]{:S(2)}, u32[]{:S(2)}) collective-permute-start(bf16[2,3,1280]{2,1,0:T(4,128)(2,1)S(1)} %pad_maximum_fusion.7), channel_id=1, source_target_pairs={{0,1},{1,0},{2,3},{3,2},{4,5},{5,4},{6,7},{7,6},{8,9},{9,8},{10,11... | collective-permute-start | bytes 46088 | tf_op jit(solution)/shard_map/ppermute | solution.py:40
  38.0 2.4 %collective-permute-done.10 = bf16[2,3,1280]{2,1,0:T(4,128)(2,1)S(1)} collective-permute-done((bf16[2,3,1280]{2,1,0:T(4,128)(2,1)S(1)}, bf16[2,3,1280]{2,1,0:T(4,128)(2,1)S(1)}, u32[]{:S(2)}, u32[]{:S(2)}) %collective-permute-start.10) | collective-permute-done | bytes 15392 | tf_op jit(solution)/shard_map/ppermute | solution.py:40
  41.2 1.9 %fusion.23 = bf16[256,272]{1,0:T(8,128)(2,1)} fusion(bf16[256,4096]{1,0:T(8,128)(2,1)S(1)} %shard_map.205, bf16[4096,16]{1,0:T(8,128)(2,1)S(1)} %copy-done.8, bf16[4096,256]{1,0:T(8,128)(2,1)S(1)} %copy-done.19), kind=kOutput, calls=%fused_computation.14 | convolution fusion | flops 574951424 | bytes 4464640 | tf_op jit(solution)/shard_map/dot_general | solution.py:470
  43.1 11.2 %fusion.18 = bf16[2,256,1024]{2,1,0:T(8,128)(2,1)S(1)} fusion(bf16[4096,2,1024]{2,1,0:T(2,128)(2,1)} %param.21, bf16[256,4096]{1,0:T(8,128)(2,1)S(1)} %shard_map.205), kind=kOutput, calls=%fused_computation.11 | convolution fusion | flops 4295491584 | bytes 19922944 | tf_op jit(solution)/shard_map/td,dkc->ktc/dot_general | solution.py:472
  56.5 2.6 %collective-permute-start.13 = (bf16[256,272]{1,0:T(8,128)(2,1)}, bf16[256,272]{1,0:T(8,128)(2,1)}, u32[]{:S(2)}, u32[]{:S(2)}) collective-permute-start(bf16[256,272]{1,0:T(8,128)(2,1)} %fusion.23), channel_id=1, source_target_pairs={{0,1},{1,0},{2,3},{3,2},{4,5},{5,4},{6,7},{7,6},{8,9},{9,8},{10,11... | collective-permute-start | bytes 417800 | tf_op jit(solution)/shard_map/ppermute | solution.py:40
  59.2 1.9 %collective-permute-start.15 = (bf16[256,1024]{1,0:T(8,128)(2,1)}, bf16[256,1024]{1,0:T(8,128)(2,1)}, u32[]{:S(2)}, u32[]{:S(2)}) collective-permute-start(bf16[256,1024]{1,0:T(8,128)(2,1)} %get-tuple-element.44), channel_id=1, source_target_pairs={{0,1},{1,0},{2,3},{3,2},{4,5},{5,4},{6,7},{7,6},{8,9},{9,8},{10,11... | collective-permute-start | bytes 1572872 | tf_op jit(solution)/shard_map/ppermute | solution.py:40
  61.1 1.4 %shard_map.206 = bf16[256,4096]{1,0:T(8,128)(2,1)S(1)} custom-call(s32[8]{0:T(128)S(1)} %broadcast_xor_fusion.places_ref, bf16[4,256,512]{2,1,0:T(8,128)(2,1)S(1)} %constant_dynamic-update-slice_fusion.refs_0_, bf16[4,256,512]{2,1,0:T(8,128)(2,1)} %collective-permute-done.11.refs_1_), custom_call_target="tpu_custom_call" | custom-call | flops 1000000 | bytes 10000 | tf_op jit(solution)/shard_map/pallas_call | solution.py:72
  62.6 1.9 %fusion.6 = f32[256,272]{0,1:T(8,128)} fusion(bf16[256,4096]{1,0:T(8,128)(2,1)S(1)} %shard_map.206, bf16[4096,16]{1,0:T(8,128)(2,1)S(1)} %copy-done.9, bf16[4096,256]{1,0:T(8,128)(2,1)S(1)} %copy-done.20), kind=kOutput, calls=%fused_computation.7 | convolution fusion | flops 574881792 | bytes 4603904 | tf_op jit(solution)/shard_map/dot_general | solution.py:470
  64.5 12.0 %fusion.8 = f32[2,256,1024]{2,1,0:T(8,128)S(1)} fusion(bf16[4096,2,1024]{2,1,0:T(2,128)(2,1)} %param.21, bf16[256,4096]{1,0:T(8,128)(2,1)S(1)} %shard_map.206), kind=kOutput, calls=%fused_computation.9 | convolution fusion | flops 4294967296 | bytes 20971520 | tf_op jit(solution)/shard_map/td,dkc->ktc/dot_general | solution.py:472
  76.5 1.1 %slice_bitcast_fusion = (f32[256,1024]{1,0:T(8,128)}, f32[256,1024]{1,0:T(8,128)S(1)}) fusion(f32[2,256,1024]{2,1,0:T(8,128)S(1)} %fusion.8), kind=kLoop, calls=%fused_computation.19 | loop fusion | bytes 4194304 | tf_op jit(solution)/shard_map/squeeze | solution.py:473
  77.7 1.1 %copy.33.own_ref = f32[256,272]{1,0:T(8,128)S(1)} copy(f32[256,272]{0,1:T(8,128)} %fusion.6) | data formatting | bytes 557056 | tf_op jit(solution)/shard_map/optimization_barrier | solution.py:489
  81.5 2.2 %shard_map.207 = (bf16[256,256]{1,0:T(8,128)(2,1)S(1)}, f32[4,256,4]{2,1,0:T(8,128)S(1)}, f32[4,4,256]{2,1,0:T(4,128)S(1)}, f32[4,4,256]{2,1,0:T(4,128)S(1)}, f3...) custom-call(s32[1,2]{1,0:T(1,128)S(1)} %copy-done.3, f32[256,272]{1,0:T(8,128)S(1)} %copy.33.own_ref, ...), custom_call_target="tpu_custom_call" | custom-call | flops 1000000 | bytes 10000 | tf_op jit(solution)/shard_map/pallas_call | solution.py:204
  86.8 7.7 %shard_map.208 = (f32[256,1024]{1,0:T(8,128)S(1)}, f32[2,16,64,256]{3,2,1,0:T(8,128)}) custom-call(s32[2,2]{1,0:T(2,128)S(1)} %and_convert_fusion.flags_ref, s32[2]{0:T(128)S(1)} %bitcast.40, f32[256,1024]{1,0:T(8,128)S(1)} %get-tuple-element.48.refs_0_, bf16[256,1024]{1,0:T(8,128)(2,1)} %collective-permute-done.12.refs_1_, ...), custom_call_target="tpu_custom_call" | custom-call | flops 1000000 | bytes 10000 | tf_op jit(solution)/shard_map/pallas_call | solution.py:354
  94.6 1.5 %multiply_reduce_fusion = (f32[256]{0:T(256)S(1)}, f32[256,1024]{1,0:T(8,128)S(1)}) fusion(f32[256,1024]{1,0:T(8,128)S(1)} %get-tuple-element.57, f32[256,1024]{1,0:T(8,128)S(1)} %copy-done.7, bf16[256,1024]{1,0:T(8,128)(2,1)} %collective-permute-done.15), kind=kLoop, calls=%fused_computation.22 | loop fusion | flops 2883328 | bytes 3671040 | tf_op jit(solution)/shard_map/reduce_sum | solution.py:521
  (95 shorter events, 14.8 us)
Async XLA Ops:
  0.6 12.8 %collective-permute-start = (bf16[256,512]{1,0:T(8,128)(2,1)}, bf16[256,512]{1,0:T(8,128)(2,1)S(1)}, u32[]{:S(2)}, u32[]{:S(2)}) collective-permute-start(bf16[256,512]{1,0:T(8,128)(2,1)} %param.20), channel_id=1, source_target_pairs={{0,16},{1,0},{2,18},{3,2},{4,20},{5,4},{6,22},{7,6},{8,24},{9,8},{... | collective-permute-start | bytes 786440 | tf_op jit(solution)/shard_map/ppermute | solution.py:90
  4.7 8.7 %collective-permute-start.1 = (bf16[256,512]{1,0:T(8,128)(2,1)}, bf16[256,512]{1,0:T(8,128)(2,1)S(1)}, u32[]{:S(2)}, u32[]{:S(2)}) collective-permute-start(bf16[256,512]{1,0:T(8,128)(2,1)} %param.20), channel_id=1, source_target_pairs={{1,16},{3,18},{5,20},{7,22},{9,24},{11,26},{13,28},{15,30},{16,1},... | collective-permute-start | bytes 786440 | tf_op jit(solution)/shard_map/ppermute | solution.py:91
  6.2 7.2 %copy-start.10 = (bf16[256,512]{1,0:T(8,128)(2,1)S(1)}, bf16[256,512]{1,0:T(8,128)(2,1)}, u32[]{:S(2)}) copy-start(bf16[256,512]{1,0:T(8,128)(2,1)} %param.20) | copy-start | bytes 786436
  6.2 13.1 %copy-start.22 = (s32[8]{0:T(128)S(1)}, s32[8]{0:T(128)}, u32[]{:S(2)}) copy-start(s32[8]{0:T(128)} %constant.99.clone) | copy-start | bytes 100
  6.2 13.1 %copy-start.12 = (bf16[4096,16]{0,1:T(8,128)(2,1)S(1)}, bf16[4096,16]{0,1:T(8,128)(2,1)}, u32[]{:S(2)}) copy-start(bf16[4096,16]{0,1:T(8,128)(2,1)} %param.22) | copy-start | bytes 393220
  9.0 31.4 %collective-permute-start.9 = (bf16[2,1024,256]{2,1,0:T(8,128)(2,1)}, bf16[2,1024,256]{2,1,0:T(8,128)(2,1)}, u32[]{:S(2)}, u32[]{:S(2)}) collective-permute-start(bf16[2,1024,256]{2,1,0:T(8,128)(2,1)} %shard_map.203), channel_id=1, source_target_pairs={{0,1},{1,0},{2,3},{3,2},{4,5},{5,4},{6,7},{7,6},{8,9},{9,8},{10,11... | collective-permute-start | bytes 3145736 | tf_op jit(solution)/shard_map/ppermute | solution.py:40
  13.5 9.3 %collective-permute-start.6 = (bf16[256,512]{1,0:T(8,128)(2,1)S(1)}, bf16[256,512]{1,0:T(8,128)(2,1)S(1)}, u32[]{:S(2)}, u32[]{:S(2)}) collective-permute-start(bf16[256,512]{1,0:T(8,128)(2,1)S(1)} %get-tuple-element.31), channel_id=1, source_target_pairs={{0,4},{4,0},{2,6},{6,2},{8,12},{12,8},{10,14},{14,10},{16,20},{20,... | collective-permute-start | bytes 786440 | tf_op jit(solution)/shard_map/ppermute | solution.py:35
  15.0 11.4 %collective-permute-start.3 = (bf16[256,512]{1,0:T(8,128)(2,1)S(1)}, bf16[256,512]{1,0:T(8,128)(2,1)S(1)}, u32[]{:S(2)}, u32[]{:S(2)}) collective-permute-start(bf16[256,512]{1,0:T(8,128)(2,1)S(1)} %get-tuple-element.31), channel_id=1, source_target_pairs={{0,8},{8,0},{2,10},{10,2},{4,12},{12,4},{6,14},{14,6},{16,24},{24,... | collective-permute-start | bytes 786440 | tf_op jit(solution)/shard_map/ppermute | solution.py:35
  20.7 6.8 %copy-start.14 = (bf16[8,3,256]{2,0,1:T(8,128)(2,1)S(1)}, bf16[8,3,256]{2,0,1:T(8,128)(2,1)}, u32[]{:S(2)}) copy-start(bf16[8,3,256]{2,0,1:T(8,128)(2,1)} %param.37) | copy-start | bytes 36868
  20.7 6.9 %copy-start.13 = (bf16[8,3,1024]{2,0,1:T(8,128)(2,1)S(1)}, bf16[8,3,1024]{2,0,1:T(8,128)(2,1)}, u32[]{:S(2)}) copy-start(bf16[8,3,1024]{2,0,1:T(8,128)(2,1)} %param.36) | copy-start | bytes 147460
  22.7 8.6 %collective-permute-start.2 = (bf16[256,512]{1,0:T(8,128)(2,1)S(1)}, bf16[256,512]{1,0:T(8,128)(2,1)S(1)}, u32[]{:S(2)}, u32[]{:S(2)}) collective-permute-start(bf16[256,512]{1,0:T(8,128)(2,1)S(1)} %get-tuple-element.33), channel_id=1, source_target_pairs={{0,8},{8,0},{2,10},{10,2},{4,12},{12,4},{6,14},{14,6},{16,24},{24,... | collective-permute-start | bytes 786440 | tf_op jit(solution)/shard_map/ppermute | solution.py:35
  26.5 7.4 %collective-permute-start.4 = (bf16[256,512]{1,0:T(8,128)(2,1)S(1)}, bf16[256,512]{1,0:T(8,128)(2,1)S(1)}, u32[]{:S(2)}, u32[]{:S(2)}) collective-permute-start(bf16[256,512]{1,0:T(8,128)(2,1)S(1)} %collective-permute-done.3), channel_id=1, source_target_pairs={{0,4},{4,0},{2,6},{6,2},{8,12},{12,8},{10,14},{14,10},{16,20},{20,... | collective-permute-start | bytes 786440 | tf_op jit(solution)/shard_map/ppermute | solution.py:35
  27.4 13.1 %collective-permute-start.7 = (bf16[3,256,512]{2,1,0:T(8,128)(2,1)S(1)}, bf16[3,256,512]{2,1,0:T(8,128)(2,1)S(1)}, u32[]{:S(2)}, u32[]{:S(2)}) collective-permute-start(bf16[3,256,512]{2,1,0:T(8,128)(2,1)S(1)} %pad_maximum_fusion.5.refs_0_), channel_id=1, source_target_pairs={{0,2},{2,0},{4,6},{6,4},{8,10},{10,8},{12,14},{14,12},{16,18},{18,... | collective-permute-start | bytes 2359304 | tf_op jit(solution)/shard_map/ppermute | solution.py:35
  33.9 6.5 %collective-permute-start.8 = (bf16[1,256,512]{2,1,0:T(8,128)(2,1)S(1)}, bf16[1,256,512]{2,1,0:T(8,128)(2,1)S(1)}, u32[]{:S(2)}, u32[]{:S(2)}) collective-permute-start(bf16[1,256,512]{2,1,0:T(8,128)(2,1)S(1)} %bitcast.37), channel_id=1, source_target_pairs={{0,2},{2,0},{4,6},{6,4},{8,10},{10,8},{12,14},{14,12},{16,18},{18,... | collective-permute-start | bytes 786440 | tf_op jit(solution)/shard_map/ppermute | solution.py:35
  33.9 6.5 %collective-permute-start.10 = (bf16[2,3,1280]{2,1,0:T(4,128)(2,1)S(1)}, bf16[2,3,1280]{2,1,0:T(4,128)(2,1)S(1)}, u32[]{:S(2)}, u32[]{:S(2)}) collective-permute-start(bf16[2,3,1280]{2,1,0:T(4,128)(2,1)S(1)} %pad_maximum_fusion.7), channel_id=1, source_target_pairs={{0,1},{1,0},{2,3},{3,2},{4,5},{5,4},{6,7},{7,6},{8,9},{9,8},{10,11... | collective-permute-start | bytes 46088 | tf_op jit(solution)/shard_map/ppermute | solution.py:40
  37.3 18.1 %collective-permute-start.5 = (bf16[2,256,512]{2,1,0:T(8,128)(2,1)S(1)}, bf16[2,256,512]{2,1,0:T(8,128)(2,1)S(1)}, u32[]{:S(2)}, u32[]{:S(2)}) collective-permute-start(bf16[2,256,512]{2,1,0:T(8,128)(2,1)S(1)} %pad_maximum_fusion.6), channel_id=1, source_target_pairs={{0,4},{4,0},{2,6},{6,2},{8,12},{12,8},{10,14},{14,10},{16,20},{20,... | collective-permute-start | bytes 1572872 | tf_op jit(solution)/shard_map/ppermute | solution.py:35
  55.5 5.6 %collective-permute-start.11 = (bf16[4,256,512]{2,1,0:T(8,128)(2,1)S(1)}, bf16[4,256,512]{2,1,0:T(8,128)(2,1)}, u32[]{:S(2)}, u32[]{:S(2)}) collective-permute-start(bf16[4,256,512]{2,1,0:T(8,128)(2,1)S(1)} %constant_dynamic-update-slice_fusion.refs_0_), channel_id=1, source_target_pairs={{0,2},{2,0},{4,6},{6,4},{8,10},{10,8},{12,14},{14,12},{16,18},{18,... | collective-permute-start | bytes 3145736 | tf_op jit(solution)/shard_map/ppermute | solution.py:35
  56.5 20.0 %copy-start.11 = (f32[2,3,1280]{2,1,0:T(4,128)}, f32[2,3,1280]{2,1,0:T(4,128)S(1)}, u32[]{:S(2)}) copy-start(f32[2,3,1280]{2,1,0:T(4,128)S(1)} %fusion.29) | copy-start | bytes 92164
  56.5 22.3 %collective-permute-start.13 = (bf16[256,272]{1,0:T(8,128)(2,1)}, bf16[256,272]{1,0:T(8,128)(2,1)}, u32[]{:S(2)}, u32[]{:S(2)}) collective-permute-start(bf16[256,272]{1,0:T(8,128)(2,1)} %fusion.23), channel_id=1, source_target_pairs={{0,1},{1,0},{2,3},{3,2},{4,5},{5,4},{6,7},{7,6},{8,9},{9,8},{10,11... | collective-permute-start | bytes 417800 | tf_op jit(solution)/shard_map/ppermute | solution.py:40
  59.1 26.2 %collective-permute-start.12 = (bf16[256,1024]{1,0:T(8,128)(2,1)}, bf16[256,1024]{1,0:T(8,128)(2,1)}, u32[]{:S(2)}, u32[]{:S(2)}) collective-permute-start(bf16[256,1024]{1,0:T(8,128)(2,1)} %get-tuple-element.43), channel_id=1, source_target_pairs={{0,1},{1,0},{2,3},{3,2},{4,5},{5,4},{6,7},{7,6},{8,9},{9,8},{10,11... | collective-permute-start | bytes 1572872 | tf_op jit(solution)/shard_map/ppermute | solution.py:40
  59.2 35.4 %collective-permute-start.15 = (bf16[256,1024]{1,0:T(8,128)(2,1)}, bf16[256,1024]{1,0:T(8,128)(2,1)}, u32[]{:S(2)}, u32[]{:S(2)}) collective-permute-start(bf16[256,1024]{1,0:T(8,128)(2,1)} %get-tuple-element.44), channel_id=1, source_target_pairs={{0,1},{1,0},{2,3},{3,2},{4,5},{5,4},{6,7},{7,6},{8,9},{9,8},{10,11... | collective-permute-start | bytes 1572872 | tf_op jit(solution)/shard_map/ppermute | solution.py:40
  83.7 1.6 %collective-permute-start.14 = (bf16[256,256]{1,0:T(8,128)(2,1)S(1)}, bf16[256,256]{1,0:T(8,128)(2,1)S(1)}, u32[]{:S(2)}, u32[]{:S(2)}) collective-permute-start(bf16[256,256]{1,0:T(8,128)(2,1)S(1)} %get-tuple-element.50), channel_id=1, source_target_pairs={{0,2},{2,0},{4,6},{6,4},{8,10},{10,8},{12,14},{14,12},{16,18},{18,... | collective-permute-start | bytes 393224 | tf_op jit(solution)/shard_map/ppermute | solution.py:35
  86.8 7.7 %copy-start.7 = (f32[256,1024]{1,0:T(8,128)S(1)}, f32[256,1024]{1,0:T(8,128)}, u32[]{:S(2)}) copy-start(f32[256,1024]{1,0:T(8,128)} %get-tuple-element.58) | copy-start | bytes 3145732
  96.0 1.4 %collective-permute-start.16 = (f32[256]{0:T(256)S(1)}, f32[256]{0:T(256)S(1)}, u32[]{:S(2)}, u32[]{:S(2)}) collective-permute-start(f32[256]{0:T(256)S(1)} %get-tuple-element.64), channel_id=1, source_target_pairs={{0,2},{2,0},{4,6},{6,4},{8,10},{10,8},{12,14},{14,12},{16,18},{18,... | collective-permute-start | bytes 3080 | tf_op jit(solution)/shard_map/ppermute | solution.py:35
  (16 other events, 38.3 us)

commit v12 on v11

--- a/solution.py
+++ b/solution.py
@@ -126,17 +126,18 @@
     return position, seg, first
 
 
-def conv_silu(values, cache_ref, kernel_ref, bias_ref, seg, offset):
-    kernel_len = kernel_ref.shape[0]
-    taps = [kernel_ref[k : k + 1, :] for k in range(kernel_len)]
-    total = bias_ref[...] + taps[kernel_len - 1] * values
+def conv_silu(values, cache_ref, const_ref, seg, offset):
+    kernel_len = cache_ref.shape[1] + 1
+    taps = [const_ref[k : k + 1, :] for k in range(kernel_len)]
+    bias = const_ref[kernel_len : kernel_len + 1, :]
+    total = bias + taps[kernel_len - 1] * values
     for lag in range(1, kernel_len):
         earlier = pltpu.roll(values, lag, 0)
         total = total + taps[kernel_len - 1 - lag] * jnp.where(offset >= lag, earlier, 0.0)
     cached = jnp.zeros_like(values)
     for request in range(cache_ref.shape[0]):
         for place in range(kernel_len - 1):
-            history = jnp.zeros_like(bias_ref[...])
+            history = jnp.zeros_like(bias)
             for lag in range(place + 1, kernel_len):
                 at = kernel_len - 1 + place - lag
                 history = history + taps[kernel_len - 1 - lag] * cache_ref[request, at : at + 1, :]
@@ -145,26 +146,26 @@
     return total * jax.nn.sigmoid(total)
 
 
-def prep_kernel(
-    count_req, got_total, starts_ref, own_ref, *refs
-):
+def prep_kernel(count_req, got_total, heads, ints_ref, own_ref, *refs):
     got = refs[:got_total]
-    cache_ref, kernel_ref, bias_ref, dt_bias_ref, a_log_ref = refs[got_total : got_total + 5]
-    bc_ref, cum_ref, cum_t_ref, step_t_ref, coef_ref, decay_ref = refs[got_total + 5 :]
+    cache_ref, const_ref = refs[got_total : got_total + 2]
+    bc_ref, cum_ref, cum_t_ref, step_t_ref, coef_ref, decay_ref = refs[got_total + 2 :]
     tokens = own_ref.shape[0]
-    channels = bias_ref.shape[1]
-    heads = dt_bias_ref.shape[1]
-    starts = [starts_ref[0, j] for j in range(count_req)]
-    total = own_ref[...]
+    channels = const_ref.shape[1]
+    kernel_len = cache_ref.shape[1] + 1
+    dt_bias = const_ref[kernel_len + 1 : kernel_len + 2, :heads]
+    a_log = const_ref[kernel_len + 2 : kernel_len + 3, :heads]
+    starts = [ints_ref[j] for j in range(count_req)]
+    total = own_ref[...].astype(F32)
     for ref in got:
         total = total + ref[...].astype(F32)
     total = total.astype(BF16).astype(F32)
     position, seg, first = token_places(starts, tokens, (tokens, channels), 0)
-    bc = conv_silu(total[:, :channels], cache_ref, kernel_ref, bias_ref, seg, position - first)
+    bc = conv_silu(total[:, :channels], cache_ref, const_ref, seg, position - first)
     bc_ref[...] = bc.astype(BF16)
-    raw = total[:, channels : channels + heads] + dt_bias_ref[...]
+    raw = total[:, channels : channels + heads] + dt_bias
     step = jnp.maximum(raw, 0.0) + jnp.log1p(jnp.exp(-jnp.abs(raw)))
-    rate = step * (-jnp.exp(a_log_ref[...]))
+    rate = step * (-jnp.exp(a_log))
     position, seg, first = token_places(starts, tokens, (tokens, tokens), 0)
     other, seg_other, first_other = token_places(starts, tokens, (tokens, tokens), 1)
     same = seg == seg_other
@@ -192,17 +193,16 @@
     decay_ref[...] = jnp.exp(ends)
 
 
-def prep(starts, own, got, cache, kernel, bias, dt_bias, a_log):
+def prep(ints, own, got, cache, const, heads):
     tokens = own.shape[0]
-    channels = bias.shape[0]
-    heads = dt_bias.shape[0]
+    channels = const.shape[1]
     count_req = cache.shape[0]
     vmem = pl.BlockSpec(memory_space=pltpu.VMEM)
     part = min(HEADS_STEP, heads)
     tall = jax.ShapeDtypeStruct((heads // part, tokens, part), F32)
     flat = jax.ShapeDtypeStruct((heads // part, part, tokens), F32)
     return pl.pallas_call(
-        functools.partial(prep_kernel, count_req, len(got)),
+        functools.partial(prep_kernel, count_req, len(got), heads),
         out_shape=[
             jax.ShapeDtypeStruct((tokens, channels), BF16),
             tall,
@@ -211,46 +211,67 @@
             tall,
             jax.ShapeDtypeStruct((8, heads), F32),
         ],
-        in_specs=[pl.BlockSpec(memory_space=pltpu.SMEM)] + [vmem] * (6 + len(got)),
+        in_specs=[pl.BlockSpec(memory_space=pltpu.SMEM)] + [vmem] * (3 + len(got)),
         out_specs=[vmem] * 6,
         compiler_params=params(),
         cost_estimate=cost(1e6, 1e4),
-    )(starts, own, *got, cache, kernel, bias[None], dt_bias[None], a_log[None])
-
-
-def pack_kernel(slots_ref, pool_ref, out_ref):
-    out_ref[...] = pool_ref[...].reshape(out_ref.shape).astype(out_ref.dtype)
-
-
-def pack(pool, slots, shape, kind):
+    )(ints, own, *got, cache, const)
+
+
+def pack_kernel(slots_ref, pool_ref, *refs):
+    out_ref = refs[-1]
+    if len(refs) == 1:
+        out_ref[...] = pool_ref[...]
+    else:
+        rows = pool_ref.shape[1] * pool_ref.shape[2]
+        states = pool_ref[0].reshape(rows, pool_ref.shape[3])
+        out_ref[0, :rows, :] = states.astype(out_ref.dtype)
+        out_ref[0, rows:, :] = refs[0][0]
+
+
+def pack(pool, slots, conv_rows=None):
     count_req = slots.shape[0]
-    block = (1,) + pool.shape[1:]
+    _, heads, width, state = pool.shape
+    block = (1, heads, width, state)
+    in_specs = [pl.BlockSpec(block, lambda j, slots: (slots[j], 0, 0, 0))]
+    if conv_rows is None:
+        out_block, kind, more = block, F32, []
+    else:
+        rows = conv_rows.shape[1]
+        out_block, kind, more = (1, heads * width + rows, state), BF16, [conv_rows]
+        in_specs.append(pl.BlockSpec((1, rows, state), lambda j, slots: (j, 0, 0)))
     return pl.pallas_call(
         pack_kernel,
-        out_shape=jax.ShapeDtypeStruct((count_req,) + shape, kind),
+        out_shape=jax.ShapeDtypeStruct((count_req,) + out_block[1:], kind),
         grid_spec=pltpu.PrefetchScalarGridSpec(
             num_scalar_prefetch=1,
             grid=(count_req,),
-            in_specs=[pl.BlockSpec(block, lambda j, slots: (slots[j], 0, 0, 0))],
-            out_specs=pl.BlockSpec((1,) + shape, lambda j, slots: (j,) + (0,) * len(shape)),
+            in_specs=in_specs,
+            out_specs=pl.BlockSpec(out_block, lambda j, slots: (j,) + (0,) * (len(out_block) - 1)),
         ),
         compiler_params=params(3 * VMEM_BYTES),
         cost_estimate=cost(0, 6 * pool[0].size * count_req),
-    )(slots, pool)
-
-
-def mixer_kernel(count_req, got_total, flags_ref, starts_ref, *refs):
+    )(slots, pool, *more)
+
+
+def mixer_kernel(count_req, got_total, ints_ref, *refs):
     own_ref = refs[0]
     got = refs[1 : 1 + got_total]
     rest = refs[1 + got_total :]
-    cache_ref, kernel_ref, bias_ref, b_ref, c_ref = rest[:5]
-    cum_ref, cum_t_ref, step_t_ref, coef_ref, decay_ref, skip_ref = rest[5:11]
-    held_ref = rest[11]
-    states = rest[12 : 12 + got_total]
-    out_ref, state_ref, scores_ref, c_part_ref, b_part_ref = rest[12 + got_total :]
+    cache_ref, const_ref, b_ref, c_ref = rest[:4]
+    cum_ref, cum_t_ref, step_t_ref, coef_ref, decay_ref, held_ref = rest[4:10]
+    states = rest[10 : 10 + got_total]
+    out_ref, state_ref, scores_ref, c_part_ref, b_part_ref = rest[10 + got_total :]
+    kernel_len = cache_ref.shape[1] + 1
+    skip = const_ref[kernel_len + 1 : kernel_len + 2, :]
+
+    def flag(request, step):
+        place = count_req + request * (got_total + 1) + step
+        return ints_ref[place].astype(F32)
+
     tokens, channels = own_ref.shape
     heads, width, state = held_ref.shape[1:]
-    starts = [starts_ref[j] for j in range(count_req)]
+    starts = [ints_ref[j] for j in range(count_req)]
 
     @pl.when(pl.program_id(0) == 0)
     def _():
@@ -268,12 +289,12 @@
             b_part_ref[:, place] = jnp.where(seg == j, b_maps, 0.0).astype(BF16)
             c_part_ref[:, place] = jnp.where(seg == j, c_maps, 0.0).astype(BF16)
 
-    total = own_ref[...]
+    total = own_ref[...].astype(F32)
     for ref in got:
         total = total + ref[...].astype(F32)
     total = total.astype(BF16).astype(F32)
     position, seg, first = token_places(starts, tokens, (tokens, channels), 0)
-    values = conv_silu(total, cache_ref, kernel_ref, bias_ref, seg, position - first)
+    values = conv_silu(total, cache_ref, const_ref, seg, position - first)
     inputs = values.astype(BF16)
     values = inputs.astype(F32)
 
@@ -304,9 +325,9 @@
     )
     for j in range(count_req):
         place = slice(j * state, (j + 1) * state)
-        start = held_ref[j].reshape(channels, state) * flags_ref[j, 0].astype(F32)
+        start = held_ref[j].reshape(channels, state) * flag(j, 0)
         for step in range(got_total):
-            start = start + states[step][j].astype(F32) * flags_ref[j, step + 1].astype(F32)
+            start = start + states[step][j].astype(F32) * flag(j, step + 1)
         from_state = from_state + lax.dot_general(
             c_part_ref[:, place],
             start.astype(BF16),
@@ -317,16 +338,15 @@
         for h in range(heads):
             rows = slice(h * width, (h + 1) * width)
             state_ref[j, h] = decay_ref[j, first_head + h] * start[rows] + fresh[rows, place]
-    out_ref[...] = result + grown_wide * from_state + skip_ref[...] * values
+    out_ref[...] = result + grown_wide * from_state + skip * values
 
 
 def mixer(
-    flags, starts, own, got, cache, kernel, bias, b_maps, c_maps, cum, cum_t, step_t, coef,
-    decay, skip, held, states
+    ints, own, got, cache, const, b_maps, c_maps, cum, cum_t, step_t, coef, decay, held, states
 ):
     tokens, channels = own.shape
     count_req, heads, width, state = held.shape
-    kernel_len = kernel.shape[0]
+    kernel_len = cache.shape[1] + 1
     part = min(HEADS_STEP, heads)
     steps = heads // part
     wide = part * width
@@ -337,8 +357,7 @@
         [pl.BlockSpec((tokens, wide), columns)] * (1 + len(got))
         + [
             pl.BlockSpec((count_req, kernel_len - 1, wide), lambda i, *_: (0, 0, i)),
-            pl.BlockSpec((kernel_len, wide), columns),
-            pl.BlockSpec((1, wide), columns),
+            pl.BlockSpec((const.shape[0], wide), columns),
             pl.BlockSpec((tokens, state), whole),
             pl.BlockSpec((tokens, state), whole),
             pl.BlockSpec((1, tokens, part), lambda i, *_: (i, 0, 0)),
@@ -346,7 +365,6 @@
             pl.BlockSpec((1, part, tokens), lambda i, *_: (i, 0, 0)),
             pl.BlockSpec((1, tokens, part), lambda i, *_: (i, 0, 0)),
             pl.BlockSpec(memory_space=pltpu.SMEM),
-            pl.BlockSpec((1, wide), columns),
         ]
         + [pl.BlockSpec((count_req, part, width, state), lambda i, *_: (0, i, 0, 0))]
         + [pl.BlockSpec((count_req, wide, state), lambda i, *_: (0, i, 0))] * len(states)
@@ -358,7 +376,7 @@
             jax.ShapeDtypeStruct((count_req, heads, width, state), F32),
         ],
         grid_spec=pltpu.PrefetchScalarGridSpec(
-            num_scalar_prefetch=2,
+            num_scalar_prefetch=1,
             grid=(steps,),
             in_specs=in_specs,
             out_specs=[
@@ -374,9 +392,8 @@
         compiler_params=params(),
         cost_estimate=cost(1e6, 1e4),
     )(
-        flags, starts, own, *got, cache, kernel, bias[None], b_maps, c_maps,
-        cum, cum_t, step_t, coef, decay,
-        jnp.repeat(skip, width)[None], held, *states
+        ints, own, *got, cache, const, b_maps, c_maps, cum, cum_t, step_t, coef, decay, held,
+        *states
     )
 
 
@@ -423,14 +440,19 @@
             jnp.sum(jnp.where(hit[:, :, None, None], pool[None], 0), 1)
             for pool in (conv_x_pool, conv_bc_pool)
         ]
-        return jnp.concatenate(parts, 2)
-
-    got_states, got_conv = [], []
+        return parts
+
+    conv_size = lags * conv_width
+    conv_rows = -(-conv_size // (16 * state)) * 16
+    x_size = lags * local_width
+
+    got_states = []
     for step in range(1, req_count):
         slots = slots_of((me + step) % req_count)
-        packed = pack(ssm_pool, slots, (heads * head_width, state), BF16)
+        flat = jnp.concatenate([part.reshape(group_reqs, -1) for part in conv_of(slots)], 1)
+        flat = jnp.pad(flat, ((0, 0), (0, conv_rows * state - conv_size)))
+        packed = pack(ssm_pool, slots, flat.reshape(group_reqs, conv_rows, state))
         got_states.append(shift_req(packed, step))
-        got_conv.append(shift_req(conv_of(slots), step))
     own_slots = slots_of(me)
     asked = lax.dynamic_slice_in_dim(state_slot, me * group_reqs, group_reqs)
     came_from = (me - asked // slot_count) % req_count
@@ -446,9 +468,26 @@
         along_x = partner_2(block, "wide", 1)
         w_step = pinned(after(w_dt, block))
         own_slots = after(own_slots, block)
-    held = pack(ssm_pool, own_slots, (heads, head_width, state), F32)
+    held = pack(ssm_pool, own_slots)
+
+    kernel_len = conv_x_w.shape[0]
+    skip = jnp.repeat(d_skip, head_width)
+    const_x = jnp.stack(
+        [conv_x_w[k] for k in range(kernel_len)]
+        + [conv_x_b, skip, norm_gain, jnp.zeros_like(skip)]
+    )
+    wide_heads = lambda array: jnp.pad(array, (0, state_part - heads))
+    const_bc = jnp.stack(
+        [conv_bc_w[k] for k in range(kernel_len)]
+        + [conv_bc_b, wide_heads(dt_bias), wide_heads(a_log), jnp.zeros_like(conv_bc_b)]
+    )
+    ints = jnp.concatenate([stretch_start[0], flags.reshape(-1)])
+    caches = conv_of(own_slots)
     if direct:
-        near_three = after(jnp.stack([block, along_z, along_x]), held, w_step)
+        const_x, const_bc, ints = after((const_x, const_bc, ints), block)
+        near_three = after(
+            jnp.stack([block, along_z, along_x]), held, w_step, const_x, const_bc, ints, *caches
+        )
         both = partner_2(after(along_z, held, w_step), "wide", 1)
         core_three = partner_2(near_three, "wide", 0)
         own_block = after(own_block, held)
@@ -457,7 +496,7 @@
         core_both = partner_2(both, "wide", 0)
         own_pair = after(jnp.stack([own_block, own_z]), both)
         own_got = partner_2(own_pair, "wide", 1)
-        core_both = after(core_both, *got_states, *got_conv)
+        core_both = after(core_both, *got_states)
         theirs = quad_arrange(
             [near_three, both, core_three, core_both], [0, 4, 2, 6, 1, 5, 3, 7]
         )
@@ -486,16 +525,19 @@
         block = quad_arrange([own_four, own_core], [0, 4, 2, 6, 1, 5, 3, 7])
     else:
         block = after(block, *parts)
-    own = lax.optimization_barrier(project(block, F32))
-
-    cache = conv_of(own_slots)
+    own = lax.optimization_barrier(project(block, BF16))
+
     for step in range(1, req_count):
-        cache = jnp.where((came_from == step)[:, None, None], got_conv[step - 1], cache)
-    cache = jnp.where(live[:, None, None], cache, 0).astype(F32)
-
+        flat = after(got_states[step - 1], block)[:, heads * head_width :]
+        flat = flat.reshape(group_reqs, -1)
+        got = [flat[:, :x_size], flat[:, x_size:conv_size]]
+        caches = [
+            jnp.where((came_from == step)[:, None, None], here.reshape(cache.shape), cache)
+            for here, cache in zip(got, caches)
+        ]
+    caches = [jnp.where(live[:, None, None], cache, 0).astype(F32) for cache in caches]
     bc_conv, cum, cum_t, step_t, coef, decay = prep(
-        stretch_start, own["map"], came["map"], cache[:, :, local_width:], conv_bc_w, conv_bc_b,
-        dt_bias, a_log
+        ints, own["map"], came["map"], caches[1], const_bc, heads
     )
     wide_index = lax.axis_index("wide")
     group_span = lax.axis_size("wide") // GROUPS
@@ -510,11 +552,10 @@
     state_width = joined.shape[1] // 2
     came_xr = [after(got, own["xr"], bc_conv) for got in came["xr"]]
     result, final_state = mixer(
-        flags, stretch_start[0], own["xr"], came_xr, cache[:, :, :local_width],
-        conv_x_w, conv_x_b, joined[:, :state_width], joined[:, state_width:], cum, cum_t,
-        step_t, coef, decay, d_skip, held, got_states
-    )
-    gate = own["z"]
+        ints, own["xr"], came_xr, caches[0], const_x, joined[:, :state_width],
+        joined[:, state_width:], cum, cum_t, step_t, coef, decay, held, got_states
+    )
+    gate = own["z"].astype(F32)
     for got in came["z"]:
         gate = gate + got.astype(F32)
     gated = result * jax.nn.silu(gate.astype(BF16).astype(F32))
@@ -522,7 +563,7 @@
     for bit_index in range(bit_total):
         square_sum = square_sum + partner_2(square_sum, "wide", bit_index)
     mean_sq = square_sum / (local_width * group_span)
-    normed = gated * lax.rsqrt(mean_sq + NORM_EPS)[:, None] * norm_gain[None, :]
+    normed = gated * lax.rsqrt(mean_sq + NORM_EPS)[:, None] * const_x[kernel_len + 2][None, :]
     return (normed.astype(BF16), final_state)
 
 

time: 98.9 us -> 106 us (1.072)
  other arithmetic: 5.49 us -> 11.5 us
  local copies, waits for them, and re-layouts: 9.76 us -> 15.7 us
  waiting for transfers between devices: 13.1 us -> 9.62 us
  starting transfers between devices: 25.1 us -> 22.3 us
  Pallas kernels: 16.7 us -> 17.8 us
    unnamed x47 -> x72, local copies, waits for them, and re-layouts: 4.16 us -> 8.12 us
    reduce_sum x2 -> x4, other arithmetic: 0.26 us -> 3.12 us  [conv_of(): jnp.sum(jnp.where(hit[:, :, None, None], pool[None], 0), 1)]
    ppermute x10, waiting for transfers between devices: 10.7 us -> 8.34 us  [partner_2(): return lax.ppermute(block, axis, route)]
    ppermute x5 -> x4, starting transfers between devices: 12.3 us -> 10.2 us  [shift_req(): lax.ppermute(block, 'req', [(i, (i + step) % count) for i in range(count)])]
    convert_element_type x1 -> x2, local copies, waits for them, and re-layouts: 1.05 us -> 3.13 us  [project(): return {'map': low, 'xr': high[1].astype(kind), 'z': high[0].astype(kind)}]
    squeeze x1 -> x0, local copies, waits for them, and re-layouts: 1.15 us -> none  [project(): return {'map': low, 'xr': high[1].astype(kind), 'z': high[0].astype(kind)}]
    ppermute x5 -> x4, waiting for transfers between devices: 2.42 us -> 1.28 us  [shift_req(): lax.ppermute(block, 'req', [(i, (i + step) % count) for i in range(count)])]
    optimization_barrier x1 -> x0, local copies, waits for them, and re-layouts: 1.12 us -> none  [on_device(): own = lax.optimization_barrier(project(block, F32))]
  transfers between devices with their start and end apart: 17 -> 16, of which waited for: 5 -> 5; matrix products, arithmetic and copies ran while one was open for 36% -> 42% of each run, Pallas kernels for 17% -> 17%
where the time goes in v12:
time: 106 us; the launch traced here: 105 us
  matrix products  26.9 us (25%)
  starting transfers between devices  22.3 us (21%)
  Pallas kernels  17.8 us (17%)
  local copies, waits for them, and re-layouts  15.7 us (15%)
  other arithmetic  11.5 us (11%)
  waiting for transfers between devices  9.62 us (9%)
  between operations  1.06 us (1%)
    dot_general x2, matrix products, project(): high = jnp.einsum('td,dkc->ktc', block, w_xz, preferred_element_type=F32)  23.7 us
    ppermute x4, starting transfers between devices, shift_req(): lax.ppermute(block, 'req', [(i, (i + step) % count) for i in range(count)])  10.2 us
    ppermute x10, waiting for transfers between devices, partner_2(): return lax.ppermute(block, axis, route)  8.34 us
    unnamed x72, local copies, waits for them, and re-layouts  8.12 us
    pallas_call x1, Pallas kernels, mixer(): pl.pallas_call(functools.partial(mixer_kernel, count_req, len(got)), out_...  7.71 us
    ppermute x10, starting transfers between devices, partner_2(): return lax.ppermute(block, axis, route)  7.34 us
    pallas_call x2, Pallas kernels, pack(): pl.pallas_call(pack_kernel, out_shape=jax.ShapeDtypeStruct((count_req,) +...  4.99 us
    ppermute x1, starting transfers between devices, near_blocks(): first = lax.ppermute(x_in, axes, first)  4.09 us
  transfers between devices with their start and end apart: 16, of which 5 were waited for; matrix products, arithmetic and copies ran while one was open for 42% of the time, Pallas kernels for 17%

profile of v12, /device:TPU:0, one launch (start us, length us, event | category | flops | bytes accessed | tf_op | source)
XLA Modules:
  0.0 104.8 jit_solution(8726638257116907481)
XLA Ops:
  0.6 4.1 %collective-permute-start = (bf16[256,512]{1,0:T(8,128)(2,1)}, bf16[256,512]{1,0:T(8,128)(2,1)S(1)}, u32[]{:S(2)}, u32[]{:S(2)}) collective-permute-start(bf16[256,512]{1,0:T(8,128)(2,1)} %param.20), channel_id=1, source_target_pairs={{0,16},{1,0},{2,18},{3,2},{4,20},{5,4},{6,22},{7,6},{8,24},{9,8},{... | collective-permute-start | bytes 786440 | tf_op jit(solution)/shard_map/ppermute | solution.py:90
  8.3 2.8 %shard_map.203 = bf16[2,1040,256]{2,1,0:T(8,128)(2,1)} custom-call(s32[2]{0:T(128)S(1)} %get-tuple-element.81.slots_ref, f32[8,16,64,256]{3,2,1,0:T(8,128)} %pool_ref.3, bf16[2,16,256]{2,1,0:T(8,128)(2,1)S(1)} %bitcast.54), custom_call_target="tpu_custom_call" | custom-call | bytes 3145728 | tf_op jit(solution)/shard_map/pallas_call | solution.py:243
  11.1 4.2 %collective-permute-start.9 = (bf16[2,1040,256]{2,1,0:T(8,128)(2,1)}, bf16[2,1040,256]{2,1,0:T(8,128)(2,1)}, u32[]{:S(2)}, u32[]{:S(2)}) collective-permute-start(bf16[2,1040,256]{2,1,0:T(8,128)(2,1)} %shard_map.203), channel_id=1, source_target_pairs={{0,1},{1,0},{2,3},{3,2},{4,5},{5,4},{6,7},{7,6},{8,9},{9,8},{10,11... | collective-permute-start | bytes 3194888 | tf_op jit(solution)/shard_map/ppermute | solution.py:40
  17.6 1.6 %collective-permute-start.3 = (bf16[256,512]{1,0:T(8,128)(2,1)S(1)}, bf16[256,512]{1,0:T(8,128)(2,1)}, u32[]{:S(2)}, u32[]{:S(2)}) collective-permute-start(bf16[256,512]{1,0:T(8,128)(2,1)S(1)} %get-tuple-element.35), channel_id=1, source_target_pairs={{0,8},{8,0},{2,10},{10,2},{4,12},{12,4},{6,14},{14,6},{16,24},{24,... | collective-permute-start | bytes 786440 | tf_op jit(solution)/shard_map/ppermute | solution.py:35
  19.3 1.5 %collective-permute-start.6 = (bf16[256,512]{1,0:T(8,128)(2,1)S(1)}, bf16[256,512]{1,0:T(8,128)(2,1)S(1)}, u32[]{:S(2)}, u32[]{:S(2)}) collective-permute-start(bf16[256,512]{1,0:T(8,128)(2,1)S(1)} %get-tuple-element.35), channel_id=1, source_target_pairs={{0,4},{4,0},{2,6},{6,2},{8,12},{12,8},{10,14},{14,10},{16,20},{20,... | collective-permute-start | bytes 786440 | tf_op jit(solution)/shard_map/ppermute | solution.py:35
  21.5 2.2 %shard_map.204.refs_11_ = f32[2,16,64,256]{3,2,1,0:T(8,128)S(1)} custom-call(s32[2]{0:T(128)S(1)} %get-tuple-element.37.slots_ref, f32[8,16,64,256]{3,2,1,0:T(8,128)} %pool_ref.3), custom_call_target="tpu_custom_call" | custom-call | bytes 3145728 | tf_op jit(solution)/shard_map/pallas_call | solution.py:243
  23.7 1.3 %copy.36 = bf16[4096,16]{1,0:T(8,128)(2,1)} copy(bf16[4096,16]{0,1:T(8,128)(2,1)S(1)} %copy-done.13) | data formatting | bytes 262144 | tf_op jit(solution)/shard_map/optimization_barrier | solution.py:84
  26.9 1.1 %pad_maximum_fusion.7.refs_0_ = bf16[3,256,512]{2,1,0:T(8,128)(2,1)S(1)} fusion(bf16[1,256,512]{2,1,0:T(8,128)(2,1)} %bitcast.57, bf16[1,256,512]{2,1,0:T(8,128)(2,1)} %bitcast.10, bf16[1,256,512]{2,1,0:T(8,128)(2,1)S(1)} %bitcast.56), kind=kLoop, calls=%fused_computation.24 | loop fusion | flops 786432 | bytes 1572864 | tf_op jit(solution)/shard_map/stack | solution.py:489
  28.6 1.5 %collective-permute-start.4 = (bf16[256,512]{1,0:T(8,128)(2,1)}, bf16[256,512]{1,0:T(8,128)(2,1)S(1)}, u32[]{:S(2)}, u32[]{:S(2)}) collective-permute-start(bf16[256,512]{1,0:T(8,128)(2,1)} %collective-permute-done.3), channel_id=1, source_target_pairs={{0,4},{4,0},{2,6},{6,2},{8,12},{12,8},{10,14},{14,10},{16,20},{20,... | collective-permute-start | bytes 786440 | tf_op jit(solution)/shard_map/ppermute | solution.py:35
  30.1 6.8 %collective-permute-done.2 = bf16[256,512]{1,0:T(8,128)(2,1)} collective-permute-done((bf16[256,512]{1,0:T(8,128)(2,1)S(1)}, bf16[256,512]{1,0:T(8,128)(2,1)}, u32[]{:S(2)}, u32[]{:S(2)}) %collective-permute-start.2) | collective-permute-done | bytes 262176 | tf_op jit(solution)/shard_map/ppermute | solution.py:35
  38.2 1.6 %collective-permute-start.5 = (bf16[2,256,512]{2,1,0:T(8,128)(2,1)S(1)}, bf16[2,256,512]{2,1,0:T(8,128)(2,1)S(1)}, u32[]{:S(2)}, u32[]{:S(2)}) collective-permute-start(bf16[2,256,512]{2,1,0:T(8,128)(2,1)S(1)} %pad_maximum_fusion.8), channel_id=1, source_target_pairs={{0,4},{4,0},{2,6},{6,2},{8,12},{12,8},{10,14},{14,10},{16,20},{20,... | collective-permute-start | bytes 1572872 | tf_op jit(solution)/shard_map/ppermute | solution.py:35
  40.6 1.3 %collective-permute-done.9.refs_12_ = bf16[2,1040,256]{2,1,0:T(8,128)(2,1)} collective-permute-done((bf16[2,1040,256]{2,1,0:T(8,128)(2,1)}, bf16[2,1040,256]{2,1,0:T(8,128)(2,1)}, u32[]{:S(2)}, u32[]{:S(2)}) %collective-permute-start.9) | collective-permute-done | bytes 1064992 | tf_op jit(solution)/shard_map/ppermute | solution.py:40
  41.9 1.3 %shard_map.205 = bf16[256,4096]{1,0:T(8,128)(2,1)S(1)} custom-call(s32[8]{0:T(128)S(1)} %broadcast_xor_fusion.places_ref, bf16[3,256,512]{2,1,0:T(8,128)(2,1)S(1)} %pad_maximum_fusion.7.refs_0_, bf16[1,256,512]{2,1,0:T(8,128)(2,1)S(1)} %bitcast.53, bf16[3,256,512]{2,1,0:T(8,128)(2,1)} %collective-permute-done.7.refs_2_, ...), custom_call_target="tpu_custom_call" | custom-call | flops 1000000 | bytes 10000 | tf_op jit(solution)/shard_map/pallas_call | solution.py:72
  43.2 1.9 %fusion.28 = bf16[256,272]{1,0:T(8,128)(2,1)} fusion(bf16[256,4096]{1,0:T(8,128)(2,1)S(1)} %shard_map.205, bf16[4096,16]{1,0:T(8,128)(2,1)S(1)} %copy-done.8, bf16[4096,256]{1,0:T(8,128)(2,1)S(1)} %copy-done.29), kind=kOutput, calls=%fused_computation.15 | convolution fusion | flops 574951424 | bytes 4464640 | tf_op jit(solution)/shard_map/dot_general | solution.py:509
  45.2 11.3 %fusion.23 = bf16[2,256,1024]{2,1,0:T(8,128)(2,1)S(1)} fusion(bf16[4096,2,1024]{2,1,0:T(2,128)(2,1)} %param.21, bf16[256,4096]{1,0:T(8,128)(2,1)S(1)} %shard_map.205), kind=kOutput, calls=%fused_computation.12 | convolution fusion | flops 4295491584 | bytes 19922944 | tf_op jit(solution)/shard_map/td,dkc->ktc/dot_general | solution.py:511
  58.4 3.9 %collective-permute-start.12 = (bf16[256,272]{1,0:T(8,128)(2,1)}, bf16[256,272]{1,0:T(8,128)(2,1)S(1)}, u32[]{:S(2)}, u32[]{:S(2)}) collective-permute-start(bf16[256,272]{1,0:T(8,128)(2,1)} %fusion.28), channel_id=1, source_target_pairs={{0,1},{1,0},{2,3},{3,2},{4,5},{5,4},{6,7},{7,6},{8,9},{9,8},{10,11... | collective-permute-start | bytes 417800 | tf_op jit(solution)/shard_map/ppermute | solution.py:40
  62.3 2.0 %collective-permute-start.14 = (bf16[256,1024]{1,0:T(8,128)(2,1)}, bf16[256,1024]{1,0:T(8,128)(2,1)}, u32[]{:S(2)}, u32[]{:S(2)}) collective-permute-start(bf16[256,1024]{1,0:T(8,128)(2,1)} %get-tuple-element.51), channel_id=1, source_target_pairs={{0,1},{1,0},{2,3},{3,2},{4,5},{5,4},{6,7},{7,6},{8,9},{9,8},{10,11... | collective-permute-start | bytes 1572872 | tf_op jit(solution)/shard_map/ppermute | solution.py:40
  64.3 1.4 %shard_map.206 = bf16[256,4096]{1,0:T(8,128)(2,1)S(1)} custom-call(s32[8]{0:T(128)S(1)} %broadcast_xor_fusion.places_ref, bf16[4,256,512]{2,1,0:T(8,128)(2,1)} %constant_dynamic-update-slice_fusion.refs_0_, bf16[4,256,512]{2,1,0:T(8,128)(2,1)S(1)} %collective-permute-done.10.refs_1_), custom_call_target="tpu_custom_call" | custom-call | flops 1000000 | bytes 10000 | tf_op jit(solution)/shard_map/pallas_call | solution.py:72
  65.7 1.3 %fusion.29.own_ref = bf16[256,272]{1,0:T(8,128)(2,1)S(1)} fusion(bf16[256,4096]{1,0:T(8,128)(2,1)S(1)} %shard_map.206, bf16[4096,16]{1,0:T(8,128)(2,1)S(1)} %copy-done.9, bf16[4096,256]{1,0:T(8,128)(2,1)S(1)} %copy-done.30), kind=kOutput, calls=%fused_computation.16 | convolution fusion | flops 574951424 | bytes 4464640 | tf_op jit(solution)/shard_map/dot_general | solution.py:509
  67.0 12.4 %fusion.18 = bf16[2,256,1024]{2,1,0:T(8,128)(2,1)} fusion(bf16[4096,2,1024]{2,1,0:T(2,128)(2,1)} %param.21, bf16[256,4096]{1,0:T(8,128)(2,1)S(1)} %shard_map.206), kind=kOutput, calls=%fused_computation.11 | convolution fusion | flops 4295491584 | bytes 19922944 | tf_op jit(solution)/shard_map/td,dkc->ktc/dot_general | solution.py:511
  80.8 2.1 %slice_bitcast_fusion = (bf16[256,1024]{1,0:T(8,128)(2,1)}, bf16[256,1024]{1,0:T(8,128)(2,1)S(1)}) fusion(bf16[2,256,1024]{2,1,0:T(8,128)(2,1)} %fusion.18), kind=kLoop, calls=%fused_computation.25 | loop fusion | bytes 2097152 | tf_op jit(solution)/shard_map/convert_element_type | solution.py:512
  83.0 2.4 %shard_map.207 = (bf16[256,256]{1,0:T(8,128)(2,1)}, f32[4,256,4]{2,1,0:T(8,128)S(1)}, f32[4,4,256]{2,1,0:T(4,128)S(1)}, f32[4,4,256]{2,1,0:T(4,128)S(1)}, f32[4,256,4]{2,1,0:T(8,128)S(1)}, /*index=5*/f32[8,16]{1,0:T(8,128)S(1)}) custom-call(s32[6]{0:T(128)S(1)} %pad_add_fusion.ints_ref, bf16[256,272]{1,0:T(8,128)(2,1)S(1)} %fusion.29.own_ref, ...), custom_call_target="tpu_custom_call" | custom-call | flops 1000000 | bytes 10000 | tf_op jit(solution)/shard_map/pallas_call | solution.py:204
  93.2 7.7 %shard_map.208 = (f32[256,1024]{1,0:T(8,128)S(1)}, f32[2,16,64,256]{3,2,1,0:T(8,128)}) custom-call(s32[6]{0:T(128)S(1)} %pad_add_fusion.ints_ref, bf16[256,1024]{1,0:T(8,128)(2,1)S(1)} %get-tuple-element.55.refs_0_, bf16[256,1024]{1,0:T(8,128)(2,1)} %collective-permute-done.11.refs_1_, f32[2,3,1024]{2,1,0:T(4,128)S(1)} %select_convert_fusion.refs_2_, ...), custom_call_target="tpu_custom_call" | custom-call | flops 1000000 | bytes 10000 | tf_op jit(solution)/shard_map/pallas_call | solution.py:372
  101.0 1.5 %multiply_reduce_fusion = (f32[256]{0:T(256)S(1)}, f32[256,1024]{1,0:T(8,128)S(1)}) fusion(f32[256,1024]{1,0:T(8,128)S(1)} %get-tuple-element.65, bf16[256,1024]{1,0:T(8,128)(2,1)} %collective-permute-done.14, bf16[256,1024]{1,0:T(8,128)(2,1)S(1)} %copy-done.7), kind=kLoop, calls=%fused_computation.22 | loop fusion | flops 3145472 | bytes 3146752 | tf_op jit(solution)/shard_map/reduce_sum | solution.py:562
  (130 shorter events, 24.6 us)
Async XLA Ops:
  0.6 16.9 %collective-permute-start = (bf16[256,512]{1,0:T(8,128)(2,1)}, bf16[256,512]{1,0:T(8,128)(2,1)S(1)}, u32[]{:S(2)}, u32[]{:S(2)}) collective-permute-start(bf16[256,512]{1,0:T(8,128)(2,1)} %param.20), channel_id=1, source_target_pairs={{0,16},{1,0},{2,18},{3,2},{4,20},{5,4},{6,22},{7,6},{8,24},{9,8},{... | collective-permute-start | bytes 786440 | tf_op jit(solution)/shard_map/ppermute | solution.py:90
  4.7 12.8 %collective-permute-start.1 = (bf16[256,512]{1,0:T(8,128)(2,1)}, bf16[256,512]{1,0:T(8,128)(2,1)S(1)}, u32[]{:S(2)}, u32[]{:S(2)}) collective-permute-start(bf16[256,512]{1,0:T(8,128)(2,1)} %param.20), channel_id=1, source_target_pairs={{1,16},{3,18},{5,20},{7,22},{9,24},{11,26},{13,28},{15,30},{16,1},... | collective-permute-start | bytes 786440 | tf_op jit(solution)/shard_map/ppermute | solution.py:91
  8.2 8.6 %copy-start.16 = (f32[4,1024]{1,0:T(4,128)S(1)}, f32[4,1024]{1,0:T(4,128)}, u32[]{:S(2)}) copy-start(f32[4,1024]{1,0:T(4,128)} %param.27) | copy-start | bytes 49156
  8.2 8.6 %copy-start.21 = (f32[1024]{0:T(1024)S(1)}, f32[1024]{0:T(1024)}, u32[]{:S(2)}) copy-start(f32[1024]{0:T(1024)} %param.28) | copy-start | bytes 12292
  8.2 9.3 %copy-start.23 = (f32[4,256]{1,0:T(4,128)S(1)}, f32[4,256]{1,0:T(4,128)}, u32[]{:S(2)}) copy-start(f32[4,256]{1,0:T(4,128)} %param.29) | copy-start | bytes 12292
  8.2 9.2 %copy-start.24 = (f32[256]{0:T(256)S(1)}, f32[256]{0:T(256)}, u32[]{:S(2)}) copy-start(f32[256]{0:T(256)} %param.30) | copy-start | bytes 3076
  8.2 9.3 %copy-start.31 = (s32[1,2]{1,0:T(1,128)S(1)}, s32[1,2]{1,0:T(1,128)}, u32[]{:S(2)}) copy-start(s32[1,2]{1,0:T(1,128)} %param.32) | copy-start | bytes 28
  8.2 9.3 %copy-start.10 = (bf16[256,512]{1,0:T(8,128)(2,1)S(1)}, bf16[256,512]{1,0:T(8,128)(2,1)}, u32[]{:S(2)}) copy-start(bf16[256,512]{1,0:T(8,128)(2,1)} %param.20) | copy-start | bytes 786436
  8.2 12.6 %copy-start.14 = (bf16[8,3,256]{2,0,1:T(8,128)(2,1)S(1)}, bf16[8,3,256]{2,0,1:T(8,128)(2,1)}, u32[]{:S(2)}) copy-start(bf16[8,3,256]{2,0,1:T(8,128)(2,1)} %param.37) | copy-start | bytes 36868
  11.1 30.8 %collective-permute-start.9 = (bf16[2,1040,256]{2,1,0:T(8,128)(2,1)}, bf16[2,1040,256]{2,1,0:T(8,128)(2,1)}, u32[]{:S(2)}, u32[]{:S(2)}) collective-permute-start(bf16[2,1040,256]{2,1,0:T(8,128)(2,1)} %shard_map.203), channel_id=1, source_target_pairs={{0,1},{1,0},{2,3},{3,2},{4,5},{5,4},{6,7},{7,6},{8,9},{9,8},{10,11... | collective-permute-start | bytes 3194888 | tf_op jit(solution)/shard_map/ppermute | solution.py:40
  17.6 8.2 %collective-permute-start.3 = (bf16[256,512]{1,0:T(8,128)(2,1)S(1)}, bf16[256,512]{1,0:T(8,128)(2,1)}, u32[]{:S(2)}, u32[]{:S(2)}) collective-permute-start(bf16[256,512]{1,0:T(8,128)(2,1)S(1)} %get-tuple-element.35), channel_id=1, source_target_pairs={{0,8},{8,0},{2,10},{10,2},{4,12},{12,4},{6,14},{14,6},{16,24},{24,... | collective-permute-start | bytes 786440 | tf_op jit(solution)/shard_map/ppermute | solution.py:35
  19.3 6.9 %collective-permute-start.6 = (bf16[256,512]{1,0:T(8,128)(2,1)S(1)}, bf16[256,512]{1,0:T(8,128)(2,1)S(1)}, u32[]{:S(2)}, u32[]{:S(2)}) collective-permute-start(bf16[256,512]{1,0:T(8,128)(2,1)S(1)} %get-tuple-element.35), channel_id=1, source_target_pairs={{0,4},{4,0},{2,6},{6,2},{8,12},{12,8},{10,14},{14,10},{16,20},{20,... | collective-permute-start | bytes 786440 | tf_op jit(solution)/shard_map/ppermute | solution.py:35
  23.7 13.5 %copy-start.32 = (s32[8]{0:T(128)S(1)}, s32[8]{0:T(128)}, u32[]{:S(2)}) copy-start(s32[8]{0:T(128)} %constant.102.clone) | copy-start | bytes 100
  28.0 13.9 %collective-permute-start.7 = (bf16[3,256,512]{2,1,0:T(8,128)(2,1)S(1)}, bf16[3,256,512]{2,1,0:T(8,128)(2,1)}, u32[]{:S(2)}, u32[]{:S(2)}) collective-permute-start(bf16[3,256,512]{2,1,0:T(8,128)(2,1)S(1)} %pad_maximum_fusion.7.refs_0_), channel_id=1, source_target_pairs={{0,2},{2,0},{4,6},{6,4},{8,10},{10,8},{12,14},{14,12},{16,18},{18,... | collective-permute-start | bytes 2359304 | tf_op jit(solution)/shard_map/ppermute | solution.py:35
  28.1 8.8 %collective-permute-start.2 = (bf16[256,512]{1,0:T(8,128)(2,1)S(1)}, bf16[256,512]{1,0:T(8,128)(2,1)}, u32[]{:S(2)}, u32[]{:S(2)}) collective-permute-start(bf16[256,512]{1,0:T(8,128)(2,1)S(1)} %get-tuple-element.38), channel_id=1, source_target_pairs={{0,8},{8,0},{2,10},{10,2},{4,12},{12,4},{6,14},{14,6},{16,24},{24,... | collective-permute-start | bytes 786440 | tf_op jit(solution)/shard_map/ppermute | solution.py:35
  28.6 8.6 %collective-permute-start.4 = (bf16[256,512]{1,0:T(8,128)(2,1)}, bf16[256,512]{1,0:T(8,128)(2,1)S(1)}, u32[]{:S(2)}, u32[]{:S(2)}) collective-permute-start(bf16[256,512]{1,0:T(8,128)(2,1)} %collective-permute-done.3), channel_id=1, source_target_pairs={{0,4},{4,0},{2,6},{6,2},{8,12},{12,8},{10,14},{14,10},{16,20},{20,... | collective-permute-start | bytes 786440 | tf_op jit(solution)/shard_map/ppermute | solution.py:35
  37.2 3.4 %collective-permute-start.8 = (bf16[1,256,512]{2,1,0:T(8,128)(2,1)S(1)}, bf16[1,256,512]{2,1,0:T(8,128)(2,1)S(1)}, u32[]{:S(2)}, u32[]{:S(2)}) collective-permute-start(bf16[1,256,512]{2,1,0:T(8,128)(2,1)S(1)} %bitcast.52), channel_id=1, source_target_pairs={{0,2},{2,0},{4,6},{6,4},{8,10},{10,8},{12,14},{14,12},{16,18},{18,... | collective-permute-start | bytes 786440 | tf_op jit(solution)/shard_map/ppermute | solution.py:35
  38.2 19.3 %collective-permute-start.5 = (bf16[2,256,512]{2,1,0:T(8,128)(2,1)S(1)}, bf16[2,256,512]{2,1,0:T(8,128)(2,1)S(1)}, u32[]{:S(2)}, u32[]{:S(2)}) collective-permute-start(bf16[2,256,512]{2,1,0:T(8,128)(2,1)S(1)} %pad_maximum_fusion.8), channel_id=1, source_target_pairs={{0,4},{4,0},{2,6},{6,2},{8,12},{12,8},{10,14},{14,10},{16,20},{20,... | collective-permute-start | bytes 1572872 | tf_op jit(solution)/shard_map/ppermute | solution.py:35
  58.3 6.0 %collective-permute-start.10 = (bf16[4,256,512]{2,1,0:T(8,128)(2,1)}, bf16[4,256,512]{2,1,0:T(8,128)(2,1)S(1)}, u32[]{:S(2)}, u32[]{:S(2)}) collective-permute-start(bf16[4,256,512]{2,1,0:T(8,128)(2,1)} %constant_dynamic-update-slice_fusion.refs_0_), channel_id=1, source_target_pairs={{0,2},{2,0},{4,6},{6,4},{8,10},{10,8},{12,14},{14,12},{16,18},{18,... | collective-permute-start | bytes 3145736 | tf_op jit(solution)/shard_map/ppermute | solution.py:35
  58.4 24.6 %collective-permute-start.12 = (bf16[256,272]{1,0:T(8,128)(2,1)}, bf16[256,272]{1,0:T(8,128)(2,1)S(1)}, u32[]{:S(2)}, u32[]{:S(2)}) collective-permute-start(bf16[256,272]{1,0:T(8,128)(2,1)} %fusion.28), channel_id=1, source_target_pairs={{0,1},{1,0},{2,3},{3,2},{4,5},{5,4},{6,7},{7,6},{8,9},{9,8},{10,11... | collective-permute-start | bytes 417800 | tf_op jit(solution)/shard_map/ppermute | solution.py:40
  62.3 25.8 %collective-permute-start.11 = (bf16[256,1024]{1,0:T(8,128)(2,1)}, bf16[256,1024]{1,0:T(8,128)(2,1)}, u32[]{:S(2)}, u32[]{:S(2)}) collective-permute-start(bf16[256,1024]{1,0:T(8,128)(2,1)} %get-tuple-element.50), channel_id=1, source_target_pairs={{0,1},{1,0},{2,3},{3,2},{4,5},{5,4},{6,7},{7,6},{8,9},{9,8},{10,11... | collective-permute-start | bytes 1572872 | tf_op jit(solution)/shard_map/ppermute | solution.py:40
  62.3 38.6 %collective-permute-start.14 = (bf16[256,1024]{1,0:T(8,128)(2,1)}, bf16[256,1024]{1,0:T(8,128)(2,1)}, u32[]{:S(2)}, u32[]{:S(2)}) collective-permute-start(bf16[256,1024]{1,0:T(8,128)(2,1)} %get-tuple-element.51), channel_id=1, source_target_pairs={{0,1},{1,0},{2,3},{3,2},{4,5},{5,4},{6,7},{7,6},{8,9},{9,8},{10,11... | collective-permute-start | bytes 1572872 | tf_op jit(solution)/shard_map/ppermute | solution.py:40
  87.4 1.6 %collective-permute-start.13 = (bf16[256,256]{1,0:T(8,128)(2,1)}, bf16[256,256]{1,0:T(8,128)(2,1)S(1)}, u32[]{:S(2)}, u32[]{:S(2)}) collective-permute-start(bf16[256,256]{1,0:T(8,128)(2,1)} %get-tuple-element.58), channel_id=1, source_target_pairs={{0,2},{2,0},{4,6},{6,4},{8,10},{10,8},{12,14},{14,12},{16,18},{18,... | collective-permute-start | bytes 393224 | tf_op jit(solution)/shard_map/ppermute | solution.py:35
  102.5 1.4 %collective-permute-start.15 = (f32[256]{0:T(256)S(1)}, f32[256]{0:T(256)S(1)}, u32[]{:S(2)}, u32[]{:S(2)}) collective-permute-start(f32[256]{0:T(256)S(1)} %get-tuple-element.68), channel_id=1, source_target_pairs={{0,2},{2,0},{4,6},{6,4},{8,10},{10,8},{12,14},{14,12},{16,18},{18,... | collective-permute-start | bytes 3080 | tf_op jit(solution)/shard_map/ppermute | solution.py:35
  (25 other events, 98.8 us)

commit v13 on v12

--- a/solution.py
+++ b/solution.py
@@ -126,8 +126,8 @@
     return position, seg, first
 
 
-def conv_silu(values, cache_ref, const_ref, seg, offset):
-    kernel_len = cache_ref.shape[1] + 1
+def conv_silu(values, cache, const_ref, seg, offset):
+    kernel_len = cache.shape[1] + 1
     taps = [const_ref[k : k + 1, :] for k in range(kernel_len)]
     bias = const_ref[kernel_len : kernel_len + 1, :]
     total = bias + taps[kernel_len - 1] * values
@@ -135,12 +135,12 @@
         earlier = pltpu.roll(values, lag, 0)
         total = total + taps[kernel_len - 1 - lag] * jnp.where(offset >= lag, earlier, 0.0)
     cached = jnp.zeros_like(values)
-    for request in range(cache_ref.shape[0]):
+    for request in range(cache.shape[0]):
         for place in range(kernel_len - 1):
             history = jnp.zeros_like(bias)
             for lag in range(place + 1, kernel_len):
                 at = kernel_len - 1 + place - lag
-                history = history + taps[kernel_len - 1 - lag] * cache_ref[request, at : at + 1, :]
+                history = history + taps[kernel_len - 1 - lag] * cache[request, at : at + 1, :]
             cached = jnp.where((seg == request) & (offset == place), history, cached)
     total = total + cached
     return total * jax.nn.sigmoid(total)
@@ -161,7 +161,7 @@
         total = total + ref[...].astype(F32)
     total = total.astype(BF16).astype(F32)
     position, seg, first = token_places(starts, tokens, (tokens, channels), 0)
-    bc = conv_silu(total[:, :channels], cache_ref, const_ref, seg, position - first)
+    bc = conv_silu(total[:, :channels], cache_ref[:, :, -channels:], const_ref, seg, position - first)
     bc_ref[...] = bc.astype(BF16)
     raw = total[:, channels : channels + heads] + dt_bias
     step = jnp.maximum(raw, 0.0) + jnp.log1p(jnp.exp(-jnp.abs(raw)))
@@ -218,40 +218,25 @@
     )(ints, own, *got, cache, const)
 
 
-def pack_kernel(slots_ref, pool_ref, *refs):
-    out_ref = refs[-1]
-    if len(refs) == 1:
-        out_ref[...] = pool_ref[...]
-    else:
-        rows = pool_ref.shape[1] * pool_ref.shape[2]
-        states = pool_ref[0].reshape(rows, pool_ref.shape[3])
-        out_ref[0, :rows, :] = states.astype(out_ref.dtype)
-        out_ref[0, rows:, :] = refs[0][0]
-
-
-def pack(pool, slots, conv_rows=None):
+def pack_kernel(slots_ref, pool_ref, out_ref):
+    out_ref[...] = pool_ref[...].reshape(out_ref.shape).astype(out_ref.dtype)
+
+
+def pack(pool, slots, shape, kind):
     count_req = slots.shape[0]
-    _, heads, width, state = pool.shape
-    block = (1, heads, width, state)
-    in_specs = [pl.BlockSpec(block, lambda j, slots: (slots[j], 0, 0, 0))]
-    if conv_rows is None:
-        out_block, kind, more = block, F32, []
-    else:
-        rows = conv_rows.shape[1]
-        out_block, kind, more = (1, heads * width + rows, state), BF16, [conv_rows]
-        in_specs.append(pl.BlockSpec((1, rows, state), lambda j, slots: (j, 0, 0)))
+    block = (1,) + pool.shape[1:]
     return pl.pallas_call(
         pack_kernel,
-        out_shape=jax.ShapeDtypeStruct((count_req,) + out_block[1:], kind),
+        out_shape=jax.ShapeDtypeStruct((count_req,) + shape, kind),
         grid_spec=pltpu.PrefetchScalarGridSpec(
             num_scalar_prefetch=1,
             grid=(count_req,),
-            in_specs=in_specs,
-            out_specs=pl.BlockSpec(out_block, lambda j, slots: (j,) + (0,) * (len(out_block) - 1)),
+            in_specs=[pl.BlockSpec(block, lambda j, slots: (slots[j], 0, 0, 0))],
+            out_specs=pl.BlockSpec((1,) + shape, lambda j, slots: (j,) + (0,) * len(shape)),
         ),
         compiler_params=params(3 * VMEM_BYTES),
         cost_estimate=cost(0, 6 * pool[0].size * count_req),
-    )(slots, pool, *more)
+    )(slots, pool)
 
 
 def mixer_kernel(count_req, got_total, ints_ref, *refs):
@@ -294,7 +279,7 @@
         total = total + ref[...].astype(F32)
     total = total.astype(BF16).astype(F32)
     position, seg, first = token_places(starts, tokens, (tokens, channels), 0)
-    values = conv_silu(total, cache_ref, const_ref, seg, position - first)
+    values = conv_silu(total, cache_ref[...], const_ref, seg, position - first)
     inputs = values.astype(BF16)
     values = inputs.astype(F32)
 
@@ -440,19 +425,30 @@
             jnp.sum(jnp.where(hit[:, :, None, None], pool[None], 0), 1)
             for pool in (conv_x_pool, conv_bc_pool)
         ]
-        return parts
-
-    conv_size = lags * conv_width
-    conv_rows = -(-conv_size // (16 * state)) * 16
-    x_size = lags * local_width
+        return jnp.concatenate(parts, 2)
 
     got_states = []
     for step in range(1, req_count):
         slots = slots_of((me + step) % req_count)
-        flat = jnp.concatenate([part.reshape(group_reqs, -1) for part in conv_of(slots)], 1)
-        flat = jnp.pad(flat, ((0, 0), (0, conv_rows * state - conv_size)))
-        packed = pack(ssm_pool, slots, flat.reshape(group_reqs, conv_rows, state))
+        packed = pack(ssm_pool, slots, (heads * head_width, state), BF16)
         got_states.append(shift_req(packed, step))
+
+    w_step = w_dt
+    if direct:
+        block = after(block, packed)
+        along_z = partner_2(block, "wide", 2)
+        along_x = partner_2(block, "wide", 1)
+        (
+            w_step, state_slot, prefix_len, stretch_start, conv_x_pool, conv_bc_pool, conv_x_w,
+            conv_x_b, conv_bc_w, conv_bc_b, d_skip, norm_gain, dt_bias, a_log
+        ) = lax.optimization_barrier((
+            (
+                w_dt, state_slot, prefix_len, stretch_start, conv_x_pool, conv_bc_pool, conv_x_w,
+                conv_x_b, conv_bc_w, conv_bc_b, d_skip, norm_gain, dt_bias, a_log
+            ),
+            block,
+        ))[0]
+        w_step = pinned(w_step)
     own_slots = slots_of(me)
     asked = lax.dynamic_slice_in_dim(state_slot, me * group_reqs, group_reqs)
     came_from = (me - asked // slot_count) % req_count
@@ -460,15 +456,12 @@
     flags = (live[:, None] & (came_from[:, None] == jnp.arange(req_count)[None, :])).astype(
         jnp.int32
     )
-
-    w_step = w_dt
-    if direct:
-        block = after(block, packed)
-        along_z = partner_2(block, "wide", 2)
-        along_x = partner_2(block, "wide", 1)
-        w_step = pinned(after(w_dt, block))
-        own_slots = after(own_slots, block)
-    held = pack(ssm_pool, own_slots)
+    held = pack(ssm_pool, own_slots, (heads, head_width, state), F32)
+    cache = conv_of(own_slots)
+    for step in range(1, req_count):
+        got = shift_req(conv_of(slots_of((me + step) % req_count)), step)
+        cache = jnp.where((came_from == step)[:, None, None], got, cache)
+    cache = jnp.where(live[:, None, None], cache, 0).astype(F32)
 
     kernel_len = conv_x_w.shape[0]
     skip = jnp.repeat(d_skip, head_width)
@@ -482,13 +475,10 @@
         + [conv_bc_b, wide_heads(dt_bias), wide_heads(a_log), jnp.zeros_like(conv_bc_b)]
     )
     ints = jnp.concatenate([stretch_start[0], flags.reshape(-1)])
-    caches = conv_of(own_slots)
     if direct:
-        const_x, const_bc, ints = after((const_x, const_bc, ints), block)
-        near_three = after(
-            jnp.stack([block, along_z, along_x]), held, w_step, const_x, const_bc, ints, *caches
-        )
-        both = partner_2(after(along_z, held, w_step), "wide", 1)
+        small = (held, w_step, const_x, const_bc, ints, cache)
+        near_three = jnp.stack([block, along_z, along_x])
+        both = partner_2(after(along_z, *small), "wide", 1)
         core_three = partner_2(near_three, "wide", 0)
         own_block = after(own_block, held)
         own_z = partner_2(own_block, "wide", 2)
@@ -506,7 +496,7 @@
     w_map = jnp.concatenate([w_bc, w_step], 1)
 
     def project(block, kind):
-        low = jnp.dot(block, w_map, preferred_element_type=F32).astype(kind)
+        low = jnp.dot(block, w_map, preferred_element_type=F32).astype(BF16)
         low, block = lax.optimization_barrier((low, block))
         high = jnp.einsum("td,dkc->ktc", block, w_xz, preferred_element_type=F32)
         return {"map": low, "xr": high[1].astype(kind), "z": high[0].astype(kind)}
@@ -525,19 +515,10 @@
         block = quad_arrange([own_four, own_core], [0, 4, 2, 6, 1, 5, 3, 7])
     else:
         block = after(block, *parts)
-    own = lax.optimization_barrier(project(block, BF16))
-
-    for step in range(1, req_count):
-        flat = after(got_states[step - 1], block)[:, heads * head_width :]
-        flat = flat.reshape(group_reqs, -1)
-        got = [flat[:, :x_size], flat[:, x_size:conv_size]]
-        caches = [
-            jnp.where((came_from == step)[:, None, None], here.reshape(cache.shape), cache)
-            for here, cache in zip(got, caches)
-        ]
-    caches = [jnp.where(live[:, None, None], cache, 0).astype(F32) for cache in caches]
+    own = lax.optimization_barrier(project(block, F32))
+
     bc_conv, cum, cum_t, step_t, coef, decay = prep(
-        ints, own["map"], came["map"], caches[1], const_bc, heads
+        ints, own["map"], came["map"], cache, const_bc, heads
     )
     wide_index = lax.axis_index("wide")
     group_span = lax.axis_size("wide") // GROUPS
@@ -552,7 +533,7 @@
     state_width = joined.shape[1] // 2
     came_xr = [after(got, own["xr"], bc_conv) for got in came["xr"]]
     result, final_state = mixer(
-        ints, own["xr"], came_xr, caches[0], const_x, joined[:, :state_width],
+        ints, own["xr"], came_xr, cache, const_x, joined[:, :state_width],
         joined[:, state_width:], cum, cum_t, step_t, coef, decay, held, got_states
     )
     gate = own["z"].astype(F32)

time: 106 us -> 105 us (level)
  starting transfers between devices: 22.3 us -> 29.1 us
  local copies, waits for them, and re-layouts: 15.7 us -> 8.94 us
  waiting for transfers between devices: 9.62 us -> 15.5 us
  other arithmetic: 11.5 us -> 6.92 us
    ppermute x4 -> x5, waiting for transfers between devices: 1.28 us -> 7.82 us  [shift_req(): lax.ppermute(block, 'req', [(i, (i + step) % count) for i in range(count)])]
    ppermute x10, starting transfers between devices: 7.34 us -> 10.8 us  [partner_2(): return lax.ppermute(block, axis, route)]
    ppermute x4 -> x5, starting transfers between devices: 10.2 us -> 13.6 us  [shift_req(): lax.ppermute(block, 'req', [(i, (i + step) % count) for i in range(count)])]
    unnamed x72 -> x51, local copies, waits for them, and re-layouts: 8.12 us -> 5.11 us
    reduce_sum x4 -> x2, other arithmetic: 3.12 us -> 0.26 us  [conv_of(): jnp.sum(jnp.where(hit[:, :, None, None], pool[None], 0), 1)]
    convert_element_type x2 -> x1, local copies, waits for them, and re-layouts: 3.13 us -> 1.03 us  [project(): return {'map': low, 'xr': high[1].astype(kind), 'z': high[0].astype(kind)}]
    squeeze x0 -> x1, local copies, waits for them, and re-layouts: none -> 1.12 us  [project(): return {'map': low, 'xr': high[1].astype(kind), 'z': high[0].astype(kind)}]
  transfers between devices with their start and end apart: 16 -> 17, of which waited for: 5 -> 4; matrix products, arithmetic and copies ran while one was open for 42% -> 33% of each run, Pallas kernels for 17% -> 16%
where the time goes in v13:
time: 105 us; the launch traced here: 104 us
  starting transfers between devices  29.1 us (28%)
  matrix products  26 us (25%)
  Pallas kernels  16.8 us (16%)
  waiting for transfers between devices  15.5 us (15%)
  local copies, waits for them, and re-layouts  8.94 us (9%)
  other arithmetic  6.92 us (7%)
    dot_general x2, matrix products, project(): high = jnp.einsum('td,dkc->ktc', block, w_xz, preferred_element_type=F32)  23.5 us
    ppermute x5, starting transfers between devices, shift_req(): lax.ppermute(block, 'req', [(i, (i + step) % count) for i in range(count)])  13.6 us
    ppermute x10, starting transfers between devices, partner_2(): return lax.ppermute(block, axis, route)  10.8 us
    ppermute x5, waiting for transfers between devices, shift_req(): lax.ppermute(block, 'req', [(i, (i + step) % count) for i in range(count)])  7.82 us
    ppermute x10, waiting for transfers between devices, partner_2(): return lax.ppermute(block, axis, route)  7.69 us
    pallas_call x1, Pallas kernels, mixer(): pl.pallas_call(functools.partial(mixer_kernel, count_req, len(got)), out_...  7.68 us
    pallas_call x2, Pallas kernels, pack(): pl.pallas_call(pack_kernel, out_shape=jax.ShapeDtypeStruct((count_req,) +...  5.14 us
    unnamed x51, local copies, waits for them, and re-layouts  5.11 us
  transfers between devices with their start and end apart: 17, of which 4 were waited for; matrix products, arithmetic and copies ran while one was open for 33% of the time, Pallas kernels for 16%

profile of v13, /device:TPU:0, one launch (start us, length us, event | category | flops | bytes accessed | tf_op | source)
XLA Modules:
  0.0 104.3 jit_solution(3322855234108848134)
XLA Ops:
  0.6 4.1 %collective-permute-start = (bf16[256,512]{1,0:T(8,128)(2,1)}, bf16[256,512]{1,0:T(8,128)(2,1)S(1)}, u32[]{:S(2)}, u32[]{:S(2)}) collective-permute-start(bf16[256,512]{1,0:T(8,128)(2,1)} %param.20), channel_id=1, source_target_pairs={{0,16},{1,0},{2,18},{3,2},{4,20},{5,4},{6,22},{7,6},{8,24},{9,8},{... | collective-permute-start | bytes 786440 | tf_op jit(solution)/shard_map/ppermute | solution.py:90
  6.2 3.0 %shard_map.203 = bf16[2,1024,256]{2,1,0:T(8,128)(2,1)} custom-call(s32[2]{0:T(128)S(1)} %subtract_clamp_fusion.2.slots_ref, f32[8,16,64,256]{3,2,1,0:T(8,128)} %pool_ref.3), custom_call_target="tpu_custom_call" | custom-call | bytes 3145728 | tf_op jit(solution)/shard_map/pallas_call | solution.py:228
  9.1 4.2 %collective-permute-start.10 = (bf16[2,1024,256]{2,1,0:T(8,128)(2,1)}, bf16[2,1024,256]{2,1,0:T(8,128)(2,1)}, u32[]{:S(2)}, u32[]{:S(2)}) collective-permute-start(bf16[2,1024,256]{2,1,0:T(8,128)(2,1)} %shard_map.203), channel_id=1, source_target_pairs={{0,1},{1,0},{2,3},{3,2},{4,5},{5,4},{6,7},{7,6},{8,9},{9,8},{10,11... | collective-permute-start | bytes 3145736 | tf_op jit(solution)/shard_map/ppermute | solution.py:40
  14.3 1.6 %collective-permute-start.7 = (bf16[256,512]{1,0:T(8,128)(2,1)S(1)}, bf16[256,512]{1,0:T(8,128)(2,1)S(1)}, u32[]{:S(2)}, u32[]{:S(2)}) collective-permute-start(bf16[256,512]{1,0:T(8,128)(2,1)S(1)} %get-tuple-element.42), channel_id=1, source_target_pairs={{0,4},{4,0},{2,6},{6,2},{8,12},{12,8},{10,14},{14,10},{16,20},{20,... | collective-permute-start | bytes 786440 | tf_op jit(solution)/shard_map/ppermute | solution.py:35
  15.8 4.3 %collective-permute-start.3 = (bf16[256,512]{1,0:T(8,128)(2,1)S(1)}, bf16[256,512]{1,0:T(8,128)(2,1)S(1)}, u32[]{:S(2)}, u32[]{:S(2)}) collective-permute-start(bf16[256,512]{1,0:T(8,128)(2,1)S(1)} %get-tuple-element.42), channel_id=1, source_target_pairs={{0,8},{8,0},{2,10},{10,2},{4,12},{12,4},{6,14},{14,6},{16,24},{24,... | collective-permute-start | bytes 786440 | tf_op jit(solution)/shard_map/ppermute | solution.py:35
  20.4 2.2 %shard_map.204.refs_11_ = f32[2,16,64,256]{3,2,1,0:T(8,128)S(1)} custom-call(s32[2]{0:T(128)S(1)} %get-tuple-element.99.slots_ref, f32[8,16,64,256]{3,2,1,0:T(8,128)} %pool_ref.3), custom_call_target="tpu_custom_call" | custom-call | bytes 3145728 | tf_op jit(solution)/shard_map/pallas_call | solution.py:228
  23.2 4.7 %collective-permute-start.4 = (bf16[2,3,1280]{2,1,0:T(4,128)(2,1)S(1)}, bf16[2,3,1280]{2,1,0:T(4,128)(2,1)S(1)}, u32[]{:S(2)}, u32[]{:S(2)}) collective-permute-start(bf16[2,3,1280]{2,1,0:T(4,128)(2,1)S(1)} %pad_maximum_fusion.9), channel_id=1, source_target_pairs={{0,1},{1,0},{2,3},{3,2},{4,5},{5,4},{6,7},{7,6},{8,9},{9,8},{10,11... | collective-permute-start | bytes 46088 | tf_op jit(solution)/shard_map/ppermute | solution.py:40
  27.9 1.3 %copy.29 = bf16[4096,16]{1,0:T(8,128)(2,1)} copy(bf16[4096,16]{0,1:T(8,128)(2,1)S(1)} %copy-done.9) | data formatting | bytes 262144 | tf_op jit(solution)/shard_map/optimization_barrier | solution.py:444
  29.3 1.2 %collective-permute-start.2 = (bf16[256,512]{1,0:T(8,128)(2,1)}, bf16[256,512]{1,0:T(8,128)(2,1)}, u32[]{:S(2)}, u32[]{:S(2)}) collective-permute-start(bf16[256,512]{1,0:T(8,128)(2,1)} %get-tuple-element.46), channel_id=1, source_target_pairs={{0,8},{8,0},{2,10},{10,2},{4,12},{12,4},{6,14},{14,6},{16,24},{24,... | collective-permute-start | bytes 786440 | tf_op jit(solution)/shard_map/ppermute | solution.py:35
  32.5 7.8 %collective-permute-done.4 = bf16[2,3,1280]{2,1,0:T(4,128)(2,1)S(1)} collective-permute-done((bf16[2,3,1280]{2,1,0:T(4,128)(2,1)S(1)}, bf16[2,3,1280]{2,1,0:T(4,128)(2,1)S(1)}, u32[]{:S(2)}, u32[]{:S(2)}) %collective-permute-start.4) | collective-permute-done | bytes 15392 | tf_op jit(solution)/shard_map/ppermute | solution.py:40
  40.4 1.6 %collective-permute-start.5 = (bf16[256,512]{1,0:T(8,128)(2,1)}, bf16[256,512]{1,0:T(8,128)(2,1)S(1)}, u32[]{:S(2)}, u32[]{:S(2)}) collective-permute-start(bf16[256,512]{1,0:T(8,128)(2,1)} %copy-done.7), channel_id=1, source_target_pairs={{0,4},{4,0},{2,6},{6,2},{8,12},{12,8},{10,14},{14,10},{16,20},{20,... | collective-permute-start | bytes 786440 | tf_op jit(solution)/shard_map/ppermute | solution.py:35
  42.0 5.3 %collective-permute-done.5 = bf16[256,512]{1,0:T(8,128)(2,1)S(1)} collective-permute-done((bf16[256,512]{1,0:T(8,128)(2,1)}, bf16[256,512]{1,0:T(8,128)(2,1)S(1)}, u32[]{:S(2)}, u32[]{:S(2)}) %collective-permute-start.5) | collective-permute-done | bytes 262176 | tf_op jit(solution)/shard_map/ppermute | solution.py:35
  48.4 1.6 %collective-permute-start.6 = (bf16[2,256,512]{2,1,0:T(8,128)(2,1)S(1)}, bf16[2,256,512]{2,1,0:T(8,128)(2,1)S(1)}, u32[]{:S(2)}, u32[]{:S(2)}) collective-permute-start(bf16[2,256,512]{2,1,0:T(8,128)(2,1)S(1)} %pad_maximum_fusion.8), channel_id=1, source_target_pairs={{0,4},{4,0},{2,6},{6,2},{8,12},{12,8},{10,14},{14,10},{16,20},{20,... | collective-permute-start | bytes 1572872 | tf_op jit(solution)/shard_map/ppermute | solution.py:35
  50.1 1.5 %shard_map.205 = bf16[256,4096]{1,0:T(8,128)(2,1)S(1)} custom-call(s32[8]{0:T(128)S(1)} %broadcast_xor_fusion.places_ref, bf16[3,256,512]{2,1,0:T(8,128)(2,1)S(1)} %pad_maximum_fusion.7.refs_0_, bf16[1,256,512]{2,1,0:T(8,128)(2,1)S(1)} %bitcast.39, bf16[3,256,512]{2,1,0:T(8,128)(2,1)} %collective-permute-done.8.refs_2_, ...), custom_call_target="tpu_custom_call" | custom-call | flops 1000000 | bytes 10000 | tf_op jit(solution)/shard_map/pallas_call | solution.py:72
  52.2 1.3 %fusion.23 = bf16[256,272]{1,0:T(8,128)(2,1)S(1)} fusion(bf16[256,4096]{1,0:T(8,128)(2,1)S(1)} %shard_map.205, bf16[4096,16]{1,0:T(8,128)(2,1)S(1)} %copy-done.5, bf16[4096,256]{1,0:T(8,128)(2,1)S(1)} %copy-done.21), kind=kOutput, calls=%fused_computation.14 | convolution fusion | flops 574951424 | bytes 4464640 | tf_op jit(solution)/shard_map/dot_general | solution.py:499
  53.4 11.3 %fusion.18 = bf16[2,256,1024]{2,1,0:T(8,128)(2,1)S(1)} fusion(bf16[4096,2,1024]{2,1,0:T(2,128)(2,1)} %param.21, bf16[256,4096]{1,0:T(8,128)(2,1)S(1)} %shard_map.205), kind=kOutput, calls=%fused_computation.11 | convolution fusion | flops 4295491584 | bytes 19922944 | tf_op jit(solution)/shard_map/td,dkc->ktc/dot_general | solution.py:501
  66.1 2.6 %collective-permute-start.13 = (bf16[256,272]{1,0:T(8,128)(2,1)S(1)}, bf16[256,272]{1,0:T(8,128)(2,1)S(1)}, u32[]{:S(2)}, u32[]{:S(2)}) collective-permute-start(bf16[256,272]{1,0:T(8,128)(2,1)S(1)} %fusion.23), channel_id=1, source_target_pairs={{0,1},{1,0},{2,3},{3,2},{4,5},{5,4},{6,7},{7,6},{8,9},{9,8},{10,11... | collective-permute-start | bytes 417800 | tf_op jit(solution)/shard_map/ppermute | solution.py:40
  68.7 2.0 %collective-permute-start.15 = (bf16[256,1024]{1,0:T(8,128)(2,1)}, bf16[256,1024]{1,0:T(8,128)(2,1)}, u32[]{:S(2)}, u32[]{:S(2)}) collective-permute-start(bf16[256,1024]{1,0:T(8,128)(2,1)} %get-tuple-element.66), channel_id=1, source_target_pairs={{0,1},{1,0},{2,3},{3,2},{4,5},{5,4},{6,7},{7,6},{8,9},{9,8},{10,11... | collective-permute-start | bytes 1572872 | tf_op jit(solution)/shard_map/ppermute | solution.py:40
  71.4 1.3 %fusion.24.own_ref = bf16[256,272]{1,0:T(8,128)(2,1)S(1)} fusion(bf16[256,4096]{1,0:T(8,128)(2,1)S(1)} %shard_map.206, bf16[4096,16]{1,0:T(8,128)(2,1)S(1)} %copy-done.5, bf16[4096,256]{1,0:T(8,128)(2,1)S(1)} %copy-done.21), kind=kOutput, calls=%fused_computation.15 | convolution fusion | flops 574951424 | bytes 4464640 | tf_op jit(solution)/shard_map/dot_general | solution.py:499
  72.7 12.2 %fusion.8 = f32[2,256,1024]{2,1,0:T(8,128)S(1)} fusion(bf16[4096,2,1024]{2,1,0:T(2,128)(2,1)} %param.21, bf16[256,4096]{1,0:T(8,128)(2,1)S(1)} %shard_map.206), kind=kOutput, calls=%fused_computation.9 | convolution fusion | flops 4294967296 | bytes 20971520 | tf_op jit(solution)/shard_map/td,dkc->ktc/dot_general | solution.py:501
  86.0 1.8 %shard_map.207 = (bf16[256,256]{1,0:T(8,128)(2,1)S(1)}, f32[4,256,4]{2,1,0:T(8,128)S(1)}, f32[4,4,256]{2,1,0:T(4,128)S(1)}, f32[4,4,256]{2,1,0:T(4,128)S(1)}, f3...) custom-call(s32[6]{0:T(128)S(1)} %pad_add_fusion.ints_ref, bf16[256,272]{1,0:T(8,128)(2,1)S(1)} %fusion.24.own_ref, ...), custom_call_target="tpu_custom_call" | custom-call | flops 1000000 | bytes 10000 | tf_op jit(solution)/shard_map/pallas_call | solution.py:204
  89.4 1.3 %collective-permute-done.14 = bf16[256,256]{1,0:T(8,128)(2,1)S(1)} collective-permute-done((bf16[256,256]{1,0:T(8,128)(2,1)S(1)}, bf16[256,256]{1,0:T(8,128)(2,1)S(1)}, u32[]{:S(2)}, u32[]{:S(2)}) %collective-permute-start.14) | collective-permute-done | bytes 131104 | tf_op jit(solution)/shard_map/ppermute | solution.py:35
  93.0 7.7 %shard_map.208 = (f32[256,1024]{1,0:T(8,128)S(1)}, f32[2,16,64,256]{3,2,1,0:T(8,128)}) custom-call(s32[6]{0:T(128)S(1)} %pad_add_fusion.ints_ref, f32[256,1024]{1,0:T(8,128)S(1)} %get-tuple-element.70.refs_0_, bf16[256,1024]{1,0:T(8,128)(2,1)} %collective-permute-done.12.refs_1_, f32[2,3,1280]{2,1,0:T(4,128)S(1)} %fusion.30.refs_1_.refs_2_, ...), custom_call_target="tpu_custom_call" | custom-call | flops 1000000 | bytes 10000 | tf_op jit(solution)/shard_map/pallas_call | solution.py:357
  100.7 1.5 %multiply_reduce_fusion = (f32[256]{0:T(256)S(1)}, f32[256,1024]{1,0:T(8,128)S(1)}) fusion(f32[256,1024]{1,0:T(8,128)S(1)} %get-tuple-element.79, f32[256,1024]{1,0:T(8,128)S(1)} %copy-done.4, bf16[256,1024]{1,0:T(8,128)(2,1)} %collective-permute-done.15), kind=kLoop, calls=%fused_computation.23 | loop fusion | flops 2883328 | bytes 3671040 | tf_op jit(solution)/shard_map/reduce_sum | solution.py:543
  (104 shorter events, 16.1 us)
Async XLA Ops:
  0.6 12.7 %collective-permute-start = (bf16[256,512]{1,0:T(8,128)(2,1)}, bf16[256,512]{1,0:T(8,128)(2,1)S(1)}, u32[]{:S(2)}, u32[]{:S(2)}) collective-permute-start(bf16[256,512]{1,0:T(8,128)(2,1)} %param.20), channel_id=1, source_target_pairs={{0,16},{1,0},{2,18},{3,2},{4,20},{5,4},{6,22},{7,6},{8,24},{9,8},{... | collective-permute-start | bytes 786440 | tf_op jit(solution)/shard_map/ppermute | solution.py:90
  4.7 8.6 %collective-permute-start.1 = (bf16[256,512]{1,0:T(8,128)(2,1)}, bf16[256,512]{1,0:T(8,128)(2,1)S(1)}, u32[]{:S(2)}, u32[]{:S(2)}) collective-permute-start(bf16[256,512]{1,0:T(8,128)(2,1)} %param.20), channel_id=1, source_target_pairs={{1,16},{3,18},{5,20},{7,22},{9,24},{11,26},{13,28},{15,30},{16,1},... | collective-permute-start | bytes 786440 | tf_op jit(solution)/shard_map/ppermute | solution.py:91
  6.2 14.0 %copy-start.22 = (s32[2]{0:T(128)S(1)}, s32[2]{0:T(128)}, u32[]{:S(2)}) copy-start(s32[2]{0:T(128)} %param.33) | copy-start | bytes 28
  9.1 40.9 %collective-permute-start.10 = (bf16[2,1024,256]{2,1,0:T(8,128)(2,1)}, bf16[2,1024,256]{2,1,0:T(8,128)(2,1)}, u32[]{:S(2)}, u32[]{:S(2)}) collective-permute-start(bf16[2,1024,256]{2,1,0:T(8,128)(2,1)} %shard_map.203), channel_id=1, source_target_pairs={{0,1},{1,0},{2,3},{3,2},{4,5},{5,4},{6,7},{7,6},{8,9},{9,8},{10,11... | collective-permute-start | bytes 3145736 | tf_op jit(solution)/shard_map/ppermute | solution.py:40
  14.3 16.4 %collective-permute-start.7 = (bf16[256,512]{1,0:T(8,128)(2,1)S(1)}, bf16[256,512]{1,0:T(8,128)(2,1)S(1)}, u32[]{:S(2)}, u32[]{:S(2)}) collective-permute-start(bf16[256,512]{1,0:T(8,128)(2,1)S(1)} %get-tuple-element.42), channel_id=1, source_target_pairs={{0,4},{4,0},{2,6},{6,2},{8,12},{12,8},{10,14},{14,10},{16,20},{20,... | collective-permute-start | bytes 786440 | tf_op jit(solution)/shard_map/ppermute | solution.py:35
  15.8 14.9 %collective-permute-start.3 = (bf16[256,512]{1,0:T(8,128)(2,1)S(1)}, bf16[256,512]{1,0:T(8,128)(2,1)S(1)}, u32[]{:S(2)}, u32[]{:S(2)}) collective-permute-start(bf16[256,512]{1,0:T(8,128)(2,1)S(1)} %get-tuple-element.42), channel_id=1, source_target_pairs={{0,8},{8,0},{2,10},{10,2},{4,12},{12,4},{6,14},{14,6},{16,24},{24,... | collective-permute-start | bytes 786440 | tf_op jit(solution)/shard_map/ppermute | solution.py:35
  20.4 10.1 %copy-start.16 = (f32[4,256]{1,0:T(4,128)S(1)}, f32[4,256]{1,0:T(4,128)}, u32[]{:S(2)}) copy-start(f32[4,256]{1,0:T(4,128)} %param.29) | copy-start | bytes 12292
  20.4 10.2 %copy-start.11 = (f32[1024]{0:T(1024)S(1)}, f32[1024]{0:T(1024)}, u32[]{:S(2)}) copy-start(f32[1024]{0:T(1024)} %param.31) | copy-start | bytes 12292
  20.4 10.2 %copy-start.12 = (f32[4,1024]{1,0:T(4,128)S(1)}, f32[4,1024]{1,0:T(4,128)}, u32[]{:S(2)}) copy-start(f32[4,1024]{1,0:T(4,128)} %param.27) | copy-start | bytes 49156
  20.4 10.2 %copy-start.15 = (f32[1024]{0:T(1024)S(1)}, f32[1024]{0:T(1024)}, u32[]{:S(2)}) copy-start(f32[1024]{0:T(1024)} %param.28) | copy-start | bytes 12292
  20.4 10.2 %copy-start.23 = (s32[1,2]{1,0:T(1,128)S(1)}, s32[1,2]{1,0:T(1,128)}, u32[]{:S(2)}) copy-start(s32[1,2]{1,0:T(1,128)} %param.32) | copy-start | bytes 28
  22.6 24.7 %copy-start.24 = (s32[8]{0:T(128)S(1)}, s32[8]{0:T(128)}, u32[]{:S(2)}) copy-start(s32[8]{0:T(128)} %constant.104.clone) | copy-start | bytes 100
  23.2 17.1 %collective-permute-start.4 = (bf16[2,3,1280]{2,1,0:T(4,128)(2,1)S(1)}, bf16[2,3,1280]{2,1,0:T(4,128)(2,1)S(1)}, u32[]{:S(2)}, u32[]{:S(2)}) collective-permute-start(bf16[2,3,1280]{2,1,0:T(4,128)(2,1)S(1)} %pad_maximum_fusion.9), channel_id=1, source_target_pairs={{0,1},{1,0},{2,3},{3,2},{4,5},{5,4},{6,7},{7,6},{8,9},{9,8},{10,11... | collective-permute-start | bytes 46088 | tf_op jit(solution)/shard_map/ppermute | solution.py:40
  29.3 12.7 %collective-permute-start.2 = (bf16[256,512]{1,0:T(8,128)(2,1)}, bf16[256,512]{1,0:T(8,128)(2,1)}, u32[]{:S(2)}, u32[]{:S(2)}) collective-permute-start(bf16[256,512]{1,0:T(8,128)(2,1)} %get-tuple-element.46), channel_id=1, source_target_pairs={{0,8},{8,0},{2,10},{10,2},{4,12},{12,4},{6,14},{14,6},{16,24},{24,... | collective-permute-start | bytes 786440 | tf_op jit(solution)/shard_map/ppermute | solution.py:35
  32.5 17.6 %collective-permute-start.8 = (bf16[3,256,512]{2,1,0:T(8,128)(2,1)S(1)}, bf16[3,256,512]{2,1,0:T(8,128)(2,1)}, u32[]{:S(2)}, u32[]{:S(2)}) collective-permute-start(bf16[3,256,512]{2,1,0:T(8,128)(2,1)S(1)} %pad_maximum_fusion.7.refs_0_), channel_id=1, source_target_pairs={{0,2},{2,0},{4,6},{6,4},{8,10},{10,8},{12,14},{14,12},{16,18},{18,... | collective-permute-start | bytes 2359304 | tf_op jit(solution)/shard_map/ppermute | solution.py:35
  40.4 6.9 %collective-permute-start.5 = (bf16[256,512]{1,0:T(8,128)(2,1)}, bf16[256,512]{1,0:T(8,128)(2,1)S(1)}, u32[]{:S(2)}, u32[]{:S(2)}) collective-permute-start(bf16[256,512]{1,0:T(8,128)(2,1)} %copy-done.7), channel_id=1, source_target_pairs={{0,4},{4,0},{2,6},{6,2},{8,12},{12,8},{10,14},{14,10},{16,20},{20,... | collective-permute-start | bytes 786440 | tf_op jit(solution)/shard_map/ppermute | solution.py:35
  47.3 2.7 %collective-permute-start.9 = (bf16[1,256,512]{2,1,0:T(8,128)(2,1)S(1)}, bf16[1,256,512]{2,1,0:T(8,128)(2,1)S(1)}, u32[]{:S(2)}, u32[]{:S(2)}) collective-permute-start(bf16[1,256,512]{2,1,0:T(8,128)(2,1)S(1)} %bitcast.38), channel_id=1, source_target_pairs={{0,2},{2,0},{4,6},{6,4},{8,10},{10,8},{12,14},{14,12},{16,18},{18,... | collective-permute-start | bytes 786440 | tf_op jit(solution)/shard_map/ppermute | solution.py:35
  48.4 17.3 %collective-permute-start.6 = (bf16[2,256,512]{2,1,0:T(8,128)(2,1)S(1)}, bf16[2,256,512]{2,1,0:T(8,128)(2,1)S(1)}, u32[]{:S(2)}, u32[]{:S(2)}) collective-permute-start(bf16[2,256,512]{2,1,0:T(8,128)(2,1)S(1)} %pad_maximum_fusion.8), channel_id=1, source_target_pairs={{0,4},{4,0},{2,6},{6,2},{8,12},{12,8},{10,14},{14,10},{16,20},{20,... | collective-permute-start | bytes 1572872 | tf_op jit(solution)/shard_map/ppermute | solution.py:35
  65.8 4.9 %collective-permute-start.11 = (bf16[4,256,512]{2,1,0:T(8,128)(2,1)S(1)}, bf16[4,256,512]{2,1,0:T(8,128)(2,1)S(1)}, u32[]{:S(2)}, u32[]{:S(2)}) collective-permute-start(bf16[4,256,512]{2,1,0:T(8,128)(2,1)S(1)} %constant_dynamic-update-slice_fusion.refs_0_), channel_id=1, source_target_pairs={{0,2},{2,0},{4,6},{6,4},{8,10},{10,8},{12,14},{14,12},{16,18},{18,... | collective-permute-start | bytes 3145736 | tf_op jit(solution)/shard_map/ppermute | solution.py:35
  66.1 19.9 %collective-permute-start.13 = (bf16[256,272]{1,0:T(8,128)(2,1)S(1)}, bf16[256,272]{1,0:T(8,128)(2,1)S(1)}, u32[]{:S(2)}, u32[]{:S(2)}) collective-permute-start(bf16[256,272]{1,0:T(8,128)(2,1)S(1)} %fusion.23), channel_id=1, source_target_pairs={{0,1},{1,0},{2,3},{3,2},{4,5},{5,4},{6,7},{7,6},{8,9},{9,8},{10,11... | collective-permute-start | bytes 417800 | tf_op jit(solution)/shard_map/ppermute | solution.py:40
  68.7 20.7 %collective-permute-start.12 = (bf16[256,1024]{1,0:T(8,128)(2,1)}, bf16[256,1024]{1,0:T(8,128)(2,1)}, u32[]{:S(2)}, u32[]{:S(2)}) collective-permute-start(bf16[256,1024]{1,0:T(8,128)(2,1)} %get-tuple-element.65), channel_id=1, source_target_pairs={{0,1},{1,0},{2,3},{3,2},{4,5},{5,4},{6,7},{7,6},{8,9},{9,8},{10,11... | collective-permute-start | bytes 1572872 | tf_op jit(solution)/shard_map/ppermute | solution.py:40
  68.7 32.0 %collective-permute-start.15 = (bf16[256,1024]{1,0:T(8,128)(2,1)}, bf16[256,1024]{1,0:T(8,128)(2,1)}, u32[]{:S(2)}, u32[]{:S(2)}) collective-permute-start(bf16[256,1024]{1,0:T(8,128)(2,1)} %get-tuple-element.66), channel_id=1, source_target_pairs={{0,1},{1,0},{2,3},{3,2},{4,5},{5,4},{6,7},{7,6},{8,9},{9,8},{10,11... | collective-permute-start | bytes 1572872 | tf_op jit(solution)/shard_map/ppermute | solution.py:40
  89.4 1.3 %collective-permute-start.14 = (bf16[256,256]{1,0:T(8,128)(2,1)S(1)}, bf16[256,256]{1,0:T(8,128)(2,1)S(1)}, u32[]{:S(2)}, u32[]{:S(2)}) collective-permute-start(bf16[256,256]{1,0:T(8,128)(2,1)S(1)} %get-tuple-element.72), channel_id=1, source_target_pairs={{0,2},{2,0},{4,6},{6,4},{8,10},{10,8},{12,14},{14,12},{16,18},{18,... | collective-permute-start | bytes 393224 | tf_op jit(solution)/shard_map/ppermute | solution.py:35
  102.2 1.2 %collective-permute-start.16 = (f32[256]{0:T(256)S(1)}, f32[256]{0:T(256)S(1)}, u32[]{:S(2)}, u32[]{:S(2)}) collective-permute-start(f32[256]{0:T(256)S(1)} %get-tuple-element.86), channel_id=1, source_target_pairs={{0,2},{2,0},{4,6},{6,4},{8,10},{10,8},{12,14},{14,12},{16,18},{18,... | collective-permute-start | bytes 3080 | tf_op jit(solution)/shard_map/ppermute | solution.py:35
  (18 other events, 70.7 us)

commit v14 on v13

--- a/solution.py
+++ b/solution.py
@@ -126,8 +126,26 @@
     return position, seg, first
 
 
+def cached_rows(ints_ref, refs, count_req, first_flag, places, per_place, at, channels):
+    rows = []
+    for request in range(count_req):
+        total = None
+        for step, ref in enumerate(refs):
+            flag = ints_ref[first_flag + request * len(refs) + step].astype(F32)
+            term = ref[request].astype(F32) * flag
+            total = term if total is None else total + term
+        index = lax.broadcasted_iota(jnp.int32, total.shape, 0)
+        rows.append([
+            jnp.sum(jnp.where(index == place * per_place + at, total, 0.0), 0, keepdims=True)[
+                :, :channels
+            ]
+            for place in range(places)
+        ])
+    return rows
+
+
 def conv_silu(values, cache, const_ref, seg, offset):
-    kernel_len = cache.shape[1] + 1
+    kernel_len = len(cache[0]) + 1
     taps = [const_ref[k : k + 1, :] for k in range(kernel_len)]
     bias = const_ref[kernel_len : kernel_len + 1, :]
     total = bias + taps[kernel_len - 1] * values
@@ -135,33 +153,35 @@
         earlier = pltpu.roll(values, lag, 0)
         total = total + taps[kernel_len - 1 - lag] * jnp.where(offset >= lag, earlier, 0.0)
     cached = jnp.zeros_like(values)
-    for request in range(cache.shape[0]):
+    for request in range(len(cache)):
         for place in range(kernel_len - 1):
             history = jnp.zeros_like(bias)
             for lag in range(place + 1, kernel_len):
                 at = kernel_len - 1 + place - lag
-                history = history + taps[kernel_len - 1 - lag] * cache[request, at : at + 1, :]
+                history = history + taps[kernel_len - 1 - lag] * cache[request][at]
             cached = jnp.where((seg == request) & (offset == place), history, cached)
     total = total + cached
     return total * jax.nn.sigmoid(total)
 
 
-def prep_kernel(count_req, got_total, heads, ints_ref, own_ref, *refs):
+def prep_kernel(count_req, got_total, heads, per_place, places, ints_ref, own_ref, *refs):
     got = refs[:got_total]
-    cache_ref, const_ref = refs[got_total : got_total + 2]
-    bc_ref, cum_ref, cum_t_ref, step_t_ref, coef_ref, decay_ref = refs[got_total + 2 :]
+    row_refs = refs[got_total : 2 * got_total + 1]
+    const_ref, bc_ref, small_ref, decay_ref = refs[2 * got_total + 1 :]
     tokens = own_ref.shape[0]
     channels = const_ref.shape[1]
-    kernel_len = cache_ref.shape[1] + 1
-    dt_bias = const_ref[kernel_len + 1 : kernel_len + 2, :heads]
-    a_log = const_ref[kernel_len + 2 : kernel_len + 3, :heads]
+    dt_bias = const_ref[places + 2 : places + 3, :heads]
+    a_log = const_ref[places + 3 : places + 4, :heads]
     starts = [ints_ref[j] for j in range(count_req)]
     total = own_ref[...].astype(F32)
     for ref in got:
         total = total + ref[...].astype(F32)
     total = total.astype(BF16).astype(F32)
     position, seg, first = token_places(starts, tokens, (tokens, channels), 0)
-    bc = conv_silu(total[:, :channels], cache_ref[:, :, -channels:], const_ref, seg, position - first)
+    cache = cached_rows(
+        ints_ref, row_refs, count_req, count_req, places, per_place, per_place - 1, channels
+    )
+    bc = conv_silu(total[:, :channels], cache, const_ref, seg, position - first)
     bc_ref[...] = bc.astype(BF16)
     raw = total[:, channels : channels + heads] + dt_bias
     step = jnp.maximum(raw, 0.0) + jnp.log1p(jnp.exp(-jnp.abs(raw)))
@@ -171,20 +191,18 @@
     same = seg == seg_other
     mask = jnp.where(same & (position >= other), 1.0, 0.0)
     after = jnp.where(same & (position < other), 1.0, 0.0)
-    cum = jnp.dot(mask, rate, precision=HIGH, preferred_element_type=F32)
     left = jnp.dot(after, rate, precision=HIGH, preferred_element_type=F32)
     cum_t = lax.dot_general(
         rate, mask, (((0,), (1,)), ((), ())), precision=HIGH, preferred_element_type=F32
     )
     step_t = step.T
-    coef = jnp.exp(left) * step
-    part = cum_ref.shape[2]
-    for i in range(cum_ref.shape[0]):
+    coef_t = (jnp.exp(left) * step).T
+    steps = small_ref.shape[0]
+    part = heads // steps
+    for i in range(steps):
         place = slice(i * part, (i + 1) * part)
-        cum_ref[i] = cum[:, place]
-        cum_t_ref[i] = cum_t[place, :]
-        step_t_ref[i] = step_t[place, :]
-        coef_ref[i] = coef[:, place]
+        for row, array in enumerate((cum_t, step_t, coef_t)):
+            small_ref[i, row * part : (row + 1) * part, :] = array[place, :]
     at, seg_at, _ = token_places(starts, tokens, (8, tokens), 1)
     row = lax.broadcasted_iota(jnp.int32, (8, tokens), 0)
     ends = jnp.dot(
@@ -193,62 +211,103 @@
     decay_ref[...] = jnp.exp(ends)
 
 
-def prep(ints, own, got, cache, const, heads):
+def prep(ints, own, got, row_arrays, row_total, const, heads, per_place, places):
     tokens = own.shape[0]
     channels = const.shape[1]
-    count_req = cache.shape[0]
-    vmem = pl.BlockSpec(memory_space=pltpu.VMEM)
     part = min(HEADS_STEP, heads)
-    tall = jax.ShapeDtypeStruct((heads // part, tokens, part), F32)
-    flat = jax.ShapeDtypeStruct((heads // part, part, tokens), F32)
+    count_req = row_arrays[0].shape[0]
+    whole = lambda *shape: pl.BlockSpec(shape, lambda i: (0,) * len(shape))
+    shapes = [(tokens, channels), (heads // part, 3 * part, tokens), (8, heads)]
     return pl.pallas_call(
-        functools.partial(prep_kernel, count_req, len(got), heads),
+        functools.partial(prep_kernel, count_req, len(got), heads, per_place, places),
         out_shape=[
-            jax.ShapeDtypeStruct((tokens, channels), BF16),
-            tall,
-            flat,
-            flat,
-            tall,
-            jax.ShapeDtypeStruct((8, heads), F32),
+            jax.ShapeDtypeStruct(shape, kind) for shape, kind in zip(shapes, (BF16, F32, F32))
         ],
-        in_specs=[pl.BlockSpec(memory_space=pltpu.SMEM)] + [vmem] * (3 + len(got)),
-        out_specs=[vmem] * 6,
+        grid=(1,),
+        in_specs=[pl.BlockSpec(memory_space=pltpu.SMEM)]
+        + [whole(*own.shape)] * (1 + len(got))
+        + [rows_spec(array, row_total) for array in row_arrays]
+        + [whole(*const.shape)],
+        out_specs=[whole(*shape) for shape in shapes],
         compiler_params=params(),
         cost_estimate=cost(1e6, 1e4),
-    )(ints, own, *got, cache, const)
-
-
-def pack_kernel(slots_ref, pool_ref, out_ref):
-    out_ref[...] = pool_ref[...].reshape(out_ref.shape).astype(out_ref.dtype)
-
-
-def pack(pool, slots, shape, kind):
+    )(ints, own, *got, *row_arrays, const)
+
+
+def rows_spec(array, row_total):
+    last = array.shape[1] // row_total - 1
+    block = (array.shape[0], row_total, array.shape[2])
+    return pl.BlockSpec(block, lambda i, *_: (0, last, 0))
+
+
+def conv_rows(slot, pool_refs, row_total, lanes):
+    rows = []
+    for place in range(pool_refs[0].shape[0]):
+        for ref in pool_refs:
+            values = ref[place].astype(F32)
+            index = lax.broadcasted_iota(jnp.int32, values.shape, 0)
+            line = jnp.sum(jnp.where(index == slot, values, 0.0), 0, keepdims=True)
+            for first in range(0, line.shape[1], lanes):
+                row = line[:, first : first + lanes]
+                if row.shape[1] < lanes:
+                    row = jnp.concatenate(
+                        [row, jnp.zeros((1, lanes - row.shape[1]), F32)], 1
+                    )
+                rows.append(row)
+    rows += [jnp.zeros((1, lanes), F32)] * (row_total - len(rows))
+    return jnp.concatenate(rows, 0)
+
+
+def pack_kernel(row_total, slots_ref, pool_ref, x_ref, bc_ref, *out_refs):
+    rows, lanes = pool_ref.shape[1] * pool_ref.shape[2], pool_ref.shape[3]
+    slot = slots_ref[pl.program_id(0)]
+    conv = conv_rows(slot, (x_ref, bc_ref), row_total, lanes)
+    if len(out_refs) == 1:
+        out_ref = out_refs[0]
+        out_ref[0, :rows, :] = pool_ref[0].reshape(rows, lanes).astype(out_ref.dtype)
+        out_ref[0, rows:, :] = conv.astype(out_ref.dtype)
+    else:
+        out_refs[0][...] = pool_ref[...]
+        out_refs[1][0] = conv
+
+
+def pack(pool, conv_pools, row_total, slots, to_send):
     count_req = slots.shape[0]
-    block = (1,) + pool.shape[1:]
+    _, heads, width, state = pool.shape
+    block = (1, heads, width, state)
+    conv_pools = [jnp.transpose(array, (1, 0, 2)) for array in conv_pools]
+    shapes = [((1, heads * width + row_total, state), BF16)]
+    if not to_send:
+        shapes = [(block, F32), ((1, row_total, state), F32)]
     return pl.pallas_call(
-        pack_kernel,
-        out_shape=jax.ShapeDtypeStruct((count_req,) + shape, kind),
+        functools.partial(pack_kernel, row_total),
+        out_shape=[
+            jax.ShapeDtypeStruct((count_req,) + shape[1:], kind) for shape, kind in shapes
+        ],
         grid_spec=pltpu.PrefetchScalarGridSpec(
             num_scalar_prefetch=1,
             grid=(count_req,),
-            in_specs=[pl.BlockSpec(block, lambda j, slots: (slots[j], 0, 0, 0))],
-            out_specs=pl.BlockSpec((1,) + shape, lambda j, slots: (j,) + (0,) * len(shape)),
+            in_specs=[pl.BlockSpec(block, lambda j, slots: (slots[j], 0, 0, 0))]
+            + [pl.BlockSpec(array.shape, lambda j, slots: (0, 0, 0)) for array in conv_pools],
+            out_specs=[
+                pl.BlockSpec(shape, functools.partial(lambda n, j, _: (j,) + (0,) * n, len(shape) - 1))
+                for shape, _ in shapes
+            ],
         ),
         compiler_params=params(3 * VMEM_BYTES),
         cost_estimate=cost(0, 6 * pool[0].size * count_req),
-    )(slots, pool)
-
-
-def mixer_kernel(count_req, got_total, ints_ref, *refs):
+    )(slots, pool, *conv_pools)
+
+
+def mixer_kernel(count_req, got_total, per_place, places, ints_ref, *refs):
     own_ref = refs[0]
     got = refs[1 : 1 + got_total]
     rest = refs[1 + got_total :]
-    cache_ref, const_ref, b_ref, c_ref = rest[:4]
-    cum_ref, cum_t_ref, step_t_ref, coef_ref, decay_ref, held_ref = rest[4:10]
-    states = rest[10 : 10 + got_total]
-    out_ref, state_ref, scores_ref, c_part_ref, b_part_ref = rest[10 + got_total :]
-    kernel_len = cache_ref.shape[1] + 1
-    skip = const_ref[kernel_len + 1 : kernel_len + 2, :]
+    row_refs = rest[: got_total + 1]
+    const_ref, b_ref, c_ref, small_ref, decay_ref, held_ref = rest[got_total + 1 : got_total + 7]
+    states = rest[got_total + 7 : 2 * got_total + 7]
+    out_ref, state_ref, scores_ref, c_part_ref, b_part_ref = rest[2 * got_total + 7 :]
+    skip = const_ref[places + 2 : places + 3, :]
 
     def flag(request, step):
         place = count_req + request * (got_total + 1) + step
@@ -279,16 +338,19 @@
         total = total + ref[...].astype(F32)
     total = total.astype(BF16).astype(F32)
     position, seg, first = token_places(starts, tokens, (tokens, channels), 0)
-    values = conv_silu(total, cache_ref[...], const_ref, seg, position - first)
+    cache = cached_rows(
+        ints_ref, row_refs, count_req, count_req, places, per_place, pl.program_id(0), channels
+    )
+    values = conv_silu(total, cache, const_ref, seg, position - first)
     inputs = values.astype(BF16)
     values = inputs.astype(F32)
 
     lane_head = lax.broadcasted_iota(jnp.int32, (tokens, channels), 1) // width
     scores = scores_ref[...]
-    cum = cum_ref[0]
-    cum_t = cum_t_ref[0]
-    step_t = step_t_ref[0]
-    coef = coef_ref[0]
+    small = small_ref[0]
+    tall = small.T
+    cum_t, step_t = small[:heads], small[heads : 2 * heads]
+    cum, coef = tall[:, :heads], tall[:, 2 * heads :]
     grown = jnp.exp(cum)
     grown_wide = jnp.zeros((tokens, channels), F32)
     coef_wide = jnp.zeros((tokens, channels), F32)
@@ -327,11 +389,11 @@
 
 
 def mixer(
-    ints, own, got, cache, const, b_maps, c_maps, cum, cum_t, step_t, coef, decay, held, states
+    ints, own, got, row_arrays, row_total, const, b_maps, c_maps, small, decay, held, states,
+    per_place, places
 ):
     tokens, channels = own.shape
     count_req, heads, width, state = held.shape
-    kernel_len = cache.shape[1] + 1
     part = min(HEADS_STEP, heads)
     steps = heads // part
     wide = part * width
@@ -340,22 +402,19 @@
 
     in_specs = (
         [pl.BlockSpec((tokens, wide), columns)] * (1 + len(got))
+        + [rows_spec(array, row_total) for array in row_arrays]
         + [
-            pl.BlockSpec((count_req, kernel_len - 1, wide), lambda i, *_: (0, 0, i)),
             pl.BlockSpec((const.shape[0], wide), columns),
             pl.BlockSpec((tokens, state), whole),
             pl.BlockSpec((tokens, state), whole),
-            pl.BlockSpec((1, tokens, part), lambda i, *_: (i, 0, 0)),
-            pl.BlockSpec((1, part, tokens), lambda i, *_: (i, 0, 0)),
-            pl.BlockSpec((1, part, tokens), lambda i, *_: (i, 0, 0)),
-            pl.BlockSpec((1, tokens, part), lambda i, *_: (i, 0, 0)),
+            pl.BlockSpec((1,) + small.shape[1:], lambda i, *_: (i, 0, 0)),
             pl.BlockSpec(memory_space=pltpu.SMEM),
         ]
         + [pl.BlockSpec((count_req, part, width, state), lambda i, *_: (0, i, 0, 0))]
         + [pl.BlockSpec((count_req, wide, state), lambda i, *_: (0, i, 0))] * len(states)
     )
     return pl.pallas_call(
-        functools.partial(mixer_kernel, count_req, len(got)),
+        functools.partial(mixer_kernel, count_req, len(got), per_place, places),
         out_shape=[
             jax.ShapeDtypeStruct((tokens, channels), F32),
             jax.ShapeDtypeStruct((count_req, heads, width, state), F32),
@@ -377,8 +436,7 @@
         compiler_params=params(),
         cost_estimate=cost(1e6, 1e4),
     )(
-        ints, own, *got, cache, const, b_maps, c_maps, cum, cum_t, step_t, coef, decay, held,
-        *states
+        ints, own, *got, *row_arrays, const, b_maps, c_maps, small, decay, held, *states
     )
 
 
@@ -409,7 +467,6 @@
     slot_count, heads, head_width, state = ssm_pool.shape
     group_reqs = prefix_len.shape[0]
     lags = conv_x_pool.shape[1]
-    conv_width = local_width + state_part
 
     direct = req_count == 2 and lax.axis_size("wide") == 16
     if direct:
@@ -419,18 +476,13 @@
         asked = lax.dynamic_slice_in_dim(state_slot, index * group_reqs, group_reqs)
         return jnp.clip(asked - me * slot_count, 0, slot_count - 1)
 
-    def conv_of(slots):
-        hit = slots[:, None] == jnp.arange(slot_count)[None, :]
-        parts = [
-            jnp.sum(jnp.where(hit[:, :, None, None], pool[None], 0), 1)
-            for pool in (conv_x_pool, conv_bc_pool)
-        ]
-        return jnp.concatenate(parts, 2)
-
+    per_place = -(-local_width // state) - (-state_part // state)
+    row_total = -(-lags * per_place // 16) * 16
+    conv_pools = (conv_x_pool, conv_bc_pool)
     got_states = []
     for step in range(1, req_count):
         slots = slots_of((me + step) % req_count)
-        packed = pack(ssm_pool, slots, (heads * head_width, state), BF16)
+        packed = pack(ssm_pool, conv_pools, row_total, slots, True)[0]
         got_states.append(shift_req(packed, step))
 
     w_step = w_dt
@@ -439,11 +491,11 @@
         along_z = partner_2(block, "wide", 2)
         along_x = partner_2(block, "wide", 1)
         (
-            w_step, state_slot, prefix_len, stretch_start, conv_x_pool, conv_bc_pool, conv_x_w,
+            w_step, state_slot, prefix_len, stretch_start, conv_x_w,
             conv_x_b, conv_bc_w, conv_bc_b, d_skip, norm_gain, dt_bias, a_log
         ) = lax.optimization_barrier((
             (
-                w_dt, state_slot, prefix_len, stretch_start, conv_x_pool, conv_bc_pool, conv_x_w,
+                w_dt, state_slot, prefix_len, stretch_start, conv_x_w,
                 conv_x_b, conv_bc_w, conv_bc_b, d_skip, norm_gain, dt_bias, a_log
             ),
             block,
@@ -456,12 +508,7 @@
     flags = (live[:, None] & (came_from[:, None] == jnp.arange(req_count)[None, :])).astype(
         jnp.int32
     )
-    held = pack(ssm_pool, own_slots, (heads, head_width, state), F32)
-    cache = conv_of(own_slots)
-    for step in range(1, req_count):
-        got = shift_req(conv_of(slots_of((me + step) % req_count)), step)
-        cache = jnp.where((came_from == step)[:, None, None], got, cache)
-    cache = jnp.where(live[:, None, None], cache, 0).astype(F32)
+    held, own_rows = pack(ssm_pool, conv_pools, row_total, own_slots, False)
 
     kernel_len = conv_x_w.shape[0]
     skip = jnp.repeat(d_skip, head_width)
@@ -476,7 +523,7 @@
     )
     ints = jnp.concatenate([stretch_start[0], flags.reshape(-1)])
     if direct:
-        small = (held, w_step, const_x, const_bc, ints, cache)
+        small = (held, w_step, const_x, const_bc, ints)
         near_three = jnp.stack([block, along_z, along_x])
         both = partner_2(after(along_z, *small), "wide", 1)
         core_three = partner_2(near_three, "wide", 0)
@@ -517,8 +564,9 @@
         block = after(block, *parts)
     own = lax.optimization_barrier(project(block, F32))
 
-    bc_conv, cum, cum_t, step_t, coef, decay = prep(
-        ints, own["map"], came["map"], cache, const_bc, heads
+    row_arrays = [own_rows] + got_states
+    bc_conv, small, decay = prep(
+        ints, own["map"], came["map"], row_arrays, row_total, const_bc, heads, per_place, lags
     )
     wide_index = lax.axis_index("wide")
     group_span = lax.axis_size("wide") // GROUPS
@@ -533,8 +581,8 @@
     state_width = joined.shape[1] // 2
     came_xr = [after(got, own["xr"], bc_conv) for got in came["xr"]]
     result, final_state = mixer(
-        ints, own["xr"], came_xr, cache, const_x, joined[:, :state_width],
-        joined[:, state_width:], cum, cum_t, step_t, coef, decay, held, got_states
+        ints, own["xr"], came_xr, row_arrays, row_total, const_x, joined[:, :state_width],
+        joined[:, state_width:], small, decay, held, got_states, per_place, lags
     )
     gate = own["z"].astype(F32)
     for got in came["z"]:

time: 105 us -> 96.9 us (0.923)
  starting transfers between devices: 29.1 us -> 24.2 us
  waiting for transfers between devices: 15.5 us -> 13.3 us
  Pallas kernels: 16.8 us -> 15.5 us
  other arithmetic: 6.92 us -> 5.72 us
    ppermute x5 -> x4, waiting for transfers between devices: 7.82 us -> 0.01 us  [shift_req(): lax.ppermute(block, 'req', [(i, (i + step) % count) for i in range(count)])]
    ppermute x10, waiting for transfers between devices: 7.69 us -> 13.2 us  [partner_2(): return lax.ppermute(block, axis, route)]
    ppermute x5 -> x4, starting transfers between devices: 13.6 us -> 10.7 us  [shift_req(): lax.ppermute(block, 'req', [(i, (i + step) % count) for i in range(count)])]
    ppermute x10, starting transfers between devices: 10.8 us -> 8.11 us  [partner_2(): return lax.ppermute(block, axis, route)]
    pallas_call x4, Pallas kernels: 14.6 us -> 13.4 us  [the longest x1 7.68 us: mixer(): pl.pallas_call(functools.partial(mixer_kernel, count_req, len(got), per_p...]
    unnamed x51 -> x45, local copies, waits for them, and re-layouts: 5.11 us -> 5.15 us
  transfers between devices with their start and end apart: 17 -> 16, of which waited for: 4 -> 5; matrix products, arithmetic and copies ran while one was open for 33% -> 36% of each run, Pallas kernels for 16% -> 16%
where the time goes in v14:
time: 96.9 us; the launch traced here: 95.7 us
  matrix products  26 us (27%)
  starting transfers between devices  24.2 us (25%)
  Pallas kernels  15.5 us (16%)
  waiting for transfers between devices  13.3 us (14%)
  local copies, waits for them, and re-layouts  9.93 us (10%)
  other arithmetic  5.72 us (6%)
  between operations  0.98 us (1%)
    dot_general x2, matrix products, project(): high = jnp.einsum('td,dkc->ktc', block, w_xz, preferred_element_type=F32)  23.5 us
    ppermute x10, waiting for transfers between devices, partner_2(): return lax.ppermute(block, axis, route)  13.2 us
    ppermute x4, starting transfers between devices, shift_req(): lax.ppermute(block, 'req', [(i, (i + step) % count) for i in range(count)])  10.7 us
    ppermute x10, starting transfers between devices, partner_2(): return lax.ppermute(block, axis, route)  8.11 us
    pallas_call x1, Pallas kernels, mixer(): pl.pallas_call(functools.partial(mixer_kernel, count_req, len(got), per_p...  7.68 us
    unnamed x45, local copies, waits for them, and re-layouts  5.15 us
    ppermute x1, starting transfers between devices, near_blocks(): first = lax.ppermute(x_in, axes, first)  4.09 us
    pallas_call x2, Pallas kernels, pack(): pl.pallas_call(functools.partial(pack_kernel, row_total), out_shape=[jax....  4.02 us
  transfers between devices with their start and end apart: 16, of which 5 were waited for; matrix products, arithmetic and copies ran while one was open for 36% of the time, Pallas kernels for 16%

profile of v14, /device:TPU:0, one launch (start us, length us, event | category | flops | bytes accessed | tf_op | source)
XLA Modules:
  0.0 95.7 jit_solution(6965797781017021392)
XLA Ops:
  0.6 4.1 %collective-permute-start = (bf16[256,512]{1,0:T(8,128)(2,1)}, bf16[256,512]{1,0:T(8,128)(2,1)S(1)}, u32[]{:S(2)}, u32[]{:S(2)}) collective-permute-start(bf16[256,512]{1,0:T(8,128)(2,1)} %param.20), channel_id=1, source_target_pairs={{0,16},{1,0},{2,18},{3,2},{4,20},{5,4},{6,22},{7,6},{8,24},{9,8},{... | collective-permute-start | bytes 786440 | tf_op jit(solution)/shard_map/ppermute | solution.py:90
  4.7 1.3 %collective-permute-start.1 = (bf16[256,512]{1,0:T(8,128)(2,1)}, bf16[256,512]{1,0:T(8,128)(2,1)}, u32[]{:S(2)}, u32[]{:S(2)}) collective-permute-start(bf16[256,512]{1,0:T(8,128)(2,1)} %param.20), channel_id=1, source_target_pairs={{1,16},{3,18},{5,20},{7,22},{9,24},{11,26},{13,28},{15,30},{16,1},... | collective-permute-start | bytes 786440 | tf_op jit(solution)/shard_map/ppermute | solution.py:91
  8.3 2.0 %shard_map.203 = bf16[2,1040,256]{2,1,0:T(8,128)(2,1)S(1)} custom-call(s32[2]{0:T(128)S(1)} %subtract_clamp_fusion.1.slots_ref, f32[8,16,64,256]{3,2,1,0:T(8,128)} %pool_ref.3, bf16[3,8,1024]{2,1,0:T(8,128)(2,1)S(1)} %bitcast.42, bf16[3,8,256]{2,1,0:T(8,128)(2,1)S(1)} %bitcast.44), custom_call_target="tpu_custom_call" | custom-call | bytes 3145728 | tf_op jit(solution)/shard_map/pallas_call | solution.py:282
  10.3 3.8 %collective-permute-start.9 = (bf16[2,1040,256]{2,1,0:T(8,128)(2,1)S(1)}, bf16[2,1040,256]{2,1,0:T(8,128)(2,1)S(1)}, u32[]{:S(2)}, u32[]{:S(2)}) collective-permute-start(bf16[2,1040,256]{2,1,0:T(8,128)(2,1)S(1)} %shard_map.203), channel_id=1, source_target_pairs={{0,1},{1,0},{2,3},{3,2},{4,5},{5,4},{6,7},{7,6},{8,9},{9,8},{10,11... | collective-permute-start | bytes 3194888 | tf_op jit(solution)/shard_map/ppermute | solution.py:40
  14.2 1.6 %collective-permute-start.6 = (bf16[256,512]{1,0:T(8,128)(2,1)S(1)}, bf16[256,512]{1,0:T(8,128)(2,1)}, u32[]{:S(2)}, u32[]{:S(2)}) collective-permute-start(bf16[256,512]{1,0:T(8,128)(2,1)S(1)} %get-tuple-element.39), channel_id=1, source_target_pairs={{0,4},{4,0},{2,6},{6,2},{8,12},{12,8},{10,14},{14,10},{16,20},{20,... | collective-permute-start | bytes 786440 | tf_op jit(solution)/shard_map/ppermute | solution.py:35
  15.8 3.5 %collective-permute-start.3 = (bf16[256,512]{1,0:T(8,128)(2,1)S(1)}, bf16[256,512]{1,0:T(8,128)(2,1)}, u32[]{:S(2)}, u32[]{:S(2)}) collective-permute-start(bf16[256,512]{1,0:T(8,128)(2,1)S(1)} %get-tuple-element.39), channel_id=1, source_target_pairs={{0,8},{8,0},{2,10},{10,2},{4,12},{12,4},{6,14},{14,6},{16,24},{24,... | collective-permute-start | bytes 786440 | tf_op jit(solution)/shard_map/ppermute | solution.py:35
  19.6 2.0 %shard_map.204 = (f32[2,16,64,256]{3,2,1,0:T(8,128)S(1)}, f32[2,16,256]{2,1,0:T(8,128)S(1)}) custom-call(s32[2]{0:T(128)S(1)} %get-tuple-element.86.slots_ref, f32[8,16,64,256]{3,2,1,0:T(8,128)} %pool_ref.3, bf16[3,8,1024]{2,1,0:T(8,128)(2,1)S(1)} %bitcast.43, bf16[3,8,256]{2,1,0:T(8,128)(2,1)S(1)} %bitcast.45), custom_call_target="tpu_custom_call" | custom-call | bytes 3145728 | tf_op jit(solution)/shard_map/pallas_call | solution.py:282
  21.6 1.3 %copy-done = f32[2,16,64,256]{3,2,1,0:T(8,128)} copy-done((f32[2,16,64,256]{3,2,1,0:T(8,128)}, f32[2,16,64,256]{3,2,1,0:T(8,128)S(1)}, u32[]{:S(2)}) %copy-start) | copy-done | bytes 2097176
  23.1 3.1 %collective-permute-done.3 = bf16[256,512]{1,0:T(8,128)(2,1)} collective-permute-done((bf16[256,512]{1,0:T(8,128)(2,1)S(1)}, bf16[256,512]{1,0:T(8,128)(2,1)}, u32[]{:S(2)}, u32[]{:S(2)}) %collective-permute-start.3) | collective-permute-done | bytes 262176 | tf_op jit(solution)/shard_map/ppermute | solution.py:35
  27.7 2.2 %copy.22 = bf16[4096,16]{1,0:T(8,128)(2,1)} copy(bf16[4096,16]{0,1:T(8,128)(2,1)} %param.22) | data formatting | bytes 262144 | tf_op jit(solution)/shard_map/optimization_barrier | solution.py:496
  30.0 1.2 %collective-permute-start.4 = (bf16[256,512]{1,0:T(8,128)(2,1)}, bf16[256,512]{1,0:T(8,128)(2,1)S(1)}, u32[]{:S(2)}, u32[]{:S(2)}) collective-permute-start(bf16[256,512]{1,0:T(8,128)(2,1)} %collective-permute-done.3), channel_id=1, source_target_pairs={{0,4},{4,0},{2,6},{6,2},{8,12},{12,8},{10,14},{14,10},{16,20},{20,... | collective-permute-start | bytes 786440 | tf_op jit(solution)/shard_map/ppermute | solution.py:35
  31.4 7.6 %collective-permute-done.4 = bf16[256,512]{1,0:T(8,128)(2,1)S(1)} collective-permute-done((bf16[256,512]{1,0:T(8,128)(2,1)}, bf16[256,512]{1,0:T(8,128)(2,1)S(1)}, u32[]{:S(2)}, u32[]{:S(2)}) %collective-permute-start.4) | collective-permute-done | bytes 262176 | tf_op jit(solution)/shard_map/ppermute | solution.py:35
  41.3 1.5 %shard_map.205 = bf16[256,4096]{1,0:T(8,128)(2,1)S(1)} custom-call(s32[8]{0:T(128)S(1)} %broadcast_xor_fusion.places_ref, bf16[3,256,512]{2,1,0:T(8,128)(2,1)S(1)} %pad_maximum_fusion.7.refs_0_, bf16[1,256,512]{2,1,0:T(8,128)(2,1)S(1)} %bitcast.41, bf16[3,256,512]{2,1,0:T(8,128)(2,1)} %collective-permute-done.7.refs_2_, ...), custom_call_target="tpu_custom_call" | custom-call | flops 1000000 | bytes 10000 | tf_op jit(solution)/shard_map/pallas_call | solution.py:72
  43.4 1.3 %fusion.23 = bf16[256,272]{1,0:T(8,128)(2,1)S(1)} fusion(bf16[256,4096]{1,0:T(8,128)(2,1)S(1)} %shard_map.205, bf16[4096,16]{1,0:T(8,128)(2,1)S(1)} %copy-done.7, bf16[4096,256]{1,0:T(8,128)(2,1)S(1)} %copy-done.18), kind=kOutput, calls=%fused_computation.14 | convolution fusion | flops 574951424 | bytes 4464640 | tf_op jit(solution)/shard_map/dot_general | solution.py:546
  44.7 11.3 %fusion.18 = bf16[2,256,1024]{2,1,0:T(8,128)(2,1)S(1)} fusion(bf16[4096,2,1024]{2,1,0:T(2,128)(2,1)} %param.21, bf16[256,4096]{1,0:T(8,128)(2,1)S(1)} %shard_map.205), kind=kOutput, calls=%fused_computation.11 | convolution fusion | flops 4295491584 | bytes 19922944 | tf_op jit(solution)/shard_map/td,dkc->ktc/dot_general | solution.py:548
  57.3 4.8 %collective-permute-start.12 = (bf16[256,272]{1,0:T(8,128)(2,1)S(1)}, bf16[256,272]{1,0:T(8,128)(2,1)S(1)}, u32[]{:S(2)}, u32[]{:S(2)}) collective-permute-start(bf16[256,272]{1,0:T(8,128)(2,1)S(1)} %fusion.23), channel_id=1, source_target_pairs={{0,1},{1,0},{2,3},{3,2},{4,5},{5,4},{6,7},{7,6},{8,9},{9,8},{10,11... | collective-permute-start | bytes 417800 | tf_op jit(solution)/shard_map/ppermute | solution.py:40
  62.2 2.0 %collective-permute-start.14 = (bf16[256,1024]{1,0:T(8,128)(2,1)}, bf16[256,1024]{1,0:T(8,128)(2,1)}, u32[]{:S(2)}, u32[]{:S(2)}) collective-permute-start(bf16[256,1024]{1,0:T(8,128)(2,1)} %get-tuple-element.62), channel_id=1, source_target_pairs={{0,1},{1,0},{2,3},{3,2},{4,5},{5,4},{6,7},{7,6},{8,9},{9,8},{10,11... | collective-permute-start | bytes 1572872 | tf_op jit(solution)/shard_map/ppermute | solution.py:40
  64.9 1.3 %fusion.24.own_ref = bf16[256,272]{1,0:T(8,128)(2,1)S(1)} fusion(bf16[256,4096]{1,0:T(8,128)(2,1)S(1)} %shard_map.206, bf16[4096,16]{1,0:T(8,128)(2,1)S(1)} %copy-done.7, bf16[4096,256]{1,0:T(8,128)(2,1)S(1)} %copy-done.18), kind=kOutput, calls=%fused_computation.15 | convolution fusion | flops 574951424 | bytes 4464640 | tf_op jit(solution)/shard_map/dot_general | solution.py:546
  66.2 12.2 %fusion.8 = f32[2,256,1024]{2,1,0:T(8,128)S(1)} fusion(bf16[4096,2,1024]{2,1,0:T(2,128)(2,1)} %param.21, bf16[256,4096]{1,0:T(8,128)(2,1)S(1)} %shard_map.206), kind=kOutput, calls=%fused_computation.9 | convolution fusion | flops 4294967296 | bytes 20971520 | tf_op jit(solution)/shard_map/td,dkc->ktc/dot_general | solution.py:548
  79.5 1.7 %shard_map.207 = (bf16[256,256]{1,0:T(8,128)(2,1)S(1)}, f32[4,12,256]{2,1,0:T(8,128)S(1)}, f32[8,16]{1,0:T(8,128)S(1)}) custom-call(s32[6]{0:T(128)S(1)} %pad_add_fusion.ints_ref, bf16[256,272]{1,0:T(8,128)(2,1)S(1)} %fusion.24.own_ref, bf16[256,272]{1,0:T(8,128)(2,1)S(1)} %collective-permute-done.12.refs_0_, ...), custom_call_target="tpu_custom_call" | custom-call | flops 1000000 | bytes 10000 | tf_op jit(solution)/shard_map/pallas_call | solution.py:221
  81.3 1.3 %collective-permute-done.13 = bf16[256,256]{1,0:T(8,128)(2,1)S(1)} collective-permute-done((bf16[256,256]{1,0:T(8,128)(2,1)S(1)}, bf16[256,256]{1,0:T(8,128)(2,1)S(1)}, u32[]{:S(2)}, u32[]{:S(2)}) %collective-permute-start.13) | collective-permute-done | bytes 131104 | tf_op jit(solution)/shard_map/ppermute | solution.py:35
  82.7 1.6 %copy-done.1 = f32[2,16,64,256]{3,2,1,0:T(8,128)S(1)} copy-done((f32[2,16,64,256]{3,2,1,0:T(8,128)S(1)}, f32[2,16,64,256]{3,2,1,0:T(8,128)}, u32[]{:S(2)}) %copy-start.1) | copy-done | bytes 2097176
  84.3 7.7 %shard_map.208 = (f32[256,1024]{1,0:T(8,128)S(1)}, f32[2,16,64,256]{3,2,1,0:T(8,128)}) custom-call(s32[6]{0:T(128)S(1)} %pad_add_fusion.ints_ref, f32[256,1024]{1,0:T(8,128)S(1)} %get-tuple-element.66.refs_0_, bf16[256,1024]{1,0:T(8,128)(2,1)S(1)} %collective-permute-done.11.refs_1_, f32[2,16,256]{2,1,0:T(8,128)S(1)} %get-tuple-element.68.refs_1_.refs_2_, ...), custom_call_target="tpu_custom_call" | custom-call | flops 1000000 | bytes 10000 | tf_op jit(solution)/shard_map/pallas_call | solution.py:416
  92.0 1.5 %multiply_reduce_fusion = (f32[256]{0:T(256)S(1)}, f32[256,1024]{1,0:T(8,128)S(1)}) fusion(f32[256,1024]{1,0:T(8,128)S(1)} %get-tuple-element.73, f32[256,1024]{1,0:T(8,128)S(1)} %copy-done.6, bf16[256,1024]{1,0:T(8,128)(2,1)} %collective-permute-done.14), kind=kLoop, calls=%fused_computation.23 | loop fusion | flops 2883328 | bytes 3671040 | tf_op jit(solution)/shard_map/reduce_sum | solution.py:591
  (90 shorter events, 12.8 us)
Async XLA Ops:
  0.6 13.5 %collective-permute-start = (bf16[256,512]{1,0:T(8,128)(2,1)}, bf16[256,512]{1,0:T(8,128)(2,1)S(1)}, u32[]{:S(2)}, u32[]{:S(2)}) collective-permute-start(bf16[256,512]{1,0:T(8,128)(2,1)} %param.20), channel_id=1, source_target_pairs={{0,16},{1,0},{2,18},{3,2},{4,20},{5,4},{6,22},{7,6},{8,24},{9,8},{... | collective-permute-start | bytes 786440 | tf_op jit(solution)/shard_map/ppermute | solution.py:90
  4.7 9.5 %collective-permute-start.1 = (bf16[256,512]{1,0:T(8,128)(2,1)}, bf16[256,512]{1,0:T(8,128)(2,1)}, u32[]{:S(2)}, u32[]{:S(2)}) collective-permute-start(bf16[256,512]{1,0:T(8,128)(2,1)} %param.20), channel_id=1, source_target_pairs={{1,16},{3,18},{5,20},{7,22},{9,24},{11,26},{13,28},{15,30},{16,1},... | collective-permute-start | bytes 786440 | tf_op jit(solution)/shard_map/ppermute | solution.py:91
  8.3 11.0 %copy-start.19 = (s32[2]{0:T(128)S(1)}, s32[2]{0:T(128)}, u32[]{:S(2)}) copy-start(s32[2]{0:T(128)} %param.33) | copy-start | bytes 28
  8.3 11.0 %copy-start.13 = (s32[4]{0:T(128)S(1)}, s32[4]{0:T(128)}, u32[]{:S(2)}) copy-start(s32[4]{0:T(128)} %param.34) | copy-start | bytes 52
  8.3 11.3 %copy-start.3 = (bf16[8,3,1024]{2,0,1:T(8,128)(2,1)S(1)}, bf16[8,3,1024]{2,0,1:T(8,128)(2,1)}, u32[]{:S(2)}) copy-start(bf16[8,3,1024]{2,0,1:T(8,128)(2,1)} %param.36) | copy-start | bytes 147460
  8.3 11.3 %copy-start.5 = (bf16[8,3,256]{2,0,1:T(8,128)(2,1)S(1)}, bf16[8,3,256]{2,0,1:T(8,128)(2,1)}, u32[]{:S(2)}) copy-start(bf16[8,3,256]{2,0,1:T(8,128)(2,1)} %param.37) | copy-start | bytes 36868
  10.3 31.0 %collective-permute-start.9 = (bf16[2,1040,256]{2,1,0:T(8,128)(2,1)S(1)}, bf16[2,1040,256]{2,1,0:T(8,128)(2,1)S(1)}, u32[]{:S(2)}, u32[]{:S(2)}) collective-permute-start(bf16[2,1040,256]{2,1,0:T(8,128)(2,1)S(1)} %shard_map.203), channel_id=1, source_target_pairs={{0,1},{1,0},{2,3},{3,2},{4,5},{5,4},{6,7},{7,6},{8,9},{9,8},{10,11... | collective-permute-start | bytes 3194888 | tf_op jit(solution)/shard_map/ppermute | solution.py:40
  14.2 8.8 %collective-permute-start.6 = (bf16[256,512]{1,0:T(8,128)(2,1)S(1)}, bf16[256,512]{1,0:T(8,128)(2,1)}, u32[]{:S(2)}, u32[]{:S(2)}) collective-permute-start(bf16[256,512]{1,0:T(8,128)(2,1)S(1)} %get-tuple-element.39), channel_id=1, source_target_pairs={{0,4},{4,0},{2,6},{6,2},{8,12},{12,8},{10,14},{14,10},{16,20},{20,... | collective-permute-start | bytes 786440 | tf_op jit(solution)/shard_map/ppermute | solution.py:35
  15.8 10.4 %collective-permute-start.3 = (bf16[256,512]{1,0:T(8,128)(2,1)S(1)}, bf16[256,512]{1,0:T(8,128)(2,1)}, u32[]{:S(2)}, u32[]{:S(2)}) collective-permute-start(bf16[256,512]{1,0:T(8,128)(2,1)S(1)} %get-tuple-element.39), channel_id=1, source_target_pairs={{0,8},{8,0},{2,10},{10,2},{4,12},{12,4},{6,14},{14,6},{16,24},{24,... | collective-permute-start | bytes 786440 | tf_op jit(solution)/shard_map/ppermute | solution.py:35
  19.6 7.9 %copy-start.16 = (f32[16]{0:T(128)S(1)}, f32[16]{0:T(128)}, u32[]{:S(2)}) copy-start(f32[16]{0:T(128)} %param.24) | copy-start | bytes 196
  19.6 7.9 %copy-start.17 = (f32[16]{0:T(128)S(1)}, f32[16]{0:T(128)}, u32[]{:S(2)}) copy-start(f32[16]{0:T(128)} %param.25) | copy-start | bytes 196
  19.6 7.9 %copy-start.15 = (f32[16]{0:T(128)S(1)}, f32[16]{0:T(128)}, u32[]{:S(2)}) copy-start(f32[16]{0:T(128)} %param.26) | copy-start | bytes 196
  23.0 16.0 %copy-start.21 = (s32[8]{0:T(128)S(1)}, s32[8]{0:T(128)}, u32[]{:S(2)}) copy-start(s32[8]{0:T(128)} %constant.95.clone) | copy-start | bytes 100
  23.0 8.4 %collective-permute-start.2 = (bf16[256,512]{1,0:T(8,128)(2,1)S(1)}, bf16[256,512]{1,0:T(8,128)(2,1)}, u32[]{:S(2)}, u32[]{:S(2)}) collective-permute-start(bf16[256,512]{1,0:T(8,128)(2,1)S(1)} %get-tuple-element.44), channel_id=1, source_target_pairs={{0,8},{8,0},{2,10},{10,2},{4,12},{12,4},{6,14},{14,6},{16,24},{24,... | collective-permute-start | bytes 786440 | tf_op jit(solution)/shard_map/ppermute | solution.py:35
  27.3 14.0 %collective-permute-start.7 = (bf16[3,256,512]{2,1,0:T(8,128)(2,1)S(1)}, bf16[3,256,512]{2,1,0:T(8,128)(2,1)}, u32[]{:S(2)}, u32[]{:S(2)}) collective-permute-start(bf16[3,256,512]{2,1,0:T(8,128)(2,1)S(1)} %pad_maximum_fusion.7.refs_0_), channel_id=1, source_target_pairs={{0,2},{2,0},{4,6},{6,4},{8,10},{10,8},{12,14},{14,12},{16,18},{18,... | collective-permute-start | bytes 2359304 | tf_op jit(solution)/shard_map/ppermute | solution.py:35
  30.0 9.0 %collective-permute-start.4 = (bf16[256,512]{1,0:T(8,128)(2,1)}, bf16[256,512]{1,0:T(8,128)(2,1)S(1)}, u32[]{:S(2)}, u32[]{:S(2)}) collective-permute-start(bf16[256,512]{1,0:T(8,128)(2,1)} %collective-permute-done.3), channel_id=1, source_target_pairs={{0,4},{4,0},{2,6},{6,2},{8,12},{12,8},{10,14},{14,10},{16,20},{20,... | collective-permute-start | bytes 786440 | tf_op jit(solution)/shard_map/ppermute | solution.py:35
  39.0 2.3 %collective-permute-start.8 = (bf16[1,256,512]{2,1,0:T(8,128)(2,1)S(1)}, bf16[1,256,512]{2,1,0:T(8,128)(2,1)S(1)}, u32[]{:S(2)}, u32[]{:S(2)}) collective-permute-start(bf16[1,256,512]{2,1,0:T(8,128)(2,1)S(1)} %bitcast.40), channel_id=1, source_target_pairs={{0,2},{2,0},{4,6},{6,4},{8,10},{10,8},{12,14},{14,12},{16,18},{18,... | collective-permute-start | bytes 786440 | tf_op jit(solution)/shard_map/ppermute | solution.py:35
  40.0 17.0 %collective-permute-start.5 = (bf16[2,256,512]{2,1,0:T(8,128)(2,1)S(1)}, bf16[2,256,512]{2,1,0:T(8,128)(2,1)S(1)}, u32[]{:S(2)}, u32[]{:S(2)}) collective-permute-start(bf16[2,256,512]{2,1,0:T(8,128)(2,1)S(1)} %pad_maximum_fusion.8), channel_id=1, source_target_pairs={{0,4},{4,0},{2,6},{6,2},{8,12},{12,8},{10,14},{14,10},{16,20},{20,... | collective-permute-start | bytes 1572872 | tf_op jit(solution)/shard_map/ppermute | solution.py:35
  57.0 7.1 %collective-permute-start.10 = (bf16[4,256,512]{2,1,0:T(8,128)(2,1)S(1)}, bf16[4,256,512]{2,1,0:T(8,128)(2,1)S(1)}, u32[]{:S(2)}, u32[]{:S(2)}) collective-permute-start(bf16[4,256,512]{2,1,0:T(8,128)(2,1)S(1)} %constant_dynamic-update-slice_fusion.refs_0_), channel_id=1, source_target_pairs={{0,2},{2,0},{4,6},{6,4},{8,10},{10,8},{12,14},{14,12},{16,18},{18,... | collective-permute-start | bytes 3145736 | tf_op jit(solution)/shard_map/ppermute | solution.py:35
  57.3 22.2 %collective-permute-start.12 = (bf16[256,272]{1,0:T(8,128)(2,1)S(1)}, bf16[256,272]{1,0:T(8,128)(2,1)S(1)}, u32[]{:S(2)}, u32[]{:S(2)}) collective-permute-start(bf16[256,272]{1,0:T(8,128)(2,1)S(1)} %fusion.23), channel_id=1, source_target_pairs={{0,1},{1,0},{2,3},{3,2},{4,5},{5,4},{6,7},{7,6},{8,9},{9,8},{10,11... | collective-permute-start | bytes 417800 | tf_op jit(solution)/shard_map/ppermute | solution.py:40
  62.2 19.1 %collective-permute-start.11 = (bf16[256,1024]{1,0:T(8,128)(2,1)}, bf16[256,1024]{1,0:T(8,128)(2,1)S(1)}, u32[]{:S(2)}, u32[]{:S(2)}) collective-permute-start(bf16[256,1024]{1,0:T(8,128)(2,1)} %get-tuple-element.61), channel_id=1, source_target_pairs={{0,1},{1,0},{2,3},{3,2},{4,5},{5,4},{6,7},{7,6},{8,9},{9,8},{10,11... | collective-permute-start | bytes 1572872 | tf_op jit(solution)/shard_map/ppermute | solution.py:40
  62.2 29.8 %collective-permute-start.14 = (bf16[256,1024]{1,0:T(8,128)(2,1)}, bf16[256,1024]{1,0:T(8,128)(2,1)}, u32[]{:S(2)}, u32[]{:S(2)}) collective-permute-start(bf16[256,1024]{1,0:T(8,128)(2,1)} %get-tuple-element.62), channel_id=1, source_target_pairs={{0,1},{1,0},{2,3},{3,2},{4,5},{5,4},{6,7},{7,6},{8,9},{9,8},{10,11... | collective-permute-start | bytes 1572872 | tf_op jit(solution)/shard_map/ppermute | solution.py:40
  81.2 1.4 %collective-permute-start.13 = (bf16[256,256]{1,0:T(8,128)(2,1)S(1)}, bf16[256,256]{1,0:T(8,128)(2,1)S(1)}, u32[]{:S(2)}, u32[]{:S(2)}) collective-permute-start(bf16[256,256]{1,0:T(8,128)(2,1)S(1)} %get-tuple-element.69), channel_id=1, source_target_pairs={{0,2},{2,0},{4,6},{6,4},{8,10},{10,8},{12,14},{14,12},{16,18},{18,... | collective-permute-start | bytes 393224 | tf_op jit(solution)/shard_map/ppermute | solution.py:35
  93.5 1.2 %collective-permute-start.15 = (f32[256]{0:T(256)S(1)}, f32[256]{0:T(256)S(1)}, u32[]{:S(2)}, u32[]{:S(2)}) collective-permute-start(f32[256]{0:T(256)S(1)} %get-tuple-element.76), channel_id=1, source_target_pairs={{0,2},{2,0},{4,6},{6,4},{8,10},{10,8},{12,14},{14,12},{16,18},{18,... | collective-permute-start | bytes 3080 | tf_op jit(solution)/shard_map/ppermute | solution.py:35
  (14 other events, 64.5 us)

commit v15 on v14

--- a/solution.py
+++ b/solution.py
@@ -258,45 +258,53 @@
     return jnp.concatenate(rows, 0)
 
 
-def pack_kernel(row_total, slots_ref, pool_ref, x_ref, bc_ref, *out_refs):
+def pack_kernel(row_total, slots_ref, pool_ref, x_ref, bc_ref, out_ref):
     rows, lanes = pool_ref.shape[1] * pool_ref.shape[2], pool_ref.shape[3]
     slot = slots_ref[pl.program_id(0)]
     conv = conv_rows(slot, (x_ref, bc_ref), row_total, lanes)
-    if len(out_refs) == 1:
-        out_ref = out_refs[0]
-        out_ref[0, :rows, :] = pool_ref[0].reshape(rows, lanes).astype(out_ref.dtype)
-        out_ref[0, rows:, :] = conv.astype(out_ref.dtype)
-    else:
-        out_refs[0][...] = pool_ref[...]
-        out_refs[1][0] = conv
-
-
-def pack(pool, conv_pools, row_total, slots, to_send):
+    out_ref[0, :rows, :] = pool_ref[0].reshape(rows, lanes).astype(out_ref.dtype)
+    out_ref[0, rows:, :] = conv.astype(out_ref.dtype)
+
+
+def pack(pool, conv_pools, row_total, slots):
     count_req = slots.shape[0]
     _, heads, width, state = pool.shape
-    block = (1, heads, width, state)
     conv_pools = [jnp.transpose(array, (1, 0, 2)) for array in conv_pools]
-    shapes = [((1, heads * width + row_total, state), BF16)]
-    if not to_send:
-        shapes = [(block, F32), ((1, row_total, state), F32)]
+    out_block = (1, heads * width + row_total, state)
     return pl.pallas_call(
         functools.partial(pack_kernel, row_total),
-        out_shape=[
-            jax.ShapeDtypeStruct((count_req,) + shape[1:], kind) for shape, kind in shapes
-        ],
+        out_shape=jax.ShapeDtypeStruct((count_req,) + out_block[1:], BF16),
         grid_spec=pltpu.PrefetchScalarGridSpec(
             num_scalar_prefetch=1,
             grid=(count_req,),
-            in_specs=[pl.BlockSpec(block, lambda j, slots: (slots[j], 0, 0, 0))]
+            in_specs=[
+                pl.BlockSpec((1, heads, width, state), lambda j, slots: (slots[j], 0, 0, 0))
+            ]
             + [pl.BlockSpec(array.shape, lambda j, slots: (0, 0, 0)) for array in conv_pools],
-            out_specs=[
-                pl.BlockSpec(shape, functools.partial(lambda n, j, _: (j,) + (0,) * n, len(shape) - 1))
-                for shape, _ in shapes
-            ],
+            out_specs=pl.BlockSpec(out_block, lambda j, slots: (j, 0, 0)),
         ),
         compiler_params=params(3 * VMEM_BYTES),
         cost_estimate=cost(0, 6 * pool[0].size * count_req),
     )(slots, pool, *conv_pools)
+
+
+def own_rows_kernel(row_total, first_slot, ints_ref, x_ref, bc_ref, out_ref):
+    for request in range(out_ref.shape[0]):
+        slot = ints_ref[first_slot + request]
+        out_ref[request] = conv_rows(slot, (x_ref, bc_ref), row_total, out_ref.shape[2])
+
+
+def own_rows_of(conv_pools, row_total, ints, count_req, lanes):
+    vmem = pl.BlockSpec(memory_space=pltpu.VMEM)
+    first_slot = ints.shape[0] - count_req
+    return pl.pallas_call(
+        functools.partial(own_rows_kernel, row_total, first_slot),
+        out_shape=jax.ShapeDtypeStruct((count_req, row_total, lanes), F32),
+        in_specs=[pl.BlockSpec(memory_space=pltpu.SMEM), vmem, vmem],
+        out_specs=vmem,
+        compiler_params=params(),
+        cost_estimate=cost(1e6, 1e4),
+    )(ints, *[jnp.transpose(array, (1, 0, 2)) for array in conv_pools])
 
 
 def mixer_kernel(count_req, got_total, per_place, places, ints_ref, *refs):
@@ -304,9 +312,10 @@
     got = refs[1 : 1 + got_total]
     rest = refs[1 + got_total :]
     row_refs = rest[: got_total + 1]
-    const_ref, b_ref, c_ref, small_ref, decay_ref, held_ref = rest[got_total + 1 : got_total + 7]
-    states = rest[got_total + 7 : 2 * got_total + 7]
-    out_ref, state_ref, scores_ref, c_part_ref, b_part_ref = rest[2 * got_total + 7 :]
+    const_ref, b_ref, c_ref, small_ref, decay_ref = rest[got_total + 1 : got_total + 6]
+    rest = rest[got_total + 6 :]
+    pools, states = rest[:count_req], rest[count_req : count_req + got_total]
+    out_ref, state_ref, scores_ref, c_part_ref, b_part_ref = rest[count_req + got_total :]
     skip = const_ref[places + 2 : places + 3, :]
 
     def flag(request, step):
@@ -314,7 +323,7 @@
         return ints_ref[place].astype(F32)
 
     tokens, channels = own_ref.shape
-    heads, width, state = held_ref.shape[1:]
+    heads, width, state = pools[0].shape[1:]
     starts = [ints_ref[j] for j in range(count_req)]
 
     @pl.when(pl.program_id(0) == 0)
@@ -372,7 +381,7 @@
     )
     for j in range(count_req):
         place = slice(j * state, (j + 1) * state)
-        start = held_ref[j].reshape(channels, state) * flag(j, 0)
+        start = pools[j][0].reshape(channels, state) * flag(j, 0)
         for step in range(got_total):
             start = start + states[step][j].astype(F32) * flag(j, step + 1)
         from_state = from_state + lax.dot_general(
@@ -389,11 +398,13 @@
 
 
 def mixer(
-    ints, own, got, row_arrays, row_total, const, b_maps, c_maps, small, decay, held, states,
+    ints, own, got, row_arrays, row_total, const, b_maps, c_maps, small, decay, pool, states,
     per_place, places
 ):
     tokens, channels = own.shape
-    count_req, heads, width, state = held.shape
+    _, heads, width, state = pool.shape
+    count_req = row_arrays[0].shape[0]
+    first_slot = ints.shape[0] - count_req
     part = min(HEADS_STEP, heads)
     steps = heads // part
     wide = part * width
@@ -410,7 +421,13 @@
             pl.BlockSpec((1,) + small.shape[1:], lambda i, *_: (i, 0, 0)),
             pl.BlockSpec(memory_space=pltpu.SMEM),
         ]
-        + [pl.BlockSpec((count_req, part, width, state), lambda i, *_: (0, i, 0, 0))]
+        + [
+            pl.BlockSpec(
+                (1, part, width, state),
+                functools.partial(lambda at, i, ints: (ints[at], i, 0, 0), first_slot + j),
+            )
+            for j in range(count_req)
+        ]
         + [pl.BlockSpec((count_req, wide, state), lambda i, *_: (0, i, 0))] * len(states)
     )
     return pl.pallas_call(
@@ -433,10 +450,11 @@
                 pltpu.VMEM((tokens, count_req * state), BF16),
             ],
         ),
-        compiler_params=params(),
+        compiler_params=params(3 * VMEM_BYTES),
         cost_estimate=cost(1e6, 1e4),
     )(
-        ints, own, *got, *row_arrays, const, b_maps, c_maps, small, decay, held, *states
+        ints, own, *got, *row_arrays, const, b_maps, c_maps, small, decay,
+        *([pool] * count_req), *states
     )
 
 
@@ -482,7 +500,7 @@
     got_states = []
     for step in range(1, req_count):
         slots = slots_of((me + step) % req_count)
-        packed = pack(ssm_pool, conv_pools, row_total, slots, True)[0]
+        packed = pack(ssm_pool, conv_pools, row_total, slots)
         got_states.append(shift_req(packed, step))
 
     w_step = w_dt
@@ -508,7 +526,6 @@
     flags = (live[:, None] & (came_from[:, None] == jnp.arange(req_count)[None, :])).astype(
         jnp.int32
     )
-    held, own_rows = pack(ssm_pool, conv_pools, row_total, own_slots, False)
 
     kernel_len = conv_x_w.shape[0]
     skip = jnp.repeat(d_skip, head_width)
@@ -521,15 +538,15 @@
         [conv_bc_w[k] for k in range(kernel_len)]
         + [conv_bc_b, wide_heads(dt_bias), wide_heads(a_log), jnp.zeros_like(conv_bc_b)]
     )
-    ints = jnp.concatenate([stretch_start[0], flags.reshape(-1)])
+    ints = jnp.concatenate([stretch_start[0], flags.reshape(-1), own_slots])
+    own_rows = own_rows_of(conv_pools, row_total, ints, group_reqs, state)
     if direct:
-        small = (held, w_step, const_x, const_bc, ints)
+        both = partner_2(along_z, "wide", 1)
+        own_block = after(own_block, along_z)
+        own_z = partner_2(own_block, "wide", 2)
         near_three = jnp.stack([block, along_z, along_x])
-        both = partner_2(after(along_z, *small), "wide", 1)
         core_three = partner_2(near_three, "wide", 0)
-        own_block = after(own_block, held)
-        own_z = partner_2(own_block, "wide", 2)
-        both = after(both[None], own_z)
+        both = after(both[None], own_z, w_step, const_x, const_bc, ints, own_rows)
         core_both = partner_2(both, "wide", 0)
         own_pair = after(jnp.stack([own_block, own_z]), both)
         own_got = partner_2(own_pair, "wide", 1)
@@ -582,7 +599,8 @@
     came_xr = [after(got, own["xr"], bc_conv) for got in came["xr"]]
     result, final_state = mixer(
         ints, own["xr"], came_xr, row_arrays, row_total, const_x, joined[:, :state_width],
-        joined[:, state_width:], small, decay, held, got_states, per_place, lags
+        joined[:, state_width:], small, decay, ssm_pool, got_states,
+        per_place, lags
     )
     gate = own["z"].astype(F32)
     for got in came["z"]:

time: 96.9 us -> 92.9 us (0.959)
  local copies, waits for them, and re-layouts: 9.93 us -> 5.49 us
  waiting for transfers between devices: 13.3 us -> 14.8 us
    unnamed x45 -> x43, local copies, waits for them, and re-layouts: 5.15 us -> 1.64 us
    ppermute x4, waiting for transfers between devices: 0.01 us -> 1.3 us  [shift_req(): lax.ppermute(block, 'req', [(i, (i + step) % count) for i in range(count)])]
    pallas_call x2, Pallas kernels: 4.02 us -> 2.82 us  [the longest x1 2.21 us: pack(): pl.pallas_call(functools.partial(pack_kernel, row_total), out_shape=jax.S...]
  transfers between devices with their start and end apart: 16 -> 16, of which waited for: 5 -> 6; matrix products, arithmetic and copies ran while one was open for 36% -> 37% of each run, Pallas kernels for 16% -> 16%
where the time goes in v15:
time: 92.9 us; the launch traced here: 92.4 us
  matrix products  26 us (28%)
  starting transfers between devices  24.1 us (26%)
  waiting for transfers between devices  14.8 us (16%)
  Pallas kernels  14.6 us (16%)
  other arithmetic  6.49 us (7%)
  local copies, waits for them, and re-layouts  5.49 us (6%)
  between operations  1.04 us (1%)
    dot_general x2, matrix products, project(): high = jnp.einsum('td,dkc->ktc', block, w_xz, preferred_element_type=F32)  23.5 us
    ppermute x10, waiting for transfers between devices, partner_2(): return lax.ppermute(block, axis, route)  13.5 us
    ppermute x4, starting transfers between devices, shift_req(): lax.ppermute(block, 'req', [(i, (i + step) % count) for i in range(count)])  10.4 us
    ppermute x10, starting transfers between devices, partner_2(): return lax.ppermute(block, axis, route)  8.9 us
    pallas_call x1, Pallas kernels, mixer(): pl.pallas_call(functools.partial(mixer_kernel, count_req, len(got), per_p...  8.04 us
    ppermute x1, starting transfers between devices, near_blocks(): first = lax.ppermute(x_in, axes, first)  4.09 us
    dot_general x2, matrix products, project(): low = jnp.dot(block, w_map, preferred_element_type=F32).astype(BF16)  2.51 us
    pallas_call x1, Pallas kernels, pack(): pl.pallas_call(functools.partial(pack_kernel, row_total), out_shape=jax.S...  2.21 us
  transfers between devices with their start and end apart: 16, of which 6 were waited for; matrix products, arithmetic and copies ran while one was open for 37% of the time, Pallas kernels for 16%

profile of v15, /device:TPU:0, one launch (start us, length us, event | category | flops | bytes accessed | tf_op | source)
XLA Modules:
  0.0 92.4 jit_solution(10801099350110763287)
XLA Ops:
  0.6 4.1 %collective-permute-start = (bf16[256,512]{1,0:T(8,128)(2,1)}, bf16[256,512]{1,0:T(8,128)(2,1)S(1)}, u32[]{:S(2)}, u32[]{:S(2)}) collective-permute-start(bf16[256,512]{1,0:T(8,128)(2,1)} %param.20), channel_id=1, source_target_pairs={{0,16},{1,0},{2,18},{3,2},{4,20},{5,4},{6,22},{7,6},{8,24},{9,8},{... | collective-permute-start | bytes 786440 | tf_op jit(solution)/shard_map/ppermute | solution.py:90
  7.7 2.2 %shard_map.203 = bf16[2,1040,256]{2,1,0:T(8,128)(2,1)S(1)} custom-call(s32[2]{0:T(128)S(1)} %subtract_clamp_fusion.1.slots_ref, f32[8,16,64,256]{3,2,1,0:T(8,128)} %refs_10_.1, bf16[3,8,1024]{2,1,0:T(8,128)(2,1)S(1)} %bitcast.42, bf16[3,8,256]{2,1,0:T(8,128)(2,1)S(1)} %bitcast.44), custom_call_target="tpu_custom_call" | custom-call | bytes 3145728 | tf_op jit(solution)/shard_map/pallas_call | solution.py:274
  10.0 4.1 %collective-permute-start.9 = (bf16[2,1040,256]{2,1,0:T(8,128)(2,1)S(1)}, bf16[2,1040,256]{2,1,0:T(8,128)(2,1)S(1)}, u32[]{:S(2)}, u32[]{:S(2)}) collective-permute-start(bf16[2,1040,256]{2,1,0:T(8,128)(2,1)S(1)} %shard_map.203), channel_id=1, source_target_pairs={{0,1},{1,0},{2,3},{3,2},{4,5},{5,4},{6,7},{7,6},{8,9},{9,8},{10,11... | collective-permute-start | bytes 3194888 | tf_op jit(solution)/shard_map/ppermute | solution.py:40
  14.8 3.6 %collective-permute-start.2 = (bf16[256,512]{1,0:T(8,128)(2,1)S(1)}, bf16[256,512]{1,0:T(8,128)(2,1)}, u32[]{:S(2)}, u32[]{:S(2)}) collective-permute-start(bf16[256,512]{1,0:T(8,128)(2,1)S(1)} %get-tuple-element.36), channel_id=1, source_target_pairs={{0,8},{8,0},{2,10},{10,2},{4,12},{12,4},{6,14},{14,6},{16,24},{24,... | collective-permute-start | bytes 786440 | tf_op jit(solution)/shard_map/ppermute | solution.py:35
  18.4 1.5 %collective-permute-start.6 = (bf16[256,512]{1,0:T(8,128)(2,1)S(1)}, bf16[256,512]{1,0:T(8,128)(2,1)}, u32[]{:S(2)}, u32[]{:S(2)}) collective-permute-start(bf16[256,512]{1,0:T(8,128)(2,1)S(1)} %get-tuple-element.36), channel_id=1, source_target_pairs={{0,4},{4,0},{2,6},{6,2},{8,12},{12,8},{10,14},{14,10},{16,20},{20,... | collective-permute-start | bytes 786440 | tf_op jit(solution)/shard_map/ppermute | solution.py:35
  20.1 1.3 %copy.22 = bf16[4096,16]{1,0:T(8,128)(2,1)} copy(bf16[4096,16]{0,1:T(8,128)(2,1)S(1)} %copy-done.7) | data formatting | bytes 262144 | tf_op jit(solution)/shard_map/optimization_barrier | solution.py:514
  21.5 4.2 %collective-permute-done.2 = bf16[256,512]{1,0:T(8,128)(2,1)} collective-permute-done((bf16[256,512]{1,0:T(8,128)(2,1)S(1)}, bf16[256,512]{1,0:T(8,128)(2,1)}, u32[]{:S(2)}, u32[]{:S(2)}) %collective-permute-start.2) | collective-permute-done | bytes 262176 | tf_op jit(solution)/shard_map/ppermute | solution.py:35
  26.5 1.1 %pad_maximum_fusion.7.refs_0_ = bf16[3,256,512]{2,1,0:T(8,128)(2,1)S(1)} fusion(bf16[1,256,512]{2,1,0:T(8,128)(2,1)} %bitcast.13, bf16[1,256,512]{2,1,0:T(8,128)(2,1)} %bitcast.12, bf16[1,256,512]{2,1,0:T(8,128)(2,1)S(1)} %bitcast.46), kind=kLoop, calls=%fused_computation.25 | loop fusion | flops 786432 | bytes 1572864 | tf_op jit(solution)/shard_map/stack | solution.py:547
  28.0 1.5 %collective-permute-start.4 = (bf16[256,512]{1,0:T(8,128)(2,1)}, bf16[256,512]{1,0:T(8,128)(2,1)S(1)}, u32[]{:S(2)}, u32[]{:S(2)}) collective-permute-start(bf16[256,512]{1,0:T(8,128)(2,1)} %collective-permute-done.2), channel_id=1, source_target_pairs={{0,4},{4,0},{2,6},{6,2},{8,12},{12,8},{10,14},{14,10},{16,20},{20,... | collective-permute-start | bytes 786440 | tf_op jit(solution)/shard_map/ppermute | solution.py:35
  30.5 6.2 %collective-permute-done.3 = bf16[256,512]{1,0:T(8,128)(2,1)} collective-permute-done((bf16[256,512]{1,0:T(8,128)(2,1)}, bf16[256,512]{1,0:T(8,128)(2,1)}, u32[]{:S(2)}, u32[]{:S(2)}) %collective-permute-start.3) | collective-permute-done | bytes 262176 | tf_op jit(solution)/shard_map/ppermute | solution.py:35
  37.8 1.6 %collective-permute-start.5 = (bf16[2,256,512]{2,1,0:T(8,128)(2,1)S(1)}, bf16[2,256,512]{2,1,0:T(8,128)(2,1)S(1)}, u32[]{:S(2)}, u32[]{:S(2)}) collective-permute-start(bf16[2,256,512]{2,1,0:T(8,128)(2,1)S(1)} %pad_maximum_fusion.8), channel_id=1, source_target_pairs={{0,4},{4,0},{2,6},{6,2},{8,12},{12,8},{10,14},{14,10},{16,20},{20,... | collective-permute-start | bytes 1572872 | tf_op jit(solution)/shard_map/ppermute | solution.py:35
  39.5 1.3 %collective-permute-done.9.refs_2_.refs_3_.refs_11_ = bf16[2,1040,256]{2,1,0:T(8,128)(2,1)S(1)} collective-permute-done((bf16[2,1040,256]{2,1,0:T(8,128)(2,1)S(1)}, bf16[2,1040,256]{2,1,0:T(8,128)(2,1)S(1)}, u32[]{:S(2)}, u32[]{:S(2)}) %collective-permute-start.9) | collective-permute-done | bytes 1064992 | tf_op jit(solution)/shard_map/ppermute | solution.py:40
  40.8 1.3 %shard_map.205 = bf16[256,4096]{1,0:T(8,128)(2,1)S(1)} custom-call(s32[8]{0:T(128)S(1)} %broadcast_xor_fusion.places_ref, bf16[3,256,512]{2,1,0:T(8,128)(2,1)S(1)} %pad_maximum_fusion.7.refs_0_, bf16[1,256,512]{2,1,0:T(8,128)(2,1)S(1)} %bitcast.41, bf16[3,256,512]{2,1,0:T(8,128)(2,1)} %collective-permute-done.7.refs_2_, ...), custom_call_target="tpu_custom_call" | custom-call | flops 1000000 | bytes 10000 | tf_op jit(solution)/shard_map/pallas_call | solution.py:72
  42.1 1.3 %fusion.23 = bf16[256,272]{1,0:T(8,128)(2,1)S(1)} fusion(bf16[256,4096]{1,0:T(8,128)(2,1)S(1)} %shard_map.205, bf16[4096,16]{1,0:T(8,128)(2,1)S(1)} %copy-done.5, bf16[4096,256]{1,0:T(8,128)(2,1)S(1)} %copy-done.18), kind=kOutput, calls=%fused_computation.14 | convolution fusion | flops 574951424 | bytes 4464640 | tf_op jit(solution)/shard_map/dot_general | solution.py:563
  43.4 11.3 %fusion.18 = bf16[2,256,1024]{2,1,0:T(8,128)(2,1)S(1)} fusion(bf16[4096,2,1024]{2,1,0:T(2,128)(2,1)} %param.21, bf16[256,4096]{1,0:T(8,128)(2,1)S(1)} %shard_map.205), kind=kOutput, calls=%fused_computation.11 | convolution fusion | flops 4295491584 | bytes 19922944 | tf_op jit(solution)/shard_map/td,dkc->ktc/dot_general | solution.py:565
  55.8 4.3 %collective-permute-start.12 = (bf16[256,272]{1,0:T(8,128)(2,1)S(1)}, bf16[256,272]{1,0:T(8,128)(2,1)S(1)}, u32[]{:S(2)}, u32[]{:S(2)}) collective-permute-start(bf16[256,272]{1,0:T(8,128)(2,1)S(1)} %fusion.23), channel_id=1, source_target_pairs={{0,1},{1,0},{2,3},{3,2},{4,5},{5,4},{6,7},{7,6},{8,9},{9,8},{10,11... | collective-permute-start | bytes 417800 | tf_op jit(solution)/shard_map/ppermute | solution.py:40
  60.1 2.0 %collective-permute-start.14 = (bf16[256,1024]{1,0:T(8,128)(2,1)}, bf16[256,1024]{1,0:T(8,128)(2,1)}, u32[]{:S(2)}, u32[]{:S(2)}) collective-permute-start(bf16[256,1024]{1,0:T(8,128)(2,1)} %get-tuple-element.57), channel_id=1, source_target_pairs={{0,1},{1,0},{2,3},{3,2},{4,5},{5,4},{6,7},{7,6},{8,9},{9,8},{10,11... | collective-permute-start | bytes 1572872 | tf_op jit(solution)/shard_map/ppermute | solution.py:40
  62.9 1.3 %fusion.24.own_ref = bf16[256,272]{1,0:T(8,128)(2,1)S(1)} fusion(bf16[256,4096]{1,0:T(8,128)(2,1)S(1)} %shard_map.206, bf16[4096,16]{1,0:T(8,128)(2,1)S(1)} %copy-done.5, bf16[4096,256]{1,0:T(8,128)(2,1)S(1)} %copy-done.18), kind=kOutput, calls=%fused_computation.15 | convolution fusion | flops 574951424 | bytes 4464640 | tf_op jit(solution)/shard_map/dot_general | solution.py:563
  64.1 12.2 %fusion.8 = f32[2,256,1024]{2,1,0:T(8,128)S(1)} fusion(bf16[4096,2,1024]{2,1,0:T(2,128)(2,1)} %param.21, bf16[256,4096]{1,0:T(8,128)(2,1)S(1)} %shard_map.206), kind=kOutput, calls=%fused_computation.9 | convolution fusion | flops 4294967296 | bytes 20971520 | tf_op jit(solution)/shard_map/td,dkc->ktc/dot_general | solution.py:565
  76.3 1.1 %slice_bitcast_fusion = (f32[256,1024]{1,0:T(8,128)}, f32[256,1024]{1,0:T(8,128)S(1)}) fusion(f32[2,256,1024]{2,1,0:T(8,128)S(1)} %fusion.8), kind=kLoop, calls=%fused_computation.20 | loop fusion | bytes 4194304 | tf_op jit(solution)/shard_map/squeeze | solution.py:566
  77.5 1.7 %shard_map.207 = (bf16[256,256]{1,0:T(8,128)(2,1)S(1)}, f32[4,12,256]{2,1,0:T(8,128)S(1)}, f32[8,16]{1,0:T(8,128)S(1)}) custom-call(s32[8]{0:T(128)S(1)} %pad_add_fusion.ints_ref, bf16[256,272]{1,0:T(8,128)(2,1)S(1)} %fusion.24.own_ref, bf16[256,272]{1,0:T(8,128)(2,1)S(1)} %collective-permute-done.12.refs_0_, f32[2,16,256]{2,1,0:T(8,128)S(1)} %shard_map.204.refs_1_.refs_2_, ...), custom_call_target="tpu_custom_call" | custom-call | flops 1000000 | bytes 10000 | tf_op jit(solution)/shard_map/pallas_call | solution.py:221
  79.2 1.3 %collective-permute-done.13 = bf16[256,256]{1,0:T(8,128)(2,1)S(1)} collective-permute-done((bf16[256,256]{1,0:T(8,128)(2,1)S(1)}, bf16[256,256]{1,0:T(8,128)(2,1)S(1)}, u32[]{:S(2)}, u32[]{:S(2)}) %collective-permute-start.13) | collective-permute-done | bytes 131104 | tf_op jit(solution)/shard_map/ppermute | solution.py:35
  80.7 8.0 %shard_map.208 = (f32[256,1024]{1,0:T(8,128)S(1)}, f32[2,16,64,256]{3,2,1,0:T(8,128)}) custom-call(s32[8]{0:T(128)S(1)} %pad_add_fusion.ints_ref, f32[256,1024]{1,0:T(8,128)S(1)} %get-tuple-element.61.refs_0_, bf16[256,1024]{1,0:T(8,128)(2,1)S(1)} %collective-permute-done.11.refs_1_, f32[2,16,256]{2,1,0:T(8,128)S(1)} %shard_map.204.refs_1_.refs_2_, ...), custom_call_target="tpu_custom_call" | custom-call | flops 1000000 | bytes 10000 | tf_op jit(solution)/shard_map/pallas_call | solution.py:433
  88.8 1.5 %multiply_reduce_fusion = (f32[256]{0:T(256)S(1)}, f32[256,1024]{1,0:T(8,128)S(1)}) fusion(f32[256,1024]{1,0:T(8,128)S(1)} %get-tuple-element.67, f32[256,1024]{1,0:T(8,128)S(1)} %copy-done.4, bf16[256,1024]{1,0:T(8,128)(2,1)} %collective-permute-done.14), kind=kLoop, calls=%fused_computation.23 | loop fusion | flops 2883328 | bytes 3671040 | tf_op jit(solution)/shard_map/reduce_sum | solution.py:609
  (88 shorter events, 11.5 us)
Async XLA Ops:
  0.6 13.4 %collective-permute-start = (bf16[256,512]{1,0:T(8,128)(2,1)}, bf16[256,512]{1,0:T(8,128)(2,1)S(1)}, u32[]{:S(2)}, u32[]{:S(2)}) collective-permute-start(bf16[256,512]{1,0:T(8,128)(2,1)} %param.20), channel_id=1, source_target_pairs={{0,16},{1,0},{2,18},{3,2},{4,20},{5,4},{6,22},{7,6},{8,24},{9,8},{... | collective-permute-start | bytes 786440 | tf_op jit(solution)/shard_map/ppermute | solution.py:90
  4.7 9.3 %collective-permute-start.1 = (bf16[256,512]{1,0:T(8,128)(2,1)}, bf16[256,512]{1,0:T(8,128)(2,1)S(1)}, u32[]{:S(2)}, u32[]{:S(2)}) collective-permute-start(bf16[256,512]{1,0:T(8,128)(2,1)} %param.20), channel_id=1, source_target_pairs={{1,16},{3,18},{5,20},{7,22},{9,24},{11,26},{13,28},{15,30},{16,1},... | collective-permute-start | bytes 786440 | tf_op jit(solution)/shard_map/ppermute | solution.py:91
  9.9 19.8 %copy-start.11 = (f32[4,256]{1,0:T(4,128)S(1)}, f32[4,256]{1,0:T(4,128)}, u32[]{:S(2)}) copy-start(f32[4,256]{1,0:T(4,128)} %param.29) | copy-start | bytes 12292
  9.9 19.8 %copy-start.13 = (f32[256]{0:T(256)S(1)}, f32[256]{0:T(256)}, u32[]{:S(2)}) copy-start(f32[256]{0:T(256)} %param.30) | copy-start | bytes 3076
  9.9 19.8 %copy-start.8 = (f32[1024]{0:T(1024)S(1)}, f32[1024]{0:T(1024)}, u32[]{:S(2)}) copy-start(f32[1024]{0:T(1024)} %param.31) | copy-start | bytes 12292
  9.9 19.8 %copy-start.9 = (f32[4,1024]{1,0:T(4,128)S(1)}, f32[4,1024]{1,0:T(4,128)}, u32[]{:S(2)}) copy-start(f32[4,1024]{1,0:T(4,128)} %param.27) | copy-start | bytes 49156
  10.0 19.8 %copy-start.10 = (f32[1024]{0:T(1024)S(1)}, f32[1024]{0:T(1024)}, u32[]{:S(2)}) copy-start(f32[1024]{0:T(1024)} %param.28) | copy-start | bytes 12292
  10.0 30.8 %collective-permute-start.9 = (bf16[2,1040,256]{2,1,0:T(8,128)(2,1)S(1)}, bf16[2,1040,256]{2,1,0:T(8,128)(2,1)S(1)}, u32[]{:S(2)}, u32[]{:S(2)}) collective-permute-start(bf16[2,1040,256]{2,1,0:T(8,128)(2,1)S(1)} %shard_map.203), channel_id=1, source_target_pairs={{0,1},{1,0},{2,3},{3,2},{4,5},{5,4},{6,7},{7,6},{8,9},{9,8},{10,11... | collective-permute-start | bytes 3194888 | tf_op jit(solution)/shard_map/ppermute | solution.py:40
  14.0 15.8 %copy-start.1 = (bf16[8,3,1024]{2,0,1:T(8,128)(2,1)S(1)}, bf16[8,3,1024]{2,0,1:T(8,128)(2,1)}, u32[]{:S(2)}) copy-start(bf16[8,3,1024]{2,0,1:T(8,128)(2,1)} %param.36) | copy-start | bytes 147460
  14.0 15.8 %copy-start.3 = (bf16[8,3,256]{2,0,1:T(8,128)(2,1)S(1)}, bf16[8,3,256]{2,0,1:T(8,128)(2,1)}, u32[]{:S(2)}) copy-start(bf16[8,3,256]{2,0,1:T(8,128)(2,1)} %param.37) | copy-start | bytes 36868
  14.1 22.7 %copy-start.20 = (s32[8]{0:T(128)S(1)}, s32[8]{0:T(128)}, u32[]{:S(2)}) copy-start(s32[8]{0:T(128)} %constant.95.clone) | copy-start | bytes 100
  14.8 10.9 %collective-permute-start.2 = (bf16[256,512]{1,0:T(8,128)(2,1)S(1)}, bf16[256,512]{1,0:T(8,128)(2,1)}, u32[]{:S(2)}, u32[]{:S(2)}) collective-permute-start(bf16[256,512]{1,0:T(8,128)(2,1)S(1)} %get-tuple-element.36), channel_id=1, source_target_pairs={{0,8},{8,0},{2,10},{10,2},{4,12},{12,4},{6,14},{14,6},{16,24},{24,... | collective-permute-start | bytes 786440 | tf_op jit(solution)/shard_map/ppermute | solution.py:35
  18.4 8.1 %collective-permute-start.6 = (bf16[256,512]{1,0:T(8,128)(2,1)S(1)}, bf16[256,512]{1,0:T(8,128)(2,1)}, u32[]{:S(2)}, u32[]{:S(2)}) collective-permute-start(bf16[256,512]{1,0:T(8,128)(2,1)S(1)} %get-tuple-element.36), channel_id=1, source_target_pairs={{0,4},{4,0},{2,6},{6,2},{8,12},{12,8},{10,14},{14,10},{16,20},{20,... | collective-permute-start | bytes 786440 | tf_op jit(solution)/shard_map/ppermute | solution.py:35
  27.6 13.2 %collective-permute-start.7 = (bf16[3,256,512]{2,1,0:T(8,128)(2,1)S(1)}, bf16[3,256,512]{2,1,0:T(8,128)(2,1)}, u32[]{:S(2)}, u32[]{:S(2)}) collective-permute-start(bf16[3,256,512]{2,1,0:T(8,128)(2,1)S(1)} %pad_maximum_fusion.7.refs_0_), channel_id=1, source_target_pairs={{0,2},{2,0},{4,6},{6,4},{8,10},{10,8},{12,14},{14,12},{16,18},{18,... | collective-permute-start | bytes 2359304 | tf_op jit(solution)/shard_map/ppermute | solution.py:35
  27.7 9.0 %collective-permute-start.3 = (bf16[256,512]{1,0:T(8,128)(2,1)}, bf16[256,512]{1,0:T(8,128)(2,1)}, u32[]{:S(2)}, u32[]{:S(2)}) collective-permute-start(bf16[256,512]{1,0:T(8,128)(2,1)} %get-tuple-element.40), channel_id=1, source_target_pairs={{0,8},{8,0},{2,10},{10,2},{4,12},{12,4},{6,14},{14,6},{16,24},{24,... | collective-permute-start | bytes 786440 | tf_op jit(solution)/shard_map/ppermute | solution.py:35
  28.0 8.7 %collective-permute-start.4 = (bf16[256,512]{1,0:T(8,128)(2,1)}, bf16[256,512]{1,0:T(8,128)(2,1)S(1)}, u32[]{:S(2)}, u32[]{:S(2)}) collective-permute-start(bf16[256,512]{1,0:T(8,128)(2,1)} %collective-permute-done.2), channel_id=1, source_target_pairs={{0,4},{4,0},{2,6},{6,2},{8,12},{12,8},{10,14},{14,10},{16,20},{20,... | collective-permute-start | bytes 786440 | tf_op jit(solution)/shard_map/ppermute | solution.py:35
  36.7 2.7 %collective-permute-start.8 = (bf16[1,256,512]{2,1,0:T(8,128)(2,1)S(1)}, bf16[1,256,512]{2,1,0:T(8,128)(2,1)S(1)}, u32[]{:S(2)}, u32[]{:S(2)}) collective-permute-start(bf16[1,256,512]{2,1,0:T(8,128)(2,1)S(1)} %bitcast.40), channel_id=1, source_target_pairs={{0,2},{2,0},{4,6},{6,4},{8,10},{10,8},{12,14},{14,12},{16,18},{18,... | collective-permute-start | bytes 786440 | tf_op jit(solution)/shard_map/ppermute | solution.py:35
  37.8 17.8 %collective-permute-start.5 = (bf16[2,256,512]{2,1,0:T(8,128)(2,1)S(1)}, bf16[2,256,512]{2,1,0:T(8,128)(2,1)S(1)}, u32[]{:S(2)}, u32[]{:S(2)}) collective-permute-start(bf16[2,256,512]{2,1,0:T(8,128)(2,1)S(1)} %pad_maximum_fusion.8), channel_id=1, source_target_pairs={{0,4},{4,0},{2,6},{6,2},{8,12},{12,8},{10,14},{14,10},{16,20},{20,... | collective-permute-start | bytes 1572872 | tf_op jit(solution)/shard_map/ppermute | solution.py:35
  55.7 6.4 %collective-permute-start.10 = (bf16[4,256,512]{2,1,0:T(8,128)(2,1)S(1)}, bf16[4,256,512]{2,1,0:T(8,128)(2,1)S(1)}, u32[]{:S(2)}, u32[]{:S(2)}) collective-permute-start(bf16[4,256,512]{2,1,0:T(8,128)(2,1)S(1)} %constant_dynamic-update-slice_fusion.refs_0_), channel_id=1, source_target_pairs={{0,2},{2,0},{4,6},{6,4},{8,10},{10,8},{12,14},{14,12},{16,18},{18,... | collective-permute-start | bytes 3145736 | tf_op jit(solution)/shard_map/ppermute | solution.py:35
  55.8 21.7 %collective-permute-start.12 = (bf16[256,272]{1,0:T(8,128)(2,1)S(1)}, bf16[256,272]{1,0:T(8,128)(2,1)S(1)}, u32[]{:S(2)}, u32[]{:S(2)}) collective-permute-start(bf16[256,272]{1,0:T(8,128)(2,1)S(1)} %fusion.23), channel_id=1, source_target_pairs={{0,1},{1,0},{2,3},{3,2},{4,5},{5,4},{6,7},{7,6},{8,9},{9,8},{10,11... | collective-permute-start | bytes 417800 | tf_op jit(solution)/shard_map/ppermute | solution.py:40
  60.1 19.1 %collective-permute-start.11 = (bf16[256,1024]{1,0:T(8,128)(2,1)}, bf16[256,1024]{1,0:T(8,128)(2,1)S(1)}, u32[]{:S(2)}, u32[]{:S(2)}) collective-permute-start(bf16[256,1024]{1,0:T(8,128)(2,1)} %get-tuple-element.56), channel_id=1, source_target_pairs={{0,1},{1,0},{2,3},{3,2},{4,5},{5,4},{6,7},{7,6},{8,9},{9,8},{10,11... | collective-permute-start | bytes 1572872 | tf_op jit(solution)/shard_map/ppermute | solution.py:40
  60.1 28.6 %collective-permute-start.14 = (bf16[256,1024]{1,0:T(8,128)(2,1)}, bf16[256,1024]{1,0:T(8,128)(2,1)}, u32[]{:S(2)}, u32[]{:S(2)}) collective-permute-start(bf16[256,1024]{1,0:T(8,128)(2,1)} %get-tuple-element.57), channel_id=1, source_target_pairs={{0,1},{1,0},{2,3},{3,2},{4,5},{5,4},{6,7},{7,6},{8,9},{9,8},{10,11... | collective-permute-start | bytes 1572872 | tf_op jit(solution)/shard_map/ppermute | solution.py:40
  79.1 1.4 %collective-permute-start.13 = (bf16[256,256]{1,0:T(8,128)(2,1)S(1)}, bf16[256,256]{1,0:T(8,128)(2,1)S(1)}, u32[]{:S(2)}, u32[]{:S(2)}) collective-permute-start(bf16[256,256]{1,0:T(8,128)(2,1)S(1)} %get-tuple-element.63), channel_id=1, source_target_pairs={{0,2},{2,0},{4,6},{6,4},{8,10},{10,8},{12,14},{14,12},{16,18},{18,... | collective-permute-start | bytes 393224 | tf_op jit(solution)/shard_map/ppermute | solution.py:35
  90.2 1.2 %collective-permute-start.15 = (f32[256]{0:T(256)S(1)}, f32[256]{0:T(256)S(1)}, u32[]{:S(2)}, u32[]{:S(2)}) collective-permute-start(f32[256]{0:T(256)S(1)} %get-tuple-element.70), channel_id=1, source_target_pairs={{0,2},{2,0},{4,6},{6,4},{8,10},{10,8},{12,14},{14,12},{16,18},{18,... | collective-permute-start | bytes 3080 | tf_op jit(solution)/shard_map/ppermute | solution.py:35
  (13 other events, 110.2 us)

commit v16 on v15

--- a/solution.py
+++ b/solution.py
@@ -41,18 +41,18 @@
 
 
 def spread_routes():
-    first, second = [], []
+    far, across, diagonal = [], [], []
     for z in range(4):
         for rest in range(4):
             for r in range(2):
                 place = (z * 4 + rest) * 2 + r
                 other = (((z + 2) % 4) * 4 + rest) * 2 + r
                 if z // 2 == r:
-                    first.append((place, other))
+                    far.append((place, other))
                 else:
-                    first.append((place, place ^ 1))
-                    second.append((place, other ^ 1))
-    return first, second
+                    across.append((place, place ^ 1))
+                    diagonal.append((place, other ^ 1))
+    return far, across, diagonal
 
 
 def arrange_kernel(places_ref, *refs):
@@ -84,13 +84,20 @@
     return lax.optimization_barrier((value, others))[0]
 
 
-def near_blocks(x_in):
-    axes = ("wide", "req")
-    first, second = spread_routes()
-    first = lax.ppermute(x_in, axes, first)
-    second = lax.ppermute(x_in, axes, second)
-    near = lax.axis_index("wide") // 8 == lax.axis_index("req")
-    return jnp.where(near, x_in, first), jnp.where(near, first, second)
+def is_near():
+    return lax.axis_index("wide") // 8 == lax.axis_index("req")
+
+
+def first_block(x_in):
+    _, across, diagonal = spread_routes()
+    diagonal = lax.ppermute(x_in, ("wide", "req"), diagonal)
+    across = lax.ppermute(x_in, ("wide", "req"), across)
+    return jnp.where(is_near(), across, diagonal)
+
+
+def first_own_block(x_in):
+    far = lax.ppermute(x_in, ("wide", "req"), spread_routes()[0])
+    return jnp.where(is_near(), x_in, far)
 
 
 def quad_arrange(stacks, apart):
@@ -488,7 +495,7 @@
 
     direct = req_count == 2 and lax.axis_size("wide") == 16
     if direct:
-        own_block, block = near_blocks(x_in)
+        block = first_block(x_in)
 
     def slots_of(index):
         asked = lax.dynamic_slice_in_dim(state_slot, index * group_reqs, group_reqs)
@@ -505,6 +512,7 @@
 
     w_step = w_dt
     if direct:
+        own_block = first_own_block(after(x_in, packed))
         block = after(block, packed)
         along_z = partner_2(block, "wide", 2)
         along_x = partner_2(block, "wide", 1)

time: 92.9 us -> 97.2 us (1.046)
  starting transfers between devices: 24.1 us -> 29.5 us
  waiting for transfers between devices: 14.8 us -> 12.9 us
    ppermute x2 -> x3, starting transfers between devices: 4.75 us -> 12 us  [the longest x1 10 us: first_own_block(): far = lax.ppermute(x_in, ('wide', 'req'), spread_routes()[0])]
    ppermute x4, starting transfers between devices: 10.4 us -> 6.85 us  [shift_req(): lax.ppermute(block, 'req', [(i, (i + step) % count) for i in range(count)])]
    ppermute x10, waiting for transfers between devices: 13.5 us -> 10.4 us  [partner_2(): return lax.ppermute(block, axis, route)]
    ppermute x2 -> x3, waiting for transfers between devices: 0.01 us -> 2.54 us  [the longest x1 2.54 us: first_own_block(): far = lax.ppermute(x_in, ('wide', 'req'), spread_routes()[0])]
    ppermute x10, starting transfers between devices: 8.9 us -> 10.6 us  [partner_2(): return lax.ppermute(block, axis, route)]
    ppermute x4, waiting for transfers between devices: 1.3 us -> 0.01 us  [shift_req(): lax.ppermute(block, 'req', [(i, (i + step) % count) for i in range(count)])]
  transfers between devices with their start and end apart: 16 -> 17, of which waited for: 6 -> 6; matrix products, arithmetic and copies ran while one was open for 37% -> 35% of each run, Pallas kernels for 16% -> 15%
where the time goes in v16:
time: 97.2 us; the launch traced here: 96.8 us
  starting transfers between devices  29.5 us (30%)
  matrix products  26 us (27%)
  Pallas kernels  14.7 us (15%)
  waiting for transfers between devices  12.9 us (13%)
  other arithmetic  6.5 us (7%)
  local copies, waits for them, and re-layouts  6.12 us (6%)
  between operations  1.04 us (1%)
    dot_general x2, matrix products, project(): high = jnp.einsum('td,dkc->ktc', block, w_xz, preferred_element_type=F32)  23.5 us
    ppermute x10, starting transfers between devices, partner_2(): return lax.ppermute(block, axis, route)  10.6 us
    ppermute x10, waiting for transfers between devices, partner_2(): return lax.ppermute(block, axis, route)  10.4 us
    ppermute x1, starting transfers between devices, first_own_block(): far = lax.ppermute(x_in, ('wide', 'req'), spread_routes()[0])  10 us
    pallas_call x1, Pallas kernels, mixer(): pl.pallas_call(functools.partial(mixer_kernel, count_req, len(got), per_p...  8.04 us
    ppermute x4, starting transfers between devices, shift_req(): lax.ppermute(block, 'req', [(i, (i + step) % count) for i in range(count)])  6.85 us
    ppermute x1, waiting for transfers between devices, first_own_block(): far = lax.ppermute(x_in, ('wide', 'req'), spread_routes()[0])  2.54 us
    dot_general x2, matrix products, project(): low = jnp.dot(block, w_map, preferred_element_type=F32).astype(BF16)  2.51 us
  transfers between devices with their start and end apart: 17, of which 6 were waited for; matrix products, arithmetic and copies ran while one was open for 35% of the time, Pallas kernels for 15%

profile of v16, /device:TPU:0, one launch (start us, length us, event | category | flops | bytes accessed | tf_op | source)
XLA Modules:
  0.0 96.8 jit_solution(8199286221769323799)
XLA Ops:
  0.6 1.3 %collective-permute-start = (bf16[256,512]{1,0:T(8,128)(2,1)}, bf16[256,512]{1,0:T(8,128)(2,1)S(1)}, u32[]{:S(2)}, u32[]{:S(2)}) collective-permute-start(bf16[256,512]{1,0:T(8,128)(2,1)} %param.20), channel_id=1, source_target_pairs={{1,0},{3,2},{5,4},{7,6},{9,8},{11,10},{13,12},{15,14},{16,17},{18,... | collective-permute-start | bytes 786440 | tf_op jit(solution)/shard_map/ppermute | solution.py:94
  4.9 2.2 %shard_map.203 = bf16[2,1040,256]{2,1,0:T(8,128)(2,1)S(1)} custom-call(s32[2]{0:T(128)S(1)} %subtract_clamp_fusion.1.slots_ref, f32[8,16,64,256]{3,2,1,0:T(8,128)} %refs_10_.1, bf16[3,8,1024]{2,1,0:T(8,128)(2,1)S(1)} %bitcast.42, bf16[3,8,256]{2,1,0:T(8,128)(2,1)S(1)} %bitcast.44), custom_call_target="tpu_custom_call" | custom-call | bytes 3145728 | tf_op jit(solution)/shard_map/pallas_call | solution.py:281
  7.1 10.0 %collective-permute-start.2 = (bf16[256,512]{1,0:T(8,128)(2,1)S(1)}, bf16[256,512]{1,0:T(8,128)(2,1)}, u32[]{:S(2)}, u32[]{:S(2)}) collective-permute-start(bf16[256,512]{1,0:T(8,128)(2,1)S(1)} %copy-done.6), channel_id=1, source_target_pairs={{0,16},{2,18},{4,20},{6,22},{8,24},{10,26},{12,28},{14,30},{17,1},... | collective-permute-start | bytes 786440 | tf_op jit(solution)/shard_map/ppermute | solution.py:99
  17.5 1.7 %collective-permute-start.3 = (bf16[256,512]{1,0:T(8,128)(2,1)S(1)}, bf16[256,512]{1,0:T(8,128)(2,1)}, u32[]{:S(2)}, u32[]{:S(2)}) collective-permute-start(bf16[256,512]{1,0:T(8,128)(2,1)S(1)} %broadcast_select_fusion.1), channel_id=1, source_target_pairs={{0,8},{8,0},{2,10},{10,2},{4,12},{12,4},{6,14},{14,6},{16,24},{24,... | collective-permute-start | bytes 786440 | tf_op jit(solution)/shard_map/ppermute | solution.py:35
  19.2 1.5 %collective-permute-start.7 = (bf16[256,512]{1,0:T(8,128)(2,1)S(1)}, bf16[256,512]{1,0:T(8,128)(2,1)}, u32[]{:S(2)}, u32[]{:S(2)}) collective-permute-start(bf16[256,512]{1,0:T(8,128)(2,1)S(1)} %broadcast_select_fusion.1), channel_id=1, source_target_pairs={{0,4},{4,0},{2,6},{6,2},{8,12},{12,8},{10,14},{14,10},{16,20},{20,... | collective-permute-start | bytes 786440 | tf_op jit(solution)/shard_map/ppermute | solution.py:35
  20.7 2.5 %collective-permute-done.2 = bf16[256,512]{1,0:T(8,128)(2,1)} collective-permute-done((bf16[256,512]{1,0:T(8,128)(2,1)S(1)}, bf16[256,512]{1,0:T(8,128)(2,1)}, u32[]{:S(2)}, u32[]{:S(2)}) %collective-permute-start.2) | collective-permute-done | bytes 262176 | tf_op jit(solution)/shard_map/ppermute | solution.py:99
  24.2 1.3 %copy.22 = bf16[4096,16]{1,0:T(8,128)(2,1)} copy(bf16[4096,16]{0,1:T(8,128)(2,1)S(1)} %copy-done.7) | data formatting | bytes 262144 | tf_op jit(solution)/shard_map/optimization_barrier | solution.py:522
  25.6 2.0 %collective-permute-done.3 = bf16[256,512]{1,0:T(8,128)(2,1)} collective-permute-done((bf16[256,512]{1,0:T(8,128)(2,1)S(1)}, bf16[256,512]{1,0:T(8,128)(2,1)}, u32[]{:S(2)}, u32[]{:S(2)}) %collective-permute-start.3) | collective-permute-done | bytes 262176 | tf_op jit(solution)/shard_map/ppermute | solution.py:35
  28.8 3.7 %collective-permute-start.4 = (bf16[256,512]{1,0:T(8,128)(2,1)}, bf16[256,512]{1,0:T(8,128)(2,1)}, u32[]{:S(2)}, u32[]{:S(2)}) collective-permute-start(bf16[256,512]{1,0:T(8,128)(2,1)} %broadcast_select_fusion), channel_id=1, source_target_pairs={{0,8},{8,0},{2,10},{10,2},{4,12},{12,4},{6,14},{14,6},{16,24},{24,... | collective-permute-start | bytes 786440 | tf_op jit(solution)/shard_map/ppermute | solution.py:35
  32.5 1.5 %collective-permute-start.5 = (bf16[256,512]{1,0:T(8,128)(2,1)}, bf16[256,512]{1,0:T(8,128)(2,1)S(1)}, u32[]{:S(2)}, u32[]{:S(2)}) collective-permute-start(bf16[256,512]{1,0:T(8,128)(2,1)} %collective-permute-done.3), channel_id=1, source_target_pairs={{0,4},{4,0},{2,6},{6,2},{8,12},{12,8},{10,14},{14,10},{16,20},{20,... | collective-permute-start | bytes 786440 | tf_op jit(solution)/shard_map/ppermute | solution.py:35
  35.0 4.7 %collective-permute-done.4 = bf16[256,512]{1,0:T(8,128)(2,1)} collective-permute-done((bf16[256,512]{1,0:T(8,128)(2,1)}, bf16[256,512]{1,0:T(8,128)(2,1)}, u32[]{:S(2)}, u32[]{:S(2)}) %collective-permute-start.4) | collective-permute-done | bytes 262176 | tf_op jit(solution)/shard_map/ppermute | solution.py:35
  39.7 1.4 %collective-permute-done.5 = bf16[256,512]{1,0:T(8,128)(2,1)S(1)} collective-permute-done((bf16[256,512]{1,0:T(8,128)(2,1)}, bf16[256,512]{1,0:T(8,128)(2,1)S(1)}, u32[]{:S(2)}, u32[]{:S(2)}) %collective-permute-start.5) | collective-permute-done | bytes 262176 | tf_op jit(solution)/shard_map/ppermute | solution.py:35
  42.2 1.6 %collective-permute-start.6 = (bf16[2,256,512]{2,1,0:T(8,128)(2,1)S(1)}, bf16[2,256,512]{2,1,0:T(8,128)(2,1)S(1)}, u32[]{:S(2)}, u32[]{:S(2)}) collective-permute-start(bf16[2,256,512]{2,1,0:T(8,128)(2,1)S(1)} %pad_maximum_fusion.8), channel_id=1, source_target_pairs={{0,4},{4,0},{2,6},{6,2},{8,12},{12,8},{10,14},{14,10},{16,20},{20,... | collective-permute-start | bytes 1572872 | tf_op jit(solution)/shard_map/ppermute | solution.py:35
  43.9 1.5 %shard_map.205 = bf16[256,4096]{1,0:T(8,128)(2,1)S(1)} custom-call(s32[8]{0:T(128)S(1)} %broadcast_xor_fusion.places_ref, bf16[3,256,512]{2,1,0:T(8,128)(2,1)S(1)} %pad_maximum_fusion.7.refs_0_, bf16[1,256,512]{2,1,0:T(8,128)(2,1)S(1)} %bitcast.41, bf16[3,256,512]{2,1,0:T(8,128)(2,1)} %collective-permute-done.8.refs_2_, ...), custom_call_target="tpu_custom_call" | custom-call | flops 1000000 | bytes 10000 | tf_op jit(solution)/shard_map/pallas_call | solution.py:72
  46.0 1.3 %fusion.23 = bf16[256,272]{1,0:T(8,128)(2,1)S(1)} fusion(bf16[256,4096]{1,0:T(8,128)(2,1)S(1)} %shard_map.205, bf16[4096,16]{1,0:T(8,128)(2,1)S(1)} %copy-done.5, bf16[4096,256]{1,0:T(8,128)(2,1)S(1)} %copy-done.18), kind=kOutput, calls=%fused_computation.14 | convolution fusion | flops 574951424 | bytes 4464640 | tf_op jit(solution)/shard_map/dot_general | solution.py:571
  47.2 11.2 %fusion.18 = bf16[2,256,1024]{2,1,0:T(8,128)(2,1)S(1)} fusion(bf16[4096,2,1024]{2,1,0:T(2,128)(2,1)} %param.21, bf16[256,4096]{1,0:T(8,128)(2,1)S(1)} %shard_map.205), kind=kOutput, calls=%fused_computation.11 | convolution fusion | flops 4295491584 | bytes 19922944 | tf_op jit(solution)/shard_map/td,dkc->ktc/dot_general | solution.py:573
  59.8 4.6 %collective-permute-start.13 = (bf16[256,272]{1,0:T(8,128)(2,1)S(1)}, bf16[256,272]{1,0:T(8,128)(2,1)S(1)}, u32[]{:S(2)}, u32[]{:S(2)}) collective-permute-start(bf16[256,272]{1,0:T(8,128)(2,1)S(1)} %fusion.23), channel_id=1, source_target_pairs={{0,1},{1,0},{2,3},{3,2},{4,5},{5,4},{6,7},{7,6},{8,9},{9,8},{10,11... | collective-permute-start | bytes 417800 | tf_op jit(solution)/shard_map/ppermute | solution.py:40
  64.5 2.0 %collective-permute-start.15 = (bf16[256,1024]{1,0:T(8,128)(2,1)}, bf16[256,1024]{1,0:T(8,128)(2,1)}, u32[]{:S(2)}, u32[]{:S(2)}) collective-permute-start(bf16[256,1024]{1,0:T(8,128)(2,1)} %get-tuple-element.59), channel_id=1, source_target_pairs={{0,1},{1,0},{2,3},{3,2},{4,5},{5,4},{6,7},{7,6},{8,9},{9,8},{10,11... | collective-permute-start | bytes 1572872 | tf_op jit(solution)/shard_map/ppermute | solution.py:40
  67.2 1.3 %fusion.24.own_ref = bf16[256,272]{1,0:T(8,128)(2,1)S(1)} fusion(bf16[256,4096]{1,0:T(8,128)(2,1)S(1)} %shard_map.206, bf16[4096,16]{1,0:T(8,128)(2,1)S(1)} %copy-done.5, bf16[4096,256]{1,0:T(8,128)(2,1)S(1)} %copy-done.18), kind=kOutput, calls=%fused_computation.15 | convolution fusion | flops 574951424 | bytes 4464640 | tf_op jit(solution)/shard_map/dot_general | solution.py:571
  68.5 12.2 %fusion.8 = f32[2,256,1024]{2,1,0:T(8,128)S(1)} fusion(bf16[4096,2,1024]{2,1,0:T(2,128)(2,1)} %param.21, bf16[256,4096]{1,0:T(8,128)(2,1)S(1)} %shard_map.206), kind=kOutput, calls=%fused_computation.9 | convolution fusion | flops 4294967296 | bytes 20971520 | tf_op jit(solution)/shard_map/td,dkc->ktc/dot_general | solution.py:573
  81.8 1.7 %shard_map.207 = (bf16[256,256]{1,0:T(8,128)(2,1)S(1)}, f32[4,12,256]{2,1,0:T(8,128)S(1)}, f32[8,16]{1,0:T(8,128)S(1)}) custom-call(s32[8]{0:T(128)S(1)} %pad_add_fusion.ints_ref, bf16[256,272]{1,0:T(8,128)(2,1)S(1)} %fusion.24.own_ref, bf16[256,272]{1,0:T(8,128)(2,1)S(1)} %collective-permute-done.13.refs_0_, f32[2,16,256]{2,1,0:T(8,128)S(1)} %shard_map.204.refs_1_.refs_2_, ...), custom_call_target="tpu_custom_call" | custom-call | flops 1000000 | bytes 10000 | tf_op jit(solution)/shard_map/pallas_call | solution.py:228
  83.6 1.3 %collective-permute-done.14 = bf16[256,256]{1,0:T(8,128)(2,1)S(1)} collective-permute-done((bf16[256,256]{1,0:T(8,128)(2,1)S(1)}, bf16[256,256]{1,0:T(8,128)(2,1)S(1)}, u32[]{:S(2)}, u32[]{:S(2)}) %collective-permute-start.14) | collective-permute-done | bytes 131104 | tf_op jit(solution)/shard_map/ppermute | solution.py:35
  85.1 8.0 %shard_map.208 = (f32[256,1024]{1,0:T(8,128)S(1)}, f32[2,16,64,256]{3,2,1,0:T(8,128)}) custom-call(s32[8]{0:T(128)S(1)} %pad_add_fusion.ints_ref, f32[256,1024]{1,0:T(8,128)S(1)} %get-tuple-element.63.refs_0_, bf16[256,1024]{1,0:T(8,128)(2,1)S(1)} %collective-permute-done.12.refs_1_, f32[2,16,256]{2,1,0:T(8,128)S(1)} %shard_map.204.refs_1_.refs_2_, ...), custom_call_target="tpu_custom_call" | custom-call | flops 1000000 | bytes 10000 | tf_op jit(solution)/shard_map/pallas_call | solution.py:440
  93.1 1.5 %multiply_reduce_fusion = (f32[256]{0:T(256)S(1)}, f32[256,1024]{1,0:T(8,128)S(1)}) fusion(f32[256,1024]{1,0:T(8,128)S(1)} %get-tuple-element.69, f32[256,1024]{1,0:T(8,128)S(1)} %copy-done.4, bf16[256,1024]{1,0:T(8,128)(2,1)} %collective-permute-done.15), kind=kLoop, calls=%fused_computation.23 | loop fusion | flops 2883328 | bytes 3671040 | tf_op jit(solution)/shard_map/reduce_sum | solution.py:617
  (91 shorter events, 13.7 us)
Async XLA Ops:
  0.6 16.8 %collective-permute-start = (bf16[256,512]{1,0:T(8,128)(2,1)}, bf16[256,512]{1,0:T(8,128)(2,1)S(1)}, u32[]{:S(2)}, u32[]{:S(2)}) collective-permute-start(bf16[256,512]{1,0:T(8,128)(2,1)} %param.20), channel_id=1, source_target_pairs={{1,0},{3,2},{5,4},{7,6},{9,8},{11,10},{13,12},{15,14},{16,17},{18,... | collective-permute-start | bytes 786440 | tf_op jit(solution)/shard_map/ppermute | solution.py:94
  1.9 15.5 %collective-permute-start.1 = (bf16[256,512]{1,0:T(8,128)(2,1)}, bf16[256,512]{1,0:T(8,128)(2,1)S(1)}, u32[]{:S(2)}, u32[]{:S(2)}) collective-permute-start(bf16[256,512]{1,0:T(8,128)(2,1)} %param.20), channel_id=1, source_target_pairs={{1,16},{3,18},{5,20},{7,22},{9,24},{11,26},{13,28},{15,30},{16,1},... | collective-permute-start | bytes 786440 | tf_op jit(solution)/shard_map/ppermute | solution.py:93
  4.9 19.1 %copy-start.19 = (s32[2]{0:T(128)S(1)}, s32[2]{0:T(128)}, u32[]{:S(2)}) copy-start(s32[2]{0:T(128)} %param.33) | copy-start | bytes 28
  4.9 19.1 %copy-start.15 = (f32[16]{0:T(128)S(1)}, f32[16]{0:T(128)}, u32[]{:S(2)}) copy-start(f32[16]{0:T(128)} %param.25) | copy-start | bytes 196
  4.9 19.1 %copy-start.16 = (f32[16]{0:T(128)S(1)}, f32[16]{0:T(128)}, u32[]{:S(2)}) copy-start(f32[16]{0:T(128)} %param.24) | copy-start | bytes 196
  4.9 19.2 %copy-start.14 = (f32[16]{0:T(128)S(1)}, f32[16]{0:T(128)}, u32[]{:S(2)}) copy-start(f32[16]{0:T(128)} %param.26) | copy-start | bytes 196
  4.9 19.3 %copy-start.7 = (bf16[4096,16]{0,1:T(8,128)(2,1)S(1)}, bf16[4096,16]{0,1:T(8,128)(2,1)}, u32[]{:S(2)}) copy-start(bf16[4096,16]{0,1:T(8,128)(2,1)} %param.22) | copy-start | bytes 393220
  7.1 18.4 %copy-start.12 = (s32[4]{0:T(128)S(1)}, s32[4]{0:T(128)}, u32[]{:S(2)}) copy-start(s32[4]{0:T(128)} %param.34) | copy-start | bytes 52
  7.1 16.1 %collective-permute-start.2 = (bf16[256,512]{1,0:T(8,128)(2,1)S(1)}, bf16[256,512]{1,0:T(8,128)(2,1)}, u32[]{:S(2)}, u32[]{:S(2)}) collective-permute-start(bf16[256,512]{1,0:T(8,128)(2,1)S(1)} %copy-done.6), channel_id=1, source_target_pairs={{0,16},{2,18},{4,20},{6,22},{8,24},{10,26},{12,28},{14,30},{17,1},... | collective-permute-start | bytes 786440 | tf_op jit(solution)/shard_map/ppermute | solution.py:99
  17.2 26.7 %collective-permute-start.10 = (bf16[2,1040,256]{2,1,0:T(8,128)(2,1)S(1)}, bf16[2,1040,256]{2,1,0:T(8,128)(2,1)S(1)}, u32[]{:S(2)}, u32[]{:S(2)}) collective-permute-start(bf16[2,1040,256]{2,1,0:T(8,128)(2,1)S(1)} %shard_map.203), channel_id=1, source_target_pairs={{0,1},{1,0},{2,3},{3,2},{4,5},{5,4},{6,7},{7,6},{8,9},{9,8},{10,11... | collective-permute-start | bytes 3194888 | tf_op jit(solution)/shard_map/ppermute | solution.py:40
  17.5 23.7 %copy-start.20 = (s32[8]{0:T(128)S(1)}, s32[8]{0:T(128)}, u32[]{:S(2)}) copy-start(s32[8]{0:T(128)} %constant.97.clone) | copy-start | bytes 100
  17.5 10.1 %collective-permute-start.3 = (bf16[256,512]{1,0:T(8,128)(2,1)S(1)}, bf16[256,512]{1,0:T(8,128)(2,1)}, u32[]{:S(2)}, u32[]{:S(2)}) collective-permute-start(bf16[256,512]{1,0:T(8,128)(2,1)S(1)} %broadcast_select_fusion.1), channel_id=1, source_target_pairs={{0,8},{8,0},{2,10},{10,2},{4,12},{12,4},{6,14},{14,6},{16,24},{24,... | collective-permute-start | bytes 786440 | tf_op jit(solution)/shard_map/ppermute | solution.py:35
  19.2 8.4 %collective-permute-start.7 = (bf16[256,512]{1,0:T(8,128)(2,1)S(1)}, bf16[256,512]{1,0:T(8,128)(2,1)}, u32[]{:S(2)}, u32[]{:S(2)}) collective-permute-start(bf16[256,512]{1,0:T(8,128)(2,1)S(1)} %broadcast_select_fusion.1), channel_id=1, source_target_pairs={{0,4},{4,0},{2,6},{6,2},{8,12},{12,8},{10,14},{14,10},{16,20},{20,... | collective-permute-start | bytes 786440 | tf_op jit(solution)/shard_map/ppermute | solution.py:35
  28.7 15.1 %collective-permute-start.8 = (bf16[3,256,512]{2,1,0:T(8,128)(2,1)S(1)}, bf16[3,256,512]{2,1,0:T(8,128)(2,1)}, u32[]{:S(2)}, u32[]{:S(2)}) collective-permute-start(bf16[3,256,512]{2,1,0:T(8,128)(2,1)S(1)} %pad_maximum_fusion.7.refs_0_), channel_id=1, source_target_pairs={{0,2},{2,0},{4,6},{6,4},{8,10},{10,8},{12,14},{14,12},{16,18},{18,... | collective-permute-start | bytes 2359304 | tf_op jit(solution)/shard_map/ppermute | solution.py:35
  28.8 10.9 %collective-permute-start.4 = (bf16[256,512]{1,0:T(8,128)(2,1)}, bf16[256,512]{1,0:T(8,128)(2,1)}, u32[]{:S(2)}, u32[]{:S(2)}) collective-permute-start(bf16[256,512]{1,0:T(8,128)(2,1)} %broadcast_select_fusion), channel_id=1, source_target_pairs={{0,8},{8,0},{2,10},{10,2},{4,12},{12,4},{6,14},{14,6},{16,24},{24,... | collective-permute-start | bytes 786440 | tf_op jit(solution)/shard_map/ppermute | solution.py:35
  32.5 8.6 %collective-permute-start.5 = (bf16[256,512]{1,0:T(8,128)(2,1)}, bf16[256,512]{1,0:T(8,128)(2,1)S(1)}, u32[]{:S(2)}, u32[]{:S(2)}) collective-permute-start(bf16[256,512]{1,0:T(8,128)(2,1)} %collective-permute-done.3), channel_id=1, source_target_pairs={{0,4},{4,0},{2,6},{6,2},{8,12},{12,8},{10,14},{14,10},{16,20},{20,... | collective-permute-start | bytes 786440 | tf_op jit(solution)/shard_map/ppermute | solution.py:35
  41.1 2.7 %collective-permute-start.9 = (bf16[1,256,512]{2,1,0:T(8,128)(2,1)S(1)}, bf16[1,256,512]{2,1,0:T(8,128)(2,1)S(1)}, u32[]{:S(2)}, u32[]{:S(2)}) collective-permute-start(bf16[1,256,512]{2,1,0:T(8,128)(2,1)S(1)} %bitcast.40), channel_id=1, source_target_pairs={{0,2},{2,0},{4,6},{6,4},{8,10},{10,8},{12,14},{14,12},{16,18},{18,... | collective-permute-start | bytes 786440 | tf_op jit(solution)/shard_map/ppermute | solution.py:35
  42.2 17.3 %collective-permute-start.6 = (bf16[2,256,512]{2,1,0:T(8,128)(2,1)S(1)}, bf16[2,256,512]{2,1,0:T(8,128)(2,1)S(1)}, u32[]{:S(2)}, u32[]{:S(2)}) collective-permute-start(bf16[2,256,512]{2,1,0:T(8,128)(2,1)S(1)} %pad_maximum_fusion.8), channel_id=1, source_target_pairs={{0,4},{4,0},{2,6},{6,2},{8,12},{12,8},{10,14},{14,10},{16,20},{20,... | collective-permute-start | bytes 1572872 | tf_op jit(solution)/shard_map/ppermute | solution.py:35
  59.6 6.9 %collective-permute-start.11 = (bf16[4,256,512]{2,1,0:T(8,128)(2,1)S(1)}, bf16[4,256,512]{2,1,0:T(8,128)(2,1)S(1)}, u32[]{:S(2)}, u32[]{:S(2)}) collective-permute-start(bf16[4,256,512]{2,1,0:T(8,128)(2,1)S(1)} %constant_dynamic-update-slice_fusion.refs_0_), channel_id=1, source_target_pairs={{0,2},{2,0},{4,6},{6,4},{8,10},{10,8},{12,14},{14,12},{16,18},{18,... | collective-permute-start | bytes 3145736 | tf_op jit(solution)/shard_map/ppermute | solution.py:35
  59.8 22.0 %collective-permute-start.13 = (bf16[256,272]{1,0:T(8,128)(2,1)S(1)}, bf16[256,272]{1,0:T(8,128)(2,1)S(1)}, u32[]{:S(2)}, u32[]{:S(2)}) collective-permute-start(bf16[256,272]{1,0:T(8,128)(2,1)S(1)} %fusion.23), channel_id=1, source_target_pairs={{0,1},{1,0},{2,3},{3,2},{4,5},{5,4},{6,7},{7,6},{8,9},{9,8},{10,11... | collective-permute-start | bytes 417800 | tf_op jit(solution)/shard_map/ppermute | solution.py:40
  64.5 19.1 %collective-permute-start.12 = (bf16[256,1024]{1,0:T(8,128)(2,1)}, bf16[256,1024]{1,0:T(8,128)(2,1)S(1)}, u32[]{:S(2)}, u32[]{:S(2)}) collective-permute-start(bf16[256,1024]{1,0:T(8,128)(2,1)} %get-tuple-element.58), channel_id=1, source_target_pairs={{0,1},{1,0},{2,3},{3,2},{4,5},{5,4},{6,7},{7,6},{8,9},{9,8},{10,11... | collective-permute-start | bytes 1572872 | tf_op jit(solution)/shard_map/ppermute | solution.py:40
  64.5 28.6 %collective-permute-start.15 = (bf16[256,1024]{1,0:T(8,128)(2,1)}, bf16[256,1024]{1,0:T(8,128)(2,1)}, u32[]{:S(2)}, u32[]{:S(2)}) collective-permute-start(bf16[256,1024]{1,0:T(8,128)(2,1)} %get-tuple-element.59), channel_id=1, source_target_pairs={{0,1},{1,0},{2,3},{3,2},{4,5},{5,4},{6,7},{7,6},{8,9},{9,8},{10,11... | collective-permute-start | bytes 1572872 | tf_op jit(solution)/shard_map/ppermute | solution.py:40
  83.5 1.4 %collective-permute-start.14 = (bf16[256,256]{1,0:T(8,128)(2,1)S(1)}, bf16[256,256]{1,0:T(8,128)(2,1)S(1)}, u32[]{:S(2)}, u32[]{:S(2)}) collective-permute-start(bf16[256,256]{1,0:T(8,128)(2,1)S(1)} %get-tuple-element.65), channel_id=1, source_target_pairs={{0,2},{2,0},{4,6},{6,4},{8,10},{10,8},{12,14},{14,12},{16,18},{18,... | collective-permute-start | bytes 393224 | tf_op jit(solution)/shard_map/ppermute | solution.py:35
  94.6 1.2 %collective-permute-start.16 = (f32[256]{0:T(256)S(1)}, f32[256]{0:T(256)S(1)}, u32[]{:S(2)}, u32[]{:S(2)}) collective-permute-start(f32[256]{0:T(256)S(1)} %get-tuple-element.72), channel_id=1, source_target_pairs={{0,2},{2,0},{4,6},{6,4},{8,10},{10,8},{12,14},{14,12},{16,18},{18,... | collective-permute-start | bytes 3080 | tf_op jit(solution)/shard_map/ppermute | solution.py:35
  (14 other events, 150.3 us)

commit v17 on v15

--- a/solution.py
+++ b/solution.py
@@ -87,8 +87,8 @@
 def near_blocks(x_in):
     axes = ("wide", "req")
     first, second = spread_routes()
+    second = lax.ppermute(x_in, axes, second)
     first = lax.ppermute(x_in, axes, first)
-    second = lax.ppermute(x_in, axes, second)
     near = lax.axis_index("wide") // 8 == lax.axis_index("req")
     return jnp.where(near, x_in, first), jnp.where(near, first, second)
 
@@ -546,14 +546,14 @@
         own_z = partner_2(own_block, "wide", 2)
         near_three = jnp.stack([block, along_z, along_x])
         core_three = partner_2(near_three, "wide", 0)
-        both = after(both[None], own_z, w_step, const_x, const_bc, ints, own_rows)
+        both = after(both[None], w_step, const_x, const_bc, ints, own_rows)
         core_both = partner_2(both, "wide", 0)
-        own_pair = after(jnp.stack([own_block, own_z]), both)
-        own_got = partner_2(own_pair, "wide", 1)
         core_both = after(core_both, *got_states)
         theirs = quad_arrange(
             [near_three, both, core_three, core_both], [0, 4, 2, 6, 1, 5, 3, 7]
         )
+        own_pair = after(jnp.stack([own_block, own_z]), theirs)
+        own_got = partner_2(own_pair, "wide", 1)
         features = [own_got, theirs]
     else:
         features = features_in_general(x_in)

time: 92.9 us -> 98.1 us (1.056)
  waiting for transfers between devices: 14.8 us -> 18 us
  starting transfers between devices: 24.1 us -> 25.1 us
    ppermute x4, waiting for transfers between devices: 1.3 us -> 8.52 us  [shift_req(): lax.ppermute(block, 'req', [(i, (i + step) % count) for i in range(count)])]
    ppermute x10, waiting for transfers between devices: 13.5 us -> 8.92 us  [partner_2(): return lax.ppermute(block, axis, route)]
    ppermute x10, starting transfers between devices: 8.9 us -> 11.9 us  [partner_2(): return lax.ppermute(block, axis, route)]
    ppermute x4, starting transfers between devices: 10.4 us -> 8.45 us  [shift_req(): lax.ppermute(block, 'req', [(i, (i + step) % count) for i in range(count)])]
    unnamed x43 -> x47, local copies, waits for them, and re-layouts: 1.64 us -> 2.36 us
  transfers between devices with their start and end apart: 16 -> 16, of which waited for: 6 -> 7; matrix products, arithmetic and copies ran while one was open for 37% -> 33% of each run, Pallas kernels for 16% -> 14%
where the time goes in v17:
time: 98.1 us; the launch traced here: 97.5 us
  matrix products  26 us (27%)
  starting transfers between devices  25.1 us (26%)
  waiting for transfers between devices  18 us (18%)
  Pallas kernels  14.6 us (15%)
  other arithmetic  6.48 us (7%)
  local copies, waits for them, and re-layouts  6.21 us (6%)
  between operations  1.09 us (1%)
    dot_general x2, matrix products, project(): high = jnp.einsum('td,dkc->ktc', block, w_xz, preferred_element_type=F32)  23.5 us
    ppermute x10, starting transfers between devices, partner_2(): return lax.ppermute(block, axis, route)  11.9 us
    ppermute x10, waiting for transfers between devices, partner_2(): return lax.ppermute(block, axis, route)  8.92 us
    ppermute x4, waiting for transfers between devices, shift_req(): lax.ppermute(block, 'req', [(i, (i + step) % count) for i in range(count)])  8.52 us
    ppermute x4, starting transfers between devices, shift_req(): lax.ppermute(block, 'req', [(i, (i + step) % count) for i in range(count)])  8.45 us
    pallas_call x1, Pallas kernels, mixer(): pl.pallas_call(functools.partial(mixer_kernel, count_req, len(got), per_p...  8.07 us
    ppermute x1, starting transfers between devices, near_blocks(): first = lax.ppermute(x_in, axes, first)  4.09 us
    dot_general x2, matrix products, project(): low = jnp.dot(block, w_map, preferred_element_type=F32).astype(BF16)  2.51 us
  transfers between devices with their start and end apart: 16, of which 7 were waited for; matrix products, arithmetic and copies ran while one was open for 33% of the time, Pallas kernels for 14%

profile of v17, /device:TPU:0, one launch (start us, length us, event | category | flops | bytes accessed | tf_op | source)
XLA Modules:
  0.0 97.5 jit_solution(1778979990797210549)
XLA Ops:
  0.6 4.1 %collective-permute-start = (bf16[256,512]{1,0:T(8,128)(2,1)}, bf16[256,512]{1,0:T(8,128)(2,1)S(1)}, u32[]{:S(2)}, u32[]{:S(2)}) collective-permute-start(bf16[256,512]{1,0:T(8,128)(2,1)} %param.20), channel_id=1, source_target_pairs={{0,16},{1,0},{2,18},{3,2},{4,20},{5,4},{6,22},{7,6},{8,24},{9,8},{... | collective-permute-start | bytes 786440 | tf_op jit(solution)/shard_map/ppermute | solution.py:91
  7.7 2.2 %shard_map.203 = bf16[2,1040,256]{2,1,0:T(8,128)(2,1)S(1)} custom-call(s32[2]{0:T(128)S(1)} %subtract_clamp_fusion.1.slots_ref, f32[8,16,64,256]{3,2,1,0:T(8,128)} %refs_10_.1, bf16[3,8,1024]{2,1,0:T(8,128)(2,1)S(1)} %bitcast.42, bf16[3,8,256]{2,1,0:T(8,128)(2,1)S(1)} %bitcast.44), custom_call_target="tpu_custom_call" | custom-call | bytes 3145728 | tf_op jit(solution)/shard_map/pallas_call | solution.py:274
  11.4 1.5 %collective-permute-start.4 = (bf16[256,512]{1,0:T(8,128)(2,1)S(1)}, bf16[256,512]{1,0:T(8,128)(2,1)S(1)}, u32[]{:S(2)}, u32[]{:S(2)}) collective-permute-start(bf16[256,512]{1,0:T(8,128)(2,1)S(1)} %get-tuple-element.36), channel_id=1, source_target_pairs={{0,4},{4,0},{2,6},{6,2},{8,12},{12,8},{10,14},{14,10},{16,20},{20,... | collective-permute-start | bytes 786440 | tf_op jit(solution)/shard_map/ppermute | solution.py:35
  12.9 7.0 %collective-permute-start.2 = (bf16[256,512]{1,0:T(8,128)(2,1)S(1)}, bf16[256,512]{1,0:T(8,128)(2,1)S(1)}, u32[]{:S(2)}, u32[]{:S(2)}) collective-permute-start(bf16[256,512]{1,0:T(8,128)(2,1)S(1)} %get-tuple-element.36), channel_id=1, source_target_pairs={{0,8},{8,0},{2,10},{10,2},{4,12},{12,4},{6,14},{14,6},{16,24},{24,... | collective-permute-start | bytes 786440 | tf_op jit(solution)/shard_map/ppermute | solution.py:35
  19.9 4.6 %collective-permute-start.8 = (bf16[2,1040,256]{2,1,0:T(8,128)(2,1)S(1)}, bf16[2,1040,256]{2,1,0:T(8,128)(2,1)S(1)}, u32[]{:S(2)}, u32[]{:S(2)}) collective-permute-start(bf16[2,1040,256]{2,1,0:T(8,128)(2,1)S(1)} %shard_map.203), channel_id=1, source_target_pairs={{0,1},{1,0},{2,3},{3,2},{4,5},{5,4},{6,7},{7,6},{8,9},{9,8},{10,11... | collective-permute-start | bytes 3194888 | tf_op jit(solution)/shard_map/ppermute | solution.py:40
  24.6 1.6 %collective-permute-done.2 = bf16[256,512]{1,0:T(8,128)(2,1)S(1)} collective-permute-done((bf16[256,512]{1,0:T(8,128)(2,1)S(1)}, bf16[256,512]{1,0:T(8,128)(2,1)S(1)}, u32[]{:S(2)}, u32[]{:S(2)}) %collective-permute-start.2) | collective-permute-done | bytes 262176 | tf_op jit(solution)/shard_map/ppermute | solution.py:35
  26.8 1.1 %pad_maximum_fusion.7.refs_0_ = bf16[3,256,512]{2,1,0:T(8,128)(2,1)S(1)} fusion(bf16[1,256,512]{2,1,0:T(8,128)(2,1)} %bitcast.49, bf16[1,256,512]{2,1,0:T(8,128)(2,1)} %bitcast.48, bf16[1,256,512]{2,1,0:T(8,128)(2,1)S(1)} %bitcast.47), kind=kLoop, calls=%fused_computation.25 | loop fusion | flops 786432 | bytes 1572864 | tf_op jit(solution)/shard_map/stack | solution.py:547
  29.3 1.3 %collective-permute-start.3 = (bf16[256,512]{1,0:T(8,128)(2,1)}, bf16[256,512]{1,0:T(8,128)(2,1)}, u32[]{:S(2)}, u32[]{:S(2)}) collective-permute-start(bf16[256,512]{1,0:T(8,128)(2,1)} %get-tuple-element.40), channel_id=1, source_target_pairs={{0,8},{8,0},{2,10},{10,2},{4,12},{12,4},{6,14},{14,6},{16,24},{24,... | collective-permute-start | bytes 786440 | tf_op jit(solution)/shard_map/ppermute | solution.py:35
  30.9 1.3 %copy.22 = bf16[4096,16]{1,0:T(8,128)(2,1)} copy(bf16[4096,16]{0,1:T(8,128)(2,1)S(1)} %copy-done.9) | data formatting | bytes 262144 | tf_op jit(solution)/shard_map/optimization_barrier | solution.py:514
  33.0 4.1 %collective-permute-done.5 = bf16[256,512]{1,0:T(8,128)(2,1)S(1)} collective-permute-done((bf16[256,512]{1,0:T(8,128)(2,1)}, bf16[256,512]{1,0:T(8,128)(2,1)S(1)}, u32[]{:S(2)}, u32[]{:S(2)}) %collective-permute-start.5) | collective-permute-done | bytes 262176 | tf_op jit(solution)/shard_map/ppermute | solution.py:35
  38.1 1.1 %pad_maximum_fusion.8 = bf16[2,256,512]{2,1,0:T(8,128)(2,1)S(1)} fusion(bf16[1,256,512]{2,1,0:T(8,128)(2,1)} %bitcast.4, bf16[1,256,512]{2,1,0:T(8,128)(2,1)} %bitcast.46), kind=kLoop, calls=%fused_computation.28 | loop fusion | flops 262144 | bytes 1048576 | tf_op jit(solution)/shard_map/stack | solution.py:555
  39.2 8.5 %collective-permute-done.8.refs_2_.refs_3_.refs_11_ = bf16[2,1040,256]{2,1,0:T(8,128)(2,1)S(1)} collective-permute-done((bf16[2,1040,256]{2,1,0:T(8,128)(2,1)S(1)}, bf16[2,1040,256]{2,1,0:T(8,128)(2,1)S(1)}, u32[]{:S(2)}, u32[]{:S(2)}) %collective-permute-start.8) | collective-permute-done | bytes 1064992 | tf_op jit(solution)/shard_map/ppermute | solution.py:40
  47.7 1.3 %shard_map.205 = bf16[256,4096]{1,0:T(8,128)(2,1)S(1)} custom-call(s32[8]{0:T(128)S(1)} %broadcast_xor_fusion.places_ref, bf16[3,256,512]{2,1,0:T(8,128)(2,1)S(1)} %pad_maximum_fusion.7.refs_0_, bf16[1,256,512]{2,1,0:T(8,128)(2,1)S(1)} %bitcast.41, bf16[3,256,512]{2,1,0:T(8,128)(2,1)} %collective-permute-done.6.refs_2_, ...), custom_call_target="tpu_custom_call" | custom-call | flops 1000000 | bytes 10000 | tf_op jit(solution)/shard_map/pallas_call | solution.py:72
  49.0 1.3 %fusion.23 = bf16[256,272]{1,0:T(8,128)(2,1)S(1)} fusion(bf16[256,4096]{1,0:T(8,128)(2,1)S(1)} %shard_map.205, bf16[4096,16]{1,0:T(8,128)(2,1)S(1)} %copy-done.5, bf16[4096,256]{1,0:T(8,128)(2,1)S(1)} %copy-done.20), kind=kOutput, calls=%fused_computation.14 | convolution fusion | flops 574951424 | bytes 4464640 | tf_op jit(solution)/shard_map/dot_general | solution.py:563
  50.9 11.3 %fusion.18 = bf16[2,256,1024]{2,1,0:T(8,128)(2,1)S(1)} fusion(bf16[4096,2,1024]{2,1,0:T(2,128)(2,1)} %param.21, bf16[256,4096]{1,0:T(8,128)(2,1)S(1)} %shard_map.205), kind=kOutput, calls=%fused_computation.11 | convolution fusion | flops 4295491584 | bytes 19922944 | tf_op jit(solution)/shard_map/td,dkc->ktc/dot_general | solution.py:565
  63.4 1.8 %collective-permute-start.12 = (bf16[256,272]{1,0:T(8,128)(2,1)S(1)}, bf16[256,272]{1,0:T(8,128)(2,1)S(1)}, u32[]{:S(2)}, u32[]{:S(2)}) collective-permute-start(bf16[256,272]{1,0:T(8,128)(2,1)S(1)} %fusion.23), channel_id=1, source_target_pairs={{0,1},{1,0},{2,3},{3,2},{4,5},{5,4},{6,7},{7,6},{8,9},{9,8},{10,11... | collective-permute-start | bytes 417800 | tf_op jit(solution)/shard_map/ppermute | solution.py:40
  65.4 1.7 %collective-permute-start.14 = (bf16[256,1024]{1,0:T(8,128)(2,1)}, bf16[256,1024]{1,0:T(8,128)(2,1)}, u32[]{:S(2)}, u32[]{:S(2)}) collective-permute-start(bf16[256,1024]{1,0:T(8,128)(2,1)} %get-tuple-element.57), channel_id=1, source_target_pairs={{0,1},{1,0},{2,3},{3,2},{4,5},{5,4},{6,7},{7,6},{8,9},{9,8},{10,11... | collective-permute-start | bytes 1572872 | tf_op jit(solution)/shard_map/ppermute | solution.py:40
  67.9 1.3 %fusion.24.own_ref = bf16[256,272]{1,0:T(8,128)(2,1)S(1)} fusion(bf16[256,4096]{1,0:T(8,128)(2,1)S(1)} %shard_map.206, bf16[4096,16]{1,0:T(8,128)(2,1)S(1)} %copy-done.5, bf16[4096,256]{1,0:T(8,128)(2,1)S(1)} %copy-done.20), kind=kOutput, calls=%fused_computation.15 | convolution fusion | flops 574951424 | bytes 4464640 | tf_op jit(solution)/shard_map/dot_general | solution.py:563
  69.2 12.2 %fusion.8 = f32[2,256,1024]{2,1,0:T(8,128)S(1)} fusion(bf16[4096,2,1024]{2,1,0:T(2,128)(2,1)} %param.21, bf16[256,4096]{1,0:T(8,128)(2,1)S(1)} %shard_map.206), kind=kOutput, calls=%fused_computation.9 | convolution fusion | flops 4294967296 | bytes 20971520 | tf_op jit(solution)/shard_map/td,dkc->ktc/dot_general | solution.py:565
  81.4 1.1 %slice_bitcast_fusion = (f32[256,1024]{1,0:T(8,128)}, f32[256,1024]{1,0:T(8,128)S(1)}) fusion(f32[2,256,1024]{2,1,0:T(8,128)S(1)} %fusion.8), kind=kLoop, calls=%fused_computation.20 | loop fusion | bytes 4194304 | tf_op jit(solution)/shard_map/squeeze | solution.py:566
  82.5 1.7 %shard_map.207 = (bf16[256,256]{1,0:T(8,128)(2,1)S(1)}, f32[4,12,256]{2,1,0:T(8,128)S(1)}, f32[8,16]{1,0:T(8,128)S(1)}) custom-call(s32[8]{0:T(128)S(1)} %pad_add_fusion.ints_ref, bf16[256,272]{1,0:T(8,128)(2,1)S(1)} %fusion.24.own_ref, bf16[256,272]{1,0:T(8,128)(2,1)S(1)} %collective-permute-done.12.refs_0_, f32[2,16,256]{2,1,0:T(8,128)S(1)} %shard_map.204.refs_1_.refs_2_, ...), custom_call_target="tpu_custom_call" | custom-call | flops 1000000 | bytes 10000 | tf_op jit(solution)/shard_map/pallas_call | solution.py:221
  84.3 1.3 %collective-permute-done.13 = bf16[256,256]{1,0:T(8,128)(2,1)S(1)} collective-permute-done((bf16[256,256]{1,0:T(8,128)(2,1)S(1)}, bf16[256,256]{1,0:T(8,128)(2,1)S(1)}, u32[]{:S(2)}, u32[]{:S(2)}) %collective-permute-start.13) | collective-permute-done | bytes 131104 | tf_op jit(solution)/shard_map/ppermute | solution.py:35
  85.8 8.1 %shard_map.208 = (f32[256,1024]{1,0:T(8,128)S(1)}, f32[2,16,64,256]{3,2,1,0:T(8,128)}) custom-call(s32[8]{0:T(128)S(1)} %pad_add_fusion.ints_ref, f32[256,1024]{1,0:T(8,128)S(1)} %get-tuple-element.61.refs_0_, bf16[256,1024]{1,0:T(8,128)(2,1)S(1)} %collective-permute-done.11.refs_1_, f32[2,16,256]{2,1,0:T(8,128)S(1)} %shard_map.204.refs_1_.refs_2_, ...), custom_call_target="tpu_custom_call" | custom-call | flops 1000000 | bytes 10000 | tf_op jit(solution)/shard_map/pallas_call | solution.py:433
  93.8 1.5 %multiply_reduce_fusion = (f32[256]{0:T(256)S(1)}, f32[256,1024]{1,0:T(8,128)S(1)}) fusion(f32[256,1024]{1,0:T(8,128)S(1)} %get-tuple-element.67, f32[256,1024]{1,0:T(8,128)S(1)} %copy-done.4, bf16[256,1024]{1,0:T(8,128)(2,1)} %collective-permute-done.14), kind=kLoop, calls=%fused_computation.23 | loop fusion | flops 2883328 | bytes 3671040 | tf_op jit(solution)/shard_map/reduce_sum | solution.py:609
  (92 shorter events, 13.4 us)
Async XLA Ops:
  0.6 10.0 %collective-permute-start = (bf16[256,512]{1,0:T(8,128)(2,1)}, bf16[256,512]{1,0:T(8,128)(2,1)S(1)}, u32[]{:S(2)}, u32[]{:S(2)}) collective-permute-start(bf16[256,512]{1,0:T(8,128)(2,1)} %param.20), channel_id=1, source_target_pairs={{0,16},{1,0},{2,18},{3,2},{4,20},{5,4},{6,22},{7,6},{8,24},{9,8},{... | collective-permute-start | bytes 786440 | tf_op jit(solution)/shard_map/ppermute | solution.py:91
  4.7 5.9 %collective-permute-start.1 = (bf16[256,512]{1,0:T(8,128)(2,1)}, bf16[256,512]{1,0:T(8,128)(2,1)S(1)}, u32[]{:S(2)}, u32[]{:S(2)}) collective-permute-start(bf16[256,512]{1,0:T(8,128)(2,1)} %param.20), channel_id=1, source_target_pairs={{1,16},{3,18},{5,20},{7,22},{9,24},{11,26},{13,28},{15,30},{16,1},... | collective-permute-start | bytes 786440 | tf_op jit(solution)/shard_map/ppermute | solution.py:90
  10.0 22.3 %copy-start.13 = (f32[4,256]{1,0:T(4,128)S(1)}, f32[4,256]{1,0:T(4,128)}, u32[]{:S(2)}) copy-start(f32[4,256]{1,0:T(4,128)} %param.29) | copy-start | bytes 12292
  10.0 22.3 %copy-start.15 = (f32[256]{0:T(256)S(1)}, f32[256]{0:T(256)}, u32[]{:S(2)}) copy-start(f32[256]{0:T(256)} %param.30) | copy-start | bytes 3076
  10.0 22.3 %copy-start.10 = (f32[1024]{0:T(1024)S(1)}, f32[1024]{0:T(1024)}, u32[]{:S(2)}) copy-start(f32[1024]{0:T(1024)} %param.31) | copy-start | bytes 12292
  10.0 22.3 %copy-start.11 = (f32[4,1024]{1,0:T(4,128)S(1)}, f32[4,1024]{1,0:T(4,128)}, u32[]{:S(2)}) copy-start(f32[4,1024]{1,0:T(4,128)} %param.27) | copy-start | bytes 49156
  10.0 22.3 %copy-start.12 = (f32[1024]{0:T(1024)S(1)}, f32[1024]{0:T(1024)}, u32[]{:S(2)}) copy-start(f32[1024]{0:T(1024)} %param.28) | copy-start | bytes 12292
  10.0 22.3 %copy-start.1 = (bf16[8,3,1024]{2,0,1:T(8,128)(2,1)S(1)}, bf16[8,3,1024]{2,0,1:T(8,128)(2,1)}, u32[]{:S(2)}) copy-start(bf16[8,3,1024]{2,0,1:T(8,128)(2,1)} %param.36) | copy-start | bytes 147460
  10.0 22.3 %copy-start.3 = (bf16[8,3,256]{2,0,1:T(8,128)(2,1)S(1)}, bf16[8,3,256]{2,0,1:T(8,128)(2,1)}, u32[]{:S(2)}) copy-start(bf16[8,3,256]{2,0,1:T(8,128)(2,1)} %param.37) | copy-start | bytes 36868
  10.0 27.1 %copy-start.22 = (s32[8]{0:T(128)S(1)}, s32[8]{0:T(128)}, u32[]{:S(2)}) copy-start(s32[8]{0:T(128)} %constant.95.clone) | copy-start | bytes 100
  11.4 13.2 %collective-permute-start.4 = (bf16[256,512]{1,0:T(8,128)(2,1)S(1)}, bf16[256,512]{1,0:T(8,128)(2,1)S(1)}, u32[]{:S(2)}, u32[]{:S(2)}) collective-permute-start(bf16[256,512]{1,0:T(8,128)(2,1)S(1)} %get-tuple-element.36), channel_id=1, source_target_pairs={{0,4},{4,0},{2,6},{6,2},{8,12},{12,8},{10,14},{14,10},{16,20},{20,... | collective-permute-start | bytes 786440 | tf_op jit(solution)/shard_map/ppermute | solution.py:35
  12.9 13.2 %collective-permute-start.2 = (bf16[256,512]{1,0:T(8,128)(2,1)S(1)}, bf16[256,512]{1,0:T(8,128)(2,1)S(1)}, u32[]{:S(2)}, u32[]{:S(2)}) collective-permute-start(bf16[256,512]{1,0:T(8,128)(2,1)S(1)} %get-tuple-element.36), channel_id=1, source_target_pairs={{0,8},{8,0},{2,10},{10,2},{4,12},{12,4},{6,14},{14,6},{16,24},{24,... | collective-permute-start | bytes 786440 | tf_op jit(solution)/shard_map/ppermute | solution.py:35
  19.9 27.8 %collective-permute-start.8 = (bf16[2,1040,256]{2,1,0:T(8,128)(2,1)S(1)}, bf16[2,1040,256]{2,1,0:T(8,128)(2,1)S(1)}, u32[]{:S(2)}, u32[]{:S(2)}) collective-permute-start(bf16[2,1040,256]{2,1,0:T(8,128)(2,1)S(1)} %shard_map.203), channel_id=1, source_target_pairs={{0,1},{1,0},{2,3},{3,2},{4,5},{5,4},{6,7},{7,6},{8,9},{9,8},{10,11... | collective-permute-start | bytes 3194888 | tf_op jit(solution)/shard_map/ppermute | solution.py:40
  28.0 19.7 %collective-permute-start.6 = (bf16[3,256,512]{2,1,0:T(8,128)(2,1)S(1)}, bf16[3,256,512]{2,1,0:T(8,128)(2,1)}, u32[]{:S(2)}, u32[]{:S(2)}) collective-permute-start(bf16[3,256,512]{2,1,0:T(8,128)(2,1)S(1)} %pad_maximum_fusion.7.refs_0_), channel_id=1, source_target_pairs={{0,2},{2,0},{4,6},{6,4},{8,10},{10,8},{12,14},{14,12},{16,18},{18,... | collective-permute-start | bytes 2359304 | tf_op jit(solution)/shard_map/ppermute | solution.py:35
  28.1 9.0 %collective-permute-start.5 = (bf16[256,512]{1,0:T(8,128)(2,1)}, bf16[256,512]{1,0:T(8,128)(2,1)S(1)}, u32[]{:S(2)}, u32[]{:S(2)}) collective-permute-start(bf16[256,512]{1,0:T(8,128)(2,1)} %copy-done.7), channel_id=1, source_target_pairs={{0,4},{4,0},{2,6},{6,2},{8,12},{12,8},{10,14},{14,10},{16,20},{20,... | collective-permute-start | bytes 786440 | tf_op jit(solution)/shard_map/ppermute | solution.py:35
  29.3 8.7 %collective-permute-start.3 = (bf16[256,512]{1,0:T(8,128)(2,1)}, bf16[256,512]{1,0:T(8,128)(2,1)}, u32[]{:S(2)}, u32[]{:S(2)}) collective-permute-start(bf16[256,512]{1,0:T(8,128)(2,1)} %get-tuple-element.40), channel_id=1, source_target_pairs={{0,8},{8,0},{2,10},{10,2},{4,12},{12,4},{6,14},{14,6},{16,24},{24,... | collective-permute-start | bytes 786440 | tf_op jit(solution)/shard_map/ppermute | solution.py:35
  37.1 2.1 %collective-permute-start.7 = (bf16[1,256,512]{2,1,0:T(8,128)(2,1)S(1)}, bf16[1,256,512]{2,1,0:T(8,128)(2,1)S(1)}, u32[]{:S(2)}, u32[]{:S(2)}) collective-permute-start(bf16[1,256,512]{2,1,0:T(8,128)(2,1)S(1)} %bitcast.40), channel_id=1, source_target_pairs={{0,2},{2,0},{4,6},{6,4},{8,10},{10,8},{12,14},{14,12},{16,18},{18,... | collective-permute-start | bytes 786440 | tf_op jit(solution)/shard_map/ppermute | solution.py:35
  50.3 12.9 %collective-permute-start.9 = (bf16[2,256,512]{2,1,0:T(8,128)(2,1)S(1)}, bf16[2,256,512]{2,1,0:T(8,128)(2,1)S(1)}, u32[]{:S(2)}, u32[]{:S(2)}) collective-permute-start(bf16[2,256,512]{2,1,0:T(8,128)(2,1)S(1)} %pad_maximum_fusion.8), channel_id=1, source_target_pairs={{0,4},{4,0},{2,6},{6,2},{8,12},{12,8},{10,14},{14,10},{16,20},{20,... | collective-permute-start | bytes 1572872 | tf_op jit(solution)/shard_map/ppermute | solution.py:35
  63.3 3.9 %collective-permute-start.10 = (bf16[4,256,512]{2,1,0:T(8,128)(2,1)S(1)}, bf16[4,256,512]{2,1,0:T(8,128)(2,1)S(1)}, u32[]{:S(2)}, u32[]{:S(2)}) collective-permute-start(bf16[4,256,512]{2,1,0:T(8,128)(2,1)S(1)} %constant_dynamic-update-slice_fusion.refs_0_), channel_id=1, source_target_pairs={{0,2},{2,0},{4,6},{6,4},{8,10},{10,8},{12,14},{14,12},{16,18},{18,... | collective-permute-start | bytes 3145736 | tf_op jit(solution)/shard_map/ppermute | solution.py:35
  63.4 19.1 %collective-permute-start.12 = (bf16[256,272]{1,0:T(8,128)(2,1)S(1)}, bf16[256,272]{1,0:T(8,128)(2,1)S(1)}, u32[]{:S(2)}, u32[]{:S(2)}) collective-permute-start(bf16[256,272]{1,0:T(8,128)(2,1)S(1)} %fusion.23), channel_id=1, source_target_pairs={{0,1},{1,0},{2,3},{3,2},{4,5},{5,4},{6,7},{7,6},{8,9},{9,8},{10,11... | collective-permute-start | bytes 417800 | tf_op jit(solution)/shard_map/ppermute | solution.py:40
  65.2 19.1 %collective-permute-start.11 = (bf16[256,1024]{1,0:T(8,128)(2,1)}, bf16[256,1024]{1,0:T(8,128)(2,1)S(1)}, u32[]{:S(2)}, u32[]{:S(2)}) collective-permute-start(bf16[256,1024]{1,0:T(8,128)(2,1)} %get-tuple-element.56), channel_id=1, source_target_pairs={{0,1},{1,0},{2,3},{3,2},{4,5},{5,4},{6,7},{7,6},{8,9},{9,8},{10,11... | collective-permute-start | bytes 1572872 | tf_op jit(solution)/shard_map/ppermute | solution.py:40
  65.4 28.4 %collective-permute-start.14 = (bf16[256,1024]{1,0:T(8,128)(2,1)}, bf16[256,1024]{1,0:T(8,128)(2,1)}, u32[]{:S(2)}, u32[]{:S(2)}) collective-permute-start(bf16[256,1024]{1,0:T(8,128)(2,1)} %get-tuple-element.57), channel_id=1, source_target_pairs={{0,1},{1,0},{2,3},{3,2},{4,5},{5,4},{6,7},{7,6},{8,9},{9,8},{10,11... | collective-permute-start | bytes 1572872 | tf_op jit(solution)/shard_map/ppermute | solution.py:40
  84.2 1.4 %collective-permute-start.13 = (bf16[256,256]{1,0:T(8,128)(2,1)S(1)}, bf16[256,256]{1,0:T(8,128)(2,1)S(1)}, u32[]{:S(2)}, u32[]{:S(2)}) collective-permute-start(bf16[256,256]{1,0:T(8,128)(2,1)S(1)} %get-tuple-element.63), channel_id=1, source_target_pairs={{0,2},{2,0},{4,6},{6,4},{8,10},{10,8},{12,14},{14,12},{16,18},{18,... | collective-permute-start | bytes 393224 | tf_op jit(solution)/shard_map/ppermute | solution.py:35
  95.3 1.2 %collective-permute-start.15 = (f32[256]{0:T(256)S(1)}, f32[256]{0:T(256)S(1)}, u32[]{:S(2)}, u32[]{:S(2)}) collective-permute-start(f32[256]{0:T(256)S(1)} %get-tuple-element.70), channel_id=1, source_target_pairs={{0,2},{2,0},{4,6},{6,4},{8,10},{10,8},{12,14},{14,12},{16,18},{18,... | collective-permute-start | bytes 3080 | tf_op jit(solution)/shard_map/ppermute | solution.py:35
  (15 other events, 173.7 us)

commit v18 on v17

--- a/solution.py
+++ b/solution.py
@@ -548,7 +548,6 @@
         core_three = partner_2(near_three, "wide", 0)
         both = after(both[None], w_step, const_x, const_bc, ints, own_rows)
         core_both = partner_2(both, "wide", 0)
-        core_both = after(core_both, *got_states)
         theirs = quad_arrange(
             [near_three, both, core_three, core_both], [0, 4, 2, 6, 1, 5, 3, 7]
         )
@@ -568,7 +567,8 @@
     came = {"map": [], "xr": [], "z": []}
     parts = []
     for step in range(1, req_count):
-        part = lax.optimization_barrier(project(features[step], BF16))
+        part = project(features[step], BF16)
+        part = after(part, *got_states) if direct else lax.optimization_barrier(part)
         for name in came:
             came[name].append(shift_req(part[name], step))
         parts.append(part)

time: 98.1 us -> 93.9 us (0.957)
  waiting for transfers between devices: 18 us -> 9.74 us
  starting transfers between devices: 25.1 us -> 28.5 us
    ppermute x4, waiting for transfers between devices: 8.52 us -> 0.01 us  [shift_req(): lax.ppermute(block, 'req', [(i, (i + step) % count) for i in range(count)])]
    ppermute x4, starting transfers between devices: 8.45 us -> 11.4 us  [shift_req(): lax.ppermute(block, 'req', [(i, (i + step) % count) for i in range(count)])]
  transfers between devices with their start and end apart: 16 -> 16, of which waited for: 7 -> 6; matrix products, arithmetic and copies ran while one was open for 33% -> 36% of each run, Pallas kernels for 14% -> 16%
where the time goes in v18:
time: 93.9 us; the launch traced here: 93.2 us
  starting transfers between devices  28.5 us (30%)
  matrix products  26 us (28%)
  Pallas kernels  14.5 us (15%)
  waiting for transfers between devices  9.74 us (10%)
  local copies, waits for them, and re-layouts  6.85 us (7%)
  other arithmetic  6.48 us (7%)
  between operations  1.09 us (1%)
    dot_general x2, matrix products, project(): high = jnp.einsum('td,dkc->ktc', block, w_xz, preferred_element_type=F32)  23.5 us
    ppermute x10, starting transfers between devices, partner_2(): return lax.ppermute(block, axis, route)  12.4 us
    ppermute x4, starting transfers between devices, shift_req(): lax.ppermute(block, 'req', [(i, (i + step) % count) for i in range(count)])  11.4 us
    ppermute x10, waiting for transfers between devices, partner_2(): return lax.ppermute(block, axis, route)  8.93 us
    pallas_call x1, Pallas kernels, mixer(): pl.pallas_call(functools.partial(mixer_kernel, count_req, len(got), per_p...  8.07 us
    ppermute x1, starting transfers between devices, near_blocks(): first = lax.ppermute(x_in, axes, first)  4.09 us
    unnamed x47, local copies, waits for them, and re-layouts  3 us
    dot_general x2, matrix products, project(): low = jnp.dot(block, w_map, preferred_element_type=F32).astype(BF16)  2.51 us
  transfers between devices with their start and end apart: 16, of which 6 were waited for; matrix products, arithmetic and copies ran while one was open for 36% of the time, Pallas kernels for 16%

profile of v18, /device:TPU:0, one launch (start us, length us, event | category | flops | bytes accessed | tf_op | source)
XLA Modules:
  0.0 93.2 jit_solution(12985861398439121666)
XLA Ops:
  0.6 4.1 %collective-permute-start = (bf16[256,512]{1,0:T(8,128)(2,1)}, bf16[256,512]{1,0:T(8,128)(2,1)S(1)}, u32[]{:S(2)}, u32[]{:S(2)}) collective-permute-start(bf16[256,512]{1,0:T(8,128)(2,1)} %param.20), channel_id=1, source_target_pairs={{0,16},{1,0},{2,18},{3,2},{4,20},{5,4},{6,22},{7,6},{8,24},{9,8},{... | collective-permute-start | bytes 786440 | tf_op jit(solution)/shard_map/ppermute | solution.py:91
  7.7 2.0 %shard_map.203 = bf16[2,1040,256]{2,1,0:T(8,128)(2,1)S(1)} custom-call(s32[2]{0:T(128)S(1)} %subtract_clamp_fusion.1.slots_ref, f32[8,16,64,256]{3,2,1,0:T(8,128)} %refs_10_.1, bf16[3,8,1024]{2,1,0:T(8,128)(2,1)S(1)} %bitcast.42, bf16[3,8,256]{2,1,0:T(8,128)(2,1)S(1)} %bitcast.44), custom_call_target="tpu_custom_call" | custom-call | bytes 3145728 | tf_op jit(solution)/shard_map/pallas_call | solution.py:274
  11.4 1.5 %collective-permute-start.4 = (bf16[256,512]{1,0:T(8,128)(2,1)S(1)}, bf16[256,512]{1,0:T(8,128)(2,1)S(1)}, u32[]{:S(2)}, u32[]{:S(2)}) collective-permute-start(bf16[256,512]{1,0:T(8,128)(2,1)S(1)} %get-tuple-element.35), channel_id=1, source_target_pairs={{0,4},{4,0},{2,6},{6,2},{8,12},{12,8},{10,14},{14,10},{16,20},{20,... | collective-permute-start | bytes 786440 | tf_op jit(solution)/shard_map/ppermute | solution.py:35
  12.9 7.0 %collective-permute-start.2 = (bf16[256,512]{1,0:T(8,128)(2,1)S(1)}, bf16[256,512]{1,0:T(8,128)(2,1)S(1)}, u32[]{:S(2)}, u32[]{:S(2)}) collective-permute-start(bf16[256,512]{1,0:T(8,128)(2,1)S(1)} %get-tuple-element.35), channel_id=1, source_target_pairs={{0,8},{8,0},{2,10},{10,2},{4,12},{12,4},{6,14},{14,6},{16,24},{24,... | collective-permute-start | bytes 786440 | tf_op jit(solution)/shard_map/ppermute | solution.py:35
  19.9 4.6 %collective-permute-start.9 = (bf16[2,1040,256]{2,1,0:T(8,128)(2,1)S(1)}, bf16[2,1040,256]{2,1,0:T(8,128)(2,1)S(1)}, u32[]{:S(2)}, u32[]{:S(2)}) collective-permute-start(bf16[2,1040,256]{2,1,0:T(8,128)(2,1)S(1)} %shard_map.203), channel_id=1, source_target_pairs={{0,1},{1,0},{2,3},{3,2},{4,5},{5,4},{6,7},{7,6},{8,9},{9,8},{10,11... | collective-permute-start | bytes 3194888 | tf_op jit(solution)/shard_map/ppermute | solution.py:40
  24.6 1.6 %collective-permute-done.2 = bf16[256,512]{1,0:T(8,128)(2,1)S(1)} collective-permute-done((bf16[256,512]{1,0:T(8,128)(2,1)S(1)}, bf16[256,512]{1,0:T(8,128)(2,1)S(1)}, u32[]{:S(2)}, u32[]{:S(2)}) %collective-permute-start.2) | collective-permute-done | bytes 262176 | tf_op jit(solution)/shard_map/ppermute | solution.py:35
  26.8 1.1 %pad_maximum_fusion.7.refs_0_ = bf16[3,256,512]{2,1,0:T(8,128)(2,1)S(1)} fusion(bf16[1,256,512]{2,1,0:T(8,128)(2,1)} %bitcast.49, bf16[1,256,512]{2,1,0:T(8,128)(2,1)} %bitcast.48, bf16[1,256,512]{2,1,0:T(8,128)(2,1)S(1)} %bitcast.47), kind=kLoop, calls=%fused_computation.25 | loop fusion | flops 786432 | bytes 1572864 | tf_op jit(solution)/shard_map/stack | solution.py:547
  29.3 1.3 %collective-permute-start.3 = (bf16[256,512]{1,0:T(8,128)(2,1)}, bf16[256,512]{1,0:T(8,128)(2,1)}, u32[]{:S(2)}, u32[]{:S(2)}) collective-permute-start(bf16[256,512]{1,0:T(8,128)(2,1)} %get-tuple-element.39), channel_id=1, source_target_pairs={{0,8},{8,0},{2,10},{10,2},{4,12},{12,4},{6,14},{14,6},{16,24},{24,... | collective-permute-start | bytes 786440 | tf_op jit(solution)/shard_map/ppermute | solution.py:35
  30.9 1.3 %copy.22 = bf16[4096,16]{1,0:T(8,128)(2,1)} copy(bf16[4096,16]{0,1:T(8,128)(2,1)S(1)} %copy-done.9) | data formatting | bytes 262144 | tf_op jit(solution)/shard_map/optimization_barrier | solution.py:514
  33.0 4.1 %collective-permute-done.5 = bf16[256,512]{1,0:T(8,128)(2,1)S(1)} collective-permute-done((bf16[256,512]{1,0:T(8,128)(2,1)}, bf16[256,512]{1,0:T(8,128)(2,1)S(1)}, u32[]{:S(2)}, u32[]{:S(2)}) %collective-permute-start.5) | collective-permute-done | bytes 262176 | tf_op jit(solution)/shard_map/ppermute | solution.py:35
  38.1 1.1 %pad_maximum_fusion.8 = bf16[2,256,512]{2,1,0:T(8,128)(2,1)S(1)} fusion(bf16[1,256,512]{2,1,0:T(8,128)(2,1)} %bitcast.4, bf16[1,256,512]{2,1,0:T(8,128)(2,1)} %bitcast.46), kind=kLoop, calls=%fused_computation.28 | loop fusion | flops 262144 | bytes 1048576 | tf_op jit(solution)/shard_map/stack | solution.py:554
  39.2 1.5 %shard_map.205 = bf16[256,4096]{1,0:T(8,128)(2,1)S(1)} custom-call(s32[8]{0:T(128)S(1)} %broadcast_xor_fusion.places_ref, bf16[3,256,512]{2,1,0:T(8,128)(2,1)S(1)} %pad_maximum_fusion.7.refs_0_, bf16[1,256,512]{2,1,0:T(8,128)(2,1)S(1)} %bitcast.41, bf16[3,256,512]{2,1,0:T(8,128)(2,1)} %collective-permute-done.6.refs_2_, ...), custom_call_target="tpu_custom_call" | custom-call | flops 1000000 | bytes 10000 | tf_op jit(solution)/shard_map/pallas_call | solution.py:72
  41.3 1.3 %fusion.23 = bf16[256,272]{1,0:T(8,128)(2,1)S(1)} fusion(bf16[256,4096]{1,0:T(8,128)(2,1)S(1)} %shard_map.205, bf16[4096,16]{1,0:T(8,128)(2,1)S(1)} %copy-done.5, bf16[4096,256]{1,0:T(8,128)(2,1)S(1)} %copy-done.20), kind=kOutput, calls=%fused_computation.14 | convolution fusion | flops 574951424 | bytes 4464640 | tf_op jit(solution)/shard_map/dot_general | solution.py:562
  42.6 1.1 %collective-permute-start.8 = (bf16[2,256,512]{2,1,0:T(8,128)(2,1)S(1)}, bf16[2,256,512]{2,1,0:T(8,128)(2,1)S(1)}, u32[]{:S(2)}, u32[]{:S(2)}) collective-permute-start(bf16[2,256,512]{2,1,0:T(8,128)(2,1)S(1)} %pad_maximum_fusion.8), channel_id=1, source_target_pairs={{0,4},{4,0},{2,6},{6,2},{8,12},{12,8},{10,14},{14,10},{16,20},{20,... | collective-permute-start | bytes 1572872 | tf_op jit(solution)/shard_map/ppermute | solution.py:35
  43.7 11.2 %fusion.18 = bf16[2,256,1024]{2,1,0:T(8,128)(2,1)S(1)} fusion(bf16[4096,2,1024]{2,1,0:T(2,128)(2,1)} %param.21, bf16[256,4096]{1,0:T(8,128)(2,1)S(1)} %shard_map.205), kind=kOutput, calls=%fused_computation.11 | convolution fusion | flops 4295491584 | bytes 19922944 | tf_op jit(solution)/shard_map/td,dkc->ktc/dot_general | solution.py:564
  56.1 4.7 %collective-permute-start.12 = (bf16[256,272]{1,0:T(8,128)(2,1)S(1)}, bf16[256,272]{1,0:T(8,128)(2,1)S(1)}, u32[]{:S(2)}, u32[]{:S(2)}) collective-permute-start(bf16[256,272]{1,0:T(8,128)(2,1)S(1)} %fusion.23), channel_id=1, source_target_pairs={{0,1},{1,0},{2,3},{3,2},{4,5},{5,4},{6,7},{7,6},{8,9},{9,8},{10,11... | collective-permute-start | bytes 417800 | tf_op jit(solution)/shard_map/ppermute | solution.py:40
  61.0 1.9 %collective-permute-start.14 = (bf16[256,1024]{1,0:T(8,128)(2,1)}, bf16[256,1024]{1,0:T(8,128)(2,1)}, u32[]{:S(2)}, u32[]{:S(2)}) collective-permute-start(bf16[256,1024]{1,0:T(8,128)(2,1)} %get-tuple-element.55), channel_id=1, source_target_pairs={{0,1},{1,0},{2,3},{3,2},{4,5},{5,4},{6,7},{7,6},{8,9},{9,8},{10,11... | collective-permute-start | bytes 1572872 | tf_op jit(solution)/shard_map/ppermute | solution.py:40
  63.6 1.3 %fusion.24.own_ref = bf16[256,272]{1,0:T(8,128)(2,1)S(1)} fusion(bf16[256,4096]{1,0:T(8,128)(2,1)S(1)} %shard_map.206, bf16[4096,16]{1,0:T(8,128)(2,1)S(1)} %copy-done.5, bf16[4096,256]{1,0:T(8,128)(2,1)S(1)} %copy-done.20), kind=kOutput, calls=%fused_computation.15 | convolution fusion | flops 574951424 | bytes 4464640 | tf_op jit(solution)/shard_map/dot_general | solution.py:562
  64.9 12.2 %fusion.8 = f32[2,256,1024]{2,1,0:T(8,128)S(1)} fusion(bf16[4096,2,1024]{2,1,0:T(2,128)(2,1)} %param.21, bf16[256,4096]{1,0:T(8,128)(2,1)S(1)} %shard_map.206), kind=kOutput, calls=%fused_computation.9 | convolution fusion | flops 4294967296 | bytes 20971520 | tf_op jit(solution)/shard_map/td,dkc->ktc/dot_general | solution.py:564
  77.1 1.1 %slice_bitcast_fusion = (f32[256,1024]{1,0:T(8,128)}, f32[256,1024]{1,0:T(8,128)S(1)}) fusion(f32[2,256,1024]{2,1,0:T(8,128)S(1)} %fusion.8), kind=kLoop, calls=%fused_computation.20 | loop fusion | bytes 4194304 | tf_op jit(solution)/shard_map/squeeze | solution.py:565
  78.2 1.7 %shard_map.207 = (bf16[256,256]{1,0:T(8,128)(2,1)S(1)}, f32[4,12,256]{2,1,0:T(8,128)S(1)}, f32[8,16]{1,0:T(8,128)S(1)}) custom-call(s32[8]{0:T(128)S(1)} %pad_add_fusion.ints_ref, bf16[256,272]{1,0:T(8,128)(2,1)S(1)} %fusion.24.own_ref, bf16[256,272]{1,0:T(8,128)(2,1)S(1)} %collective-permute-done.12.refs_0_, f32[2,16,256]{2,1,0:T(8,128)S(1)} %shard_map.204.refs_1_.refs_2_, ...), custom_call_target="tpu_custom_call" | custom-call | flops 1000000 | bytes 10000 | tf_op jit(solution)/shard_map/pallas_call | solution.py:221
  80.0 1.3 %collective-permute-done.13 = bf16[256,256]{1,0:T(8,128)(2,1)S(1)} collective-permute-done((bf16[256,256]{1,0:T(8,128)(2,1)S(1)}, bf16[256,256]{1,0:T(8,128)(2,1)S(1)}, u32[]{:S(2)}, u32[]{:S(2)}) %collective-permute-start.13) | collective-permute-done | bytes 131104 | tf_op jit(solution)/shard_map/ppermute | solution.py:35
  81.5 8.1 %shard_map.208 = (f32[256,1024]{1,0:T(8,128)S(1)}, f32[2,16,64,256]{3,2,1,0:T(8,128)}) custom-call(s32[8]{0:T(128)S(1)} %pad_add_fusion.ints_ref, f32[256,1024]{1,0:T(8,128)S(1)} %get-tuple-element.59.refs_0_, bf16[256,1024]{1,0:T(8,128)(2,1)S(1)} %collective-permute-done.11.refs_1_, f32[2,16,256]{2,1,0:T(8,128)S(1)} %shard_map.204.refs_1_.refs_2_, ...), custom_call_target="tpu_custom_call" | custom-call | flops 1000000 | bytes 10000 | tf_op jit(solution)/shard_map/pallas_call | solution.py:433
  89.5 1.5 %multiply_reduce_fusion = (f32[256]{0:T(256)S(1)}, f32[256,1024]{1,0:T(8,128)S(1)}) fusion(f32[256,1024]{1,0:T(8,128)S(1)} %get-tuple-element.65, f32[256,1024]{1,0:T(8,128)S(1)} %copy-done.4, bf16[256,1024]{1,0:T(8,128)(2,1)} %collective-permute-done.14), kind=kLoop, calls=%fused_computation.23 | loop fusion | flops 2883328 | bytes 3671040 | tf_op jit(solution)/shard_map/reduce_sum | solution.py:609
  (92 shorter events, 13.5 us)
Async XLA Ops:
  0.6 10.0 %collective-permute-start = (bf16[256,512]{1,0:T(8,128)(2,1)}, bf16[256,512]{1,0:T(8,128)(2,1)S(1)}, u32[]{:S(2)}, u32[]{:S(2)}) collective-permute-start(bf16[256,512]{1,0:T(8,128)(2,1)} %param.20), channel_id=1, source_target_pairs={{0,16},{1,0},{2,18},{3,2},{4,20},{5,4},{6,22},{7,6},{8,24},{9,8},{... | collective-permute-start | bytes 786440 | tf_op jit(solution)/shard_map/ppermute | solution.py:91
  4.7 5.9 %collective-permute-start.1 = (bf16[256,512]{1,0:T(8,128)(2,1)}, bf16[256,512]{1,0:T(8,128)(2,1)S(1)}, u32[]{:S(2)}, u32[]{:S(2)}) collective-permute-start(bf16[256,512]{1,0:T(8,128)(2,1)} %param.20), channel_id=1, source_target_pairs={{1,16},{3,18},{5,20},{7,22},{9,24},{11,26},{13,28},{15,30},{16,1},... | collective-permute-start | bytes 786440 | tf_op jit(solution)/shard_map/ppermute | solution.py:90
  9.7 22.5 %copy-start.13 = (f32[4,256]{1,0:T(4,128)S(1)}, f32[4,256]{1,0:T(4,128)}, u32[]{:S(2)}) copy-start(f32[4,256]{1,0:T(4,128)} %param.29) | copy-start | bytes 12292
  9.8 22.5 %copy-start.15 = (f32[256]{0:T(256)S(1)}, f32[256]{0:T(256)}, u32[]{:S(2)}) copy-start(f32[256]{0:T(256)} %param.30) | copy-start | bytes 3076
  9.8 22.5 %copy-start.10 = (f32[1024]{0:T(1024)S(1)}, f32[1024]{0:T(1024)}, u32[]{:S(2)}) copy-start(f32[1024]{0:T(1024)} %param.31) | copy-start | bytes 12292
  9.8 22.5 %copy-start.11 = (f32[4,1024]{1,0:T(4,128)S(1)}, f32[4,1024]{1,0:T(4,128)}, u32[]{:S(2)}) copy-start(f32[4,1024]{1,0:T(4,128)} %param.27) | copy-start | bytes 49156
  9.8 22.5 %copy-start.12 = (f32[1024]{0:T(1024)S(1)}, f32[1024]{0:T(1024)}, u32[]{:S(2)}) copy-start(f32[1024]{0:T(1024)} %param.28) | copy-start | bytes 12292
  9.8 22.5 %copy-start.1 = (bf16[8,3,1024]{2,0,1:T(8,128)(2,1)S(1)}, bf16[8,3,1024]{2,0,1:T(8,128)(2,1)}, u32[]{:S(2)}) copy-start(bf16[8,3,1024]{2,0,1:T(8,128)(2,1)} %param.36) | copy-start | bytes 147460
  9.8 22.5 %copy-start.3 = (bf16[8,3,256]{2,0,1:T(8,128)(2,1)S(1)}, bf16[8,3,256]{2,0,1:T(8,128)(2,1)}, u32[]{:S(2)}) copy-start(bf16[8,3,256]{2,0,1:T(8,128)(2,1)} %param.37) | copy-start | bytes 36868
  9.8 27.3 %copy-start.22 = (s32[8]{0:T(128)S(1)}, s32[8]{0:T(128)}, u32[]{:S(2)}) copy-start(s32[8]{0:T(128)} %constant.95.clone) | copy-start | bytes 100
  11.4 13.2 %collective-permute-start.4 = (bf16[256,512]{1,0:T(8,128)(2,1)S(1)}, bf16[256,512]{1,0:T(8,128)(2,1)S(1)}, u32[]{:S(2)}, u32[]{:S(2)}) collective-permute-start(bf16[256,512]{1,0:T(8,128)(2,1)S(1)} %get-tuple-element.35), channel_id=1, source_target_pairs={{0,4},{4,0},{2,6},{6,2},{8,12},{12,8},{10,14},{14,10},{16,20},{20,... | collective-permute-start | bytes 786440 | tf_op jit(solution)/shard_map/ppermute | solution.py:35
  12.9 13.2 %collective-permute-start.2 = (bf16[256,512]{1,0:T(8,128)(2,1)S(1)}, bf16[256,512]{1,0:T(8,128)(2,1)S(1)}, u32[]{:S(2)}, u32[]{:S(2)}) collective-permute-start(bf16[256,512]{1,0:T(8,128)(2,1)S(1)} %get-tuple-element.35), channel_id=1, source_target_pairs={{0,8},{8,0},{2,10},{10,2},{4,12},{12,4},{6,14},{14,6},{16,24},{24,... | collective-permute-start | bytes 786440 | tf_op jit(solution)/shard_map/ppermute | solution.py:35
  19.9 36.1 %collective-permute-start.9 = (bf16[2,1040,256]{2,1,0:T(8,128)(2,1)S(1)}, bf16[2,1040,256]{2,1,0:T(8,128)(2,1)S(1)}, u32[]{:S(2)}, u32[]{:S(2)}) collective-permute-start(bf16[2,1040,256]{2,1,0:T(8,128)(2,1)S(1)} %shard_map.203), channel_id=1, source_target_pairs={{0,1},{1,0},{2,3},{3,2},{4,5},{5,4},{6,7},{7,6},{8,9},{9,8},{10,11... | collective-permute-start | bytes 3194888 | tf_op jit(solution)/shard_map/ppermute | solution.py:40
  28.0 11.2 %collective-permute-start.6 = (bf16[3,256,512]{2,1,0:T(8,128)(2,1)S(1)}, bf16[3,256,512]{2,1,0:T(8,128)(2,1)}, u32[]{:S(2)}, u32[]{:S(2)}) collective-permute-start(bf16[3,256,512]{2,1,0:T(8,128)(2,1)S(1)} %pad_maximum_fusion.7.refs_0_), channel_id=1, source_target_pairs={{0,2},{2,0},{4,6},{6,4},{8,10},{10,8},{12,14},{14,12},{16,18},{18,... | collective-permute-start | bytes 2359304 | tf_op jit(solution)/shard_map/ppermute | solution.py:35
  28.1 9.0 %collective-permute-start.5 = (bf16[256,512]{1,0:T(8,128)(2,1)}, bf16[256,512]{1,0:T(8,128)(2,1)S(1)}, u32[]{:S(2)}, u32[]{:S(2)}) collective-permute-start(bf16[256,512]{1,0:T(8,128)(2,1)} %copy-done.7), channel_id=1, source_target_pairs={{0,4},{4,0},{2,6},{6,2},{8,12},{12,8},{10,14},{14,10},{16,20},{20,... | collective-permute-start | bytes 786440 | tf_op jit(solution)/shard_map/ppermute | solution.py:35
  29.3 8.7 %collective-permute-start.3 = (bf16[256,512]{1,0:T(8,128)(2,1)}, bf16[256,512]{1,0:T(8,128)(2,1)}, u32[]{:S(2)}, u32[]{:S(2)}) collective-permute-start(bf16[256,512]{1,0:T(8,128)(2,1)} %get-tuple-element.39), channel_id=1, source_target_pairs={{0,8},{8,0},{2,10},{10,2},{4,12},{12,4},{6,14},{14,6},{16,24},{24,... | collective-permute-start | bytes 786440 | tf_op jit(solution)/shard_map/ppermute | solution.py:35
  37.1 2.1 %collective-permute-start.7 = (bf16[1,256,512]{2,1,0:T(8,128)(2,1)S(1)}, bf16[1,256,512]{2,1,0:T(8,128)(2,1)S(1)}, u32[]{:S(2)}, u32[]{:S(2)}) collective-permute-start(bf16[1,256,512]{2,1,0:T(8,128)(2,1)S(1)} %bitcast.40), channel_id=1, source_target_pairs={{0,2},{2,0},{4,6},{6,4},{8,10},{10,8},{12,14},{14,12},{16,18},{18,... | collective-permute-start | bytes 786440 | tf_op jit(solution)/shard_map/ppermute | solution.py:35
  42.6 13.5 %collective-permute-start.8 = (bf16[2,256,512]{2,1,0:T(8,128)(2,1)S(1)}, bf16[2,256,512]{2,1,0:T(8,128)(2,1)S(1)}, u32[]{:S(2)}, u32[]{:S(2)}) collective-permute-start(bf16[2,256,512]{2,1,0:T(8,128)(2,1)S(1)} %pad_maximum_fusion.8), channel_id=1, source_target_pairs={{0,4},{4,0},{2,6},{6,2},{8,12},{12,8},{10,14},{14,10},{16,20},{20,... | collective-permute-start | bytes 1572872 | tf_op jit(solution)/shard_map/ppermute | solution.py:35
  56.1 6.8 %collective-permute-start.10 = (bf16[4,256,512]{2,1,0:T(8,128)(2,1)S(1)}, bf16[4,256,512]{2,1,0:T(8,128)(2,1)S(1)}, u32[]{:S(2)}, u32[]{:S(2)}) collective-permute-start(bf16[4,256,512]{2,1,0:T(8,128)(2,1)S(1)} %constant_dynamic-update-slice_fusion.refs_0_), channel_id=1, source_target_pairs={{0,2},{2,0},{4,6},{6,4},{8,10},{10,8},{12,14},{14,12},{16,18},{18,... | collective-permute-start | bytes 3145736 | tf_op jit(solution)/shard_map/ppermute | solution.py:35
  56.1 22.1 %collective-permute-start.12 = (bf16[256,272]{1,0:T(8,128)(2,1)S(1)}, bf16[256,272]{1,0:T(8,128)(2,1)S(1)}, u32[]{:S(2)}, u32[]{:S(2)}) collective-permute-start(bf16[256,272]{1,0:T(8,128)(2,1)S(1)} %fusion.23), channel_id=1, source_target_pairs={{0,1},{1,0},{2,3},{3,2},{4,5},{5,4},{6,7},{7,6},{8,9},{9,8},{10,11... | collective-permute-start | bytes 417800 | tf_op jit(solution)/shard_map/ppermute | solution.py:40
  60.9 19.1 %collective-permute-start.11 = (bf16[256,1024]{1,0:T(8,128)(2,1)}, bf16[256,1024]{1,0:T(8,128)(2,1)S(1)}, u32[]{:S(2)}, u32[]{:S(2)}) collective-permute-start(bf16[256,1024]{1,0:T(8,128)(2,1)} %get-tuple-element.54), channel_id=1, source_target_pairs={{0,1},{1,0},{2,3},{3,2},{4,5},{5,4},{6,7},{7,6},{8,9},{9,8},{10,11... | collective-permute-start | bytes 1572872 | tf_op jit(solution)/shard_map/ppermute | solution.py:40
  61.0 28.6 %collective-permute-start.14 = (bf16[256,1024]{1,0:T(8,128)(2,1)}, bf16[256,1024]{1,0:T(8,128)(2,1)}, u32[]{:S(2)}, u32[]{:S(2)}) collective-permute-start(bf16[256,1024]{1,0:T(8,128)(2,1)} %get-tuple-element.55), channel_id=1, source_target_pairs={{0,1},{1,0},{2,3},{3,2},{4,5},{5,4},{6,7},{7,6},{8,9},{9,8},{10,11... | collective-permute-start | bytes 1572872 | tf_op jit(solution)/shard_map/ppermute | solution.py:40
  79.9 1.4 %collective-permute-start.13 = (bf16[256,256]{1,0:T(8,128)(2,1)S(1)}, bf16[256,256]{1,0:T(8,128)(2,1)S(1)}, u32[]{:S(2)}, u32[]{:S(2)}) collective-permute-start(bf16[256,256]{1,0:T(8,128)(2,1)S(1)} %get-tuple-element.61), channel_id=1, source_target_pairs={{0,2},{2,0},{4,6},{6,4},{8,10},{10,8},{12,14},{14,12},{16,18},{18,... | collective-permute-start | bytes 393224 | tf_op jit(solution)/shard_map/ppermute | solution.py:35
  91.0 1.2 %collective-permute-start.15 = (f32[256]{0:T(256)S(1)}, f32[256]{0:T(256)S(1)}, u32[]{:S(2)}, u32[]{:S(2)}) collective-permute-start(f32[256]{0:T(256)S(1)} %get-tuple-element.68), channel_id=1, source_target_pairs={{0,2},{2,0},{4,6},{6,4},{8,10},{10,8},{12,14},{14,12},{16,18},{18,... | collective-permute-start | bytes 3080 | tf_op jit(solution)/shard_map/ppermute | solution.py:35
  (15 other events, 158.9 us)

commit v19 on v18

--- a/solution.py
+++ b/solution.py
@@ -544,12 +544,12 @@
         both = partner_2(along_z, "wide", 1)
         own_block = after(own_block, along_z)
         own_z = partner_2(own_block, "wide", 2)
-        near_three = jnp.stack([block, along_z, along_x])
-        core_three = partner_2(near_three, "wide", 0)
+        near_three = [array[None] for array in (block, along_z, along_x)]
+        core_three = [partner_2(array, "wide", 0) for array in near_three]
         both = after(both[None], w_step, const_x, const_bc, ints, own_rows)
-        core_both = partner_2(both, "wide", 0)
+        core_both = after(partner_2(both, "wide", 0), *got_states)
         theirs = quad_arrange(
-            [near_three, both, core_three, core_both], [0, 4, 2, 6, 1, 5, 3, 7]
+            near_three + [both] + core_three + [core_both], [0, 4, 2, 6, 1, 5, 3, 7]
         )
         own_pair = after(jnp.stack([own_block, own_z]), theirs)
         own_got = partner_2(own_pair, "wide", 1)

time: 93.9 us -> 93.7 us (level)
  waiting for transfers between devices: 9.74 us -> 15.5 us
  starting transfers between devices: 28.5 us -> 23.9 us
    ppermute x4, waiting for transfers between devices: 0.01 us -> 4.45 us  [shift_req(): lax.ppermute(block, 'req', [(i, (i + step) % count) for i in range(count)])]
    ppermute x4, starting transfers between devices: 11.4 us -> 9.06 us  [shift_req(): lax.ppermute(block, 'req', [(i, (i + step) % count) for i in range(count)])]
    ppermute x10 -> x12, starting transfers between devices: 12.4 us -> 10.1 us  [partner_2(): return lax.ppermute(block, axis, route)]
    ppermute x10 -> x12, waiting for transfers between devices: 8.93 us -> 11.1 us  [partner_2(): return lax.ppermute(block, axis, route)]
    unnamed x47 -> x41, local copies, waits for them, and re-layouts: 3 us -> 1.64 us
    another operation x1 -> x0, other arithmetic: 1.12 us -> none  [on_device(): near_three = jnp.stack([block, along_z, along_x])]
  transfers between devices with their start and end apart: 16 -> 18, of which waited for: 6 -> 6; matrix products, arithmetic and copies ran while one was open for 36% -> 36% of each run, Pallas kernels for 16% -> 14%
where the time goes in v19:
time: 93.7 us; the launch traced here: 93.2 us
  matrix products  26 us (28%)
  starting transfers between devices  23.9 us (26%)
  waiting for transfers between devices  15.5 us (17%)
  Pallas kernels  14.2 us (15%)
  other arithmetic  6.31 us (7%)
  local copies, waits for them, and re-layouts  6.22 us (7%)
  between operations  1.03 us (1%)
    dot_general x2, matrix products, project(): high = jnp.einsum('td,dkc->ktc', block, w_xz, preferred_element_type=F32)  23.5 us
    ppermute x12, waiting for transfers between devices, partner_2(): return lax.ppermute(block, axis, route)  11.1 us
    ppermute x12, starting transfers between devices, partner_2(): return lax.ppermute(block, axis, route)  10.1 us
    ppermute x4, starting transfers between devices, shift_req(): lax.ppermute(block, 'req', [(i, (i + step) % count) for i in range(count)])  9.06 us
    pallas_call x1, Pallas kernels, mixer(): pl.pallas_call(functools.partial(mixer_kernel, count_req, len(got), per_p...  8.05 us
    ppermute x4, waiting for transfers between devices, shift_req(): lax.ppermute(block, 'req', [(i, (i + step) % count) for i in range(count)])  4.45 us
    ppermute x1, starting transfers between devices, near_blocks(): first = lax.ppermute(x_in, axes, first)  4.09 us
    dot_general x2, matrix products, project(): low = jnp.dot(block, w_map, preferred_element_type=F32).astype(BF16)  2.54 us
  transfers between devices with their start and end apart: 18, of which 6 were waited for; matrix products, arithmetic and copies ran while one was open for 36% of the time, Pallas kernels for 14%

profile of v19, /device:TPU:0, one launch (start us, length us, event | category | flops | bytes accessed | tf_op | source)
XLA Modules:
  0.0 93.2 jit_solution(9759030193961900333)
XLA Ops:
  0.6 4.1 %collective-permute-start = (bf16[256,512]{1,0:T(8,128)(2,1)}, bf16[256,512]{1,0:T(8,128)(2,1)S(1)}, u32[]{:S(2)}, u32[]{:S(2)}) collective-permute-start(bf16[256,512]{1,0:T(8,128)(2,1)} %param.20), channel_id=1, source_target_pairs={{0,16},{1,0},{2,18},{3,2},{4,20},{5,4},{6,22},{7,6},{8,24},{9,8},{... | collective-permute-start | bytes 786440 | tf_op jit(solution)/shard_map/ppermute | solution.py:91
  7.7 2.0 %shard_map.203 = bf16[2,1040,256]{2,1,0:T(8,128)(2,1)S(1)} custom-call(s32[2]{0:T(128)S(1)} %subtract_clamp_fusion.1.slots_ref, f32[8,16,64,256]{3,2,1,0:T(8,128)} %refs_10_.1, bf16[3,8,1024]{2,1,0:T(8,128)(2,1)S(1)} %bitcast.48, bf16[3,8,256]{2,1,0:T(8,128)(2,1)S(1)} %bitcast.50), custom_call_target="tpu_custom_call" | custom-call | bytes 3145728 | tf_op jit(solution)/shard_map/pallas_call | solution.py:274
  9.8 4.5 %collective-permute-start.10 = (bf16[2,1040,256]{2,1,0:T(8,128)(2,1)S(1)}, bf16[2,1040,256]{2,1,0:T(8,128)(2,1)S(1)}, u32[]{:S(2)}, u32[]{:S(2)}) collective-permute-start(bf16[2,1040,256]{2,1,0:T(8,128)(2,1)S(1)} %shard_map.203), channel_id=1, source_target_pairs={{0,1},{1,0},{2,3},{3,2},{4,5},{5,4},{6,7},{7,6},{8,9},{9,8},{10,11... | collective-permute-start | bytes 3194888 | tf_op jit(solution)/shard_map/ppermute | solution.py:40
  15.1 1.5 %collective-permute-start.4 = (bf16[256,512]{1,0:T(8,128)(2,1)S(1)}, bf16[256,512]{1,0:T(8,128)(2,1)S(1)}, u32[]{:S(2)}, u32[]{:S(2)}) collective-permute-start(bf16[256,512]{1,0:T(8,128)(2,1)S(1)} %get-tuple-element.36), channel_id=1, source_target_pairs={{0,4},{4,0},{2,6},{6,2},{8,12},{12,8},{10,14},{14,10},{16,20},{20,... | collective-permute-start | bytes 786440 | tf_op jit(solution)/shard_map/ppermute | solution.py:35
  16.5 3.4 %collective-permute-start.2 = (bf16[256,512]{1,0:T(8,128)(2,1)S(1)}, bf16[256,512]{1,0:T(8,128)(2,1)S(1)}, u32[]{:S(2)}, u32[]{:S(2)}) collective-permute-start(bf16[256,512]{1,0:T(8,128)(2,1)S(1)} %get-tuple-element.36), channel_id=1, source_target_pairs={{0,8},{8,0},{2,10},{10,2},{4,12},{12,4},{6,14},{14,6},{16,24},{24,... | collective-permute-start | bytes 786440 | tf_op jit(solution)/shard_map/ppermute | solution.py:35
  20.0 6.1 %collective-permute-done.2 = bf16[256,512]{1,0:T(8,128)(2,1)S(1)} collective-permute-done((bf16[256,512]{1,0:T(8,128)(2,1)S(1)}, bf16[256,512]{1,0:T(8,128)(2,1)S(1)}, u32[]{:S(2)}, u32[]{:S(2)}) %collective-permute-start.2) | collective-permute-done | bytes 262176 | tf_op jit(solution)/shard_map/ppermute | solution.py:35
  26.1 1.7 %collective-permute-start.3 = (bf16[256,512]{1,0:T(8,128)(2,1)}, bf16[256,512]{1,0:T(8,128)(2,1)}, u32[]{:S(2)}, u32[]{:S(2)}) collective-permute-start(bf16[256,512]{1,0:T(8,128)(2,1)} %get-tuple-element.40), channel_id=1, source_target_pairs={{0,8},{8,0},{2,10},{10,2},{4,12},{12,4},{6,14},{14,6},{16,24},{24,... | collective-permute-start | bytes 786440 | tf_op jit(solution)/shard_map/ppermute | solution.py:35
  28.8 2.2 %copy.22 = bf16[4096,16]{1,0:T(8,128)(2,1)} copy(bf16[4096,16]{0,1:T(8,128)(2,1)} %param.22) | data formatting | bytes 262144 | tf_op jit(solution)/shard_map/optimization_barrier | solution.py:514
  32.4 2.3 %collective-permute-done.5 = bf16[256,512]{1,0:T(8,128)(2,1)S(1)} collective-permute-done((bf16[256,512]{1,0:T(8,128)(2,1)S(1)}, bf16[256,512]{1,0:T(8,128)(2,1)S(1)}, u32[]{:S(2)}, u32[]{:S(2)}) %collective-permute-start.5) | collective-permute-done | bytes 262176 | tf_op jit(solution)/shard_map/ppermute | solution.py:35
  35.2 1.1 %pad_maximum_fusion.7 = bf16[2,256,512]{2,1,0:T(8,128)(2,1)S(1)} fusion(bf16[1,256,512]{2,1,0:T(8,128)(2,1)} %bitcast.4, bf16[1,256,512]{2,1,0:T(8,128)(2,1)} %bitcast.3), kind=kLoop, calls=%fused_computation.27 | loop fusion | flops 262144 | bytes 1048576 | tf_op jit(solution)/shard_map/stack | solution.py:554
  36.6 4.4 %collective-permute-done.10.refs_2_.refs_3_.refs_11_ = bf16[2,1040,256]{2,1,0:T(8,128)(2,1)S(1)} collective-permute-done((bf16[2,1040,256]{2,1,0:T(8,128)(2,1)S(1)}, bf16[2,1040,256]{2,1,0:T(8,128)(2,1)S(1)}, u32[]{:S(2)}, u32[]{:S(2)}) %collective-permute-start.10) | collective-permute-done | bytes 1064992 | tf_op jit(solution)/shard_map/ppermute | solution.py:40
  41.0 1.1 %shard_map.205 = bf16[256,4096]{1,0:T(8,128)(2,1)S(1)} custom-call(s32[8]{0:T(128)S(1)} %broadcast_xor_fusion.places_ref, bf16[1,256,512]{2,1,0:T(8,128)(2,1)S(1)} %bitcast.41, bf16[1,256,512]{2,1,0:T(8,128)(2,1)S(1)} %bitcast.45, bf16[1,256,512]{2,1,0:T(8,128)(2,1)S(1)} %bitcast.43, bf16[1,256,512]{2,1,0:T(8,128)(2,1)S(1)} %bitcast.47, ...), custom_call_target="tpu_custom_call" | custom-call | flops 1000000 | bytes 10000 | tf_op jit(solution)/shard_map/pallas_call | solution.py:72
  42.2 1.3 %fusion.23 = bf16[256,272]{1,0:T(8,128)(2,1)S(1)} fusion(bf16[256,4096]{1,0:T(8,128)(2,1)S(1)} %shard_map.205, bf16[4096,16]{1,0:T(8,128)(2,1)S(1)} %copy-done.5, bf16[4096,256]{1,0:T(8,128)(2,1)S(1)} %copy-done.17), kind=kOutput, calls=%fused_computation.14 | convolution fusion | flops 574951424 | bytes 4464640 | tf_op jit(solution)/shard_map/dot_general | solution.py:562
  43.4 1.6 %collective-permute-start.11 = (bf16[2,256,512]{2,1,0:T(8,128)(2,1)S(1)}, bf16[2,256,512]{2,1,0:T(8,128)(2,1)S(1)}, u32[]{:S(2)}, u32[]{:S(2)}) collective-permute-start(bf16[2,256,512]{2,1,0:T(8,128)(2,1)S(1)} %pad_maximum_fusion.7), channel_id=1, source_target_pairs={{0,4},{4,0},{2,6},{6,2},{8,12},{12,8},{10,14},{14,10},{16,20},{20,... | collective-permute-start | bytes 1572872 | tf_op jit(solution)/shard_map/ppermute | solution.py:35
  45.0 11.3 %fusion.18 = bf16[2,256,1024]{2,1,0:T(8,128)(2,1)S(1)} fusion(bf16[4096,2,1024]{2,1,0:T(2,128)(2,1)} %param.21, bf16[256,4096]{1,0:T(8,128)(2,1)S(1)} %shard_map.205), kind=kOutput, calls=%fused_computation.11 | convolution fusion | flops 4295491584 | bytes 19922944 | tf_op jit(solution)/shard_map/td,dkc->ktc/dot_general | solution.py:564
  57.3 2.5 %collective-permute-start.14 = (bf16[256,272]{1,0:T(8,128)(2,1)S(1)}, bf16[256,272]{1,0:T(8,128)(2,1)S(1)}, u32[]{:S(2)}, u32[]{:S(2)}) collective-permute-start(bf16[256,272]{1,0:T(8,128)(2,1)S(1)} %fusion.23), channel_id=1, source_target_pairs={{0,1},{1,0},{2,3},{3,2},{4,5},{5,4},{6,7},{7,6},{8,9},{9,8},{10,11... | collective-permute-start | bytes 417800 | tf_op jit(solution)/shard_map/ppermute | solution.py:40
  59.9 1.9 %collective-permute-start.16 = (bf16[256,1024]{1,0:T(8,128)(2,1)}, bf16[256,1024]{1,0:T(8,128)(2,1)}, u32[]{:S(2)}, u32[]{:S(2)}) collective-permute-start(bf16[256,1024]{1,0:T(8,128)(2,1)} %get-tuple-element.57), channel_id=1, source_target_pairs={{0,1},{1,0},{2,3},{3,2},{4,5},{5,4},{6,7},{7,6},{8,9},{9,8},{10,11... | collective-permute-start | bytes 1572872 | tf_op jit(solution)/shard_map/ppermute | solution.py:40
  62.6 1.3 %fusion.24.own_ref = bf16[256,272]{1,0:T(8,128)(2,1)S(1)} fusion(bf16[256,4096]{1,0:T(8,128)(2,1)S(1)} %shard_map.206, bf16[4096,16]{1,0:T(8,128)(2,1)S(1)} %copy-done.5, bf16[4096,256]{1,0:T(8,128)(2,1)S(1)} %copy-done.17), kind=kOutput, calls=%fused_computation.15 | convolution fusion | flops 574951424 | bytes 4464640 | tf_op jit(solution)/shard_map/dot_general | solution.py:562
  63.9 12.2 %fusion.8 = f32[2,256,1024]{2,1,0:T(8,128)S(1)} fusion(bf16[4096,2,1024]{2,1,0:T(2,128)(2,1)} %param.21, bf16[256,4096]{1,0:T(8,128)(2,1)S(1)} %shard_map.206), kind=kOutput, calls=%fused_computation.9 | convolution fusion | flops 4294967296 | bytes 20971520 | tf_op jit(solution)/shard_map/td,dkc->ktc/dot_general | solution.py:564
  76.1 1.1 %slice_bitcast_fusion = (f32[256,1024]{1,0:T(8,128)}, f32[256,1024]{1,0:T(8,128)S(1)}) fusion(f32[2,256,1024]{2,1,0:T(8,128)S(1)} %fusion.8), kind=kLoop, calls=%fused_computation.20 | loop fusion | bytes 4194304 | tf_op jit(solution)/shard_map/squeeze | solution.py:565
  77.2 1.7 %shard_map.207 = (bf16[256,256]{1,0:T(8,128)(2,1)S(1)}, f32[4,12,256]{2,1,0:T(8,128)S(1)}, f32[8,16]{1,0:T(8,128)S(1)}) custom-call(s32[8]{0:T(128)S(1)} %pad_add_fusion.ints_ref, bf16[256,272]{1,0:T(8,128)(2,1)S(1)} %fusion.24.own_ref, bf16[256,272]{1,0:T(8,128)(2,1)S(1)} %collective-permute-done.14.refs_0_, f32[2,16,256]{2,1,0:T(8,128)S(1)} %shard_map.204.refs_1_.refs_2_, ...), custom_call_target="tpu_custom_call" | custom-call | flops 1000000 | bytes 10000 | tf_op jit(solution)/shard_map/pallas_call | solution.py:221
  79.0 1.4 %collective-permute-done.15 = bf16[256,256]{1,0:T(8,128)(2,1)} collective-permute-done((bf16[256,256]{1,0:T(8,128)(2,1)S(1)}, bf16[256,256]{1,0:T(8,128)(2,1)}, u32[]{:S(2)}, u32[]{:S(2)}) %collective-permute-start.15) | collective-permute-done | bytes 131104 | tf_op jit(solution)/shard_map/ppermute | solution.py:35
  81.5 8.1 %shard_map.208 = (f32[256,1024]{1,0:T(8,128)S(1)}, f32[2,16,64,256]{3,2,1,0:T(8,128)}) custom-call(s32[8]{0:T(128)S(1)} %pad_add_fusion.ints_ref, f32[256,1024]{1,0:T(8,128)S(1)} %get-tuple-element.61.refs_0_, bf16[256,1024]{1,0:T(8,128)(2,1)S(1)} %collective-permute-done.13.refs_1_, f32[2,16,256]{2,1,0:T(8,128)S(1)} %shard_map.204.refs_1_.refs_2_, ...), custom_call_target="tpu_custom_call" | custom-call | flops 1000000 | bytes 10000 | tf_op jit(solution)/shard_map/pallas_call | solution.py:433
  89.6 1.5 %multiply_reduce_fusion = (f32[256]{0:T(256)S(1)}, f32[256,1024]{1,0:T(8,128)S(1)}) fusion(f32[256,1024]{1,0:T(8,128)S(1)} %get-tuple-element.67, f32[256,1024]{1,0:T(8,128)S(1)} %copy-done.4, bf16[256,1024]{1,0:T(8,128)(2,1)} %collective-permute-done.16), kind=kLoop, calls=%fused_computation.23 | loop fusion | flops 2883328 | bytes 3671040 | tf_op jit(solution)/shard_map/reduce_sum | solution.py:609
  (89 shorter events, 12.0 us)
Async XLA Ops:
  0.6 13.7 %collective-permute-start = (bf16[256,512]{1,0:T(8,128)(2,1)}, bf16[256,512]{1,0:T(8,128)(2,1)S(1)}, u32[]{:S(2)}, u32[]{:S(2)}) collective-permute-start(bf16[256,512]{1,0:T(8,128)(2,1)} %param.20), channel_id=1, source_target_pairs={{0,16},{1,0},{2,18},{3,2},{4,20},{5,4},{6,22},{7,6},{8,24},{9,8},{... | collective-permute-start | bytes 786440 | tf_op jit(solution)/shard_map/ppermute | solution.py:91
  4.7 9.6 %collective-permute-start.1 = (bf16[256,512]{1,0:T(8,128)(2,1)}, bf16[256,512]{1,0:T(8,128)(2,1)S(1)}, u32[]{:S(2)}, u32[]{:S(2)}) collective-permute-start(bf16[256,512]{1,0:T(8,128)(2,1)} %param.20), channel_id=1, source_target_pairs={{1,16},{3,18},{5,20},{7,22},{9,24},{11,26},{13,28},{15,30},{16,1},... | collective-permute-start | bytes 786440 | tf_op jit(solution)/shard_map/ppermute | solution.py:90
  9.7 21.3 %copy-start.7 = (f32[1024]{0:T(1024)S(1)}, f32[1024]{0:T(1024)}, u32[]{:S(2)}) copy-start(f32[1024]{0:T(1024)} %param.31) | copy-start | bytes 12292
  9.7 21.3 %copy-start.8 = (f32[4,1024]{1,0:T(4,128)S(1)}, f32[4,1024]{1,0:T(4,128)}, u32[]{:S(2)}) copy-start(f32[4,1024]{1,0:T(4,128)} %param.27) | copy-start | bytes 49156
  9.8 21.3 %copy-start.16 = (s32[1,2]{1,0:T(1,128)S(1)}, s32[1,2]{1,0:T(1,128)}, u32[]{:S(2)}) copy-start(s32[1,2]{1,0:T(1,128)} %param.32) | copy-start | bytes 28
  9.8 21.4 %copy-start.1 = (bf16[8,3,1024]{2,0,1:T(8,128)(2,1)S(1)}, bf16[8,3,1024]{2,0,1:T(8,128)(2,1)}, u32[]{:S(2)}) copy-start(bf16[8,3,1024]{2,0,1:T(8,128)(2,1)} %param.36) | copy-start | bytes 147460
  9.8 21.4 %copy-start.3 = (bf16[8,3,256]{2,0,1:T(8,128)(2,1)S(1)}, bf16[8,3,256]{2,0,1:T(8,128)(2,1)}, u32[]{:S(2)}) copy-start(bf16[8,3,256]{2,0,1:T(8,128)(2,1)} %param.37) | copy-start | bytes 36868
  9.8 25.4 %copy-start.19 = (s32[8]{0:T(128)S(1)}, s32[8]{0:T(128)}, u32[]{:S(2)}) copy-start(s32[8]{0:T(128)} %constant.95.clone) | copy-start | bytes 100
  9.8 31.2 %collective-permute-start.10 = (bf16[2,1040,256]{2,1,0:T(8,128)(2,1)S(1)}, bf16[2,1040,256]{2,1,0:T(8,128)(2,1)S(1)}, u32[]{:S(2)}, u32[]{:S(2)}) collective-permute-start(bf16[2,1040,256]{2,1,0:T(8,128)(2,1)S(1)} %shard_map.203), channel_id=1, source_target_pairs={{0,1},{1,0},{2,3},{3,2},{4,5},{5,4},{6,7},{7,6},{8,9},{9,8},{10,11... | collective-permute-start | bytes 3194888 | tf_op jit(solution)/shard_map/ppermute | solution.py:40
  15.1 16.8 %collective-permute-start.4 = (bf16[256,512]{1,0:T(8,128)(2,1)S(1)}, bf16[256,512]{1,0:T(8,128)(2,1)S(1)}, u32[]{:S(2)}, u32[]{:S(2)}) collective-permute-start(bf16[256,512]{1,0:T(8,128)(2,1)S(1)} %get-tuple-element.36), channel_id=1, source_target_pairs={{0,4},{4,0},{2,6},{6,2},{8,12},{12,8},{10,14},{14,10},{16,20},{20,... | collective-permute-start | bytes 786440 | tf_op jit(solution)/shard_map/ppermute | solution.py:35
  16.5 9.6 %collective-permute-start.2 = (bf16[256,512]{1,0:T(8,128)(2,1)S(1)}, bf16[256,512]{1,0:T(8,128)(2,1)S(1)}, u32[]{:S(2)}, u32[]{:S(2)}) collective-permute-start(bf16[256,512]{1,0:T(8,128)(2,1)S(1)} %get-tuple-element.36), channel_id=1, source_target_pairs={{0,8},{8,0},{2,10},{10,2},{4,12},{12,4},{6,14},{14,6},{16,24},{24,... | collective-permute-start | bytes 786440 | tf_op jit(solution)/shard_map/ppermute | solution.py:35
  26.1 8.5 %collective-permute-start.3 = (bf16[256,512]{1,0:T(8,128)(2,1)}, bf16[256,512]{1,0:T(8,128)(2,1)}, u32[]{:S(2)}, u32[]{:S(2)}) collective-permute-start(bf16[256,512]{1,0:T(8,128)(2,1)} %get-tuple-element.40), channel_id=1, source_target_pairs={{0,8},{8,0},{2,10},{10,2},{4,12},{12,4},{6,14},{14,6},{16,24},{24,... | collective-permute-start | bytes 786440 | tf_op jit(solution)/shard_map/ppermute | solution.py:35
  27.9 6.8 %collective-permute-start.5 = (bf16[256,512]{1,0:T(8,128)(2,1)S(1)}, bf16[256,512]{1,0:T(8,128)(2,1)S(1)}, u32[]{:S(2)}, u32[]{:S(2)}) collective-permute-start(bf16[256,512]{1,0:T(8,128)(2,1)S(1)} %collective-permute-done.2), channel_id=1, source_target_pairs={{0,4},{4,0},{2,6},{6,2},{8,12},{12,8},{10,14},{14,10},{16,20},{20,... | collective-permute-start | bytes 786440 | tf_op jit(solution)/shard_map/ppermute | solution.py:35
  28.8 12.3 %collective-permute-start.6 = (bf16[1,256,512]{2,1,0:T(8,128)(2,1)S(1)}, bf16[1,256,512]{2,1,0:T(8,128)(2,1)}, u32[]{:S(2)}, u32[]{:S(2)}) collective-permute-start(bf16[1,256,512]{2,1,0:T(8,128)(2,1)S(1)} %bitcast.40), channel_id=1, source_target_pairs={{0,2},{2,0},{4,6},{6,4},{8,10},{10,8},{12,14},{14,12},{16,18},{18,... | collective-permute-start | bytes 786440 | tf_op jit(solution)/shard_map/ppermute | solution.py:35
  31.8 9.2 %collective-permute-start.8 = (bf16[1,256,512]{2,1,0:T(8,128)(2,1)S(1)}, bf16[1,256,512]{2,1,0:T(8,128)(2,1)S(1)}, u32[]{:S(2)}, u32[]{:S(2)}) collective-permute-start(bf16[1,256,512]{2,1,0:T(8,128)(2,1)S(1)} %bitcast.42), channel_id=1, source_target_pairs={{0,2},{2,0},{4,6},{6,4},{8,10},{10,8},{12,14},{14,12},{16,18},{18,... | collective-permute-start | bytes 786440 | tf_op jit(solution)/shard_map/ppermute | solution.py:35
  34.7 6.4 %collective-permute-start.7 = (bf16[1,256,512]{2,1,0:T(8,128)(2,1)S(1)}, bf16[1,256,512]{2,1,0:T(8,128)(2,1)S(1)}, u32[]{:S(2)}, u32[]{:S(2)}) collective-permute-start(bf16[1,256,512]{2,1,0:T(8,128)(2,1)S(1)} %bitcast.44), channel_id=1, source_target_pairs={{0,2},{2,0},{4,6},{6,4},{8,10},{10,8},{12,14},{14,12},{16,18},{18,... | collective-permute-start | bytes 786440 | tf_op jit(solution)/shard_map/ppermute | solution.py:35
  34.7 1.9 %collective-permute-start.9 = (bf16[1,256,512]{2,1,0:T(8,128)(2,1)S(1)}, bf16[1,256,512]{2,1,0:T(8,128)(2,1)S(1)}, u32[]{:S(2)}, u32[]{:S(2)}) collective-permute-start(bf16[1,256,512]{2,1,0:T(8,128)(2,1)S(1)} %bitcast.46), channel_id=1, source_target_pairs={{0,2},{2,0},{4,6},{6,4},{8,10},{10,8},{12,14},{14,12},{16,18},{18,... | collective-permute-start | bytes 786440 | tf_op jit(solution)/shard_map/ppermute | solution.py:35
  43.4 13.7 %collective-permute-start.11 = (bf16[2,256,512]{2,1,0:T(8,128)(2,1)S(1)}, bf16[2,256,512]{2,1,0:T(8,128)(2,1)S(1)}, u32[]{:S(2)}, u32[]{:S(2)}) collective-permute-start(bf16[2,256,512]{2,1,0:T(8,128)(2,1)S(1)} %pad_maximum_fusion.7), channel_id=1, source_target_pairs={{0,4},{4,0},{2,6},{6,2},{8,12},{12,8},{10,14},{14,10},{16,20},{20,... | collective-permute-start | bytes 1572872 | tf_op jit(solution)/shard_map/ppermute | solution.py:35
  57.2 4.6 %collective-permute-start.12 = (bf16[4,256,512]{2,1,0:T(8,128)(2,1)S(1)}, bf16[4,256,512]{2,1,0:T(8,128)(2,1)S(1)}, u32[]{:S(2)}, u32[]{:S(2)}) collective-permute-start(bf16[4,256,512]{2,1,0:T(8,128)(2,1)S(1)} %constant_dynamic-update-slice_fusion.refs_0_), channel_id=1, source_target_pairs={{0,2},{2,0},{4,6},{6,4},{8,10},{10,8},{12,14},{14,12},{16,18},{18,... | collective-permute-start | bytes 3145736 | tf_op jit(solution)/shard_map/ppermute | solution.py:35
  57.3 19.9 %collective-permute-start.14 = (bf16[256,272]{1,0:T(8,128)(2,1)S(1)}, bf16[256,272]{1,0:T(8,128)(2,1)S(1)}, u32[]{:S(2)}, u32[]{:S(2)}) collective-permute-start(bf16[256,272]{1,0:T(8,128)(2,1)S(1)} %fusion.23), channel_id=1, source_target_pairs={{0,1},{1,0},{2,3},{3,2},{4,5},{5,4},{6,7},{7,6},{8,9},{9,8},{10,11... | collective-permute-start | bytes 417800 | tf_op jit(solution)/shard_map/ppermute | solution.py:40
  59.8 19.1 %collective-permute-start.13 = (bf16[256,1024]{1,0:T(8,128)(2,1)S(1)}, bf16[256,1024]{1,0:T(8,128)(2,1)S(1)}, u32[]{:S(2)}, u32[]{:S(2)}) collective-permute-start(bf16[256,1024]{1,0:T(8,128)(2,1)S(1)} %get-tuple-element.56), channel_id=1, source_target_pairs={{0,1},{1,0},{2,3},{3,2},{4,5},{5,4},{6,7},{7,6},{8,9},{9,8},{10,11... | collective-permute-start | bytes 1572872 | tf_op jit(solution)/shard_map/ppermute | solution.py:40
  59.9 29.6 %collective-permute-start.16 = (bf16[256,1024]{1,0:T(8,128)(2,1)}, bf16[256,1024]{1,0:T(8,128)(2,1)}, u32[]{:S(2)}, u32[]{:S(2)}) collective-permute-start(bf16[256,1024]{1,0:T(8,128)(2,1)} %get-tuple-element.57), channel_id=1, source_target_pairs={{0,1},{1,0},{2,3},{3,2},{4,5},{5,4},{6,7},{7,6},{8,9},{9,8},{10,11... | collective-permute-start | bytes 1572872 | tf_op jit(solution)/shard_map/ppermute | solution.py:40
  78.9 1.5 %collective-permute-start.15 = (bf16[256,256]{1,0:T(8,128)(2,1)S(1)}, bf16[256,256]{1,0:T(8,128)(2,1)}, u32[]{:S(2)}, u32[]{:S(2)}) collective-permute-start(bf16[256,256]{1,0:T(8,128)(2,1)S(1)} %get-tuple-element.63), channel_id=1, source_target_pairs={{0,2},{2,0},{4,6},{6,4},{8,10},{10,8},{12,14},{14,12},{16,18},{18,... | collective-permute-start | bytes 393224 | tf_op jit(solution)/shard_map/ppermute | solution.py:35
  91.1 1.2 %collective-permute-start.17 = (f32[256]{0:T(256)S(1)}, f32[256]{0:T(256)S(1)}, u32[]{:S(2)}, u32[]{:S(2)}) collective-permute-start(f32[256]{0:T(256)S(1)} %get-tuple-element.70), channel_id=1, source_target_pairs={{0,2},{2,0},{4,6},{6,4},{8,10},{10,8},{12,14},{14,12},{16,18},{18,... | collective-permute-start | bytes 3080 | tf_op jit(solution)/shard_map/ppermute | solution.py:35
  (14 other events, 179.3 us)
